TPU v7x, 32 devices: a whole 2x2x4 slice. The times are simulated.
32 devices in a mesh: dp: 8 (over z, core), fsdp: 4 (over y, x).
Axes of the slice: x: 2, y: 2, z: 4, core: 2. Of those that a mesh axis runs over, the one named last changes fastest.
Arguments:
- tokens: bfloat16 [4096, 768], P(('dp', 'fsdp')), may hold values from -6 to 6
- lengths: int32 [32, 4], P(('dp', 'fsdp')), may hold values from 0 to 128, as said below
- ln_attn_gain: bfloat16 [768], P(('dp', 'fsdp')), may hold values from 0.25 to 1.75
- ln_attn_bias: bfloat16 [768], P(('dp', 'fsdp')), may hold values from -3 to 3
- ln_mlp_gain: bfloat16 [768], P(('dp', 'fsdp')), may hold values from 0.25 to 1.75
- ln_mlp_bias: bfloat16 [768], P(('dp', 'fsdp')), may hold values from -3 to 3
- w_qkv: bfloat16 [768, 2304], P(('dp', 'fsdp')), may hold values from -0.21875 to 0.21875
- b_qkv: bfloat16 [2304], P(('dp', 'fsdp')), may hold values from -3 to 3
- w_out: bfloat16 [768, 768], P(('dp', 'fsdp')), may hold values from -0.875 to 0.875
- b_out: bfloat16 [768], P(('dp', 'fsdp')), may hold values from -3 to 3
- w_fc1: bfloat16 [768, 3072], P(('dp', 'fsdp')), may hold values from -0.21875 to 0.21875
- b_fc1: bfloat16 [3072], P(('dp', 'fsdp')), may hold values from -3 to 3
- w_fc2: bfloat16 [3072, 768], P(('dp', 'fsdp')), may hold values from -0.21875 to 0.21875
- b_fc2: bfloat16 [768], P(('dp', 'fsdp')), may hold values from -3 to 3
- cotangent: bfloat16 [4096, 768], P(('dp', 'fsdp')), may hold values from -6 to 6
Outputs:
- output: bfloat16 [4096, 768], P(('dp', 'fsdp'))
- grad_tokens: float32 [4096, 768], P(('dp', 'fsdp'))
- grad_ln_attn_gain: float32 [768], P(('dp', 'fsdp'))
- grad_ln_attn_bias: float32 [768], P(('dp', 'fsdp'))
- grad_ln_mlp_gain: float32 [768], P(('dp', 'fsdp'))
- grad_ln_mlp_bias: float32 [768], P(('dp', 'fsdp'))
- grad_w_qkv: float32 [768, 2304], P(('dp', 'fsdp'))
- grad_b_qkv: float32 [2304], P(('dp', 'fsdp'))
- grad_w_out: float32 [768, 768], P(('dp', 'fsdp'))
- grad_b_out: float32 [768], P(('dp', 'fsdp'))
- grad_w_fc1: float32 [768, 3072], P(('dp', 'fsdp'))
- grad_b_fc1: float32 [3072], P(('dp', 'fsdp'))
- grad_w_fc2: float32 [3072, 768], P(('dp', 'fsdp'))
- grad_b_fc2: float32 [768], P(('dp', 'fsdp'))
Inputs may be any that keep to these rules, and one draw needn't show every extreme that they name: `lengths`: row d lists the sequences packed from the first row of device d in slot order, 0 for an unused slot; each row sums to at most 128; in every draw one device holds a single sequence of 128 tokens.
All inputs are finite; a program needn't handle non-finite values.
Results may differ from a plain program's by a relative error of at most 0.0092.
Values may be sent and summed in bfloat16 or wider, within the bound.
No kernel may reach another device: no remote copies, remote signals or barrier semaphores. Data moves between devices by JAX's collectives and lax.ppermute only.
A program may use at most 192 MiB of HBM per device.

v0:
```python
import math

import jax
import jax.numpy as jnp
from jax import lax
from jax.sharding import PartitionSpec as P

HEADS = 12
HEAD = 64
ROT = 16


epsilon = 1e-05
neg_large = -1e30
inv_sqrt_two = 1.0 / math.sqrt(2.0)
inv_sqrt_tau = 1.0 / math.sqrt(2.0 * math.pi)


def layout(seq_lengths, row_count):
    row_index = jnp.arange(row_count, dtype=jnp.int32)
    slot_count = seq_lengths.shape[0]
    ends = jnp.cumsum(seq_lengths)
    starts = ends - seq_lengths
    segment = jnp.sum((row_index[:, None] >= ends[None, :]).astype(jnp.int32), axis=1)
    live_rows = row_index < ends[-1]
    unique_seg = jnp.where(live_rows, segment, slot_count + row_index)
    slot_index = jnp.arange(slot_count, dtype=jnp.int32)
    first_row = jnp.sum(
        jnp.where(segment[:, None] == slot_index[None, :], starts[None, :], 0), axis=1
    )
    position = jnp.where(live_rows, row_index - first_row, 0)
    attn_mask = (unique_seg[:, None] == unique_seg[None, :]) & (
        row_index[None, :] <= row_index[:, None]
    )
    half_rot = ROT // 2
    inverse_freq = 10000.0 ** (-(2.0 * jnp.arange(half_rot, dtype=jnp.float32)) / ROT)
    angle = position.astype(jnp.float32)[:, None] * inverse_freq[None, :]
    return (
        live_rows.astype(jnp.float32),
        attn_mask,
        jnp.cos(angle)[:, None, :],
        jnp.sin(angle)[:, None, :],
    )


def layer_normalize(values_in, gain_vector, shift_vector):
    center = jnp.mean(values_in, axis=-1, keepdims=True)
    mean_removed_input = values_in - center
    variance = jnp.mean(mean_removed_input * mean_removed_input, axis=-1, keepdims=True)
    reciprocal_deviation = lax.rsqrt(variance + epsilon)
    normalized_input = mean_removed_input * reciprocal_deviation
    return (normalized_input * gain_vector + shift_vector, normalized_input, reciprocal_deviation)


def norm_backward_rule(norm_gradient, gain_vector, normalized_input, reciprocal_deviation):
    normalized_gradient = norm_gradient * gain_vector
    mean_correction = jnp.mean(normalized_gradient, axis=-1, keepdims=True)
    projection_correction = jnp.mean(normalized_gradient * normalized_input, axis=-1, keepdims=True)
    input_gradient = reciprocal_deviation * (
        normalized_gradient - mean_correction - normalized_input * projection_correction
    )
    return (
        input_gradient,
        jnp.sum(norm_gradient * normalized_input, axis=0),
        jnp.sum(norm_gradient, axis=0),
    )


def rotate(part, cosine, sine):
    half_rot = ROT // 2
    first = part[..., :half_rot]
    second = part[..., half_rot:ROT]
    return jnp.concatenate(
        [first * cosine - second * sine, second * cosine + first * sine, part[..., ROT:]], axis=-1
    )


def unrotate(part, cosine, sine):
    half_rot = ROT // 2
    first = part[..., :half_rot]
    second = part[..., half_rot:ROT]
    return jnp.concatenate(
        [first * cosine + second * sine, second * cosine - first * sine, part[..., ROT:]], axis=-1
    )


def contract(left, right, left_dim, right_dim):
    return lax.dot_general(
        left, right, (((left_dim,), (right_dim,)), ((), ())), preferred_element_type=jnp.float32
    )


def masked_scores(q_low, k_low, attn_mask):
    scores = jnp.einsum("qhd,khd->hqk", q_low, k_low, preferred_element_type=jnp.float32) * 0.125
    return jnp.where(attn_mask[None], scores, neg_large)


def local(
    tokens,
    lengths,
    ln_attn_gain,
    ln_attn_bias,
    ln_mlp_gain,
    ln_mlp_bias,
    w_qkv,
    b_qkv,
    w_out,
    b_out,
    w_fc1,
    b_fc1,
    w_fc2,
    b_fc2,
    cotangent,
):
    gathered = (
        lax.all_gather(ln_attn_gain, ("dp", "fsdp"), axis=0, tiled=True),
        lax.all_gather(ln_attn_bias, ("dp", "fsdp"), axis=0, tiled=True),
        lax.all_gather(ln_mlp_gain, ("dp", "fsdp"), axis=0, tiled=True),
        lax.all_gather(ln_mlp_bias, ("dp", "fsdp"), axis=0, tiled=True),
        lax.all_gather(w_qkv, ("dp", "fsdp"), axis=0, tiled=True),
        lax.all_gather(b_qkv, ("dp", "fsdp"), axis=0, tiled=True),
        lax.all_gather(w_out, ("dp", "fsdp"), axis=0, tiled=True),
        lax.all_gather(b_out, ("dp", "fsdp"), axis=0, tiled=True),
        lax.all_gather(w_fc1, ("dp", "fsdp"), axis=0, tiled=True),
        lax.all_gather(b_fc1, ("dp", "fsdp"), axis=0, tiled=True),
        lax.all_gather(w_fc2, ("dp", "fsdp"), axis=0, tiled=True),
        lax.all_gather(b_fc2, ("dp", "fsdp"), axis=0, tiled=True),
    )
    (
        gain_one,
        bias_one,
        gain_two,
        bias_two,
        full_qkv,
        full_qkv_bias,
        full_out,
        full_out_bias,
        full_up,
        full_up_bias,
        full_down,
        full_down_bias,
    ) = gathered
    row_count = tokens.shape[0]
    model_width = tokens.shape[1]
    live_rows, attn_mask, cosine, sine = layout(lengths[0], row_count)
    resid = tokens.astype(jnp.float32)
    first_norm_output, first_normalized_input, first_reciprocal_scale = layer_normalize(
        resid, gain_one.astype(jnp.float32), bias_one.astype(jnp.float32)
    )
    second_norm_output, second_normalized_input, second_reciprocal_scale = layer_normalize(
        resid, gain_two.astype(jnp.float32), bias_two.astype(jnp.float32)
    )
    low_one = first_norm_output.astype(jnp.bfloat16)
    low_two = second_norm_output.astype(jnp.bfloat16)
    qkv = jnp.dot(low_one, full_qkv, preferred_element_type=jnp.float32) + full_qkv_bias.astype(
        jnp.float32
    )
    query_rows = qkv[:, :model_width].reshape(row_count, HEADS, HEAD)
    key_rows = qkv[:, model_width : 2 * model_width].reshape(row_count, HEADS, HEAD)
    value_rows = qkv[:, 2 * model_width :].reshape(row_count, HEADS, HEAD)
    q_low = rotate(query_rows, cosine, sine).astype(jnp.bfloat16)
    k_low = rotate(key_rows, cosine, sine).astype(jnp.bfloat16)
    v_low = value_rows.astype(jnp.bfloat16)
    scores = masked_scores(q_low, k_low, attn_mask)
    row_peak = jnp.max(scores, axis=-1, keepdims=True)
    exponent = jnp.exp(scores - row_peak)
    row_total = jnp.sum(exponent, axis=-1, keepdims=True)
    probs = exponent / row_total
    log_total = row_peak + jnp.log(row_total)
    mixed = jnp.einsum(
        "hqk,khd->qhd", probs.astype(jnp.bfloat16), v_low, preferred_element_type=jnp.float32
    )
    mixed_low = mixed.reshape(row_count, model_width).astype(jnp.bfloat16)
    attn_branch = jnp.dot(
        mixed_low, full_out, preferred_element_type=jnp.float32
    ) + full_out_bias.astype(jnp.float32)
    up_rows = jnp.dot(low_two, full_up, preferred_element_type=jnp.float32) + full_up_bias.astype(
        jnp.float32
    )
    act_low = jax.nn.gelu(up_rows, approximate=False).astype(jnp.bfloat16)
    mlp_branch = jnp.dot(
        act_low, full_down, preferred_element_type=jnp.float32
    ) + full_down_bias.astype(jnp.float32)
    output = (live_rows[:, None] * (resid + attn_branch + mlp_branch)).astype(jnp.bfloat16)
    first_gain_cotangent, second_gain_cotangent, back_qkv, back_out, back_up, back_down = (
        lax.all_gather(ln_attn_gain, ("dp", "fsdp"), axis=0, tiled=True),
        lax.all_gather(ln_mlp_gain, ("dp", "fsdp"), axis=0, tiled=True),
        lax.all_gather(w_qkv, ("dp", "fsdp"), axis=0, tiled=True),
        lax.all_gather(w_out, ("dp", "fsdp"), axis=0, tiled=True),
        lax.all_gather(w_fc1, ("dp", "fsdp"), axis=0, tiled=True),
        lax.all_gather(w_fc2, ("dp", "fsdp"), axis=0, tiled=True),
    )
    upstream = cotangent.astype(jnp.float32) * live_rows[:, None]
    upstream_low = upstream.astype(jnp.bfloat16)
    grad_down = contract(act_low, upstream_low, 0, 0)
    grad_branch_bias = jnp.sum(upstream, axis=0)
    d_act = contract(upstream_low, back_down, 1, 1)
    slope = (
        0.5 * (1.0 + lax.erf(up_rows * inv_sqrt_two))
        + up_rows * jnp.exp(-0.5 * up_rows * up_rows) * inv_sqrt_tau
    )
    d_up_low = (d_act * slope).astype(jnp.bfloat16)
    grad_up = contract(low_two, d_up_low, 0, 0)
    grad_up_bias = jnp.sum(d_up_low.astype(jnp.float32), axis=0)
    second_norm_gradient = contract(d_up_low, back_up, 1, 1)
    dx_two, grad_gain_two, grad_bias_two = norm_backward_rule(
        second_norm_gradient,
        second_gain_cotangent.astype(jnp.float32),
        second_normalized_input,
        second_reciprocal_scale,
    )
    grad_out = contract(mixed_low, upstream_low, 0, 0)
    d_mixed = (
        contract(upstream_low, back_out, 1, 1).astype(jnp.bfloat16).reshape(row_count, HEADS, HEAD)
    )
    probs_again = jnp.exp(masked_scores(q_low, k_low, attn_mask) - log_total)
    d_probs = jnp.einsum("qhd,khd->hqk", d_mixed, v_low, preferred_element_type=jnp.float32)
    d_values = jnp.einsum(
        "hqk,qhd->khd",
        probs_again.astype(jnp.bfloat16),
        d_mixed,
        preferred_element_type=jnp.float32,
    )
    row_delta = jnp.sum(probs_again * d_probs, axis=-1, keepdims=True)
    d_scores = (probs_again * (d_probs - row_delta)).astype(jnp.bfloat16)
    d_query = (
        jnp.einsum("hqk,khd->qhd", d_scores, k_low, preferred_element_type=jnp.float32) * 0.125
    )
    d_keys = jnp.einsum("hqk,qhd->khd", d_scores, q_low, preferred_element_type=jnp.float32) * 0.125
    d_query = unrotate(d_query, cosine, sine).reshape(row_count, model_width)
    d_keys = unrotate(d_keys, cosine, sine).reshape(row_count, model_width)
    d_qkv_low = jnp.concatenate(
        [d_query, d_keys, d_values.reshape(row_count, model_width)], axis=1
    ).astype(jnp.bfloat16)
    grad_qkv = contract(low_one, d_qkv_low, 0, 0)
    grad_qkv_bias = jnp.sum(d_qkv_low.astype(jnp.float32), axis=0)
    first_norm_gradient = contract(d_qkv_low, back_qkv, 1, 1)
    dx_one, grad_gain_one, grad_bias_one = norm_backward_rule(
        first_norm_gradient,
        first_gain_cotangent.astype(jnp.float32),
        first_normalized_input,
        first_reciprocal_scale,
    )
    grad_tokens = upstream + dx_one + dx_two
    (
        shard_gain_one,
        shard_bias_one,
        shard_gain_two,
        shard_bias_two,
        shard_qkv,
        shard_qkv_bias,
        shard_out,
        shard_branch_bias,
        shard_up,
        shard_up_bias,
        shard_down,
    ) = (
        lax.psum_scatter(grad_gain_one, ("dp", "fsdp"), scatter_dimension=0, tiled=True),
        lax.psum_scatter(grad_bias_one, ("dp", "fsdp"), scatter_dimension=0, tiled=True),
        lax.psum_scatter(grad_gain_two, ("dp", "fsdp"), scatter_dimension=0, tiled=True),
        lax.psum_scatter(grad_bias_two, ("dp", "fsdp"), scatter_dimension=0, tiled=True),
        lax.psum_scatter(grad_qkv, ("dp", "fsdp"), scatter_dimension=0, tiled=True),
        lax.psum_scatter(grad_qkv_bias, ("dp", "fsdp"), scatter_dimension=0, tiled=True),
        lax.psum_scatter(grad_out, ("dp", "fsdp"), scatter_dimension=0, tiled=True),
        lax.psum_scatter(grad_branch_bias, ("dp", "fsdp"), scatter_dimension=0, tiled=True),
        lax.psum_scatter(grad_up, ("dp", "fsdp"), scatter_dimension=0, tiled=True),
        lax.psum_scatter(grad_up_bias, ("dp", "fsdp"), scatter_dimension=0, tiled=True),
        lax.psum_scatter(grad_down, ("dp", "fsdp"), scatter_dimension=0, tiled=True),
    )
    return (
        output,
        grad_tokens,
        shard_gain_one,
        shard_bias_one,
        shard_gain_two,
        shard_bias_two,
        shard_qkv,
        shard_qkv_bias,
        shard_out,
        shard_branch_bias,
        shard_up,
        shard_up_bias,
        shard_down,
        shard_branch_bias,
    )


def solution(mesh):
    return jax.shard_map(
        local,
        mesh=mesh,
        in_specs=(
            P(("dp", "fsdp"), None),
            P(("dp", "fsdp"), None),
            P(("dp", "fsdp")),
            P(("dp", "fsdp")),
            P(("dp", "fsdp")),
            P(("dp", "fsdp")),
            P(("dp", "fsdp"), None),
            P(("dp", "fsdp")),
            P(("dp", "fsdp"), None),
            P(("dp", "fsdp")),
            P(("dp", "fsdp"), None),
            P(("dp", "fsdp")),
            P(("dp", "fsdp"), None),
            P(("dp", "fsdp")),
            P(("dp", "fsdp"), None),
        ),
        out_specs=(
            P(("dp", "fsdp"), None),
            P(("dp", "fsdp"), None),
            P(("dp", "fsdp")),
            P(("dp", "fsdp")),
            P(("dp", "fsdp")),
            P(("dp", "fsdp")),
            P(("dp", "fsdp"), None),
            P(("dp", "fsdp")),
            P(("dp", "fsdp"), None),
            P(("dp", "fsdp")),
            P(("dp", "fsdp"), None),
            P(("dp", "fsdp")),
            P(("dp", "fsdp"), None),
            P(("dp", "fsdp")),
        ),
        check_vma=False,
    )
```

profile of v0, /device:TPU:0, one launch (start us, length us, event | category | flops | bytes accessed | tf_op | source)
XLA Modules:
  0.0 780.0 jit_solution(3444944322095371591)
XLA Ops:
  7.2 0.7 all-gather.5.cloned.1.call-update
  8.0 0.7 all-gather.7.cloned.1.call-update
  8.7 0.7 all-gather.9.cloned.1.call-update
  10.0 0.8 reduce-window.4
  10.9 0.6 slice.54
  11.4 0.8 dynamic-update-slice
  12.3 0.8 dynamic-update-slice.1
  13.1 0.8 dynamic-update-slice.7
  13.9 0.8 dynamic-update-slice.4
  14.8 0.8 dynamic-update-slice.5
  15.6 0.8 dynamic-update-slice.3
  16.5 0.8 dynamic-update-slice.2
  17.3 0.8 dynamic-update-slice.6
  18.1 42.6 %all-reduce.16 = (bf16[3072]{0:T(1024)(128)(2,1)S(1)}, bf16[768]{0:T(1024)(128)(2,1)S(1)}, bf16[768]{0:T(1024)(128)(2,1)S(1)}, bf16[768]{0:T(1024)(128)(2,1)S(1)...) all-reduce(bf16[3072]{0:T(1024)(128)(2,1)S(1)} %dynamic-update-slic, ...), channel_id=1, replica_groups=mesh['dp'=8,'fsdp'=4] {'dp','fsdp'}, use_global_device_ids=true, to_apply=%add.6 | all-reduce | flops 9984 | bytes 39936
  60.8 0.7 fusion.55
  61.5 0.7 fusion.54
  62.2 1.0 convert_reduce_fusion.2
  63.3 1.1 fusion.48
  64.4 0.7 select_convert_fusion
  65.3 8.7 %all-gather.5.cloned.1.call-done = bf16[768,2304]{1,0:T(8,128)(2,1)} async-done(((bf16[24,2304]{1,0:T(8,128)(2,1)}), bf16[768,2304]{1,0:T(8,128)(2,1)}) %all-gather.5.cloned.1.call-update) | async-done | bytes 3538960 | tf_op jit(solution)/shard_map/all_gather | solution.py:120
  74.0 2.8 convolution_add_fusion
  78.3 0.7 copy-done.3
  78.9 1.9 fusion.68
  80.9 48.9 %all-gather.7.cloned.1.call-done = bf16[768,768]{1,0:T(8,128)(2,1)} async-done(((bf16[24,768]{1,0:T(8,128)(2,1)}), bf16[768,768]{1,0:T(8,128)(2,1)}) %all-gather.7.cloned.1.call-update) | async-done | bytes 1179664 | tf_op jit(solution)/shard_map/all_gather | solution.py:122
  129.8 1.8 convolution_convert_fusion.1
  133.6 4.1 fusion.62
  138.0 57.2 %all-gather.9.cloned.1.call-done = bf16[768,3072]{1,0:T(8,128)(2,1)} async-done(((bf16[24,3072]{1,0:T(8,128)(2,1)}), bf16[768,3072]{1,0:T(8,128)(2,1)}) %all-gather.9.cloned.1.call-update) | async-done | bytes 4718608 | tf_op jit(solution)/shard_map/all_gather | solution.py:124
  195.2 7.6 fusion.3
  202.8 57.6 %all-gather.11.cloned.1.call-done = bf16[3072,768]{1,0:T(8,128)(2,1)} async-done(((bf16[96,768]{1,0:T(8,128)(2,1)}), bf16[3072,768]{1,0:T(8,128)(2,1)}) %all-gather.11.cloned.1.call-update) | async-done | bytes 4718608 | tf_op jit(solution)/shard_map/all_gather | solution.py:126
  260.3 4.6 convert_reduce_fusion
  264.9 5.1 fusion.59
  270.1 5.1 fusion.66
  275.5 4.2 fusion.74
  279.7 1.5 fusion.46
  281.3 1.1 fusion.51
  282.4 40.5 %all-reduce.15 = (f32[768]{0:T(1024)S(1)}, f32[768]{0:T(1024)S(1)}, f32[768]{0:T(1024)S(1)}, f32[768]{0:T(1024)S(1)}, f32[2304]{0:T(1024)S(1)}, /*index=5*/f32[768]{0:T(1024)S(1)}, f32[3072]{0:T(1024)S(1)}) all-reduce(f32[768]{0:T(1024)S(1)} %get-tuple-element.16, ...), channel_id=2, replica_groups=mesh['dp'=8,'fsdp'=4] {'dp','fsdp'}, use_global_device_ids=true, to_apply=%region_13.14.clone | all-reduce | flops 9216 | bytes 73728
  322.9 0.6 dynamic-slice
  323.6 0.6 dynamic-slice.1
  324.2 0.6 dynamic-slice.2
  324.8 0.6 dynamic-slice.3
  325.3 0.6 dynamic-slice.6
  325.9 0.6 dynamic-slice.4
  326.5 3.2 convolution_add_fusion.3
  329.8 1.1 fusion.21
  330.8 33.3 %reduce-scatter.7.cloned.1.call-done = f32[24,768]{1,0:T(8,128)} async-done(((f32[768,768]{1,0:T(8,128)}), f32[24,768]{1,0:T(8,128)}) %reduce-scatter.7.cloned.1.call-update) | async-done | bytes 73744 | tf_op jit(solution)/shard_map/reduce_scatter | solution.py:264
  364.1 125.3 %reduce-scatter.5.cloned.1.call-done = f32[24,2304]{1,0:T(8,128)} async-done(((f32[768,2304]{1,0:T(8,128)}), f32[24,2304]{1,0:T(8,128)}) %reduce-scatter.5.cloned.1.call-update) | async-done | bytes 221200 | tf_op jit(solution)/shard_map/reduce_scatter | solution.py:262
  489.4 141.2 %reduce-scatter.9.cloned.1.call-done = f32[24,3072]{1,0:T(8,128)} async-done(((f32[768,3072]{1,0:T(8,128)}), f32[24,3072]{1,0:T(8,128)}) %reduce-scatter.9.cloned.1.call-update) | async-done | bytes 294928 | tf_op jit(solution)/shard_map/reduce_scatter | solution.py:266
  630.6 142.1 %reduce-scatter.11.cloned.1.call-done = f32[96,768]{1,0:T(8,128)} async-done(((f32[3072,768]{1,0:T(8,128)}), f32[96,768]{1,0:T(8,128)}) %reduce-scatter.11.cloned.1.call-update) | async-done | bytes 294928 | tf_op jit(solution)/shard_map/reduce_scatter | solution.py:268
  (75 shorter events, 5.7 us)
Async XLA Ops:
  7.2 66.8 %all-gather.5.cloned.1.call-start = ((), (), s32[]{:S(2)}) async-start(), calls=%async_computation.4 | async-start | bytes 3649536 | tf_op jit(solution)/shard_map/all_gather | solution.py:120
  7.9 121.8 %all-gather.7.cloned.1.call-start = ((), (), s32[]{:S(2)}) async-start(), calls=%async_computation.5 | async-start | bytes 1216512 | tf_op jit(solution)/shard_map/all_gather | solution.py:122
  8.7 186.5 %all-gather.9.cloned.1.call-start = ((), (), s32[]{:S(2)}) async-start(), calls=%async_computation.6 | async-start | bytes 4866048 | tf_op jit(solution)/shard_map/all_gather | solution.py:124
  9.4 250.9 %all-gather.11.cloned.1.call-start = ((), (), s32[]{:S(2)}) async-start(), calls=%async_computation.7 | async-start | bytes 4866048 | tf_op jit(solution)/shard_map/all_gather | solution.py:126
  10.0 354.1 %reduce-scatter.7.cloned.1.call-start = ((), (), s32[]{:S(2)}) async-start(), calls=%async_computation.9 | async-start | bytes 2433024 | tf_op jit(solution)/shard_map/reduce_scatter | solution.py:264
  78.0 0.9 copy-start.3
  80.8 408.6 %reduce-scatter.5.cloned.1.call-start = ((), (), s32[]{:S(2)}) async-start(), calls=%async_computation.8 | async-start | bytes 7299072 | tf_op jit(solution)/shard_map/reduce_scatter | solution.py:262
  132.7 0.9 copy-start
  137.7 492.9 %reduce-scatter.9.cloned.1.call-start = ((), (), s32[]{:S(2)}) async-start(), calls=%async_computation.10 | async-start | bytes 9732096 | tf_op jit(solution)/shard_map/reduce_scatter | solution.py:266
  270.0 502.6 %reduce-scatter.11.cloned.1.call-start = ((), (), s32[]{:S(2)}) async-start(), calls=%async_computation.11 | async-start | bytes 9732096 | tf_op jit(solution)/shard_map/reduce_scatter | solution.py:268
  275.5 4.3 copy-start.2
  323.6 449.1 %copy-start.4 = (f32[24]{0:T(128)}, f32[24]{0:T(128)S(1)}, u32[]{:S(2)}) copy-start(f32[24]{0:T(128)S(1)} %dynamic-slice.5) | copy-start | bytes 292
  326.5 3.2 copy-start.1
Sparse Core Ops, SparseCore 0:
  10.9 63.0 all-gather.4
  76.9 52.8 all-gather.6
  132.7 62.4 all-gather.8
  197.9 62.3 all-gather.10
  266.0 98.0 reduce-scatter.6
  371.2 118.1 reduce-scatter.4
  495.9 134.6 reduce-scatter.8
  638.1 134.5 reduce-scatter.10
where the time goes:
time: 781 us; the launch traced here: 780 us
  waiting for transfers between devices  617 us (79%)
  blocking collectives  83.1 us (11%)
  matrix products  45 us (6%)
  between operations  14.5 us (2%)
  local copies, waits for them, and re-layouts  13 us (2%)
    reduce_scatter x1, waiting for transfers between devices, local(): lax.psum_scatter(grad_down, ('dp', 'fsdp'), scatter_dimension=0, tiled=True)  142 us
    reduce_scatter x1, waiting for transfers between devices, local(): lax.psum_scatter(grad_up, ('dp', 'fsdp'), scatter_dimension=0, tiled=True)  141 us
    reduce_scatter x1, waiting for transfers between devices, local(): lax.psum_scatter(grad_qkv, ('dp', 'fsdp'), scatter_dimension=0, tiled=True)  125 us
    unnamed x2, blocking collectives  83.1 us
    all_gather x1, waiting for transfers between devices, local(): lax.all_gather(w_fc2, ('dp', 'fsdp'), axis=0, tiled=True)  57.6 us
    all_gather x1, waiting for transfers between devices, local(): lax.all_gather(w_fc1, ('dp', 'fsdp'), axis=0, tiled=True)  57.2 us
    all_gather x1, waiting for transfers between devices, local(): lax.all_gather(w_out, ('dp', 'fsdp'), axis=0, tiled=True)  48.9 us
    reduce_scatter x1, waiting for transfers between devices, local(): lax.psum_scatter(grad_out, ('dp', 'fsdp'), scatter_dimension=0, tiled=True)  33.3 us
  transfers between devices with their start and end apart: 8, of which 8 were waited for; matrix products, arithmetic and copies ran while one was open for 8% of the time, Pallas kernels for 0%

commit v1 on v0

v1 whole, which is shorter than its diff:
```python
import math

import jax
import jax.numpy as jnp
from jax import lax
from jax.sharding import Mesh
from jax.sharding import PartitionSpec as P

HEADS = 12
HEAD = 64
ROT = 16
TP = 4
BF = jnp.bfloat16
F32 = jnp.float32

epsilon = 1e-05
neg_large = -1e30
inv_sqrt_two = 1.0 / math.sqrt(2.0)
inv_sqrt_tau = 1.0 / math.sqrt(2.0 * math.pi)


def xor_pairs(count, bit):
    return [(i, i ^ bit) for i in range(count)]


def pick(array, index, axis=0):
    return lax.dynamic_index_in_dim(array, index, axis, keepdims=False)


def unxor(slots, rank):
    bit = 1
    while bit < len(slots):
        flip = (rank & bit) != 0
        slots = [jnp.where(flip, slots[k ^ bit], slots[k]) for k in range(len(slots))]
        bit *= 2
    return slots


def gather_t(block, rank):
    one = lax.ppermute(block, "t", xor_pairs(TP, 1))
    two = lax.ppermute(block, "t", xor_pairs(TP, 2))
    near = lax.ppermute(block, "t", [(1, 2), (2, 1)])
    far = lax.ppermute(two, "t", [(2, 3), (1, 0)])
    middle = (rank == 1) | (rank == 2)
    return [block, one, two, jnp.where(middle, near, far)]


def scatter_t(slots):
    low = [slot.astype(BF) for slot in slots]
    one = lax.ppermute(low[1], "t", xor_pairs(TP, 1))
    near = lax.ppermute(low[3], "t", [(1, 2), (2, 1)])
    relay = lax.ppermute(low[3], "t", [(0, 1), (3, 2)])
    two = lax.ppermute((slots[2] + relay.astype(F32)).astype(BF), "t", xor_pairs(TP, 2))
    return slots[0] + one.astype(F32) + near.astype(F32) + two.astype(F32)


def exchange_t(pieces):
    return [pieces[0]] + [
        lax.ppermute(pieces[k], "t", xor_pairs(TP, k)) for k in range(1, TP)
    ]


def gather_q(block, rank, sizes):
    if sizes != (2, 4):
        return lax.all_gather(block, ("dq", "fsdp"), axis=0, tiled=False)
    half = block.shape[0] // 2
    one = lax.ppermute(block, "fsdp", xor_pairs(4, 1))
    two = lax.ppermute(block, "fsdp", xor_pairs(4, 2))
    upper = lax.ppermute(one[:half], "fsdp", xor_pairs(4, 2))
    lower = lax.ppermute(two[half:], "fsdp", xor_pairs(4, 1))
    three = jnp.concatenate([upper, lower], axis=0)
    mine = [block, one, two, three]
    other = [lax.ppermute(part, "dq", xor_pairs(2, 1)) for part in mine]
    return jnp.stack(unxor(mine + other, rank))


def scatter_q(blocks, rank, sizes):
    if sizes != (2, 4):
        return lax.psum_scatter(
            blocks.astype(BF), ("dq", "fsdp"), scatter_dimension=0, tiled=False
        ).astype(F32)
    core, spot = rank // 4, rank % 4
    halves = blocks.reshape((2, 4) + blocks.shape[1:])
    keep = pick(halves, core)
    send = pick(halves, 1 - core).astype(BF)
    pair = keep + lax.ppermute(send, "dq", xor_pairs(2, 1)).astype(F32)
    mine, one, two, three = [pick(pair, spot ^ k) for k in range(4)]
    half = mine.shape[0] // 2
    three = three.astype(BF)
    upper = lax.ppermute(three[:half], "fsdp", xor_pairs(4, 1))
    lower = lax.ppermute(three[half:], "fsdp", xor_pairs(4, 2))
    two = jnp.concatenate([two[:half] + upper.astype(F32), two[half:]], axis=0)
    one = jnp.concatenate([one[:half], one[half:] + lower.astype(F32)], axis=0)
    one = lax.ppermute(one.astype(BF), "fsdp", xor_pairs(4, 1))
    two = lax.ppermute(two.astype(BF), "fsdp", xor_pairs(4, 2))
    return mine + one.astype(F32) + two.astype(F32)


def layout(seq_lengths, row_count):
    row_index = jnp.arange(row_count, dtype=jnp.int32)
    slot_count = seq_lengths.shape[0]
    ends = jnp.cumsum(seq_lengths)
    starts = ends - seq_lengths
    segment = jnp.sum((row_index[:, None] >= ends[None, :]).astype(jnp.int32), axis=1)
    live_rows = row_index < ends[-1]
    unique_seg = jnp.where(live_rows, segment, slot_count + row_index)
    slot_index = jnp.arange(slot_count, dtype=jnp.int32)
    first_row = jnp.sum(
        jnp.where(segment[:, None] == slot_index[None, :], starts[None, :], 0), axis=1
    )
    position = jnp.where(live_rows, row_index - first_row, 0)
    attn_mask = (unique_seg[:, None] == unique_seg[None, :]) & (
        row_index[None, :] <= row_index[:, None]
    )
    half_rot = ROT // 2
    inverse_freq = 10000.0 ** (-(2.0 * jnp.arange(half_rot, dtype=jnp.float32)) / ROT)
    angle = position.astype(jnp.float32)[:, None] * inverse_freq[None, :]
    return (
        live_rows.astype(jnp.float32),
        attn_mask,
        jnp.cos(angle)[:, None, :],
        jnp.sin(angle)[:, None, :],
    )


def rotate(part, cosine, sine):
    half_rot = ROT // 2
    first = part[..., :half_rot]
    second = part[..., half_rot:ROT]
    return jnp.concatenate(
        [first * cosine - second * sine, second * cosine + first * sine, part[..., ROT:]], axis=-1
    )


def contract(left, right, left_dim, right_dim):
    return lax.dot_general(
        left, right, (((left_dim,), (right_dim,)), ((), ())), preferred_element_type=F32
    )


def local(
    sizes,
    tokens,
    lengths,
    ln_attn_gain,
    ln_attn_bias,
    ln_mlp_gain,
    ln_mlp_bias,
    w_qkv,
    b_qkv,
    w_out,
    b_out,
    w_fc1,
    b_fc1,
    w_fc2,
    b_fc2,
    cotangent,
):
    t = lax.axis_index("t")
    q = lax.axis_index("dq") * sizes[1] + lax.axis_index("fsdp")
    qs = sizes[0] * sizes[1]
    rows, width = tokens.shape
    shard = w_qkv.shape[0]
    part = width // TP
    hidden = w_fc1.shape[1] // TP
    units = w_fc2.shape[0]
    heads = HEADS // TP

    vectors = jnp.concatenate(
        [
            item.reshape(shard, -1)
            for item in (
                ln_attn_gain, ln_attn_bias, ln_mlp_gain, ln_mlp_bias, b_qkv, b_out, b_fc1, b_fc2
            )
        ],
        axis=1,
    )
    n_vec = vectors.shape[1]
    low_lengths = jnp.broadcast_to(lengths.astype(BF), (shard, lengths.shape[1]))
    small = jnp.concatenate([vectors, low_lengths], axis=1)
    qkv_parts = w_qkv.reshape(shard, 3, TP, part)
    fc1_parts = w_fc1.reshape(shard, TP, hidden)
    pieces = [
        jnp.concatenate(
            [
                pick(qkv_parts, t ^ k, 2).reshape(shard, 3 * part),
                small,
                pick(fc1_parts, t ^ k, 1),
            ],
            axis=1,
        )
        for k in range(TP)
    ]
    pieces = exchange_t(pieces)
    at = 3 * part
    group_lengths = [piece[0, at + n_vec : at + n_vec + 4].astype(jnp.int32) for piece in pieces]
    mine = jnp.stack(unxor(pieces, t))
    columns = gather_q(mine, q, sizes)
    columns = columns.transpose(1, 0, 2, 3).reshape(width, -1)
    mat_qkv = columns[:, : 3 * part]
    vecs = columns[:, at : at + n_vec].astype(F32)
    mat_up = columns[:, at + small.shape[1] :]
    tail = gather_q(jnp.concatenate([w_fc2, w_out], axis=0), q, sizes)
    mat_down = tail[:, :units].reshape(qs * units, width)
    mat_out = tail[:, units:].reshape(part, width)

    vecs_t = vecs.T
    gain_one, bias_one, gain_two, bias_two = vecs_t[0], vecs_t[1], vecs_t[2], vecs_t[3]
    all_b_qkv = vecs[:, 4:7].reshape(3, TP, part)
    vec_qkv = pick(all_b_qkv, t, 1).reshape(3 * part)
    vec_out = vecs_t[7]
    vec_up = pick(vecs[:, 8:12].reshape(TP, hidden), t)
    vec_down = vecs_t[12]

    token_slots = gather_t(tokens, t)
    upstream_slots = gather_t(cotangent, t)
    layouts = [layout(item, rows) for item in group_lengths]
    live = jnp.concatenate([item[0] for item in layouts])[:, None]
    attn_mask = jnp.stack([item[1] for item in layouts])[:, None]
    cosine = jnp.concatenate([item[2] for item in layouts])
    sine = jnp.concatenate([item[3] for item in layouts])
    resid = jnp.concatenate(token_slots).astype(F32)
    upstream_low = jnp.concatenate(upstream_slots) * live.astype(BF)

    center = jnp.mean(resid, axis=-1, keepdims=True)
    removed = resid - center
    rstd = lax.rsqrt(jnp.mean(removed * removed, axis=-1, keepdims=True) + epsilon)
    xhat = removed * rstd
    low_one = (xhat * gain_one + bias_one).astype(BF)
    low_two = (xhat * gain_two + bias_two).astype(BF)

    up_rows = contract(low_two, mat_up, 1, 0) + vec_up
    phi = 0.5 * (1.0 + lax.erf(up_rows * inv_sqrt_two))
    act_low = (up_rows * phi).astype(BF)
    slope = phi + up_rows * jnp.exp(-0.5 * up_rows * up_rows) * inv_sqrt_tau
    mlp_share = contract(act_low, mat_down, 1, 0)
    grad_down = contract(act_low, upstream_low, 0, 0)
    d_up_low = (contract(upstream_low, mat_down, 1, 1) * slope).astype(BF)
    grad_up = contract(low_two, d_up_low, 0, 0)
    grad_up_bias = jnp.sum(d_up_low.astype(F32), axis=0)
    d_h2 = contract(d_up_low, mat_up, 1, 1)

    count = TP * rows
    qkv = (contract(low_one, mat_qkv, 1, 0) + vec_qkv).reshape(count, 3, heads, HEAD)
    q_low = rotate(qkv[:, 0], cosine, sine).astype(BF).reshape(TP, rows, heads, HEAD)
    k_low = rotate(qkv[:, 1], cosine, sine).astype(BF).reshape(TP, rows, heads, HEAD)
    v_low = qkv[:, 2].astype(BF).reshape(TP, rows, heads, HEAD)
    scores = jnp.einsum("gqhd,gkhd->ghqk", q_low, k_low, preferred_element_type=F32) * 0.125
    scores = jnp.where(attn_mask, scores, neg_large)
    exponent = jnp.exp(scores - jnp.max(scores, axis=-1, keepdims=True))
    probs = exponent / jnp.sum(exponent, axis=-1, keepdims=True)
    probs_low = probs.astype(BF)
    mixed = jnp.einsum("ghqk,gkhd->gqhd", probs_low, v_low, preferred_element_type=F32)
    mixed_low = mixed.reshape(count, part).astype(BF)
    out_share = (mlp_share + contract(mixed_low, mat_out, 1, 0)).reshape(TP, rows, width)
    out_sum = scatter_t([out_share[k] for k in range(TP)])
    output = live[:rows] * (resid[:rows] + out_sum + vec_out + vec_down)

    grad_out = contract(mixed_low, upstream_low, 0, 0)
    d_mixed = contract(upstream_low, mat_out, 1, 1).astype(BF).reshape(TP, rows, heads, HEAD)
    d_probs = jnp.einsum("gqhd,gkhd->ghqk", d_mixed, v_low, preferred_element_type=F32)
    d_values = jnp.einsum("ghqk,gqhd->gkhd", probs_low, d_mixed, preferred_element_type=F32)
    delta = jnp.sum(probs * d_probs, axis=-1, keepdims=True)
    d_scores = (probs * (d_probs - delta)).astype(BF)
    d_query = jnp.einsum("ghqk,gkhd->gqhd", d_scores, k_low, preferred_element_type=F32) * 0.125
    d_keys = jnp.einsum("ghqk,gqhd->gkhd", d_scores, q_low, preferred_element_type=F32) * 0.125
    d_query = rotate(d_query.reshape(count, heads, HEAD), cosine, -sine).reshape(count, part)
    d_keys = rotate(d_keys.reshape(count, heads, HEAD), cosine, -sine).reshape(count, part)
    d_qkv = jnp.concatenate([d_query, d_keys, d_values.reshape(count, part)], axis=1).astype(BF)
    grad_qkv = contract(low_one, d_qkv, 0, 0)
    grad_qkv_bias = jnp.sum(d_qkv.astype(F32), axis=0)
    d_h1 = contract(d_qkv, mat_qkv, 1, 1)

    e_share = (d_h1 * gain_one + d_h2 * gain_two).reshape(TP, rows, width)
    e_sum = scatter_t([e_share[k] for k in range(TP)])
    own_xhat = xhat[:rows]
    dx = rstd[:rows] * (
        e_sum
        - jnp.mean(e_sum, axis=-1, keepdims=True)
        - own_xhat * jnp.mean(e_sum * own_xhat, axis=-1, keepdims=True)
    )
    own_upstream = upstream_low[:rows].astype(F32)
    grad_tokens = own_upstream + dx

    zero_qkv = jnp.zeros((3, TP, part), F32)
    full_b_qkv = lax.dynamic_update_index_in_dim(
        zero_qkv, grad_qkv_bias.reshape(3, 1, part), t, 1
    ).reshape(width, 3)
    zero_up = jnp.zeros((TP, hidden), F32)
    full_b_up = lax.dynamic_update_index_in_dim(zero_up, grad_up_bias[None], t, 0).reshape(width, 4)
    lanes = jnp.stack(
        [
            jnp.sum(d_h1 * xhat, axis=0),
            jnp.sum(d_h1, axis=0),
            jnp.sum(d_h2 * xhat, axis=0),
            jnp.sum(d_h2, axis=0),
            jnp.sum(own_upstream, axis=0),
        ],
        axis=1,
    )
    vec_grads = jnp.concatenate([lanes, full_b_qkv, full_b_up], axis=1)

    tail_grads = jnp.concatenate(
        [grad_down.reshape(qs, units, width), grad_out.reshape(qs, shard, width)], axis=1
    )
    tail_sum = scatter_q(tail_grads, q, sizes)
    shard_down, shard_out = tail_sum[:units], tail_sum[units:]
    column_grads = jnp.concatenate([grad_qkv, vec_grads, grad_up], axis=1)
    column_grads = column_grads.reshape(TP, qs, shard, -1).transpose(1, 0, 2, 3)
    column_sum = scatter_q(column_grads, q, sizes)
    low_sum = column_sum.astype(BF)
    got = exchange_t([pick(low_sum, t ^ k) for k in range(TP)])
    got = [pick(column_sum, t)] + [item.astype(F32) for item in got[1:]]
    vec_sum = sum(item[:, at : at + 12] for item in got)
    got = jnp.stack(unxor(got, t))
    shard_qkv = (
        got[:, :, : 3 * part].reshape(TP, shard, 3, part).transpose(1, 2, 0, 3).reshape(shard, -1)
    )
    shard_up = got[:, :, at + 12 :].transpose(1, 0, 2).reshape(shard, -1)
    shard_branch_bias = vec_sum[:, 4]
    return (
        output.astype(BF),
        grad_tokens,
        vec_sum[:, 0],
        vec_sum[:, 1],
        vec_sum[:, 2],
        vec_sum[:, 3],
        shard_qkv,
        vec_sum[:, 5:8].reshape(-1),
        shard_out,
        shard_branch_bias,
        shard_up,
        vec_sum[:, 8:12].reshape(-1),
        shard_down,
        shard_branch_bias,
    )


def solution(mesh):
    nd, nf = mesh.shape["dp"], mesh.shape["fsdp"]
    sizes = (nd // TP, nf)
    inner = Mesh(mesh.devices.reshape((TP,) + sizes), ("t", "dq", "fsdp"))
    axes = ("t", "dq", "fsdp")
    matrix, vector = P(axes, None), P(axes)
    return jax.shard_map(
        lambda *args: local(sizes, *args),
        mesh=inner,
        in_specs=(
            matrix, matrix, vector, vector, vector, vector, matrix, vector,
            matrix, vector, matrix, vector, matrix, vector, matrix,
        ),
        out_specs=(
            matrix, matrix, vector, vector, vector, vector, matrix, vector,
            matrix, vector, matrix, vector, matrix, vector,
        ),
        check_vma=False,
    )
```

time: 781 us -> 238 us (0.30)
  waiting for transfers between devices: 617 us -> 53.4 us
  blocking collectives: 83.1 us -> 0 us
  starting transfers between devices: 0.5 us -> 56.1 us
  local copies, waits for them, and re-layouts: 13 us -> 59.6 us
  other arithmetic: 7.11 us -> 35.7 us
  matrix products: 45 us -> 29.4 us
  between operations: 14.5 us -> 2.33 us
    reduce_scatter x4 -> x0, waiting for transfers between devices: 442 us -> none  [the longest x1 142 us: local(): lax.psum_scatter(grad_down, ('dp', 'fsdp'), scatter_dimension=0, tiled=True)]
    all_gather x4 -> x0, waiting for transfers between devices: 172 us -> none  [the longest x1 57.6 us: local(): lax.all_gather(w_fc2, ('dp', 'fsdp'), axis=0, tiled=True)]
    unnamed x2 -> x0, blocking collectives: 83.1 us -> none
    ppermute x0 -> x48, starting transfers between devices: none -> 56.1 us  [the longest x6 9.03 us: exchange_t(): lax.ppermute(pieces[k], 't', xor_pairs(TP, k))]
    ppermute x0 -> x48, waiting for transfers between devices: none -> 53.4 us  [the longest x2 11.3 us: gather_t(): two = lax.ppermute(block, 't', xor_pairs(TP, 2))]
    reshape x0 -> x25, local copies, waits for them, and re-layouts: none -> 16.9 us  [the longest x8 5.99 us: local(): item.reshape(shard, -1)]
    concatenate x0 -> x16, local copies, waits for them, and re-layouts: none -> 15.7 us  [the longest x8 13.7 us: local(): column_grads = jnp.concatenate([grad_qkv, vec_grads, grad_up], axis=1)]
    dot_general x10 -> x5, matrix products: 16.6 us -> 4.14 us  [the longest x1 1.78 us: local(): jnp.einsum('ghqk,gqhd->gkhd', probs_low, d_mixed, preferred_element_type=...]
  transfers between devices with their start and end apart: 8 -> 48, of which waited for: 8 -> 15; matrix products, arithmetic and copies ran while one was open for 8% -> 35% of each run, Pallas kernels for 0% -> 0%
where the time goes in v1:
time: 238 us; the launch traced here: 237 us
  local copies, waits for them, and re-layouts  59.6 us (25%)
  starting transfers between devices  56.1 us (24%)
  waiting for transfers between devices  53.4 us (22%)
  other arithmetic  35.7 us (15%)
  matrix products  29.4 us (12%)
    dot_general x12, matrix products, contract(): lax.dot_general(left, right, (((left_dim,), (right_dim,)), ((), ())), pre...  23 us
    concatenate x8, local copies, waits for them, and re-layouts, local(): column_grads = jnp.concatenate([grad_qkv, vec_grads, grad_up], axis=1)  13.7 us
    ppermute x2, waiting for transfers between devices, gather_t(): two = lax.ppermute(block, 't', xor_pairs(TP, 2))  11.3 us
    ppermute x6, starting transfers between devices, exchange_t(): lax.ppermute(pieces[k], 't', xor_pairs(TP, k))  9.03 us
    ppermute x2, waiting for transfers between devices, scatter_t(): lax.ppermute((slots[2] + relay.astype(F32)).astype(BF), 't', xor_pairs(TP...  8.77 us
    unnamed x146, local copies, waits for them, and re-layouts  8.41 us
    unnamed x16, other arithmetic  6.58 us
    ppermute x2, waiting for transfers between devices, gather_t(): far = lax.ppermute(two, 't', [(2, 3), (1, 0)])  6.27 us
  transfers between devices with their start and end apart: 48, of which 15 were waited for; matrix products, arithmetic and copies ran while one was open for 35% of the time, Pallas kernels for 0%

profile of v1, /device:TPU:0, one launch (start us, length us, event | category | flops | bytes accessed | tf_op | source)
XLA Modules:
  0.0 236.6 jit_solution(12095225412354065671)
XLA Ops:
  2.3 2.9 %collective-permute-start.15 = (bf16[120,768]{1,0:T(8,128)(2,1)S(1)}, bf16[120,768]{1,0:T(8,128)(2,1)S(1)}, u32[]{:S(2)}, u32[]{:S(2)}) collective-permute-start(bf16[120,768]{1,0:T(8,128)(2,1)S(1)} %constant_dynamic-update-slice_fusion.2), channel_id=1, source_target_pairs={{0,1},{1,0},{2,3},{3,2},{4,5},{5,4},{6,7},{7,6},{8,9},{9,8},{10,11... | collective-permute-start | bytes 552968 | tf_op jit(solution)/shard_map/ppermute | solution.py:67
  5.3 1.5 collective-permute-start.17
  18.0 3.7 %collective-permute-start.4 = (bf16[24,1361]{1,0:T(8,128)(2,1)S(1)}, bf16[24,1361]{1,0:T(8,128)(2,1)S(1)}, u32[]{:S(2)}, u32[]{:S(2)}) collective-permute-start(bf16[24,1361]{1,0:T(8,128)(2,1)S(1)} %concatenate.132), channel_id=1, source_target_pairs={{0,24},{8,16},{16,8},{24,0},{1,25},{9,17},{17,9},{25,1},{2,26},{10... | collective-permute-start | bytes 195992 | tf_op jit(solution)/shard_map/ppermute | solution.py:59
  25.2 3.1 %collective-permute-start.1 = (bf16[128,768]{1,0:T(8,128)(2,1)S(1)}, bf16[128,768]{1,0:T(8,128)(2,1)S(1)}, u32[]{:S(2)}, u32[]{:S(2)}) collective-permute-start(bf16[128,768]{1,0:T(8,128)(2,1)S(1)} %copy-done.9), channel_id=1, source_target_pairs={{0,16},{8,24},{16,0},{24,8},{1,17},{9,25},{17,1},{25,9},{2,18},{10... | collective-permute-start | bytes 589832 | tf_op jit(solution)/shard_map/ppermute | solution.py:41
  43.1 1.6 collective-permute-start.18
  46.8 1.6 collective-permute-start.16
  49.7 1.8 collective-permute-done.16
  51.5 3.8 %collective-permute-start = (bf16[128,768]{1,0:T(8,128)(2,1)S(1)}, bf16[128,768]{1,0:T(8,128)(2,1)S(1)}, u32[]{:S(2)}, u32[]{:S(2)}) collective-permute-start(bf16[128,768]{1,0:T(8,128)(2,1)S(1)} %copy-done.9), channel_id=1, source_target_pairs={{0,8},{8,0},{16,24},{24,16},{1,9},{9,1},{17,25},{25,17},{2,10},{10... | collective-permute-start | bytes 589832 | tf_op jit(solution)/shard_map/ppermute | solution.py:40
  56.2 2.8 %collective-permute-start.28 = (bf16[128,768]{1,0:T(8,128)(2,1)S(1)}, bf16[128,768]{1,0:T(8,128)(2,1)S(1)}, u32[]{:S(2)}, u32[]{:S(2)}) collective-permute-start(bf16[128,768]{1,0:T(8,128)(2,1)S(1)} %copy-done.43), channel_id=1, source_target_pairs={{0,16},{8,24},{16,0},{24,8},{1,17},{9,25},{17,1},{25,9},{2,18},{10... | collective-permute-start | bytes 589832 | tf_op jit(solution)/shard_map/ppermute | solution.py:41
  59.1 2.1 collective-permute-done
  61.2 11.3 %collective-permute-done.28 = bf16[128,768]{1,0:T(8,128)(2,1)S(1)} collective-permute-done((bf16[128,768]{1,0:T(8,128)(2,1)S(1)}, bf16[128,768]{1,0:T(8,128)(2,1)S(1)}, u32[]{:S(2)}, u32[]{:S(2)}) %collective-permute-start.28) | collective-permute-done | bytes 196640 | tf_op jit(solution)/shard_map/ppermute | solution.py:41
  72.5 1.5 collective-permute-start.30
  74.7 6.3 %collective-permute-done.30 = bf16[128,768]{1,0:T(8,128)(2,1)S(1)} collective-permute-done((bf16[128,768]{1,0:T(8,128)(2,1)S(1)}, bf16[128,768]{1,0:T(8,128)(2,1)S(1)}, u32[]{:S(2)}, u32[]{:S(2)}) %collective-permute-start.30) | collective-permute-done | bytes 196640 | tf_op jit(solution)/shard_map/ppermute | solution.py:43
  81.0 1.6 collective-permute-start.8
  82.8 4.3 %collective-permute-done.8 = bf16[2,24,1361]{2,1,0:T(8,128)(2,1)S(1)} collective-permute-done((bf16[2,24,1361]{2,1,0:T(8,128)(2,1)S(1)}, bf16[2,24,1361]{2,1,0:T(8,128)(2,1)S(1)}, u32[]{:S(2)}, u32[]{:S(2)}) %collective-permute-start.8) | collective-permute-done | bytes 130688 | tf_op jit(solution)/shard_map/ppermute | solution.py:69
  88.3 4.0 %collective-permute-done.10 = bf16[2,24,1361]{2,1,0:T(8,128)(2,1)S(1)} collective-permute-done((bf16[2,24,1361]{2,1,0:T(8,128)(2,1)S(1)}, bf16[2,24,1361]{2,1,0:T(8,128)(2,1)S(1)}, u32[]{:S(2)}, u32[]{:S(2)}) %collective-permute-start.10) | collective-permute-done | bytes 130688 | tf_op jit(solution)/shard_map/ppermute | solution.py:70
  97.9 1.7 reshape.1154
  101.1 1.5 bitcast_dynamic-update-slice_fusion.6
  106.1 1.8 reshape.1147
  110.7 1.8 slice_reduce_fusion.1
  112.5 2.1 convolution_add_fusion.2
  116.8 2.3 fusion.104
  122.7 1.8 reshape.1145
  125.3 4.1 %multiply_convert_fusion = (bf16[512,768]{1,0:T(8,128)(2,1)S(1)}, f32[512,768]{1,0:T(8,128)}) fusion(f32[768]{0:T(1024)S(1)} %fusion.73, bf16[768,1361]{1,0:T(8,128)(2,1)} %bitcast.306, f32[768]{0:T(1024)} %get-tuple-element.24, f32[768]{0:T(1024)} %get-tuple-element.25, f32[512]{0:T(512)} %copy-done.60, f32[512]{0:T(512)} %copy-done.50, ...), kind=kOutput, calls=%fused_computation.19 | convolution fusion | flops 611450880 | bytes 4340736 | tf_op jit(solution)/shard_map/dot_general | solution.py:136
  129.4 2.0 fusion.105
  132.1 2.3 collective-permute-start.25
  135.7 1.8 fusion.18
  141.0 1.7 convert_reduce_fusion
  144.1 3.0 %fusion.95 = (f32[768]{0:T(1024)S(1)}, f32[768]{0:T(1024)S(1)}, bf16[512,768]{1,0:T(8,128)(2,1)S(1)}, f32[512,768]{1,0:T(8,128)}, f32[768]{0:T(1024)S(1)}, /*index=5*/f32[768]{0:T(1024)S(1)}, f32[512,768]{1,0:T(8,128)}) fusion(f32[512]{0:T(512)S(1)} %copy-done.62, f32[512]{0:T(512)S(1)} %copy-done.52, bf16[128,768]{1,0:T(8,128)(2,1)S(1)} %copy-done.5, ...), kind=kOutput, calls=%fused_computation.354 | convolution fusion | flops 611841024 | bytes 8282112 | tf_op jit(solution)/shard_map/dot_general | solution.py:136
  147.8 2.8 %collective-permute-start.33 = (bf16[128,768]{1,0:T(8,128)(2,1)}, bf16[128,768]{1,0:T(8,128)(2,1)}, u32[]{:S(2)}, u32[]{:S(2)}) collective-permute-start(bf16[128,768]{1,0:T(8,128)(2,1)} %get-tuple-element.82), channel_id=1, source_target_pairs={{0,8},{24,16},{1,9},{25,17},{2,10},{26,18},{3,11},{27,19},{4,12},{... | collective-permute-start | bytes 589832 | tf_op jit(solution)/shard_map/ppermute | solution.py:52
  153.7 2.4 %fusion.92 = f32[768,576]{1,0:T(8,128)} fusion(bf16[512,192]{0,1:T(8,128)(2,1)S(1)} %bitcast.323, bf16[512,192]{0,1:T(8,128)(2,1)S(1)} %bitcast.326, bf16[512,192]{0,1:T(8,128)(2,1)S(1)} %bitcast.329, f32[768]{0:T(1024)S(1)} %copy-done.56, f32[768]{0:T(1024)S(1)} %copy-done.58, f32[512]{0:T(512)S(1)} %copy-done.62, f32[512]{0:T(512)S(1)} %copy-done.52, ...), kind=kOutput, calls=%fused_computation.351 | convolution fusion | flops 459866112 | bytes 3155968 | tf_op jit(solution)/shard_map/dot_general | solution.py:136
  156.1 2.5 %fusion.93 = f32[768,768]{1,0:T(8,128)} fusion(bf16[512,768]{1,0:T(8,128)(2,1)S(1)} %get-tuple-element.144, f32[768]{0:T(1024)S(1)} %copy-done.53, f32[768]{0:T(1024)S(1)} %copy-done.54, f32[512]{0:T(512)S(1)} %copy-done.62, f32[512]{0:T(512)S(1)} %copy-done.52, bf16[128,768]{1,0:T(8,128)(2,1)S(1)} %copy-done.5, bf16[128,768]{1,0:T(8,128)(2,1)S(1)} %copy-done.12, ...), kind=kOutput, calls=%fused_computation.352 | convolution fusion | flops 609091584 | bytes 3942400 | tf_op jit(solution)/shard_map/dot_general | solution.py:136
  168.6 2.0 fusion.28
  174.0 1.8 fusion.33
  175.8 3.2 %collective-permute-done.31 = bf16[128,768]{1,0:T(8,128)(2,1)S(1)} collective-permute-done((bf16[128,768]{1,0:T(8,128)(2,1)S(1)}, bf16[128,768]{1,0:T(8,128)(2,1)S(1)}, u32[]{:S(2)}, u32[]{:S(2)}) %collective-permute-start.31) | collective-permute-done | bytes 196640 | tf_op jit(solution)/shard_map/ppermute | solution.py:50
  179.0 1.7 collective-permute-start.26
  180.7 8.8 %collective-permute-done.34 = bf16[128,768]{1,0:T(8,128)(2,1)S(1)} collective-permute-done((bf16[128,768]{1,0:T(8,128)(2,1)S(1)}, bf16[128,768]{1,0:T(8,128)(2,1)S(1)}, u32[]{:S(2)}, u32[]{:S(2)}) %collective-permute-start.34) | collective-permute-done | bytes 196640 | tf_op jit(solution)/shard_map/ppermute | solution.py:53
  191.8 7.0 %concatenate.164 = f32[4,8,24,1356]{3,2,1,0:T(8,128)} concatenate(f32[4,8,24,576]{3,2,1,0:T(8,128)} %bitcast.310, f32[4,8,24,1]{3,2,1,0:T(8,128)} %concatenate.171, f32[4,8,24,1]{3,2,1,0:T(8,128)} %concatenate.172, f32[4,8,24,1]{3,2,1,0:T(8,128)} %concatenate.173, f32[4,8,24,1]{3,2,1,0:T(8,128)} %concatenate.174, f32[4,8,24,1]{3,2,1,0:T(8,128)S(1)} %concatenate.175, ...), dimensions={3} | concatenate | bytes 8331264 | tf_op jit(solution)/shard_map/concatenate | solution.py:308
  198.8 1.8 fusion.19
  201.3 2.0 fusion.40
  204.9 1.6 collective-permute-start.44
  207.9 1.5 collective-permute-start.38
  209.4 3.2 %collective-permute-done.36 = bf16[2,24,1356]{2,1,0:T(8,128)(2,1)S(1)} collective-permute-done((bf16[2,24,1356]{2,1,0:T(8,128)(2,1)S(1)}, bf16[2,24,1356]{2,1,0:T(8,128)(2,1)S(1)}, u32[]{:S(2)}, u32[]{:S(2)}) %collective-permute-start.36) | collective-permute-done | bytes 130208 | tf_op jit(solution)/shard_map/ppermute | solution.py:91
  214.7 1.5 collective-permute-start.37
  217.0 1.5 collective-permute-start.45
  218.6 5.0 %collective-permute-done.39 = bf16[4,24,1356]{2,1,0:T(8,128)(2,1)S(1)} collective-permute-done((bf16[4,24,1356]{2,1,0:T(8,128)(2,1)S(1)}, bf16[4,24,1356]{2,1,0:T(8,128)(2,1)S(1)}, u32[]{:S(2)}, u32[]{:S(2)}) %collective-permute-start.39) | collective-permute-done | bytes 260384 | tf_op jit(solution)/shard_map/ppermute | solution.py:95
  223.9 2.2 collective-permute-start.42
  226.1 2.2 collective-permute-start.40
  (404 shorter events, 98.0 us)
Async XLA Ops:
  2.3 43.7 %collective-permute-start.15 = (bf16[120,768]{1,0:T(8,128)(2,1)S(1)}, bf16[120,768]{1,0:T(8,128)(2,1)S(1)}, u32[]{:S(2)}, u32[]{:S(2)}) collective-permute-start(bf16[120,768]{1,0:T(8,128)(2,1)S(1)} %constant_dynamic-update-slice_fusion.2), channel_id=1, source_target_pairs={{0,1},{1,0},{2,3},{3,2},{4,5},{5,4},{6,7},{7,6},{8,9},{9,8},{10,11... | collective-permute-start | bytes 552968 | tf_op jit(solution)/shard_map/ppermute | solution.py:67
  5.3 37.8 %collective-permute-start.17 = (bf16[120,768]{1,0:T(8,128)(2,1)S(1)}, bf16[120,768]{1,0:T(8,128)(2,1)S(1)}, u32[]{:S(2)}, u32[]{:S(2)}) collective-permute-start(bf16[120,768]{1,0:T(8,128)(2,1)S(1)} %constant_dynamic-update-slice_fusion.2), channel_id=1, source_target_pairs={{0,2},{1,3},{2,0},{3,1},{4,6},{5,7},{6,4},{7,5},{8,10},{9,11},{10,... | collective-permute-start | bytes 552968 | tf_op jit(solution)/shard_map/ppermute | solution.py:68
  18.0 7.1 %collective-permute-start.4 = (bf16[24,1361]{1,0:T(8,128)(2,1)S(1)}, bf16[24,1361]{1,0:T(8,128)(2,1)S(1)}, u32[]{:S(2)}, u32[]{:S(2)}) collective-permute-start(bf16[24,1361]{1,0:T(8,128)(2,1)S(1)} %concatenate.132), channel_id=1, source_target_pairs={{0,24},{8,16},{16,8},{24,0},{1,25},{9,17},{17,9},{25,1},{2,26},{10... | collective-permute-start | bytes 195992 | tf_op jit(solution)/shard_map/ppermute | solution.py:59
  21.9 6.3 %collective-permute-start.5 = (bf16[24,1361]{1,0:T(8,128)(2,1)S(1)}, bf16[24,1361]{1,0:T(8,128)(2,1)S(1)}, u32[]{:S(2)}, u32[]{:S(2)}) collective-permute-start(bf16[24,1361]{1,0:T(8,128)(2,1)S(1)} %concatenate.133), channel_id=1, source_target_pairs={{0,16},{8,24},{16,0},{24,8},{1,17},{9,25},{17,1},{25,9},{2,18},{10... | collective-permute-start | bytes 195992 | tf_op jit(solution)/shard_map/ppermute | solution.py:59
  22.3 6.1 %collective-permute-start.6 = (bf16[24,1361]{1,0:T(8,128)(2,1)S(1)}, bf16[24,1361]{1,0:T(8,128)(2,1)S(1)}, u32[]{:S(2)}, u32[]{:S(2)}) collective-permute-start(bf16[24,1361]{1,0:T(8,128)(2,1)S(1)} %concatenate.134), channel_id=1, source_target_pairs={{0,8},{8,0},{16,24},{24,16},{1,9},{9,1},{17,25},{25,17},{2,10},{10... | collective-permute-start | bytes 195992 | tf_op jit(solution)/shard_map/ppermute | solution.py:59
  25.2 21.6 %collective-permute-start.1 = (bf16[128,768]{1,0:T(8,128)(2,1)S(1)}, bf16[128,768]{1,0:T(8,128)(2,1)S(1)}, u32[]{:S(2)}, u32[]{:S(2)}) collective-permute-start(bf16[128,768]{1,0:T(8,128)(2,1)S(1)} %copy-done.9), channel_id=1, source_target_pairs={{0,16},{8,24},{16,0},{24,8},{1,17},{9,25},{17,1},{25,9},{2,18},{10... | collective-permute-start | bytes 589832 | tf_op jit(solution)/shard_map/ppermute | solution.py:41
  29.8 21.7 %collective-permute-start.7 = (bf16[4,24,1361]{2,1,0:T(8,128)(2,1)}, bf16[4,24,1361]{2,1,0:T(8,128)(2,1)S(1)}, u32[]{:S(2)}, u32[]{:S(2)}) collective-permute-start(bf16[4,24,1361]{2,1,0:T(8,128)(2,1)} %pad_maximum_fusion.5), channel_id=1, source_target_pairs={{0,1},{1,0},{2,3},{3,2},{4,5},{5,4},{6,7},{7,6},{8,9},{9,8},{10,11... | collective-permute-start | bytes 783944 | tf_op jit(solution)/shard_map/ppermute | solution.py:67
  30.3 25.0 %collective-permute-start.9 = (bf16[4,24,1361]{2,1,0:T(8,128)(2,1)}, bf16[4,24,1361]{2,1,0:T(8,128)(2,1)S(1)}, u32[]{:S(2)}, u32[]{:S(2)}) collective-permute-start(bf16[4,24,1361]{2,1,0:T(8,128)(2,1)} %pad_maximum_fusion.5), channel_id=1, source_target_pairs={{0,2},{1,3},{2,0},{3,1},{4,6},{5,7},{6,4},{7,5},{8,10},{9,11},{10,... | collective-permute-start | bytes 783944 | tf_op jit(solution)/shard_map/ppermute | solution.py:68
  43.1 5.2 %collective-permute-start.18 = (bf16[60,768]{1,0:T(8,128)(2,1)S(1)}, bf16[60,768]{1,0:T(8,128)(2,1)S(1)}, u32[]{:S(2)}, u32[]{:S(2)}) collective-permute-start(bf16[60,768]{1,0:T(8,128)(2,1)S(1)} %slice.398), channel_id=1, source_target_pairs={{0,1},{1,0},{2,3},{3,2},{4,5},{5,4},{6,7},{7,6},{8,9},{9,8},{10,11... | collective-permute-start | bytes 276488 | tf_op jit(solution)/shard_map/ppermute | solution.py:70
  46.1 10.1 %collective-permute-start.2 = (bf16[128,768]{1,0:T(8,128)(2,1)S(1)}, bf16[128,768]{1,0:T(8,128)(2,1)S(1)}, u32[]{:S(2)}, u32[]{:S(2)}) collective-permute-start(bf16[128,768]{1,0:T(8,128)(2,1)S(1)} %copy-done.9), channel_id=1, source_target_pairs={{8,16},{16,8},{9,17},{17,9},{10,18},{18,10},{11,19},{19,11},{12,20... | collective-permute-start | bytes 589832 | tf_op jit(solution)/shard_map/ppermute | solution.py:42
  46.8 4.7 %collective-permute-start.16 = (bf16[60,768]{1,0:T(8,128)(2,1)S(1)}, bf16[60,768]{1,0:T(8,128)(2,1)S(1)}, u32[]{:S(2)}, u32[]{:S(2)}) collective-permute-start(bf16[60,768]{1,0:T(8,128)(2,1)S(1)} %slice.397), channel_id=1, source_target_pairs={{0,2},{1,3},{2,0},{3,1},{4,6},{5,7},{6,4},{7,5},{8,10},{9,11},{10,... | collective-permute-start | bytes 276488 | tf_op jit(solution)/shard_map/ppermute | solution.py:69
  48.4 10.6 %collective-permute-start.3 = (bf16[128,768]{1,0:T(8,128)(2,1)S(1)}, bf16[128,768]{1,0:T(8,128)(2,1)S(1)}, u32[]{:S(2)}, u32[]{:S(2)}) collective-permute-start(bf16[128,768]{1,0:T(8,128)(2,1)S(1)} %collective-permute-done.1), channel_id=1, source_target_pairs={{16,24},{8,0},{17,25},{9,1},{18,26},{10,2},{19,27},{11,3},{20,28},... | collective-permute-start | bytes 589832 | tf_op jit(solution)/shard_map/ppermute | solution.py:43
  51.5 41.5 %collective-permute-start.22 = (bf16[120,768]{1,0:T(8,128)(2,1)S(1)}, bf16[120,768]{1,0:T(8,128)(2,1)S(1)}, u32[]{:S(2)}, u32[]{:S(2)}) collective-permute-start(bf16[120,768]{1,0:T(8,128)(2,1)S(1)} %constant_dynamic-update-slice_fusion.2), channel_id=1, source_target_pairs={{0,4},{4,0},{1,5},{5,1},{2,6},{6,2},{3,7},{7,3},{8,12},{12,8},{9,1... | collective-permute-start | bytes 552968 | tf_op jit(solution)/shard_map/ppermute | solution.py:73
  51.5 9.7 %collective-permute-start = (bf16[128,768]{1,0:T(8,128)(2,1)S(1)}, bf16[128,768]{1,0:T(8,128)(2,1)S(1)}, u32[]{:S(2)}, u32[]{:S(2)}) collective-permute-start(bf16[128,768]{1,0:T(8,128)(2,1)S(1)} %copy-done.9), channel_id=1, source_target_pairs={{0,8},{8,0},{16,24},{24,16},{1,9},{9,1},{17,25},{25,17},{2,10},{10... | collective-permute-start | bytes 589832 | tf_op jit(solution)/shard_map/ppermute | solution.py:40
  55.3 19.3 %collective-permute-start.29 = (bf16[128,768]{1,0:T(8,128)(2,1)S(1)}, bf16[128,768]{1,0:T(8,128)(2,1)S(1)}, u32[]{:S(2)}, u32[]{:S(2)}) collective-permute-start(bf16[128,768]{1,0:T(8,128)(2,1)S(1)} %copy-done.43), channel_id=1, source_target_pairs={{8,16},{16,8},{9,17},{17,9},{10,18},{18,10},{11,19},{19,11},{12,20... | collective-permute-start | bytes 589832 | tf_op jit(solution)/shard_map/ppermute | solution.py:42
  56.2 16.4 %collective-permute-start.28 = (bf16[128,768]{1,0:T(8,128)(2,1)S(1)}, bf16[128,768]{1,0:T(8,128)(2,1)S(1)}, u32[]{:S(2)}, u32[]{:S(2)}) collective-permute-start(bf16[128,768]{1,0:T(8,128)(2,1)S(1)} %copy-done.43), channel_id=1, source_target_pairs={{0,16},{8,24},{16,0},{24,8},{1,17},{9,25},{17,1},{25,9},{2,18},{10... | collective-permute-start | bytes 589832 | tf_op jit(solution)/shard_map/ppermute | solution.py:41
  59.0 22.0 %collective-permute-start.27 = (bf16[128,768]{1,0:T(8,128)(2,1)S(1)}, bf16[128,768]{1,0:T(8,128)(2,1)S(1)}, u32[]{:S(2)}, u32[]{:S(2)}) collective-permute-start(bf16[128,768]{1,0:T(8,128)(2,1)S(1)} %copy-done.43), channel_id=1, source_target_pairs={{0,8},{8,0},{16,24},{24,16},{1,9},{9,1},{17,25},{25,17},{2,10},{10... | collective-permute-start | bytes 589832 | tf_op jit(solution)/shard_map/ppermute | solution.py:40
  61.2 38.4 %collective-permute-start.14 = (bf16[4,24,1361]{2,1,0:T(8,128)(2,1)}, bf16[4,24,1361]{2,1,0:T(8,128)(2,1)}, u32[]{:S(2)}, u32[]{:S(2)}) collective-permute-start(bf16[4,24,1361]{2,1,0:T(8,128)(2,1)} %pad_maximum_fusion.5), channel_id=1, source_target_pairs={{0,4},{4,0},{1,5},{5,1},{2,6},{6,2},{3,7},{7,3},{8,12},{12,8},{9,1... | collective-permute-start | bytes 783944 | tf_op jit(solution)/shard_map/ppermute | solution.py:73
  72.5 8.4 %collective-permute-start.30 = (bf16[128,768]{1,0:T(8,128)(2,1)S(1)}, bf16[128,768]{1,0:T(8,128)(2,1)S(1)}, u32[]{:S(2)}, u32[]{:S(2)}) collective-permute-start(bf16[128,768]{1,0:T(8,128)(2,1)S(1)} %collective-permute-done.28), channel_id=1, source_target_pairs={{16,24},{8,0},{17,25},{9,1},{18,26},{10,2},{19,27},{11,3},{20,28},... | collective-permute-start | bytes 589832 | tf_op jit(solution)/shard_map/ppermute | solution.py:43
  74.6 18.8 %collective-permute-start.21 = (bf16[120,768]{1,0:T(8,128)(2,1)S(1)}, bf16[120,768]{1,0:T(8,128)(2,1)S(1)}, u32[]{:S(2)}, u32[]{:S(2)}) collective-permute-start(bf16[120,768]{1,0:T(8,128)(2,1)S(1)} %collective-permute-done.15), channel_id=1, source_target_pairs={{0,4},{4,0},{1,5},{5,1},{2,6},{6,2},{3,7},{7,3},{8,12},{12,8},{9,1... | collective-permute-start | bytes 552968 | tf_op jit(solution)/shard_map/ppermute | solution.py:73
  81.0 12.6 %collective-permute-start.20 = (bf16[120,768]{1,0:T(8,128)(2,1)S(1)}, bf16[120,768]{1,0:T(8,128)(2,1)S(1)}, u32[]{:S(2)}, u32[]{:S(2)}) collective-permute-start(bf16[120,768]{1,0:T(8,128)(2,1)S(1)} %collective-permute-done.17), channel_id=1, source_target_pairs={{0,4},{4,0},{1,5},{5,1},{2,6},{6,2},{3,7},{7,3},{8,12},{12,8},{9,1... | collective-permute-start | bytes 552968 | tf_op jit(solution)/shard_map/ppermute | solution.py:73
  81.0 6.1 %collective-permute-start.8 = (bf16[2,24,1361]{2,1,0:T(8,128)(2,1)S(1)}, bf16[2,24,1361]{2,1,0:T(8,128)(2,1)S(1)}, u32[]{:S(2)}, u32[]{:S(2)}) collective-permute-start(bf16[2,24,1361]{2,1,0:T(8,128)(2,1)S(1)} %slice.390), channel_id=1, source_target_pairs={{0,2},{1,3},{2,0},{3,1},{4,6},{5,7},{6,4},{7,5},{8,10},{9,11},{10,... | collective-permute-start | bytes 391976 | tf_op jit(solution)/shard_map/ppermute | solution.py:69
  87.1 5.2 %collective-permute-start.10 = (bf16[2,24,1361]{2,1,0:T(8,128)(2,1)S(1)}, bf16[2,24,1361]{2,1,0:T(8,128)(2,1)S(1)}, u32[]{:S(2)}, u32[]{:S(2)}) collective-permute-start(bf16[2,24,1361]{2,1,0:T(8,128)(2,1)S(1)} %slice.391), channel_id=1, source_target_pairs={{0,1},{1,0},{2,3},{3,2},{4,5},{5,4},{6,7},{7,6},{8,9},{9,8},{10,11... | collective-permute-start | bytes 391976 | tf_op jit(solution)/shard_map/ppermute | solution.py:70
  92.3 1.7 collective-permute-start.19
  92.9 6.7 %collective-permute-start.13 = (bf16[4,24,1361]{2,1,0:T(8,128)(2,1)S(1)}, bf16[4,24,1361]{2,1,0:T(8,128)(2,1)}, u32[]{:S(2)}, u32[]{:S(2)}) collective-permute-start(bf16[4,24,1361]{2,1,0:T(8,128)(2,1)S(1)} %collective-permute-done.7), channel_id=1, source_target_pairs={{0,4},{4,0},{1,5},{5,1},{2,6},{6,2},{3,7},{7,3},{8,12},{12,8},{9,1... | collective-permute-start | bytes 783944 | tf_op jit(solution)/shard_map/ppermute | solution.py:73
  93.5 6.2 %collective-permute-start.12 = (bf16[4,24,1361]{2,1,0:T(8,128)(2,1)S(1)}, bf16[4,24,1361]{2,1,0:T(8,128)(2,1)}, u32[]{:S(2)}, u32[]{:S(2)}) collective-permute-start(bf16[4,24,1361]{2,1,0:T(8,128)(2,1)S(1)} %collective-permute-done.9), channel_id=1, source_target_pairs={{0,4},{4,0},{1,5},{5,1},{2,6},{6,2},{3,7},{7,3},{8,12},{12,8},{9,1... | collective-permute-start | bytes 783944 | tf_op jit(solution)/shard_map/ppermute | solution.py:73
  93.5 6.1 %collective-permute-start.11 = (bf16[4,24,1361]{2,1,0:T(8,128)(2,1)}, bf16[4,24,1361]{2,1,0:T(8,128)(2,1)}, u32[]{:S(2)}, u32[]{:S(2)}) collective-permute-start(bf16[4,24,1361]{2,1,0:T(8,128)(2,1)} %constant_dynamic-update-slice_fusion), channel_id=1, source_target_pairs={{0,4},{4,0},{1,5},{5,1},{2,6},{6,2},{3,7},{7,3},{8,12},{12,8},{9,1... | collective-permute-start | bytes 783944 | tf_op jit(solution)/shard_map/ppermute | solution.py:73
  132.1 40.8 %collective-permute-start.25 = (bf16[128,768]{1,0:T(8,128)(2,1)}, bf16[128,768]{1,0:T(8,128)(2,1)}, u32[]{:S(2)}, u32[]{:S(2)}) collective-permute-start(bf16[128,768]{1,0:T(8,128)(2,1)} %get-tuple-element.84), channel_id=1, source_target_pairs={{0,8},{24,16},{1,9},{25,17},{2,10},{26,18},{3,11},{27,19},{4,12},{... | collective-permute-start | bytes 589832 | tf_op jit(solution)/shard_map/ppermute | solution.py:52
  134.4 66.5 %collective-permute-start.24 = (bf16[128,768]{1,0:T(8,128)(2,1)}, bf16[128,768]{1,0:T(8,128)(2,1)}, u32[]{:S(2)}, u32[]{:S(2)}) collective-permute-start(bf16[128,768]{1,0:T(8,128)(2,1)} %get-tuple-element.84), channel_id=1, source_target_pairs={{8,16},{16,8},{9,17},{17,9},{10,18},{18,10},{11,19},{19,11},{12,20... | collective-permute-start | bytes 589832 | tf_op jit(solution)/shard_map/ppermute | solution.py:51
  147.8 22.8 %collective-permute-start.33 = (bf16[128,768]{1,0:T(8,128)(2,1)}, bf16[128,768]{1,0:T(8,128)(2,1)}, u32[]{:S(2)}, u32[]{:S(2)}) collective-permute-start(bf16[128,768]{1,0:T(8,128)(2,1)} %get-tuple-element.82), channel_id=1, source_target_pairs={{0,8},{24,16},{1,9},{25,17},{2,10},{26,18},{3,11},{27,19},{4,12},{... | collective-permute-start | bytes 589832 | tf_op jit(solution)/shard_map/ppermute | solution.py:52
  150.6 25.2 %collective-permute-start.32 = (bf16[128,768]{1,0:T(8,128)(2,1)}, bf16[128,768]{1,0:T(8,128)(2,1)}, u32[]{:S(2)}, u32[]{:S(2)}) collective-permute-start(bf16[128,768]{1,0:T(8,128)(2,1)} %get-tuple-element.82), channel_id=1, source_target_pairs={{8,16},{16,8},{9,17},{17,9},{10,18},{18,10},{11,19},{19,11},{12,20... | collective-permute-start | bytes 589832 | tf_op jit(solution)/shard_map/ppermute | solution.py:51
  152.8 48.1 %collective-permute-start.23 = (bf16[128,768]{1,0:T(8,128)(2,1)}, bf16[128,768]{1,0:T(8,128)(2,1)}, u32[]{:S(2)}, u32[]{:S(2)}) collective-permute-start(bf16[128,768]{1,0:T(8,128)(2,1)} %get-tuple-element.83), channel_id=1, source_target_pairs={{0,8},{8,0},{16,24},{24,16},{1,9},{9,1},{17,25},{25,17},{2,10},{10... | collective-permute-start | bytes 589832 | tf_op jit(solution)/shard_map/ppermute | solution.py:50
  170.6 8.4 %collective-permute-start.31 = (bf16[128,768]{1,0:T(8,128)(2,1)S(1)}, bf16[128,768]{1,0:T(8,128)(2,1)S(1)}, u32[]{:S(2)}, u32[]{:S(2)}) collective-permute-start(bf16[128,768]{1,0:T(8,128)(2,1)S(1)} %copy-done.42), channel_id=1, source_target_pairs={{0,8},{8,0},{16,24},{24,16},{1,9},{9,1},{17,25},{25,17},{2,10},{10... | collective-permute-start | bytes 589832 | tf_op jit(solution)/shard_map/ppermute | solution.py:50
  172.9 16.5 %collective-permute-start.34 = (bf16[128,768]{1,0:T(8,128)(2,1)S(1)}, bf16[128,768]{1,0:T(8,128)(2,1)S(1)}, u32[]{:S(2)}, u32[]{:S(2)}) collective-permute-start(bf16[128,768]{1,0:T(8,128)(2,1)S(1)} %fusion.30), channel_id=1, source_target_pairs={{0,16},{8,24},{16,0},{24,8},{1,17},{9,25},{17,1},{25,9},{2,18},{10... | collective-permute-start | bytes 589832 | tf_op jit(solution)/shard_map/ppermute | solution.py:53
  175.8 27.5 %collective-permute-start.43 = (bf16[4,120,768]{2,1,0:T(8,128)(2,1)}, bf16[4,120,768]{2,1,0:T(8,128)(2,1)}, u32[]{:S(2)}, u32[]{:S(2)}) collective-permute-start(bf16[4,120,768]{2,1,0:T(8,128)(2,1)} %fusion.28), channel_id=1, source_target_pairs={{0,4},{4,0},{1,5},{5,1},{2,6},{6,2},{3,7},{7,3},{8,12},{12,8},{9,1... | collective-permute-start | bytes 2211848 | tf_op jit(solution)/shard_map/ppermute | solution.py:86
  179.0 21.9 %collective-permute-start.26 = (bf16[128,768]{1,0:T(8,128)(2,1)}, bf16[128,768]{1,0:T(8,128)(2,1)}, u32[]{:S(2)}, u32[]{:S(2)}) collective-permute-start(bf16[128,768]{1,0:T(8,128)(2,1)} %fusion.33), channel_id=1, source_target_pairs={{0,16},{8,24},{16,0},{24,8},{1,17},{9,25},{17,1},{25,9},{2,18},{10... | collective-permute-start | bytes 589832 | tf_op jit(solution)/shard_map/ppermute | solution.py:53
  200.6 6.4 %collective-permute-start.35 = (bf16[4,4,24,1356]{3,2,1,0:T(8,128)(2,1)S(1)}, bf16[4,4,24,1356]{3,2,1,0:T(8,128)(2,1)S(1)}, u32[]{:S(2)}, u32[]{:S(2)}) collective-permute-start(bf16[4,4,24,1356]{3,2,1,0:T(8,128)(2,1)S(1)} %fusion.19), channel_id=1, source_target_pairs={{0,4},{4,0},{1,5},{5,1},{2,6},{6,2},{3,7},{7,3},{8,12},{12,8},{9,1... | collective-permute-start | bytes 3124232 | tf_op jit(solution)/shard_map/ppermute | solution.py:86
  204.9 11.3 %collective-permute-start.44 = (bf16[60,768]{1,0:T(8,128)(2,1)S(1)}, bf16[60,768]{1,0:T(8,128)(2,1)S(1)}, u32[]{:S(2)}, u32[]{:S(2)}) collective-permute-start(bf16[60,768]{1,0:T(8,128)(2,1)S(1)} %get-tuple-element.105), channel_id=1, source_target_pairs={{0,2},{1,3},{2,0},{3,1},{4,6},{5,7},{6,4},{7,5},{8,10},{9,11},{10,... | collective-permute-start | bytes 276488 | tf_op jit(solution)/shard_map/ppermute | solution.py:91
  206.4 9.7 %collective-permute-start.46 = (bf16[60,768]{1,0:T(8,128)(2,1)S(1)}, bf16[60,768]{1,0:T(8,128)(2,1)S(1)}, u32[]{:S(2)}, u32[]{:S(2)}) collective-permute-start(bf16[60,768]{1,0:T(8,128)(2,1)S(1)} %get-tuple-element.106), channel_id=1, source_target_pairs={{0,1},{1,0},{2,3},{3,2},{4,5},{5,4},{6,7},{7,6},{8,9},{9,8},{10,11... | collective-permute-start | bytes 276488 | tf_op jit(solution)/shard_map/ppermute | solution.py:90
  207.3 5.3 %collective-permute-start.36 = (bf16[2,24,1356]{2,1,0:T(8,128)(2,1)S(1)}, bf16[2,24,1356]{2,1,0:T(8,128)(2,1)S(1)}, u32[]{:S(2)}, u32[]{:S(2)}) collective-permute-start(bf16[2,24,1356]{2,1,0:T(8,128)(2,1)S(1)} %get-tuple-element.99), channel_id=1, source_target_pairs={{0,2},{1,3},{2,0},{3,1},{4,6},{5,7},{6,4},{7,5},{8,10},{9,11},{10,... | collective-permute-start | bytes 390536 | tf_op jit(solution)/shard_map/ppermute | solution.py:91
  207.9 6.0 %collective-permute-start.38 = (bf16[2,24,1356]{2,1,0:T(8,128)(2,1)S(1)}, bf16[2,24,1356]{2,1,0:T(8,128)(2,1)S(1)}, u32[]{:S(2)}, u32[]{:S(2)}) collective-permute-start(bf16[2,24,1356]{2,1,0:T(8,128)(2,1)S(1)} %get-tuple-element.100), channel_id=1, source_target_pairs={{0,1},{1,0},{2,3},{3,2},{4,5},{5,4},{6,7},{7,6},{8,9},{9,8},{10,11... | collective-permute-start | bytes 390536 | tf_op jit(solution)/shard_map/ppermute | solution.py:90
  214.1 9.5 %collective-permute-start.39 = (bf16[4,24,1356]{2,1,0:T(8,128)(2,1)S(1)}, bf16[4,24,1356]{2,1,0:T(8,128)(2,1)S(1)}, u32[]{:S(2)}, u32[]{:S(2)}) collective-permute-start(bf16[4,24,1356]{2,1,0:T(8,128)(2,1)S(1)} %pad_maximum_fusion.7), channel_id=1, source_target_pairs={{0,2},{1,3},{2,0},{3,1},{4,6},{5,7},{6,4},{7,5},{8,10},{9,11},{10,... | collective-permute-start | bytes 781064 | tf_op jit(solution)/shard_map/ppermute | solution.py:95
  214.7 9.1 %collective-permute-start.37 = (bf16[4,24,1356]{2,1,0:T(8,128)(2,1)S(1)}, bf16[4,24,1356]{2,1,0:T(8,128)(2,1)S(1)}, u32[]{:S(2)}, u32[]{:S(2)}) collective-permute-start(bf16[4,24,1356]{2,1,0:T(8,128)(2,1)S(1)} %pad_maximum_fusion.6), channel_id=1, source_target_pairs={{0,1},{1,0},{2,3},{3,2},{4,5},{5,4},{6,7},{7,6},{8,9},{9,8},{10,11... | collective-permute-start | bytes 781064 | tf_op jit(solution)/shard_map/ppermute | solution.py:94
  216.3 12.1 %collective-permute-start.47 = (bf16[120,768]{1,0:T(8,128)(2,1)S(1)}, bf16[120,768]{1,0:T(8,128)(2,1)S(1)}, u32[]{:S(2)}, u32[]{:S(2)}) collective-permute-start(bf16[120,768]{1,0:T(8,128)(2,1)S(1)} %pad_maximum_fusion.13), channel_id=1, source_target_pairs={{0,2},{1,3},{2,0},{3,1},{4,6},{5,7},{6,4},{7,5},{8,10},{9,11},{10,... | collective-permute-start | bytes 552968 | tf_op jit(solution)/shard_map/ppermute | solution.py:95
  217.0 11.3 %collective-permute-start.45 = (bf16[120,768]{1,0:T(8,128)(2,1)S(1)}, bf16[120,768]{1,0:T(8,128)(2,1)S(1)}, u32[]{:S(2)}, u32[]{:S(2)}) collective-permute-start(bf16[120,768]{1,0:T(8,128)(2,1)S(1)} %pad_maximum_fusion.12), channel_id=1, source_target_pairs={{0,1},{1,0},{2,3},{3,2},{4,5},{5,4},{6,7},{7,6},{8,9},{9,8},{10,11... | collective-permute-start | bytes 552968 | tf_op jit(solution)/shard_map/ppermute | solution.py:94
  223.9 6.2 %collective-permute-start.42 = (bf16[24,1356]{1,0:T(8,128)(2,1)S(1)}, bf16[24,1356]{1,0:T(8,128)(2,1)S(1)}, u32[]{:S(2)}, u32[]{:S(2)}) collective-permute-start(bf16[24,1356]{1,0:T(8,128)(2,1)S(1)} %get-tuple-element.97), channel_id=1, source_target_pairs={{0,24},{8,16},{16,8},{24,0},{1,25},{9,17},{17,9},{25,1},{2,26},{10... | collective-permute-start | bytes 195272 | tf_op jit(solution)/shard_map/ppermute | solution.py:59
  226.1 5.4 %collective-permute-start.41 = (bf16[24,1356]{1,0:T(8,128)(2,1)S(1)}, bf16[24,1356]{1,0:T(8,128)(2,1)S(1)}, u32[]{:S(2)}, u32[]{:S(2)}) collective-permute-start(bf16[24,1356]{1,0:T(8,128)(2,1)S(1)} %get-tuple-element.98), channel_id=1, source_target_pairs={{0,16},{8,24},{16,0},{24,8},{1,17},{9,25},{17,1},{25,9},{2,18},{10... | collective-permute-start | bytes 195272 | tf_op jit(solution)/shard_map/ppermute | solution.py:59
  226.1 5.4 %collective-permute-start.40 = (bf16[24,1356]{1,0:T(8,128)(2,1)S(1)}, bf16[24,1356]{1,0:T(8,128)(2,1)S(1)}, u32[]{:S(2)}, u32[]{:S(2)}) collective-permute-start(bf16[24,1356]{1,0:T(8,128)(2,1)S(1)} %get-tuple-element.96), channel_id=1, source_target_pairs={{0,8},{8,0},{16,24},{24,16},{1,9},{9,1},{17,25},{25,17},{2,10},{10... | collective-permute-start | bytes 195272 | tf_op jit(solution)/shard_map/ppermute | solution.py:59
  (67 other events, 680.9 us)

commit v2 on v1

--- a/solution.py
+++ b/solution.py
@@ -3,6 +3,8 @@
 import jax
 import jax.numpy as jnp
 from jax import lax
+from jax.experimental import pallas as pl
+from jax.experimental.pallas import tpu as pltpu
 from jax.sharding import Mesh
 from jax.sharding import PartitionSpec as P
 
@@ -138,6 +140,491 @@
     )
 
 
+ROWS = 128
+COUNT = TP * ROWS
+WIDTH = 768
+SHARD = 24
+LANES = 1408
+QKV_AT = 768
+VEC_AT = 1344
+G_HEADS = HEADS // TP
+QUARTER = WIDTH // TP
+PARAMS = pltpu.CompilerParams(vmem_limit_bytes=48 * 1024 * 1024)
+
+
+def iota(shape, axis):
+    return lax.broadcasted_iota(jnp.int32, shape, axis)
+
+
+def split(number, by):
+    quotient = jnp.floor((number.astype(F32) + 0.5) * (1.0 / by)).astype(jnp.int32)
+    return quotient, number - quotient * by
+
+
+def hot(condition):
+    return jnp.where(condition, 1.0, 0.0).astype(BF)
+
+
+def owner_of_block(block, t, q):
+    return ((block & 3) ^ t) * 8 + ((block >> 2) ^ q)
+
+
+def feature_order(t, q):
+    block, row = split(iota((1, WIDTH), 1), SHARD)
+    return hot(iota((WIDTH, 1), 0) == owner_of_block(block, t, q) * SHARD + row)
+
+
+def head_order(q):
+    lane = iota((1, 256), 1)
+    row = lane & 31
+    place = ((lane >> 5) ^ q) * SHARD + row
+    place = jnp.where(row < SHARD, place, -1)
+    return hot(iota((QUARTER, 1), 0) == place)
+
+
+def vector_rows():
+    at = iota((160, 1), 0)
+    return hot(iota((1, WIDTH), 1) == (at & 31) * SHARD + (at >> 5))
+
+
+def dot(left, right, left_dim=1, right_dim=0):
+    return lax.dot_general(
+        left, right, (((left_dim,), (right_dim,)), ((), ())), preferred_element_type=F32
+    )
+
+
+def placing(number, length, owners):
+    owner, element = split(number, length)
+    return jnp.where(owners == owner, 1.0, 0.0), hot(iota((length, 1), 0) == element)
+
+
+def all_places(t, q):
+    block = iota((32, 1), 0)
+    owners = owner_of_block(block, t, q)
+    lane = iota((1, WIDTH), 1)
+    third, rest = split(iota((1, 3 * QUARTER), 1), QUARTER)
+    return (
+        placing(lane, SHARD, block),
+        placing(lane, SHARD, owners),
+        placing(third * WIDTH + t * QUARTER + rest, 3 * SHARD, owners),
+        placing(lane + t * WIDTH, 4 * SHARD, owners),
+    )
+
+
+def spread(values, places):
+    mask, element = places
+    return jnp.sum(dot(values.astype(BF), element) * mask, axis=0, keepdims=True)
+
+
+def collect(row, places):
+    mask, element = places
+    return dot((mask * row).astype(BF), element, 1, 1)
+
+
+def prepare_kernel(place, w_qkv, w_fc1, vector, *pieces):
+    t = place[0]
+    row = iota((SHARD, 64), 0)
+    packed = jnp.zeros((SHARD, 64), F32)
+    for i in range(5):
+        packed = jnp.where(row == i, vector[:, 64 * i : 64 * i + 64], packed)
+    packed = packed.astype(BF)
+    for rank in range(TP):
+
+        @pl.when(t == rank)
+        def _(rank=rank):
+            for k in range(TP):
+                r = rank ^ k
+                at = QUARTER * r
+                pieces[k][:, :] = jnp.concatenate(
+                    [
+                        w_fc1[:, WIDTH * r : WIDTH * (r + 1)],
+                        w_qkv[:, at : at + QUARTER],
+                        w_qkv[:, WIDTH + at : WIDTH + at + QUARTER],
+                        w_qkv[:, 2 * WIDTH + at : 2 * WIDTH + at + QUARTER],
+                        packed,
+                    ],
+                    axis=1,
+                )
+
+
+def normalize_kernel(place, *refs):
+    *slots, xhat, order = refs
+    order[:, :] = feature_order(place[0], place[1])
+    for k in range(TP):
+        rows = dot(slots[k][:, :], order[:, :])
+        removed = rows - jnp.mean(rows, axis=-1, keepdims=True)
+        variance = jnp.mean(removed * removed, axis=-1, keepdims=True)
+        xhat[ROWS * k : ROWS * (k + 1), :] = removed * lax.rsqrt(variance + epsilon)
+
+
+def frequency_lanes():
+    member = iota((1, 128), 1) & 7
+    lanes = jnp.zeros((1, 128), F32)
+    for i in range(ROT // 2):
+        lanes = jnp.where(member == i, 10000.0 ** (-2.0 * i / ROT), lanes)
+    return lanes
+
+
+def turn(values, cosine, sine):
+    member = iota((1, 384), 1) & 63
+    ahead = pltpu.roll(values, 384 - ROT // 2, 1)
+    behind = pltpu.roll(values, ROT // 2, 1)
+    partner = jnp.where(member < ROT // 2, ahead, behind)
+    return values * jnp.concatenate([cosine] * 3, axis=1) + partner * jnp.concatenate(
+        [sine] * 3, axis=1
+    )
+
+
+def gathered_blocks(refs, rows):
+    for core in range(2):
+        own, pair, third = refs[3 * core : 3 * core + 3]
+        yield 4 * core, own, 0
+        yield 4 * core + 1, pair, 0
+        yield 4 * core + 2, pair, rows
+        yield 4 * core + 3, third, 0
+
+
+def forward_kernel(place, xhat, *refs):
+    columns, tails, cots = refs[:6], refs[6:12], refs[12:16]
+    (
+        mat, h_one, h_two, d_up, q_low, k_low, v_low, probs, d_mixed, gains, cosine, sine,
+        out_zero, out_one, out_two, out_three, tail_keep, tail_send,
+        down, out_mat, upstream, mixed, grad_down,
+    ) = refs[16:]
+    t, q = place[0], place[1]
+    for kq, ref, at in gathered_blocks(columns, 96):
+        mat[96 * kq : 96 * kq + 96, :] = ref[at : at + 96, :]
+    for kq, ref, at in gathered_blocks(tails, 128):
+        first = pl.multiple_of((q ^ kq) * 96, 32)
+        down[pl.ds(first, 96), :] = ref[at : at + 96, :]
+        out_mat[32 * kq : 32 * kq + 32, :] = ref[at + 96 : at + 128, :]
+
+    slots, plain, of_qkv, of_up = all_places(t, q)
+    packed = dot(vector_rows(), mat[:, VEC_AT:])
+    vectors = jnp.concatenate([packed[32 * i : 32 * i + 32] for i in range(5)], axis=1)
+    gain_one, bias_one, gain_two, bias_two = [
+        spread(vectors[:, SHARD * i : SHARD * i + SHARD], slots) for i in range(4)
+    ]
+    vec_qkv = spread(vectors[:, 96:168], of_qkv)
+    vec_up = spread(vectors[:, 192:288], of_up)
+    vec_out = spread(vectors[:, 168:192], plain) + spread(vectors[:, 288:312], plain)
+    gains[:, :] = jnp.concatenate([gain_one, gain_two, vec_out, jnp.zeros((5, WIDTH), F32)], axis=0)
+
+    column = iota((1, ROWS), 1).astype(F32)
+    line = iota((ROWS, 1), 0).astype(F32)
+    masks = []
+    for k in range(TP):
+        end = jnp.zeros((1, 1), F32)
+        segment_line, segment_column = jnp.zeros((ROWS, 1), F32), jnp.zeros((1, ROWS), F32)
+        first_line = jnp.zeros((ROWS, 1), F32)
+        for s in range(4):
+            size = vectors[k : k + 1, 312 + s : 313 + s]
+            end = end + size
+            first_line = first_line + jnp.where(line >= end, size, 0.0)
+            segment_line = segment_line + jnp.where(line >= end, 1.0, 0.0)
+            segment_column = segment_column + jnp.where(column >= end, 1.0, 0.0)
+        live = line < end
+        masks.append(
+            (line == column) | (live & (segment_line == segment_column) & (column <= line))
+        )
+        angle = jnp.where(live, line - first_line, 0.0) * frequency_lanes()
+        member = iota((1, 128), 1) & 63
+        at = slice(ROWS * k, ROWS * (k + 1))
+        cosine[at, :] = jnp.where(member < ROT, jnp.cos(angle), 1.0)
+        sine[at, :] = jnp.where(member < ROT, jnp.sin(angle), 0.0) * jnp.where(
+            member < ROT // 2, -1.0, 1.0
+        )
+        upstream[at, :] = (cots[k][:, :].astype(F32) * jnp.where(live, 1.0, 0.0)).astype(BF)
+
+    h_two[:, :] = (xhat[:, :] * gain_two + bias_two).astype(BF)
+    up = dot(h_two[:, :], mat[:, :WIDTH]) + vec_up
+    phi = 0.5 * (1.0 + lax.erf(up * inv_sqrt_two))
+    act = (up * phi).astype(BF)
+    slope = phi + up * jnp.exp(-0.5 * up * up) * inv_sqrt_tau
+    share = dot(act, down[:, :])
+    grad_down[:, :] = dot(act, upstream[:, :], 0, 0)
+    d_up[:, :] = (dot(upstream[:, :], down[:, :], 1, 1) * slope).astype(BF)
+
+    h_one[:, :] = (xhat[:, :] * gain_one + bias_one).astype(BF)
+    qkv = dot(h_one[:, :], mat[:, QKV_AT:VEC_AT]) + vec_qkv
+    turned = turn(qkv[:, : 2 * QUARTER], cosine[:, :], sine[:, :])
+    q_low[:, :] = turned[:, :QUARTER].astype(BF)
+    k_low[:, :] = turned[:, QUARTER:].astype(BF)
+    v_low[:, :] = qkv[:, 2 * QUARTER :].astype(BF)
+    for k in range(TP):
+        at = slice(ROWS * k, ROWS * (k + 1))
+        for head in range(G_HEADS):
+            lanes = slice(HEAD * head, HEAD * (head + 1))
+            scores = dot(q_low[at, lanes], k_low[at, lanes], 1, 1) * 0.125
+            scores = jnp.where(masks[k], scores, neg_large)
+            exponent = jnp.exp(scores - jnp.max(scores, axis=-1, keepdims=True))
+            chances = exponent / jnp.sum(exponent, axis=-1, keepdims=True)
+            probs[G_HEADS * k + head] = chances
+            mixed[at, lanes] = dot(chances.astype(BF), v_low[at, lanes]).astype(BF)
+    order = head_order(q)
+    mixed_slots = dot(mixed[:, :], order).astype(BF)
+    share = share + dot(mixed_slots, out_mat[:, :])
+    out_zero[:, :] = share[:ROWS]
+    out_one[:, :] = share[ROWS : 2 * ROWS].astype(BF)
+    out_two[:, :] = share[2 * ROWS : 3 * ROWS]
+    out_three[:, :] = share[3 * ROWS :].astype(BF)
+    d_slots = dot(upstream[:, :], out_mat[:, :], 1, 1).astype(BF)
+    d_mixed[:, :] = dot(d_slots, order, 1, 1).astype(BF)
+    grad_out = dot(mixed_slots, upstream[:, :], 0, 0)
+    for kq in range(8):
+        target = tail_keep if kq < 4 else tail_send
+        at = 128 * (kq % 4)
+        first = pl.multiple_of((q ^ kq) * 96, 32)
+        target[at : at + 96, :] = grad_down[pl.ds(first, 96), :].astype(target.dtype)
+        target[at + 96 : at + 128, :] = grad_out[32 * kq : 32 * kq + 32].astype(target.dtype)
+
+
+def backward_kernel(
+    place, xhat, order, mat, h_one, h_two, d_up, q_low, k_low, v_low, probs, d_mixed, gains, cosine,
+    sine, cot, live, e_zero, e_one, e_two, e_three, col_keep, col_send, d_turned, d_qkv,
+):
+    t, q = place[0], place[1]
+    for k in range(TP):
+        at = slice(ROWS * k, ROWS * (k + 1))
+        for head in range(G_HEADS):
+            lanes = slice(HEAD * head, HEAD * (head + 1))
+            chances = probs[G_HEADS * k + head]
+            d_out = d_mixed[at, lanes]
+            d_probs = dot(d_out, v_low[at, lanes], 1, 1)
+            delta = jnp.sum(chances * d_probs, axis=-1, keepdims=True)
+            d_scores = (chances * (d_probs - delta)).astype(BF)
+            d_turned[at, lanes] = dot(d_scores, k_low[at, lanes]) * 0.125
+            d_turned[at, QUARTER + HEAD * head : QUARTER + HEAD * (head + 1)] = (
+                dot(d_scores, q_low[at, lanes], 0, 0) * 0.125
+            )
+            d_qkv[at, 2 * QUARTER + HEAD * head : 2 * QUARTER + HEAD * (head + 1)] = dot(
+                chances.astype(BF), d_out, 0, 0
+            ).astype(BF)
+    d_qkv[:, : 2 * QUARTER] = turn(d_turned[:, :], cosine[:, :], -sine[:, :]).astype(BF)
+
+    d_one = dot(d_qkv[:, :], mat[:, QKV_AT:VEC_AT], 1, 1)
+    d_two = dot(d_up[:, :], mat[:, :WIDTH], 1, 1)
+    share = (d_one * gains[0:1, :] + d_two * gains[1:2, :]).astype(BF)
+    share = dot(share, order[:, :], 1, 1)
+    e_zero[:, :] = share[:ROWS]
+    e_one[:, :] = share[ROWS : 2 * ROWS].astype(BF)
+    e_two[:, :] = share[2 * ROWS : 3 * ROWS]
+    e_three[:, :] = share[3 * ROWS :].astype(BF)
+
+    slots, plain, of_qkv, of_up = all_places(t, q)
+
+    def total(rows):
+        return jnp.sum(rows, axis=0, keepdims=True)
+
+    vectors = jnp.concatenate(
+        [
+            collect(total(d_one * xhat[:, :]), slots),
+            collect(total(d_one), slots),
+            collect(total(d_two * xhat[:, :]), slots),
+            collect(total(d_two), slots),
+            collect(total(cot[:, :].astype(F32) * live[:, :]), plain),
+            collect(total(d_qkv[:, :].astype(F32)), of_qkv),
+            collect(total(d_up[:, :].astype(F32)), of_up),
+            jnp.zeros((32, 32), F32),
+        ],
+        axis=1,
+    ).astype(BF)
+    packed = jnp.concatenate([vectors[:, 64 * i : 64 * i + 64] for i in range(5)], axis=0)
+    grads = jnp.concatenate(
+        [
+            dot(h_two[:, :], d_up[:, :], 0, 0),
+            dot(h_one[:, :], d_qkv[:, :], 0, 0),
+            dot(vector_rows(), packed, 0, 0),
+        ],
+        axis=1,
+    )
+    col_keep[:, :] = grads[:384]
+    col_send[:, :] = grads[384:].astype(BF)
+
+
+def columns_kernel(place, zero, one, two, three, qkv, up, *vectors):
+    t = place[0]
+    parts = [zero[:, :]] + [ref[:, :].astype(F32) for ref in (one, two, three)]
+    for rank in range(TP):
+
+        @pl.when(t == rank)
+        def _(rank=rank):
+            by_rank = [parts[rank ^ s] for s in range(TP)]
+            up[:, :] = jnp.concatenate([item[:, :WIDTH] for item in by_rank], axis=1)
+            qkv[:, :] = jnp.concatenate(
+                [
+                    item[:, QKV_AT + QUARTER * i : QKV_AT + QUARTER * (i + 1)]
+                    for i in range(3)
+                    for item in by_rank
+                ],
+                axis=1,
+            )
+
+    packed = sum(item[:8, VEC_AT:] for item in parts)
+    row = jnp.concatenate([packed[i : i + 1] for i in range(5)], axis=1)
+    at = 0
+    for ref in vectors:
+        size = ref.shape[1]
+        ref[:, :] = row[:, at : at + size]
+        at += size
+
+
+def output_kernel(zero, one, two, three, tokens, live, gains, output):
+    share = zero[:, :] + one[:, :].astype(F32) + two[:, :].astype(F32) + three[:, :].astype(F32)
+    output[:, :] = (live[:, :] * (tokens[:, :].astype(F32) + share + gains[2:3, :])).astype(BF)
+
+
+def input_kernel(zero, one, two, three, tokens, cot, live, grad):
+    e = zero[:, :] + one[:, :].astype(F32) + two[:, :].astype(F32) + three[:, :].astype(F32)
+    rows = tokens[:, :].astype(F32)
+    removed = rows - jnp.mean(rows, axis=-1, keepdims=True)
+    rstd = lax.rsqrt(jnp.mean(removed * removed, axis=-1, keepdims=True) + epsilon)
+    xhat = removed * rstd
+    dx = rstd * (
+        e - jnp.mean(e, axis=-1, keepdims=True) - xhat * jnp.mean(e * xhat, axis=-1, keepdims=True)
+    )
+    grad[:, :] = cot[:, :].astype(F32) * live[:, :] + dx
+
+
+def call(kernel, name, outs, *args, scratch=()):
+    space = [pl.BlockSpec(memory_space=pltpu.VMEM)] * len(args)
+    if args[0].dtype == jnp.int32:
+        space[0] = pl.BlockSpec(memory_space=pltpu.SMEM)
+    shapes = [jax.ShapeDtypeStruct(shape, kind) for shape, kind in outs]
+    return pl.pallas_call(
+        kernel,
+        name=name,
+        out_shape=shapes,
+        in_specs=space,
+        out_specs=[pl.BlockSpec(memory_space=pltpu.VMEM)] * len(shapes),
+        scratch_shapes=[pltpu.VMEM(shape, kind) for shape, kind in scratch],
+        compiler_params=PARAMS,
+    )(*args)
+
+
+def gather_plane(block):
+    half = block.shape[0] // 2
+    one = lax.ppermute(block, "fsdp", xor_pairs(4, 1))
+    two = lax.ppermute(block, "fsdp", xor_pairs(4, 2))
+    upper = lax.ppermute(one[:half], "fsdp", xor_pairs(4, 2))
+    lower = lax.ppermute(two[half:], "fsdp", xor_pairs(4, 1))
+    mine = [block, jnp.concatenate([one, two], axis=0), jnp.concatenate([upper, lower], axis=0)]
+    return mine + [lax.ppermute(part, "dq", xor_pairs(2, 1)) for part in mine]
+
+
+def scatter_plane(keep, send):
+    rows = keep.shape[0] // 4
+    half = rows // 2
+    pair = keep + lax.ppermute(send, "dq", xor_pairs(2, 1)).astype(F32)
+    mine, one, two, three = [pair[rows * k : rows * (k + 1)] for k in range(4)]
+    three = three.astype(BF)
+    upper = lax.ppermute(three[:half], "fsdp", xor_pairs(4, 1))
+    lower = lax.ppermute(three[half:], "fsdp", xor_pairs(4, 2))
+    two = jnp.concatenate([two[:half] + upper.astype(F32), two[half:]], axis=0)
+    one = jnp.concatenate([one[:half], one[half:] + lower.astype(F32)], axis=0)
+    one = lax.ppermute(one.astype(BF), "fsdp", xor_pairs(4, 1))
+    two = lax.ppermute(two.astype(BF), "fsdp", xor_pairs(4, 2))
+    return mine + one.astype(F32) + two.astype(F32)
+
+
+def gather_rows(block):
+    one = lax.ppermute(block, "t", xor_pairs(TP, 1))
+    two = lax.ppermute(block, "t", xor_pairs(TP, 2))
+    near = lax.ppermute(block, "t", [(1, 2), (2, 1)])
+    far = lax.ppermute(two, "t", [(2, 3), (1, 0)])
+    return [block, one, two, near + far]
+
+
+def scatter_rows(one, two, three):
+    relay = lax.ppermute(three, "t", [(0, 1), (3, 2)])
+    near = lax.ppermute(three, "t", [(1, 2), (2, 1)])
+    one = lax.ppermute(one, "t", xor_pairs(TP, 1))
+    two = lax.ppermute((two + relay.astype(F32)).astype(BF), "t", xor_pairs(TP, 2))
+    return one, two, near
+
+
+def plane_local(
+    tokens, lengths, ln_attn_gain, ln_attn_bias, ln_mlp_gain, ln_mlp_bias, w_qkv, b_qkv,
+    w_out, b_out, w_fc1, b_fc1, w_fc2, b_fc2, cotangent,
+):
+    t = lax.axis_index("t")
+    q = lax.axis_index("dq") * 4 + lax.axis_index("fsdp")
+    place = jnp.stack([t, q]).astype(jnp.int32)
+    live = jnp.where(iota((ROWS, 1), 0) < jnp.sum(lengths), 1.0, 0.0)
+    vector = jnp.concatenate(
+        [
+            ln_attn_gain, ln_attn_bias, ln_mlp_gain, ln_mlp_bias, b_qkv, b_out, b_fc1, b_fc2,
+            lengths[0].astype(BF), jnp.zeros((68,), BF),
+        ]
+    )
+    pieces = call(
+        prepare_kernel, "prepare", [((SHARD, LANES), BF)] * TP, place, w_qkv, w_fc1,
+        vector.astype(F32)[None],
+    )
+    tail = gather_plane(jnp.concatenate([w_fc2, w_out, jnp.zeros((8, WIDTH), BF)], axis=0))
+    columns = gather_plane(jnp.concatenate(exchange_t(pieces), axis=0))
+    token_slots = gather_rows(tokens)
+    cot_slots = gather_rows(cotangent)
+    wide = (COUNT, WIDTH)
+    xhat, order = call(
+        normalize_kernel, "normalize", [(wide, F32), ((WIDTH, WIDTH), BF)], place, *token_slots
+    )
+    third = (COUNT, QUARTER)
+    block = (ROWS, WIDTH)
+    (
+        mat, h_one, h_two, d_up, q_low, k_low, v_low, probs, d_mixed, gains, cosine, sine,
+        out_zero, out_one, out_two, out_three, tail_keep, tail_send,
+    ) = call(
+        forward_kernel,
+        "forward",
+        [
+            ((WIDTH, LANES), BF), (wide, BF), (wide, BF), (wide, BF), (third, BF), (third, BF),
+            (third, BF), ((HEADS, ROWS, ROWS), F32), (third, BF), ((8, WIDTH), F32),
+            ((COUNT, 128), F32), ((COUNT, 128), F32),
+            (block, F32), (block, BF), (block, F32), (block, BF), (wide, F32), (wide, BF),
+        ],
+        place, xhat, *columns, *tail, *cot_slots,
+        scratch=[
+            ((WIDTH, WIDTH), BF), ((256, WIDTH), BF), (wide, BF), (third, BF),
+            ((WIDTH, WIDTH), F32),
+        ],
+    )
+    out_arrived = scatter_rows(out_one, out_two, out_three)
+    tail_sum = scatter_plane(tail_keep, tail_send)
+    e_zero, e_one, e_two, e_three, col_keep, col_send = call(
+        backward_kernel,
+        "backward",
+        [
+            (block, F32), (block, BF), (block, F32), (block, BF),
+            ((384, LANES), F32), ((384, LANES), BF),
+        ],
+        place, xhat, order, mat, h_one, h_two, d_up, q_low, k_low, v_low, probs, d_mixed, gains,
+        cosine, sine, cotangent, live,
+        scratch=[((COUNT, 2 * QUARTER), F32), ((COUNT, 3 * QUARTER), BF)],
+    )
+    e_arrived = scatter_rows(e_one, e_two, e_three)
+    col_sum = scatter_plane(col_keep, col_send)
+    low_sum = col_sum.astype(BF)
+    arrived = exchange_t([low_sum[SHARD * k : SHARD * (k + 1)] for k in range(TP)])
+    (output,) = call(
+        output_kernel, "output", [(block, BF)], out_zero, *out_arrived, tokens, live, gains
+    )
+    (grad_tokens,) = call(
+        input_kernel, "input_gradient", [(block, F32)], e_zero, *e_arrived, tokens, cotangent, live
+    )
+    sizes = [SHARD] * 5 + [3 * SHARD, 4 * SHARD]
+    shard_qkv, shard_up, *vectors = call(
+        columns_kernel, "columns",
+        [((SHARD, 3 * WIDTH), F32), ((SHARD, 4 * WIDTH), F32)] + [((1, n), F32) for n in sizes],
+        place, col_sum[:SHARD], *arrived[1:],
+    )
+    g_one, b_one, g_two, b_two, branch, qkv_bias, up_bias = [item[0] for item in vectors]
+    return (
+        output, grad_tokens, g_one, b_one, g_two, b_two, shard_qkv, qkv_bias,
+        tail_sum[96 : 96 + SHARD], branch, shard_up, up_bias, tail_sum[:96], branch,
+    )
+
+
 def local(
     sizes,
     tokens,
@@ -156,6 +643,11 @@
     b_fc2,
     cotangent,
 ):
+    if sizes == (2, 4) and w_qkv.shape == (SHARD, 3 * WIDTH) and tokens.shape == (ROWS, WIDTH):
+        return plane_local(
+            tokens, lengths, ln_attn_gain, ln_attn_bias, ln_mlp_gain, ln_mlp_bias, w_qkv, b_qkv,
+            w_out, b_out, w_fc1, b_fc1, w_fc2, b_fc2, cotangent,
+        )
     t = lax.axis_index("t")
     q = lax.axis_index("dq") * sizes[1] + lax.axis_index("fsdp")
     qs = sizes[0] * sizes[1]

time: 238 us -> 172 us (0.72)
  local copies, waits for them, and re-layouts: 59.6 us -> 14.6 us
  Pallas kernels: 0 us -> 32.2 us
  other arithmetic: 35.7 us -> 4.08 us
  matrix products: 29.4 us -> 0 us
  starting transfers between devices: 56.1 us -> 61.6 us
  waiting for transfers between devices: 53.4 us -> 57.5 us
    pallas_call x0 -> x7, Pallas kernels: none -> 32.2 us  [call(): pl.pallas_call(kernel, name=name, out_shape=shapes, in_specs=space, out_s...]
    dot_general x17 -> x0, matrix products: 27.2 us -> none  [the longest x12 23 us: contract(): lax.dot_general(left, right, (((left_dim,), (right_dim,)), ((), ())), pre...]
    reshape x25 -> x0, local copies, waits for them, and re-layouts: 16.9 us -> none  [the longest x8 5.99 us: local(): item.reshape(shard, -1)]
    concatenate x16 -> x7, local copies, waits for them, and re-layouts: 15.7 us -> 1.02 us  [the longest x1 0.86 us: plane_local(): jnp.concatenate([ln_attn_gain, ln_attn_bias, ln_mlp_gain, ln_mlp_bias, b_...]
    convert_element_type x19 -> x4, other arithmetic: 11.8 us -> 0.2 us  [the longest x1 0.11 us: plane_local(): low_sum = col_sum.astype(BF)]
    slice x29 -> x10, local copies, waits for them, and re-layouts: 10.1 us -> 1.51 us  [the longest x1 0.73 us: plane_local(): tail_sum[:96]]
    unnamed x16 -> x0, other arithmetic: 6.58 us -> none
    another operation x16 -> x5, other arithmetic: 5.22 us -> 0.59 us
  transfers between devices with their start and end apart: 48 -> 46, of which waited for: 15 -> 16; matrix products, arithmetic and copies ran while one was open for 35% -> 4% of each run, Pallas kernels for 0% -> 3%
where the time goes in v2:
time: 172 us; the launch traced here: 171 us
  starting transfers between devices  61.6 us (36%)
  waiting for transfers between devices  57.5 us (33%)
  Pallas kernels  32.2 us (19%)
  local copies, waits for them, and re-layouts  14.6 us (8%)
  other arithmetic  4.08 us (2%)
    pallas_call x7, Pallas kernels, call(): pl.pallas_call(kernel, name=name, out_shape=shapes, in_specs=space, out_s...  32.2 us
    ppermute x2, waiting for transfers between devices, scatter_rows(): lax.ppermute((two + relay.astype(F32)).astype(BF), 't', xor_pairs(TP, 2))  16.4 us
    unnamed x38, local copies, waits for them, and re-layouts  12 us
    ppermute x6, starting transfers between devices, exchange_t(): lax.ppermute(pieces[k], 't', xor_pairs(TP, k))  11.3 us
    ppermute x2, waiting for transfers between devices, gather_rows(): far = lax.ppermute(two, 't', [(2, 3), (1, 0)])  7.91 us
    ppermute x2, starting transfers between devices, gather_rows(): one = lax.ppermute(block, 't', xor_pairs(TP, 1))  7.55 us
    ppermute x2, waiting for transfers between devices, gather_plane(): two = lax.ppermute(block, 'fsdp', xor_pairs(4, 2))  6.25 us
    ppermute x2, waiting for transfers between devices, scatter_rows(): relay = lax.ppermute(three, 't', [(0, 1), (3, 2)])  6.24 us
  transfers between devices with their start and end apart: 46, of which 16 were waited for; matrix products, arithmetic and copies ran while one was open for 4% of the time, Pallas kernels for 3%

profile of v2, /device:TPU:0, one launch (start us, length us, event | category | flops | bytes accessed | tf_op | source)
XLA Modules:
  0.0 171.2 jit_solution(5527866781204608667)
XLA Ops:
  0.6 4.1 %collective-permute-start.1 = (bf16[128,768]{1,0:T(8,128)(2,1)}, bf16[128,768]{1,0:T(8,128)(2,1)S(1)}, u32[]{:S(2)}, u32[]{:S(2)}) collective-permute-start(bf16[128,768]{1,0:T(8,128)(2,1)} %tokens.3), channel_id=1, source_target_pairs={{0,16},{8,24},{16,0},{24,8},{1,17},{9,25},{17,1},{25,9},{2,18},{10... | collective-permute-start | bytes 589832 | tf_op jit(solution)/shard_map/ppermute | solution.py:532
  5.4 2.9 %collective-permute-start = (bf16[128,768]{1,0:T(8,128)(2,1)}, bf16[128,768]{1,0:T(8,128)(2,1)S(1)}, u32[]{:S(2)}, u32[]{:S(2)}) collective-permute-start(bf16[128,768]{1,0:T(8,128)(2,1)} %tokens.3), channel_id=1, source_target_pairs={{0,8},{8,0},{16,24},{24,16},{1,9},{9,1},{17,25},{25,17},{2,10},{10... | collective-permute-start | bytes 589832 | tf_op jit(solution)/shard_map/ppermute | solution.py:531
  8.3 1.4 fusion.14
  13.5 3.4 %collective-permute-start.5 = (bf16[24,1408]{1,0:T(8,128)(2,1)S(1)}, bf16[24,1408]{1,0:T(8,128)(2,1)S(1)}, u32[]{:S(2)}, u32[]{:S(2)}) collective-permute-start(bf16[24,1408]{1,0:T(8,128)(2,1)S(1)} %get-tuple-element.56), channel_id=1, source_target_pairs={{0,16},{8,24},{16,0},{24,8},{1,17},{9,25},{17,1},{25,9},{2,18},{10... | collective-permute-start | bytes 202760 | tf_op jit(solution)/shard_map/ppermute | solution.py:61
  18.1 3.3 %collective-permute-start.6 = (bf16[24,1408]{1,0:T(8,128)(2,1)S(1)}, bf16[24,1408]{1,0:T(8,128)(2,1)S(1)}, u32[]{:S(2)}, u32[]{:S(2)}) collective-permute-start(bf16[24,1408]{1,0:T(8,128)(2,1)S(1)} %get-tuple-element.57), channel_id=1, source_target_pairs={{0,24},{8,16},{16,8},{24,0},{1,25},{9,17},{17,9},{25,1},{2,26},{10... | collective-permute-start | bytes 202760 | tf_op jit(solution)/shard_map/ppermute | solution.py:61
  21.4 1.3 collective-permute-done.5
  22.7 1.5 collective-permute-start.14
  24.2 1.6 collective-permute-start.15
  25.8 3.5 %collective-permute-done.14 = bf16[128,768]{1,0:T(8,128)(2,1)S(1)} collective-permute-done((bf16[128,768]{1,0:T(8,128)(2,1)S(1)}, bf16[128,768]{1,0:T(8,128)(2,1)S(1)}, u32[]{:S(2)}, u32[]{:S(2)}) %collective-permute-start.14) | collective-permute-done | bytes 196640 | tf_op jit(solution)/shard_map/ppermute | solution.py:507
  29.4 1.9 %collective-permute-start.7 = (bf16[96,1408]{1,0:T(8,128)(2,1)S(1)}, bf16[96,1408]{1,0:T(8,128)(2,1)S(1)}, u32[]{:S(2)}, u32[]{:S(2)}) collective-permute-start(bf16[96,1408]{1,0:T(8,128)(2,1)S(1)} %constant_dynamic-update-slice_fusion.refs_0_), channel_id=1, source_target_pairs={{0,1},{1,0},{2,3},{3,2},{4,5},{5,4},{6,7},{7,6},{8,9},{9,8},{10,11... | collective-permute-start | bytes 811016 | tf_op jit(solution)/shard_map/ppermute | solution.py:507
  31.3 1.6 collective-permute-start.16
  32.9 4.2 %collective-permute-done.16 = bf16[64,768]{1,0:T(8,128)(2,1)S(1)} collective-permute-done((bf16[64,768]{1,0:T(8,128)(2,1)S(1)}, bf16[64,768]{1,0:T(8,128)(2,1)S(1)}, u32[]{:S(2)}, u32[]{:S(2)}) %collective-permute-start.16) | collective-permute-done | bytes 98336 | tf_op jit(solution)/shard_map/ppermute | solution.py:509
  37.1 1.5 collective-permute-start.8
  38.8 6.2 %collective-permute-done.8 = bf16[96,1408]{1,0:T(8,128)(2,1)S(1)} collective-permute-done((bf16[96,1408]{1,0:T(8,128)(2,1)S(1)}, bf16[96,1408]{1,0:T(8,128)(2,1)S(1)}, u32[]{:S(2)}, u32[]{:S(2)}) %collective-permute-start.8) | collective-permute-done | bytes 270368 | tf_op jit(solution)/shard_map/ppermute | solution.py:508
  45.0 1.5 collective-permute-start.9
  47.5 4.7 %collective-permute-start.21 = (bf16[128,768]{1,0:T(8,128)(2,1)S(1)}, bf16[128,768]{1,0:T(8,128)(2,1)S(1)}, u32[]{:S(2)}, u32[]{:S(2)}) collective-permute-start(bf16[128,768]{1,0:T(8,128)(2,1)S(1)} %copy-done.1), channel_id=1, source_target_pairs={{0,8},{8,0},{16,24},{24,16},{1,9},{9,1},{17,25},{25,17},{2,10},{10... | collective-permute-start | bytes 589832 | tf_op jit(solution)/shard_map/ppermute | solution.py:531
  52.7 1.7 %collective-permute-done.22.refs_14_ = bf16[128,768]{1,0:T(8,128)(2,1)S(1)} collective-permute-done((bf16[128,768]{1,0:T(8,128)(2,1)S(1)}, bf16[128,768]{1,0:T(8,128)(2,1)S(1)}, u32[]{:S(2)}, u32[]{:S(2)}) %collective-permute-start.22) | collective-permute-done | bytes 196640 | tf_op jit(solution)/shard_map/ppermute | solution.py:532
  54.4 1.6 collective-permute-start.17
  56.0 1.3 collective-permute-start.3
  58.2 1.5 collective-permute-start.24
  59.8 4.6 %collective-permute-done.3 = bf16[128,768]{1,0:T(8,128)(2,1)S(1)} collective-permute-done((bf16[128,768]{1,0:T(8,128)(2,1)S(1)}, bf16[128,768]{1,0:T(8,128)(2,1)S(1)}, u32[]{:S(2)}, u32[]{:S(2)}) %collective-permute-start.3) | collective-permute-done | bytes 196640 | tf_op jit(solution)/shard_map/ppermute | solution.py:534
  64.4 3.3 %collective-permute-done.24 = bf16[128,768]{1,0:T(8,128)(2,1)S(1)} collective-permute-done((bf16[128,768]{1,0:T(8,128)(2,1)S(1)}, bf16[128,768]{1,0:T(8,128)(2,1)S(1)}, u32[]{:S(2)}, u32[]{:S(2)}) %collective-permute-start.24) | collective-permute-done | bytes 196640 | tf_op jit(solution)/shard_map/ppermute | solution.py:534
  68.5 1.7 %normalize.1 = (f32[512,768]{1,0:T(8,128)S(1)}, bf16[768,768]{1,0:T(8,128)(2,1)S(1)}) custom-call(s32[2]{0:T(128)S(1)} %pad_add_fusion.place, bf16[128,768]{1,0:T(8,128)(2,1)S(1)} %copy-done.2, bf16[128,768]{1,0:T(8,128)(2,1)S(1)} %collective-permute-done.refs_1_, bf16[128,768]{1,0:T(8,128)(2,1)S(1)} %collective-permute-done.1.refs_2_, ...), custom_call_target="tpu_custom_call" | custom-call | tf_op jit(solution)/shard_map/normalize/pallas_call | solution.py:494
  70.2 1.2 copy-done
  73.3 13.8 %forward.1 = (bf16[768,1408]{1,0:T(8,128)(2,1)}, bf16[512,768]{1,0:T(8,128)(2,1)}, bf16[512,768]{1,0:T(8,128)(2,1)}, bf16[512,768]{1,0:T(8,128)(2,1)}, bf16[512,...) custom-call(s32[2]{0:T(128)S(1)} %pad_add_fusion.place, ...), custom_call_target="tpu_custom_call" | custom-call | tf_op jit(solution)/shard_map/forward/pallas_call | solution.py:494
  91.7 12.3 %backward.1 = (f32[128,768]{1,0:T(8,128)S(1)}, bf16[128,768]{1,0:T(8,128)(2,1)S(1)}, f32[128,768]{1,0:T(8,128)S(1)}, bf16[128,768]{1,0:T(8,128)(2,1)S(1)}, f32[3...) custom-call(s32[2]{0:T(128)S(1)} %pad_add_fusion.place, f32[512,768]{1,0:T(8,128)} %copy-done, bf16[768,768]{1,0:T(8,128)(2,1)} %copy-done.3, ...), custom_call_target="tpu_custom_call" | custom-call | tf_op jit(solution)/shard_map/backward/pallas_call | solution.py:494
  104.0 1.5 collective-permute-start.30
  106.7 1.4 collective-permute-start.29
  108.2 2.6 %collective-permute-done.30 = bf16[128,768]{1,0:T(8,128)(2,1)S(1)} collective-permute-done((bf16[128,768]{1,0:T(8,128)(2,1)S(1)}, bf16[128,768]{1,0:T(8,128)(2,1)S(1)}, u32[]{:S(2)}, u32[]{:S(2)}) %collective-permute-start.30) | collective-permute-done | bytes 196640 | tf_op jit(solution)/shard_map/ppermute | solution.py:539
  110.7 4.4 %collective-permute-start.26 = (bf16[128,768]{1,0:T(8,128)(2,1)S(1)}, bf16[128,768]{1,0:T(8,128)(2,1)S(1)}, u32[]{:S(2)}, u32[]{:S(2)}) collective-permute-start(bf16[128,768]{1,0:T(8,128)(2,1)S(1)} %get-tuple-element.61), channel_id=1, source_target_pairs={{0,8},{24,16},{1,9},{25,17},{2,10},{26,18},{3,11},{27,19},{4,12},{... | collective-permute-start | bytes 589832 | tf_op jit(solution)/shard_map/ppermute | solution.py:539
  115.2 3.7 %collective-permute-done.26 = bf16[128,768]{1,0:T(8,128)(2,1)S(1)} collective-permute-done((bf16[128,768]{1,0:T(8,128)(2,1)S(1)}, bf16[128,768]{1,0:T(8,128)(2,1)S(1)}, u32[]{:S(2)}, u32[]{:S(2)}) %collective-permute-start.26) | collective-permute-done | bytes 196640 | tf_op jit(solution)/shard_map/ppermute | solution.py:539
  118.9 2.6 %collective-permute-start.31 = (bf16[128,768]{1,0:T(8,128)(2,1)S(1)}, bf16[128,768]{1,0:T(8,128)(2,1)S(1)}, u32[]{:S(2)}, u32[]{:S(2)}) collective-permute-start(bf16[128,768]{1,0:T(8,128)(2,1)S(1)} %add_convert_fusion), channel_id=1, source_target_pairs={{0,16},{8,24},{16,0},{24,8},{1,17},{9,25},{17,1},{25,9},{2,18},{10... | collective-permute-start | bytes 589832 | tf_op jit(solution)/shard_map/ppermute | solution.py:542
  122.2 2.2 %collective-permute-start.25 = (bf16[128,768]{1,0:T(8,128)(2,1)S(1)}, bf16[128,768]{1,0:T(8,128)(2,1)S(1)}, u32[]{:S(2)}, u32[]{:S(2)}) collective-permute-start(bf16[128,768]{1,0:T(8,128)(2,1)S(1)} %get-tuple-element.59), channel_id=1, source_target_pairs={{0,8},{8,0},{16,24},{24,16},{1,9},{9,1},{17,25},{25,17},{2,10},{10... | collective-permute-start | bytes 589832 | tf_op jit(solution)/shard_map/ppermute | solution.py:541
  124.4 8.4 %collective-permute-done.31.two = bf16[128,768]{1,0:T(8,128)(2,1)S(1)} collective-permute-done((bf16[128,768]{1,0:T(8,128)(2,1)S(1)}, bf16[128,768]{1,0:T(8,128)(2,1)S(1)}, u32[]{:S(2)}, u32[]{:S(2)}) %collective-permute-start.31) | collective-permute-done | bytes 196640 | tf_op jit(solution)/shard_map/ppermute | solution.py:542
  134.0 8.0 %collective-permute-done.27.two = bf16[128,768]{1,0:T(8,128)(2,1)S(1)} collective-permute-done((bf16[128,768]{1,0:T(8,128)(2,1)S(1)}, bf16[128,768]{1,0:T(8,128)(2,1)S(1)}, u32[]{:S(2)}, u32[]{:S(2)}) %collective-permute-start.27) | collective-permute-done | bytes 196640 | tf_op jit(solution)/shard_map/ppermute | solution.py:542
  143.0 1.4 copy-done.10
  144.7 1.2 collective-permute-start.34
  147.0 1.6 collective-permute-start.42
  148.9 1.9 %collective-permute-done.34 = bf16[48,1408]{1,0:T(8,128)(2,1)S(1)} collective-permute-done((bf16[48,1408]{1,0:T(8,128)(2,1)S(1)}, bf16[48,1408]{1,0:T(8,128)(2,1)S(1)}, u32[]{:S(2)}, u32[]{:S(2)}) %collective-permute-start.34) | collective-permute-done | bytes 135200 | tf_op jit(solution)/shard_map/ppermute | solution.py:522
  150.8 1.2 collective-permute-done.36
  152.7 1.7 collective-permute-start.37
  155.0 1.4 collective-permute-start.45
  156.5 4.4 %collective-permute-done.35 = bf16[96,1408]{1,0:T(8,128)(2,1)S(1)} collective-permute-done((bf16[96,1408]{1,0:T(8,128)(2,1)S(1)}, bf16[96,1408]{1,0:T(8,128)(2,1)S(1)}, u32[]{:S(2)}, u32[]{:S(2)}) %collective-permute-start.35) | collective-permute-done | bytes 270368 | tf_op jit(solution)/shard_map/ppermute | solution.py:525
  161.1 1.3 collective-permute-start.39
  162.4 3.0 %collective-permute-start.40 = (bf16[24,1408]{1,0:T(8,128)(2,1)S(1)}, bf16[24,1408]{1,0:T(8,128)(2,1)S(1)}, u32[]{:S(2)}, u32[]{:S(2)}) collective-permute-start(bf16[24,1408]{1,0:T(8,128)(2,1)S(1)} %get-tuple-element.110), channel_id=1, source_target_pairs={{0,24},{8,16},{16,8},{24,0},{1,25},{9,17},{17,9},{25,1},{2,26},{10... | collective-permute-start | bytes 202760 | tf_op jit(solution)/shard_map/ppermute | solution.py:61
  166.9 1.6 collective-permute-done.40.three
  168.5 1.5 columns.1
  170.0 1.2 copy.37
  (127 shorter events, 24.2 us)
Async XLA Ops:
  0.6 45.9 %collective-permute-start.1 = (bf16[128,768]{1,0:T(8,128)(2,1)}, bf16[128,768]{1,0:T(8,128)(2,1)S(1)}, u32[]{:S(2)}, u32[]{:S(2)}) collective-permute-start(bf16[128,768]{1,0:T(8,128)(2,1)} %tokens.3), channel_id=1, source_target_pairs={{0,16},{8,24},{16,0},{24,8},{1,17},{9,25},{17,1},{25,9},{2,18},{10... | collective-permute-start | bytes 589832 | tf_op jit(solution)/shard_map/ppermute | solution.py:532
  4.7 42.1 %collective-permute-start.2 = (bf16[128,768]{1,0:T(8,128)(2,1)}, bf16[128,768]{1,0:T(8,128)(2,1)S(1)}, u32[]{:S(2)}, u32[]{:S(2)}) collective-permute-start(bf16[128,768]{1,0:T(8,128)(2,1)} %tokens.3), channel_id=1, source_target_pairs={{8,16},{16,8},{9,17},{17,9},{10,18},{18,10},{11,19},{19,11},{12,20... | collective-permute-start | bytes 589832 | tf_op jit(solution)/shard_map/ppermute | solution.py:533
  5.4 42.1 %collective-permute-start = (bf16[128,768]{1,0:T(8,128)(2,1)}, bf16[128,768]{1,0:T(8,128)(2,1)S(1)}, u32[]{:S(2)}, u32[]{:S(2)}) collective-permute-start(bf16[128,768]{1,0:T(8,128)(2,1)} %tokens.3), channel_id=1, source_target_pairs={{0,8},{8,0},{16,24},{24,16},{1,9},{9,1},{17,25},{25,17},{2,10},{10... | collective-permute-start | bytes 589832 | tf_op jit(solution)/shard_map/ppermute | solution.py:531
  13.4 4.7 %collective-permute-start.4 = (bf16[24,1408]{1,0:T(8,128)(2,1)S(1)}, bf16[24,1408]{1,0:T(8,128)(2,1)S(1)}, u32[]{:S(2)}, u32[]{:S(2)}) collective-permute-start(bf16[24,1408]{1,0:T(8,128)(2,1)S(1)} %get-tuple-element.55), channel_id=1, source_target_pairs={{0,8},{8,0},{16,24},{24,16},{1,9},{9,1},{17,25},{25,17},{2,10},{10... | collective-permute-start | bytes 202760 | tf_op jit(solution)/shard_map/ppermute | solution.py:61
  13.5 9.2 %collective-permute-start.5 = (bf16[24,1408]{1,0:T(8,128)(2,1)S(1)}, bf16[24,1408]{1,0:T(8,128)(2,1)S(1)}, u32[]{:S(2)}, u32[]{:S(2)}) collective-permute-start(bf16[24,1408]{1,0:T(8,128)(2,1)S(1)} %get-tuple-element.56), channel_id=1, source_target_pairs={{0,16},{8,24},{16,0},{24,8},{1,17},{9,25},{17,1},{25,9},{2,18},{10... | collective-permute-start | bytes 202760 | tf_op jit(solution)/shard_map/ppermute | solution.py:61
  18.1 6.2 %collective-permute-start.6 = (bf16[24,1408]{1,0:T(8,128)(2,1)S(1)}, bf16[24,1408]{1,0:T(8,128)(2,1)S(1)}, u32[]{:S(2)}, u32[]{:S(2)}) collective-permute-start(bf16[24,1408]{1,0:T(8,128)(2,1)S(1)} %get-tuple-element.57), channel_id=1, source_target_pairs={{0,24},{8,16},{16,8},{24,0},{1,25},{9,17},{17,9},{25,1},{2,26},{10... | collective-permute-start | bytes 202760 | tf_op jit(solution)/shard_map/ppermute | solution.py:61
  22.7 6.7 %collective-permute-start.14 = (bf16[128,768]{1,0:T(8,128)(2,1)S(1)}, bf16[128,768]{1,0:T(8,128)(2,1)S(1)}, u32[]{:S(2)}, u32[]{:S(2)}) collective-permute-start(bf16[128,768]{1,0:T(8,128)(2,1)S(1)} %maximum_maximum_fusion.refs_6_), channel_id=1, source_target_pairs={{0,1},{1,0},{2,3},{3,2},{4,5},{5,4},{6,7},{7,6},{8,9},{9,8},{10,11... | collective-permute-start | bytes 589832 | tf_op jit(solution)/shard_map/ppermute | solution.py:507
  24.2 7.0 %collective-permute-start.15 = (bf16[128,768]{1,0:T(8,128)(2,1)S(1)}, bf16[128,768]{1,0:T(8,128)(2,1)S(1)}, u32[]{:S(2)}, u32[]{:S(2)}) collective-permute-start(bf16[128,768]{1,0:T(8,128)(2,1)S(1)} %maximum_maximum_fusion.refs_6_), channel_id=1, source_target_pairs={{0,2},{1,3},{2,0},{3,1},{4,6},{5,7},{6,4},{7,5},{8,10},{9,11},{10,... | collective-permute-start | bytes 589832 | tf_op jit(solution)/shard_map/ppermute | solution.py:508
  29.4 9.3 %collective-permute-start.7 = (bf16[96,1408]{1,0:T(8,128)(2,1)S(1)}, bf16[96,1408]{1,0:T(8,128)(2,1)S(1)}, u32[]{:S(2)}, u32[]{:S(2)}) collective-permute-start(bf16[96,1408]{1,0:T(8,128)(2,1)S(1)} %constant_dynamic-update-slice_fusion.refs_0_), channel_id=1, source_target_pairs={{0,1},{1,0},{2,3},{3,2},{4,5},{5,4},{6,7},{7,6},{8,9},{9,8},{10,11... | collective-permute-start | bytes 811016 | tf_op jit(solution)/shard_map/ppermute | solution.py:507
  31.3 5.8 %collective-permute-start.16 = (bf16[64,768]{1,0:T(8,128)(2,1)S(1)}, bf16[64,768]{1,0:T(8,128)(2,1)S(1)}, u32[]{:S(2)}, u32[]{:S(2)}) collective-permute-start(bf16[64,768]{1,0:T(8,128)(2,1)S(1)} %slice.122), channel_id=1, source_target_pairs={{0,2},{1,3},{2,0},{3,1},{4,6},{5,7},{6,4},{7,5},{8,10},{9,11},{10,... | collective-permute-start | bytes 294920 | tf_op jit(solution)/shard_map/ppermute | solution.py:509
  32.9 35.5 %copy-start.2 = (bf16[128,768]{1,0:T(8,128)(2,1)S(1)}, bf16[128,768]{1,0:T(8,128)(2,1)}, u32[]{:S(2)}) copy-start(bf16[128,768]{1,0:T(8,128)(2,1)} %tokens.3) | copy-start | bytes 589828
  37.1 7.9 %collective-permute-start.8 = (bf16[96,1408]{1,0:T(8,128)(2,1)S(1)}, bf16[96,1408]{1,0:T(8,128)(2,1)S(1)}, u32[]{:S(2)}, u32[]{:S(2)}) collective-permute-start(bf16[96,1408]{1,0:T(8,128)(2,1)S(1)} %constant_dynamic-update-slice_fusion.refs_0_), channel_id=1, source_target_pairs={{0,2},{1,3},{2,0},{3,1},{4,6},{5,7},{6,4},{7,5},{8,10},{9,11},{10,... | collective-permute-start | bytes 811016 | tf_op jit(solution)/shard_map/ppermute | solution.py:508
  38.6 13.9 %collective-permute-start.18 = (bf16[128,768]{1,0:T(8,128)(2,1)S(1)}, bf16[128,768]{1,0:T(8,128)(2,1)S(1)}, u32[]{:S(2)}, u32[]{:S(2)}) collective-permute-start(bf16[128,768]{1,0:T(8,128)(2,1)S(1)} %maximum_maximum_fusion.refs_6_), channel_id=1, source_target_pairs={{0,4},{4,0},{1,5},{5,1},{2,6},{6,2},{3,7},{7,3},{8,12},{12,8},{9,1... | collective-permute-start | bytes 589832 | tf_op jit(solution)/shard_map/ppermute | solution.py:512
  45.0 7.1 %collective-permute-start.9 = (bf16[48,1408]{1,0:T(8,128)(2,1)S(1)}, bf16[48,1408]{1,0:T(8,128)(2,1)S(1)}, u32[]{:S(2)}, u32[]{:S(2)}) collective-permute-start(bf16[48,1408]{1,0:T(8,128)(2,1)S(1)} %slice.120), channel_id=1, source_target_pairs={{0,2},{1,3},{2,0},{3,1},{4,6},{5,7},{6,4},{7,5},{8,10},{9,11},{10,... | collective-permute-start | bytes 405512 | tf_op jit(solution)/shard_map/ppermute | solution.py:509
  46.6 26.0 %copy-start.12 = (bf16[192,1408]{1,0:T(8,128)(2,1)}, bf16[192,1408]{1,0:T(8,128)(2,1)S(1)}, u32[]{:S(2)}) copy-start(bf16[192,1408]{1,0:T(8,128)(2,1)S(1)} %constant_dynamic-update-slice_fusion.4.refs_1_) | copy-start | bytes 1622020
  46.6 7.8 %collective-permute-start.22 = (bf16[128,768]{1,0:T(8,128)(2,1)S(1)}, bf16[128,768]{1,0:T(8,128)(2,1)S(1)}, u32[]{:S(2)}, u32[]{:S(2)}) collective-permute-start(bf16[128,768]{1,0:T(8,128)(2,1)S(1)} %copy-done.1), channel_id=1, source_target_pairs={{0,16},{8,24},{16,0},{24,8},{1,17},{9,25},{17,1},{25,9},{2,18},{10... | collective-permute-start | bytes 589832 | tf_op jit(solution)/shard_map/ppermute | solution.py:532
  46.8 9.2 %collective-permute-start.23 = (bf16[128,768]{1,0:T(8,128)(2,1)S(1)}, bf16[128,768]{1,0:T(8,128)(2,1)S(1)}, u32[]{:S(2)}, u32[]{:S(2)}) collective-permute-start(bf16[128,768]{1,0:T(8,128)(2,1)S(1)} %copy-done.1), channel_id=1, source_target_pairs={{8,16},{16,8},{9,17},{17,9},{10,18},{18,10},{11,19},{19,11},{12,20... | collective-permute-start | bytes 589832 | tf_op jit(solution)/shard_map/ppermute | solution.py:533
  47.5 9.8 %collective-permute-start.21 = (bf16[128,768]{1,0:T(8,128)(2,1)S(1)}, bf16[128,768]{1,0:T(8,128)(2,1)S(1)}, u32[]{:S(2)}, u32[]{:S(2)}) collective-permute-start(bf16[128,768]{1,0:T(8,128)(2,1)S(1)} %copy-done.1), channel_id=1, source_target_pairs={{0,8},{8,0},{16,24},{24,16},{1,9},{9,1},{17,25},{25,17},{2,10},{10... | collective-permute-start | bytes 589832 | tf_op jit(solution)/shard_map/ppermute | solution.py:531
  52.1 6.1 %collective-permute-start.10 = (bf16[48,1408]{1,0:T(8,128)(2,1)S(1)}, bf16[48,1408]{1,0:T(8,128)(2,1)S(1)}, u32[]{:S(2)}, u32[]{:S(2)}) collective-permute-start(bf16[48,1408]{1,0:T(8,128)(2,1)S(1)} %slice.121), channel_id=1, source_target_pairs={{0,1},{1,0},{2,3},{3,2},{4,5},{5,4},{6,7},{7,6},{8,9},{9,8},{10,11... | collective-permute-start | bytes 405512 | tf_op jit(solution)/shard_map/ppermute | solution.py:510
  52.6 19.9 %collective-permute-start.19 = (bf16[256,768]{1,0:T(8,128)(2,1)S(1)}, bf16[256,768]{1,0:T(8,128)(2,1)S(1)}, u32[]{:S(2)}, u32[]{:S(2)}) collective-permute-start(bf16[256,768]{1,0:T(8,128)(2,1)S(1)} %constant_dynamic-update-slice_fusion.8.refs_7_), channel_id=1, source_target_pairs={{0,4},{4,0},{1,5},{5,1},{2,6},{6,2},{3,7},{7,3},{8,12},{12,8},{9,1... | collective-permute-start | bytes 1179656 | tf_op jit(solution)/shard_map/ppermute | solution.py:512
  54.4 5.3 %collective-permute-start.17 = (bf16[64,768]{1,0:T(8,128)(2,1)S(1)}, bf16[64,768]{1,0:T(8,128)(2,1)S(1)}, u32[]{:S(2)}, u32[]{:S(2)}) collective-permute-start(bf16[64,768]{1,0:T(8,128)(2,1)S(1)} %slice.123), channel_id=1, source_target_pairs={{0,1},{1,0},{2,3},{3,2},{4,5},{5,4},{6,7},{7,6},{8,9},{9,8},{10,11... | collective-permute-start | bytes 294920 | tf_op jit(solution)/shard_map/ppermute | solution.py:510
  56.0 8.4 %collective-permute-start.3 = (bf16[128,768]{1,0:T(8,128)(2,1)S(1)}, bf16[128,768]{1,0:T(8,128)(2,1)S(1)}, u32[]{:S(2)}, u32[]{:S(2)}) collective-permute-start(bf16[128,768]{1,0:T(8,128)(2,1)S(1)} %collective-permute-done.1.refs_2_), channel_id=1, source_target_pairs={{16,24},{8,0},{17,25},{9,1},{18,26},{10,2},{19,27},{11,3},{20,28},... | collective-permute-start | bytes 589832 | tf_op jit(solution)/shard_map/ppermute | solution.py:534
  57.3 15.3 %collective-permute-start.12 = (bf16[192,1408]{1,0:T(8,128)(2,1)S(1)}, bf16[192,1408]{1,0:T(8,128)(2,1)S(1)}, u32[]{:S(2)}, u32[]{:S(2)}) collective-permute-start(bf16[192,1408]{1,0:T(8,128)(2,1)S(1)} %constant_dynamic-update-slice_fusion.4.refs_1_), channel_id=1, source_target_pairs={{0,4},{4,0},{1,5},{5,1},{2,6},{6,2},{3,7},{7,3},{8,12},{12,8},{9,1... | collective-permute-start | bytes 1622024 | tf_op jit(solution)/shard_map/ppermute | solution.py:512
  58.2 9.5 %collective-permute-start.24 = (bf16[128,768]{1,0:T(8,128)(2,1)S(1)}, bf16[128,768]{1,0:T(8,128)(2,1)S(1)}, u32[]{:S(2)}, u32[]{:S(2)}) collective-permute-start(bf16[128,768]{1,0:T(8,128)(2,1)S(1)} %collective-permute-done.22.refs_14_), channel_id=1, source_target_pairs={{16,24},{8,0},{17,25},{9,1},{18,26},{10,2},{19,27},{11,3},{20,28},... | collective-permute-start | bytes 589832 | tf_op jit(solution)/shard_map/ppermute | solution.py:534
  59.7 12.7 %collective-permute-start.11 = (bf16[96,1408]{1,0:T(8,128)(2,1)S(1)}, bf16[96,1408]{1,0:T(8,128)(2,1)S(1)}, u32[]{:S(2)}, u32[]{:S(2)}) collective-permute-start(bf16[96,1408]{1,0:T(8,128)(2,1)S(1)} %constant_dynamic-update-slice_fusion.refs_0_), channel_id=1, source_target_pairs={{0,4},{4,0},{1,5},{5,1},{2,6},{6,2},{3,7},{7,3},{8,12},{12,8},{9,1... | collective-permute-start | bytes 811016 | tf_op jit(solution)/shard_map/ppermute | solution.py:512
  64.4 8.1 %collective-permute-start.13 = (bf16[96,1408]{1,0:T(8,128)(2,1)S(1)}, bf16[96,1408]{1,0:T(8,128)(2,1)S(1)}, u32[]{:S(2)}, u32[]{:S(2)}) collective-permute-start(bf16[96,1408]{1,0:T(8,128)(2,1)S(1)} %constant_dynamic-update-slice_fusion.6.refs_2_), channel_id=1, source_target_pairs={{0,4},{4,0},{1,5},{5,1},{2,6},{6,2},{3,7},{7,3},{8,12},{12,8},{9,1... | collective-permute-start | bytes 811016 | tf_op jit(solution)/shard_map/ppermute | solution.py:512
  67.7 4.8 %collective-permute-start.20 = (bf16[128,768]{1,0:T(8,128)(2,1)S(1)}, bf16[128,768]{1,0:T(8,128)(2,1)S(1)}, u32[]{:S(2)}, u32[]{:S(2)}) collective-permute-start(bf16[128,768]{1,0:T(8,128)(2,1)S(1)} %constant_dynamic-update-slice_fusion.10.refs_8_), channel_id=1, source_target_pairs={{0,4},{4,0},{1,5},{5,1},{2,6},{6,2},{3,7},{7,3},{8,12},{12,8},{9,1... | collective-permute-start | bytes 589832 | tf_op jit(solution)/shard_map/ppermute | solution.py:512
  104.0 6.7 %collective-permute-start.30 = (bf16[128,768]{1,0:T(8,128)(2,1)S(1)}, bf16[128,768]{1,0:T(8,128)(2,1)S(1)}, u32[]{:S(2)}, u32[]{:S(2)}) collective-permute-start(bf16[128,768]{1,0:T(8,128)(2,1)S(1)} %get-tuple-element.78), channel_id=1, source_target_pairs={{0,8},{24,16},{1,9},{25,17},{2,10},{26,18},{3,11},{27,19},{4,12},{... | collective-permute-start | bytes 589832 | tf_op jit(solution)/shard_map/ppermute | solution.py:539
  105.5 37.3 %collective-permute-start.41 = (bf16[512,768]{1,0:T(8,128)(2,1)S(1)}, bf16[512,768]{1,0:T(8,128)(2,1)S(1)}, u32[]{:S(2)}, u32[]{:S(2)}) collective-permute-start(bf16[512,768]{1,0:T(8,128)(2,1)S(1)} %copy-done.14), channel_id=1, source_target_pairs={{0,4},{4,0},{1,5},{5,1},{2,6},{6,2},{3,7},{7,3},{8,12},{12,8},{9,1... | collective-permute-start | bytes 2359304 | tf_op jit(solution)/shard_map/ppermute | solution.py:518
  105.9 37.1 %collective-permute-start.33 = (bf16[384,1408]{1,0:T(8,128)(2,1)}, bf16[384,1408]{1,0:T(8,128)(2,1)S(1)}, u32[]{:S(2)}, u32[]{:S(2)}) collective-permute-start(bf16[384,1408]{1,0:T(8,128)(2,1)} %get-tuple-element.80), channel_id=1, source_target_pairs={{0,4},{4,0},{1,5},{5,1},{2,6},{6,2},{3,7},{7,3},{8,12},{12,8},{9,1... | collective-permute-start | bytes 3244040 | tf_op jit(solution)/shard_map/ppermute | solution.py:518
  106.1 16.2 %collective-permute-start.32 = (bf16[128,768]{1,0:T(8,128)(2,1)S(1)}, bf16[128,768]{1,0:T(8,128)(2,1)S(1)}, u32[]{:S(2)}, u32[]{:S(2)}) collective-permute-start(bf16[128,768]{1,0:T(8,128)(2,1)S(1)} %get-tuple-element.78), channel_id=1, source_target_pairs={{8,16},{16,8},{9,17},{17,9},{10,18},{18,10},{11,19},{19,11},{12,20... | collective-permute-start | bytes 589832 | tf_op jit(solution)/shard_map/ppermute | solution.py:540
  106.7 14.8 %collective-permute-start.29 = (bf16[128,768]{1,0:T(8,128)(2,1)S(1)}, bf16[128,768]{1,0:T(8,128)(2,1)S(1)}, u32[]{:S(2)}, u32[]{:S(2)}) collective-permute-start(bf16[128,768]{1,0:T(8,128)(2,1)S(1)} %get-tuple-element.76), channel_id=1, source_target_pairs={{0,8},{8,0},{16,24},{24,16},{1,9},{9,1},{17,25},{25,17},{2,10},{10... | collective-permute-start | bytes 589832 | tf_op jit(solution)/shard_map/ppermute | solution.py:541
  110.7 8.1 %collective-permute-start.26 = (bf16[128,768]{1,0:T(8,128)(2,1)S(1)}, bf16[128,768]{1,0:T(8,128)(2,1)S(1)}, u32[]{:S(2)}, u32[]{:S(2)}) collective-permute-start(bf16[128,768]{1,0:T(8,128)(2,1)S(1)} %get-tuple-element.61), channel_id=1, source_target_pairs={{0,8},{24,16},{1,9},{25,17},{2,10},{26,18},{3,11},{27,19},{4,12},{... | collective-permute-start | bytes 589832 | tf_op jit(solution)/shard_map/ppermute | solution.py:539
  118.9 13.9 %collective-permute-start.31 = (bf16[128,768]{1,0:T(8,128)(2,1)S(1)}, bf16[128,768]{1,0:T(8,128)(2,1)S(1)}, u32[]{:S(2)}, u32[]{:S(2)}) collective-permute-start(bf16[128,768]{1,0:T(8,128)(2,1)S(1)} %add_convert_fusion), channel_id=1, source_target_pairs={{0,16},{8,24},{16,0},{24,8},{1,17},{9,25},{17,1},{25,9},{2,18},{10... | collective-permute-start | bytes 589832 | tf_op jit(solution)/shard_map/ppermute | solution.py:542
  121.5 12.4 %collective-permute-start.28 = (bf16[128,768]{1,0:T(8,128)(2,1)S(1)}, bf16[128,768]{1,0:T(8,128)(2,1)S(1)}, u32[]{:S(2)}, u32[]{:S(2)}) collective-permute-start(bf16[128,768]{1,0:T(8,128)(2,1)S(1)} %get-tuple-element.61), channel_id=1, source_target_pairs={{8,16},{16,8},{9,17},{17,9},{10,18},{18,10},{11,19},{19,11},{12,20... | collective-permute-start | bytes 589832 | tf_op jit(solution)/shard_map/ppermute | solution.py:540
  122.2 11.7 %collective-permute-start.25 = (bf16[128,768]{1,0:T(8,128)(2,1)S(1)}, bf16[128,768]{1,0:T(8,128)(2,1)S(1)}, u32[]{:S(2)}, u32[]{:S(2)}) collective-permute-start(bf16[128,768]{1,0:T(8,128)(2,1)S(1)} %get-tuple-element.59), channel_id=1, source_target_pairs={{0,8},{8,0},{16,24},{24,16},{1,9},{9,1},{17,25},{25,17},{2,10},{10... | collective-permute-start | bytes 589832 | tf_op jit(solution)/shard_map/ppermute | solution.py:541
  132.8 9.1 %collective-permute-start.27 = (bf16[128,768]{1,0:T(8,128)(2,1)S(1)}, bf16[128,768]{1,0:T(8,128)(2,1)S(1)}, u32[]{:S(2)}, u32[]{:S(2)}) collective-permute-start(bf16[128,768]{1,0:T(8,128)(2,1)S(1)} %add_convert_fusion.1), channel_id=1, source_target_pairs={{0,16},{8,24},{16,0},{24,8},{1,17},{9,25},{17,1},{25,9},{2,18},{10... | collective-permute-start | bytes 589832 | tf_op jit(solution)/shard_map/ppermute | solution.py:542
  144.7 6.1 %collective-permute-start.34 = (bf16[48,1408]{1,0:T(8,128)(2,1)S(1)}, bf16[48,1408]{1,0:T(8,128)(2,1)S(1)}, u32[]{:S(2)}, u32[]{:S(2)}) collective-permute-start(bf16[48,1408]{1,0:T(8,128)(2,1)S(1)} %get-tuple-element.105), channel_id=1, source_target_pairs={{0,2},{1,3},{2,0},{3,1},{4,6},{5,7},{6,4},{7,5},{8,10},{9,11},{10,... | collective-permute-start | bytes 405512 | tf_op jit(solution)/shard_map/ppermute | solution.py:522
  145.8 6.1 %collective-permute-start.36 = (bf16[48,1408]{1,0:T(8,128)(2,1)S(1)}, bf16[48,1408]{1,0:T(8,128)(2,1)S(1)}, u32[]{:S(2)}, u32[]{:S(2)}) collective-permute-start(bf16[48,1408]{1,0:T(8,128)(2,1)S(1)} %get-tuple-element.104), channel_id=1, source_target_pairs={{0,1},{1,0},{2,3},{3,2},{4,5},{5,4},{6,7},{7,6},{8,9},{9,8},{10,11... | collective-permute-start | bytes 405512 | tf_op jit(solution)/shard_map/ppermute | solution.py:521
  147.0 7.4 %collective-permute-start.42 = (bf16[64,768]{1,0:T(8,128)(2,1)S(1)}, bf16[64,768]{1,0:T(8,128)(2,1)S(1)}, u32[]{:S(2)}, u32[]{:S(2)}) collective-permute-start(bf16[64,768]{1,0:T(8,128)(2,1)S(1)} %get-tuple-element.109), channel_id=1, source_target_pairs={{0,2},{1,3},{2,0},{3,1},{4,6},{5,7},{6,4},{7,5},{8,10},{9,11},{10,... | collective-permute-start | bytes 294920 | tf_op jit(solution)/shard_map/ppermute | solution.py:522
  148.6 5.8 %collective-permute-start.44 = (bf16[64,768]{1,0:T(8,128)(2,1)S(1)}, bf16[64,768]{1,0:T(8,128)(2,1)S(1)}, u32[]{:S(2)}, u32[]{:S(2)}) collective-permute-start(bf16[64,768]{1,0:T(8,128)(2,1)S(1)} %get-tuple-element.108), channel_id=1, source_target_pairs={{0,1},{1,0},{2,3},{3,2},{4,5},{5,4},{6,7},{7,6},{8,9},{9,8},{10,11... | collective-permute-start | bytes 294920 | tf_op jit(solution)/shard_map/ppermute | solution.py:521
  152.1 8.8 %collective-permute-start.35 = (bf16[96,1408]{1,0:T(8,128)(2,1)S(1)}, bf16[96,1408]{1,0:T(8,128)(2,1)S(1)}, u32[]{:S(2)}, u32[]{:S(2)}) collective-permute-start(bf16[96,1408]{1,0:T(8,128)(2,1)S(1)} %pad_maximum_fusion), channel_id=1, source_target_pairs={{0,1},{1,0},{2,3},{3,2},{4,5},{5,4},{6,7},{7,6},{8,9},{9,8},{10,11... | collective-permute-start | bytes 811016 | tf_op jit(solution)/shard_map/ppermute | solution.py:525
  152.7 8.1 %collective-permute-start.37 = (bf16[96,1408]{1,0:T(8,128)(2,1)S(1)}, bf16[96,1408]{1,0:T(8,128)(2,1)S(1)}, u32[]{:S(2)}, u32[]{:S(2)}) collective-permute-start(bf16[96,1408]{1,0:T(8,128)(2,1)S(1)} %pad_maximum_fusion.1), channel_id=1, source_target_pairs={{0,2},{1,3},{2,0},{3,1},{4,6},{5,7},{6,4},{7,5},{8,10},{9,11},{10,... | collective-permute-start | bytes 811016 | tf_op jit(solution)/shard_map/ppermute | solution.py:526
  154.5 11.0 %collective-permute-start.43 = (bf16[128,768]{1,0:T(8,128)(2,1)S(1)}, bf16[128,768]{1,0:T(8,128)(2,1)S(1)}, u32[]{:S(2)}, u32[]{:S(2)}) collective-permute-start(bf16[128,768]{1,0:T(8,128)(2,1)S(1)} %pad_maximum_fusion.2), channel_id=1, source_target_pairs={{0,1},{1,0},{2,3},{3,2},{4,5},{5,4},{6,7},{7,6},{8,9},{9,8},{10,11... | collective-permute-start | bytes 589832 | tf_op jit(solution)/shard_map/ppermute | solution.py:525
  155.0 10.4 %collective-permute-start.45 = (bf16[128,768]{1,0:T(8,128)(2,1)S(1)}, bf16[128,768]{1,0:T(8,128)(2,1)S(1)}, u32[]{:S(2)}, u32[]{:S(2)}) collective-permute-start(bf16[128,768]{1,0:T(8,128)(2,1)S(1)} %pad_maximum_fusion.3), channel_id=1, source_target_pairs={{0,2},{1,3},{2,0},{3,1},{4,6},{5,7},{6,4},{7,5},{8,10},{9,11},{10,... | collective-permute-start | bytes 589832 | tf_op jit(solution)/shard_map/ppermute | solution.py:526
  161.0 5.9 %collective-permute-start.38 = (bf16[24,1408]{1,0:T(8,128)(2,1)S(1)}, bf16[24,1408]{1,0:T(8,128)(2,1)S(1)}, u32[]{:S(2)}, u32[]{:S(2)}) collective-permute-start(bf16[24,1408]{1,0:T(8,128)(2,1)S(1)} %get-tuple-element.112), channel_id=1, source_target_pairs={{0,8},{8,0},{16,24},{24,16},{1,9},{9,1},{17,25},{25,17},{2,10},{10... | collective-permute-start | bytes 202760 | tf_op jit(solution)/shard_map/ppermute | solution.py:61
  161.1 5.8 %collective-permute-start.39 = (bf16[24,1408]{1,0:T(8,128)(2,1)S(1)}, bf16[24,1408]{1,0:T(8,128)(2,1)S(1)}, u32[]{:S(2)}, u32[]{:S(2)}) collective-permute-start(bf16[24,1408]{1,0:T(8,128)(2,1)S(1)} %get-tuple-element.111), channel_id=1, source_target_pairs={{0,16},{8,24},{16,0},{24,8},{1,17},{9,25},{17,1},{25,9},{2,18},{10... | collective-permute-start | bytes 202760 | tf_op jit(solution)/shard_map/ppermute | solution.py:61
  162.4 6.1 %collective-permute-start.40 = (bf16[24,1408]{1,0:T(8,128)(2,1)S(1)}, bf16[24,1408]{1,0:T(8,128)(2,1)S(1)}, u32[]{:S(2)}, u32[]{:S(2)}) collective-permute-start(bf16[24,1408]{1,0:T(8,128)(2,1)S(1)} %get-tuple-element.110), channel_id=1, source_target_pairs={{0,24},{8,16},{16,8},{24,0},{1,25},{9,17},{17,9},{25,1},{2,26},{10... | collective-permute-start | bytes 202760 | tf_op jit(solution)/shard_map/ppermute | solution.py:61
  (13 other events, 57.1 us)

commit v3 on v2

--- a/solution.py
+++ b/solution.py
@@ -144,12 +144,11 @@
 COUNT = TP * ROWS
 WIDTH = 768
 SHARD = 24
-LANES = 1408
-QKV_AT = 768
-VEC_AT = 1344
+VEC_AT = 576
+NARROW = 640
+SCALE = 10**10
 G_HEADS = HEADS // TP
 QUARTER = WIDTH // TP
-PARAMS = pltpu.CompilerParams(vmem_limit_bytes=48 * 1024 * 1024)
 
 
 def iota(shape, axis):
@@ -221,13 +220,15 @@
     return dot((mask * row).astype(BF), element, 1, 1)
 
 
-def prepare_kernel(place, w_qkv, w_fc1, vector, *pieces):
+def prepare_kernel(place, w_qkv, w_fc1, vector, tokens, *pieces):
     t = place[0]
     row = iota((SHARD, 64), 0)
     packed = jnp.zeros((SHARD, 64), F32)
     for i in range(5):
         packed = jnp.where(row == i, vector[:, 64 * i : 64 * i + 64], packed)
-    packed = packed.astype(BF)
+    packed = jnp.concatenate([packed.astype(BF), jnp.zeros((SHARD, 128), BF)], axis=1)
+    pieces[1][48:, :] = tokens[:, :]
+    pieces[2][48:, :] = tokens[:, :]
     for rank in range(TP):
 
         @pl.when(t == rank)
@@ -235,9 +236,8 @@
             for k in range(TP):
                 r = rank ^ k
                 at = QUARTER * r
-                pieces[k][:, :] = jnp.concatenate(
+                lower = jnp.concatenate(
                     [
-                        w_fc1[:, WIDTH * r : WIDTH * (r + 1)],
                         w_qkv[:, at : at + QUARTER],
                         w_qkv[:, WIDTH + at : WIDTH + at + QUARTER],
                         w_qkv[:, 2 * WIDTH + at : 2 * WIDTH + at + QUARTER],
@@ -245,13 +245,24 @@
                     ],
                     axis=1,
                 )
+                pieces[k][:48, :] = jnp.concatenate(
+                    [w_fc1[:, WIDTH * r : WIDTH * (r + 1)], lower], axis=0
+                )
+
+
+def merge_kernel(zero, one, two, three, columns):
+    parts = [ref[:48, :] for ref in (zero, one, two, three)]
+    columns[:, :] = jnp.concatenate(
+        [part[:SHARD] for part in parts] + [part[SHARD:] for part in parts], axis=0
+    )
 
 
 def normalize_kernel(place, *refs):
     *slots, xhat, order = refs
     order[:, :] = feature_order(place[0], place[1])
     for k in range(TP):
-        rows = dot(slots[k][:, :], order[:, :])
+        first = 48 if slots[k].shape[0] == 48 + ROWS else 0
+        rows = dot(slots[k][first : first + ROWS, :], order[:, :])
         removed = rows - jnp.mean(rows, axis=-1, keepdims=True)
         variance = jnp.mean(removed * removed, axis=-1, keepdims=True)
         xhat[ROWS * k : ROWS * (k + 1), :] = removed * lax.rsqrt(variance + epsilon)
@@ -275,32 +286,20 @@
     )
 
 
-def gathered_blocks(refs, rows):
-    for core in range(2):
-        own, pair, third = refs[3 * core : 3 * core + 3]
-        yield 4 * core, own, 0
-        yield 4 * core + 1, pair, 0
-        yield 4 * core + 2, pair, rows
-        yield 4 * core + 3, third, 0
-
-
 def forward_kernel(place, xhat, *refs):
-    columns, tails, cots = refs[:6], refs[6:12], refs[12:16]
+    columns = refs[:2]
     (
-        mat, h_one, h_two, d_up, q_low, k_low, v_low, probs, d_mixed, gains, cosine, sine,
-        out_zero, out_one, out_two, out_three, tail_keep, tail_send,
-        down, out_mat, upstream, mixed, grad_down,
-    ) = refs[16:]
+        mat_up, mat_qkv, h_one, h_two, act, slope, q_low, k_low, v_low, probs, mixed_slots, gains,
+        cosine, sine, live, mixed,
+    ) = refs[2:]
     t, q = place[0], place[1]
-    for kq, ref, at in gathered_blocks(columns, 96):
-        mat[96 * kq : 96 * kq + 96, :] = ref[at : at + 96, :]
-    for kq, ref, at in gathered_blocks(tails, 128):
-        first = pl.multiple_of((q ^ kq) * 96, 32)
-        down[pl.ds(first, 96), :] = ref[at : at + 96, :]
-        out_mat[32 * kq : 32 * kq + 32, :] = ref[at + 96 : at + 128, :]
+    for kq in range(8):
+        ref, at = columns[kq // 4], 192 * (kq % 4)
+        mat_up[96 * kq : 96 * kq + 96, :] = ref[at : at + 96, :]
+        mat_qkv[96 * kq : 96 * kq + 96, :] = ref[at + 96 : at + 192, :NARROW]
 
     slots, plain, of_qkv, of_up = all_places(t, q)
-    packed = dot(vector_rows(), mat[:, VEC_AT:])
+    packed = dot(vector_rows(), mat_qkv[:, VEC_AT:])
     vectors = jnp.concatenate([packed[32 * i : 32 * i + 32] for i in range(5)], axis=1)
     gain_one, bias_one, gain_two, bias_two = [
         spread(vectors[:, SHARD * i : SHARD * i + SHARD], slots) for i in range(4)
@@ -323,30 +322,27 @@
             first_line = first_line + jnp.where(line >= end, size, 0.0)
             segment_line = segment_line + jnp.where(line >= end, 1.0, 0.0)
             segment_column = segment_column + jnp.where(column >= end, 1.0, 0.0)
-        live = line < end
+        lives = line < end
         masks.append(
-            (line == column) | (live & (segment_line == segment_column) & (column <= line))
+            (line == column) | (lives & (segment_line == segment_column) & (column <= line))
         )
-        angle = jnp.where(live, line - first_line, 0.0) * frequency_lanes()
+        angle = jnp.where(lives, line - first_line, 0.0) * frequency_lanes()
         member = iota((1, 128), 1) & 63
         at = slice(ROWS * k, ROWS * (k + 1))
         cosine[at, :] = jnp.where(member < ROT, jnp.cos(angle), 1.0)
         sine[at, :] = jnp.where(member < ROT, jnp.sin(angle), 0.0) * jnp.where(
             member < ROT // 2, -1.0, 1.0
         )
-        upstream[at, :] = (cots[k][:, :].astype(F32) * jnp.where(live, 1.0, 0.0)).astype(BF)
+        live[at, :] = jnp.where(lives, 1.0, 0.0)
 
     h_two[:, :] = (xhat[:, :] * gain_two + bias_two).astype(BF)
-    up = dot(h_two[:, :], mat[:, :WIDTH]) + vec_up
+    up = dot(h_two[:, :], mat_up[:, :]) + vec_up
     phi = 0.5 * (1.0 + lax.erf(up * inv_sqrt_two))
-    act = (up * phi).astype(BF)
-    slope = phi + up * jnp.exp(-0.5 * up * up) * inv_sqrt_tau
-    share = dot(act, down[:, :])
-    grad_down[:, :] = dot(act, upstream[:, :], 0, 0)
-    d_up[:, :] = (dot(upstream[:, :], down[:, :], 1, 1) * slope).astype(BF)
+    act[:, :] = (up * phi).astype(BF)
+    slope[:, :] = phi + up * jnp.exp(-0.5 * up * up) * inv_sqrt_tau
 
     h_one[:, :] = (xhat[:, :] * gain_one + bias_one).astype(BF)
-    qkv = dot(h_one[:, :], mat[:, QKV_AT:VEC_AT]) + vec_qkv
+    qkv = dot(h_one[:, :], mat_qkv[:, :VEC_AT]) + vec_qkv
     turned = turn(qkv[:, : 2 * QUARTER], cosine[:, :], sine[:, :])
     q_low[:, :] = turned[:, :QUARTER].astype(BF)
     k_low[:, :] = turned[:, QUARTER:].astype(BF)
@@ -361,29 +357,51 @@
             chances = exponent / jnp.sum(exponent, axis=-1, keepdims=True)
             probs[G_HEADS * k + head] = chances
             mixed[at, lanes] = dot(chances.astype(BF), v_low[at, lanes]).astype(BF)
-    order = head_order(q)
-    mixed_slots = dot(mixed[:, :], order).astype(BF)
-    share = share + dot(mixed_slots, out_mat[:, :])
-    out_zero[:, :] = share[:ROWS]
-    out_one[:, :] = share[ROWS : 2 * ROWS].astype(BF)
-    out_two[:, :] = share[2 * ROWS : 3 * ROWS]
-    out_three[:, :] = share[3 * ROWS :].astype(BF)
-    d_slots = dot(upstream[:, :], out_mat[:, :], 1, 1).astype(BF)
-    d_mixed[:, :] = dot(d_slots, order, 1, 1).astype(BF)
-    grad_out = dot(mixed_slots, upstream[:, :], 0, 0)
+    mixed_slots[:, :] = dot(mixed[:, :], head_order(q)).astype(BF)
+
+
+def share_kernel(place, act, mixed_slots, *refs):
+    tails, down, out_mat, shares = refs[:2], refs[2], refs[3], refs[4:]
+    q = place[1]
     for kq in range(8):
-        target = tail_keep if kq < 4 else tail_send
-        at = 128 * (kq % 4)
+        ref, at = tails[kq // 4], 128 * (kq % 4)
+        first = pl.multiple_of((q ^ kq) * 96, 32)
+        down[pl.ds(first, 96), :] = ref[at : at + 96, :]
+        out_mat[32 * kq : 32 * kq + 32, :] = ref[at + 96 : at + 128, :]
+    total = dot(act[:, :], down[:, :]) + dot(mixed_slots[:, :], out_mat[:, :])
+    for k in range(TP):
+        shares[k][:, :] = total[ROWS * k : ROWS * (k + 1)].astype(shares[k].dtype)
+
+
+def upstream_kernel(place, *refs):
+    cots = refs[:4]
+    (
+        live, h_two, act, slope, mixed_slots, down, out_mat, d_up, d_mixed, keep, send,
+        upstream, grad_down,
+    ) = refs[4:]
+    q = place[1]
+    for k in range(TP):
+        at = slice(ROWS * k, ROWS * (k + 1))
+        last = cots[k].shape[0]
+        upstream[at, :] = (cots[k][last - ROWS :, :].astype(F32) * live[at, :]).astype(BF)
+    d_up[:, :] = (dot(upstream[:, :], down[:, :], 1, 1) * slope[:, :]).astype(BF)
+    grad_up = dot(h_two[:, :], d_up[:, :], 0, 0)
+    grad_down[:, :] = dot(act[:, :], upstream[:, :], 0, 0)
+    grad_out = dot(mixed_slots[:, :], upstream[:, :], 0, 0)
+    for kq in range(8):
+        target = keep if kq < 4 else send
+        at = 224 * (kq % 4)
         first = pl.multiple_of((q ^ kq) * 96, 32)
         target[at : at + 96, :] = grad_down[pl.ds(first, 96), :].astype(target.dtype)
         target[at + 96 : at + 128, :] = grad_out[32 * kq : 32 * kq + 32].astype(target.dtype)
-
-
-def backward_kernel(
-    place, xhat, order, mat, h_one, h_two, d_up, q_low, k_low, v_low, probs, d_mixed, gains, cosine,
-    sine, cot, live, e_zero, e_one, e_two, e_three, col_keep, col_send, d_turned, d_qkv,
+        target[at + 128 : at + 224, :] = grad_up[96 * kq : 96 * kq + 96].astype(target.dtype)
+    d_slots = dot(upstream[:, :], out_mat[:, :], 1, 1).astype(BF)
+    d_mixed[:, :] = dot(d_slots, head_order(q), 1, 1).astype(BF)
+
+
+def attention_kernel(
+    q_low, k_low, v_low, probs, d_mixed, cosine, sine, d_qkv, d_turned
 ):
-    t, q = place[0], place[1]
     for k in range(TP):
         at = slice(ROWS * k, ROWS * (k + 1))
         for head in range(G_HEADS):
@@ -402,14 +420,18 @@
             ).astype(BF)
     d_qkv[:, : 2 * QUARTER] = turn(d_turned[:, :], cosine[:, :], -sine[:, :]).astype(BF)
 
-    d_one = dot(d_qkv[:, :], mat[:, QKV_AT:VEC_AT], 1, 1)
-    d_two = dot(d_up[:, :], mat[:, :WIDTH], 1, 1)
+
+def backward_kernel(
+    place, xhat, order, mat_up, mat_qkv, h_one, d_up, d_qkv, gains, cot, live, *refs
+):
+    shares, (keep, send) = refs[:4], refs[4:]
+    t, q = place[0], place[1]
+    d_one = dot(d_qkv[:, :], mat_qkv[:, :VEC_AT], 1, 1)
+    d_two = dot(d_up[:, :], mat_up[:, :], 1, 1)
     share = (d_one * gains[0:1, :] + d_two * gains[1:2, :]).astype(BF)
     share = dot(share, order[:, :], 1, 1)
-    e_zero[:, :] = share[:ROWS]
-    e_one[:, :] = share[ROWS : 2 * ROWS].astype(BF)
-    e_two[:, :] = share[2 * ROWS : 3 * ROWS]
-    e_three[:, :] = share[3 * ROWS :].astype(BF)
+    for k in range(TP):
+        shares[k][:, :] = share[ROWS * k : ROWS * (k + 1)].astype(shares[k].dtype)
 
     slots, plain, of_qkv, of_up = all_places(t, q)
 
@@ -422,7 +444,7 @@
             collect(total(d_one), slots),
             collect(total(d_two * xhat[:, :]), slots),
             collect(total(d_two), slots),
-            collect(total(cot[:, :].astype(F32) * live[:, :]), plain),
+            collect(total(cot[:, :].astype(F32) * live[:ROWS, :]), plain),
             collect(total(d_qkv[:, :].astype(F32)), of_qkv),
             collect(total(d_up[:, :].astype(F32)), of_up),
             jnp.zeros((32, 32), F32),
@@ -431,15 +453,10 @@
     ).astype(BF)
     packed = jnp.concatenate([vectors[:, 64 * i : 64 * i + 64] for i in range(5)], axis=0)
     grads = jnp.concatenate(
-        [
-            dot(h_two[:, :], d_up[:, :], 0, 0),
-            dot(h_one[:, :], d_qkv[:, :], 0, 0),
-            dot(vector_rows(), packed, 0, 0),
-        ],
-        axis=1,
-    )
-    col_keep[:, :] = grads[:384]
-    col_send[:, :] = grads[384:].astype(BF)
+        [dot(h_one[:, :], d_qkv[:, :], 0, 0), dot(vector_rows(), packed, 0, 0)], axis=1
+    )
+    keep[:, :] = grads[:384]
+    send[:, :] = grads[384:].astype(BF)
 
 
 def columns_kernel(place, zero, one, two, three, qkv, up, *vectors):
@@ -453,20 +470,21 @@
             up[:, :] = jnp.concatenate([item[:, :WIDTH] for item in by_rank], axis=1)
             qkv[:, :] = jnp.concatenate(
                 [
-                    item[:, QKV_AT + QUARTER * i : QKV_AT + QUARTER * (i + 1)]
+                    item[:, WIDTH + QUARTER * i : WIDTH + QUARTER * (i + 1)]
                     for i in range(3)
                     for item in by_rank
                 ],
                 axis=1,
             )
 
-    packed = sum(item[:8, VEC_AT:] for item in parts)
+    packed = sum(item[:8, WIDTH + VEC_AT :] for item in parts)
     row = jnp.concatenate([packed[i : i + 1] for i in range(5)], axis=1)
     at = 0
-    for ref in vectors:
+    for ref in vectors[:-1]:
         size = ref.shape[1]
         ref[:, :] = row[:, at : at + size]
         at += size
+    vectors[-1][:, :] = row[:, 4 * SHARD : 5 * SHARD]
 
 
 def output_kernel(zero, one, two, three, tokens, live, gains, output):
@@ -486,7 +504,7 @@
     grad[:, :] = cot[:, :].astype(F32) * live[:, :] + dx
 
 
-def call(kernel, name, outs, *args, scratch=()):
+def call(kernel, name, outs, *args, scratch=(), mib=16, us=1):
     space = [pl.BlockSpec(memory_space=pltpu.VMEM)] * len(args)
     if args[0].dtype == jnp.int32:
         space[0] = pl.BlockSpec(memory_space=pltpu.SMEM)
@@ -498,49 +516,40 @@
         in_specs=space,
         out_specs=[pl.BlockSpec(memory_space=pltpu.VMEM)] * len(shapes),
         scratch_shapes=[pltpu.VMEM(shape, kind) for shape, kind in scratch],
-        compiler_params=PARAMS,
+        cost_estimate=pl.CostEstimate(flops=us * SCALE, transcendentals=0, bytes_accessed=us * SCALE // 1000),
+        compiler_params=pltpu.CompilerParams(vmem_limit_bytes=mib * 1024 * 1024),
     )(*args)
 
 
-def gather_plane(block):
-    half = block.shape[0] // 2
-    one = lax.ppermute(block, "fsdp", xor_pairs(4, 1))
-    two = lax.ppermute(block, "fsdp", xor_pairs(4, 2))
-    upper = lax.ppermute(one[:half], "fsdp", xor_pairs(4, 2))
-    lower = lax.ppermute(two[half:], "fsdp", xor_pairs(4, 1))
-    mine = [block, jnp.concatenate([one, two], axis=0), jnp.concatenate([upper, lower], axis=0)]
-    return mine + [lax.ppermute(part, "dq", xor_pairs(2, 1)) for part in mine]
-
-
-def scatter_plane(keep, send):
-    rows = keep.shape[0] // 4
+def after(array, *others):
+    return lax.optimization_barrier((array, others))[0]
+
+
+def xor_permutes(block, axis, count):
+    return [lax.ppermute(block, axis, xor_pairs(count, k)) for k in range(1, 4)]
+
+
+def plane_pair(keep, send):
+    return keep + lax.ppermute(send, "dq", xor_pairs(2, 1)).astype(F32)
+
+
+def plane_relay(pair):
+    rows = pair.shape[0] // 4
+    three = pair[3 * rows :].astype(BF)
+    upper = lax.ppermute(three[: rows // 2], "fsdp", xor_pairs(4, 1))
+    lower = lax.ppermute(three[rows // 2 :], "fsdp", xor_pairs(4, 2))
+    return upper, lower
+
+
+def plane_last(pair, upper, lower):
+    rows = pair.shape[0] // 4
     half = rows // 2
-    pair = keep + lax.ppermute(send, "dq", xor_pairs(2, 1)).astype(F32)
-    mine, one, two, three = [pair[rows * k : rows * (k + 1)] for k in range(4)]
-    three = three.astype(BF)
-    upper = lax.ppermute(three[:half], "fsdp", xor_pairs(4, 1))
-    lower = lax.ppermute(three[half:], "fsdp", xor_pairs(4, 2))
+    mine, one, two = [pair[rows * k : rows * (k + 1)] for k in range(3)]
     two = jnp.concatenate([two[:half] + upper.astype(F32), two[half:]], axis=0)
     one = jnp.concatenate([one[:half], one[half:] + lower.astype(F32)], axis=0)
     one = lax.ppermute(one.astype(BF), "fsdp", xor_pairs(4, 1))
     two = lax.ppermute(two.astype(BF), "fsdp", xor_pairs(4, 2))
     return mine + one.astype(F32) + two.astype(F32)
-
-
-def gather_rows(block):
-    one = lax.ppermute(block, "t", xor_pairs(TP, 1))
-    two = lax.ppermute(block, "t", xor_pairs(TP, 2))
-    near = lax.ppermute(block, "t", [(1, 2), (2, 1)])
-    far = lax.ppermute(two, "t", [(2, 3), (1, 0)])
-    return [block, one, two, near + far]
-
-
-def scatter_rows(one, two, three):
-    relay = lax.ppermute(three, "t", [(0, 1), (3, 2)])
-    near = lax.ppermute(three, "t", [(1, 2), (2, 1)])
-    one = lax.ppermute(one, "t", xor_pairs(TP, 1))
-    two = lax.ppermute((two + relay.astype(F32)).astype(BF), "t", xor_pairs(TP, 2))
-    return one, two, near
 
 
 def plane_local(
@@ -557,71 +566,108 @@
             lengths[0].astype(BF), jnp.zeros((68,), BF),
         ]
     )
+    block = (ROWS, WIDTH)
+    piece = ((48, WIDTH), BF)
+    tail = jnp.concatenate([w_fc2, w_out, jnp.zeros((8, WIDTH), BF)], axis=0)
+    tail_one = lax.ppermute(tail, "fsdp", xor_pairs(4, 1))
+    tail_two = lax.ppermute(tail, "fsdp", xor_pairs(4, 2))
+    tail_three = lax.ppermute(after(tail, tail_one), "fsdp", xor_pairs(4, 3))
+    piece_rows = ((48 + ROWS, WIDTH), BF)
     pieces = call(
-        prepare_kernel, "prepare", [((SHARD, LANES), BF)] * TP, place, w_qkv, w_fc1,
-        vector.astype(F32)[None],
-    )
-    tail = gather_plane(jnp.concatenate([w_fc2, w_out, jnp.zeros((8, WIDTH), BF)], axis=0))
-    columns = gather_plane(jnp.concatenate(exchange_t(pieces), axis=0))
-    token_slots = gather_rows(tokens)
-    cot_slots = gather_rows(cotangent)
+        prepare_kernel, "prepare", [piece, piece_rows, piece_rows, piece],
+        place, w_qkv, w_fc1, vector.astype(F32)[None], tokens,
+    )
+    pieces = exchange_t(pieces)
+    token_one, token_two = pieces[1], pieces[2]
+    (columns,) = call(merge_kernel, "merge", [((192, WIDTH), BF)], *pieces)
+    columns = after(columns, tail_one, tail_two, tail_three)
+    rows_three = lax.ppermute(
+        after(jnp.concatenate([tokens, cotangent], axis=0), token_one), "t", xor_pairs(TP, 3)
+    )
+    arrived = xor_permutes(columns, "fsdp", 4)
+    columns = jnp.concatenate([columns] + arrived, axis=0)
+    columns = [columns, lax.ppermute(columns, "dq", xor_pairs(2, 1))]
+    tail = jnp.concatenate([tail, tail_one, tail_two, tail_three], axis=0)
+    tail = [tail, lax.ppermute(tail, "dq", xor_pairs(2, 1))]
     wide = (COUNT, WIDTH)
     xhat, order = call(
-        normalize_kernel, "normalize", [(wide, F32), ((WIDTH, WIDTH), BF)], place, *token_slots
-    )
+        normalize_kernel, "normalize", [(wide, F32), ((WIDTH, WIDTH), BF)],
+        place, tokens, token_one, token_two, rows_three,
+    )
+    cot = after(cotangent, xhat)
+    cot_slots = [lax.ppermute(cot, "t", xor_pairs(TP, k)) for k in (1, 2)] + [rows_three]
     third = (COUNT, QUARTER)
-    block = (ROWS, WIDTH)
     (
-        mat, h_one, h_two, d_up, q_low, k_low, v_low, probs, d_mixed, gains, cosine, sine,
-        out_zero, out_one, out_two, out_three, tail_keep, tail_send,
+        mat_up, mat_qkv, h_one, h_two, act, slope, q_low, k_low, v_low, probs, mixed_slots, gains,
+        cosine, sine, lives,
     ) = call(
         forward_kernel,
         "forward",
         [
-            ((WIDTH, LANES), BF), (wide, BF), (wide, BF), (wide, BF), (third, BF), (third, BF),
-            (third, BF), ((HEADS, ROWS, ROWS), F32), (third, BF), ((8, WIDTH), F32),
-            ((COUNT, 128), F32), ((COUNT, 128), F32),
-            (block, F32), (block, BF), (block, F32), (block, BF), (wide, F32), (wide, BF),
+            ((WIDTH, WIDTH), BF), ((WIDTH, NARROW), BF),
+            (wide, BF), (wide, BF), (wide, BF), (wide, F32), (third, BF), (third, BF),
+            (third, BF), ((HEADS, ROWS, ROWS), F32), ((COUNT, 256), BF), ((8, WIDTH), F32),
+            ((COUNT, 128), F32), ((COUNT, 128), F32), ((COUNT, 1), F32),
         ],
-        place, xhat, *columns, *tail, *cot_slots,
-        scratch=[
-            ((WIDTH, WIDTH), BF), ((256, WIDTH), BF), (wide, BF), (third, BF),
-            ((WIDTH, WIDTH), F32),
-        ],
-    )
-    out_arrived = scatter_rows(out_one, out_two, out_three)
-    tail_sum = scatter_plane(tail_keep, tail_send)
-    e_zero, e_one, e_two, e_three, col_keep, col_send = call(
+        place, xhat, *columns,
+        scratch=[(third, BF)],
+        us=8,
+    )
+    shares = [(block, F32)] + [(block, BF)] * 3
+    down, out_mat, *out = call(
+        share_kernel, "share", [((WIDTH, WIDTH), BF), ((256, WIDTH), BF)] + shares,
+        place, act, mixed_slots, *tail,
+        us=2,
+    )
+    out = exchange_t(out)
+    d_up, d_mixed, tail_keep, tail_send = call(
+        upstream_kernel,
+        "upstream",
+        [(wide, BF), (third, BF), ((896, WIDTH), F32), ((896, WIDTH), BF)],
+        place, cotangent, *cot_slots, lives, h_two, act, slope, mixed_slots, down, out_mat,
+        scratch=[(wide, BF), ((WIDTH, WIDTH), F32)],
+        us=4,
+    )
+    tail_pair = plane_pair(tail_keep, tail_send)
+    (d_qkv,) = call(
+        attention_kernel, "attention", [((COUNT, 3 * QUARTER), BF)],
+        q_low, k_low, v_low, probs, d_mixed, cosine, sine,
+        scratch=[((COUNT, 2 * QUARTER), F32)],
+        us=5,
+    )
+    d_qkv = after(d_qkv, tail_pair, out[1])
+    tail_relay = plane_relay(tail_pair)
+    *e, col_keep, col_send = call(
         backward_kernel,
         "backward",
-        [
-            (block, F32), (block, BF), (block, F32), (block, BF),
-            ((384, LANES), F32), ((384, LANES), BF),
-        ],
-        place, xhat, order, mat, h_one, h_two, d_up, q_low, k_low, v_low, probs, d_mixed, gains,
-        cosine, sine, cotangent, live,
-        scratch=[((COUNT, 2 * QUARTER), F32), ((COUNT, 3 * QUARTER), BF)],
-    )
-    e_arrived = scatter_rows(e_one, e_two, e_three)
-    col_sum = scatter_plane(col_keep, col_send)
+        shares + [((384, NARROW), F32), ((384, NARROW), BF)],
+        place, xhat, order, mat_up, mat_qkv, h_one, d_up, d_qkv, gains, cotangent, lives,
+        us=4,
+    )
+    col_pair = plane_pair(col_keep, after(col_send, tail_relay, out[2:]))
+    col_relay = plane_relay(col_pair)
+    e = exchange_t([after(item, out, col_pair) for item in e])
+    col_sum = plane_last(col_pair, *col_relay)
+    tail_sum = plane_last(tail_pair, *tail_relay)
+    col_sum = jnp.concatenate([tail_sum[128:], col_sum], axis=1)
     low_sum = col_sum.astype(BF)
     arrived = exchange_t([low_sum[SHARD * k : SHARD * (k + 1)] for k in range(TP)])
     (output,) = call(
-        output_kernel, "output", [(block, BF)], out_zero, *out_arrived, tokens, live, gains
+        output_kernel, "output", [(block, BF)], *out, tokens, after(live, col_relay), gains
     )
     (grad_tokens,) = call(
-        input_kernel, "input_gradient", [(block, F32)], e_zero, *e_arrived, tokens, cotangent, live
-    )
-    sizes = [SHARD] * 5 + [3 * SHARD, 4 * SHARD]
+        input_kernel, "input_gradient", [(block, F32)], *e, tokens, cotangent, live
+    )
+    sizes = [SHARD] * 5 + [3 * SHARD, 4 * SHARD, SHARD]
     shard_qkv, shard_up, *vectors = call(
         columns_kernel, "columns",
         [((SHARD, 3 * WIDTH), F32), ((SHARD, 4 * WIDTH), F32)] + [((1, n), F32) for n in sizes],
         place, col_sum[:SHARD], *arrived[1:],
     )
-    g_one, b_one, g_two, b_two, branch, qkv_bias, up_bias = [item[0] for item in vectors]
+    g_one, b_one, g_two, b_two, branch, qkv_bias, up_bias, again = [item[0] for item in vectors]
     return (
         output, grad_tokens, g_one, b_one, g_two, b_two, shard_qkv, qkv_bias,
-        tail_sum[96 : 96 + SHARD], branch, shard_up, up_bias, tail_sum[:96], branch,
+        tail_sum[96 : 96 + SHARD], branch, shard_up, up_bias, tail_sum[:96], again,
     )
 
 

time: 172 us -> 115 us (0.67)
  waiting for transfers between devices: 57.5 us -> 32.5 us
  starting transfers between devices: 61.6 us -> 46.1 us
  local copies, waits for them, and re-layouts: 14.6 us -> 5.25 us
  Pallas kernels: 32.2 us -> 27.1 us
    ppermute x40 -> x21, waiting for transfers between devices: 54.6 us -> 18.9 us  [the longest x3 8.39 us: xor_permutes(): return [lax.ppermute(block, axis, xor_pairs(count, k)) for k in range(1, 4)]]
    ppermute x40 -> x21, starting transfers between devices: 50.3 us -> 26.9 us  [the longest x2 6.89 us: plane_local(): lax.ppermute(cot, 't', xor_pairs(TP, k))]
    ppermute x6 -> x12, waiting for transfers between devices: 2.92 us -> 13.6 us  [exchange_t(): lax.ppermute(pieces[k], 't', xor_pairs(TP, k))]
    unnamed x38 -> x24, local copies, waits for them, and re-layouts: 12 us -> 2.86 us
    ppermute x6 -> x12, starting transfers between devices: 11.3 us -> 19.3 us  [exchange_t(): lax.ppermute(pieces[k], 't', xor_pairs(TP, k))]
    pallas_call x7 -> x11, Pallas kernels: 32.2 us -> 27.1 us  [call(): pl.pallas_call(kernel, name=name, out_shape=shapes, in_specs=space, out_s...]
  transfers between devices with their start and end apart: 46 -> 33, of which waited for: 16 -> 16; matrix products, arithmetic and copies ran while one was open for 4% -> 3% of each run, Pallas kernels for 3% -> 18%
where the time goes in v3:
time: 115 us
  starting transfers between devices  46.1 us (40%)
  waiting for transfers between devices  32.5 us (28%)
  Pallas kernels  27.1 us (24%)
  local copies, waits for them, and re-layouts  5.25 us (5%)
  other arithmetic  3.09 us (3%)
    pallas_call x11, Pallas kernels, call(): pl.pallas_call(kernel, name=name, out_shape=shapes, in_specs=space, out_s...  27.1 us
    ppermute x12, starting transfers between devices, exchange_t(): lax.ppermute(pieces[k], 't', xor_pairs(TP, k))  19.3 us
    ppermute x12, waiting for transfers between devices, exchange_t(): lax.ppermute(pieces[k], 't', xor_pairs(TP, k))  13.6 us
    ppermute x3, waiting for transfers between devices, xor_permutes(): return [lax.ppermute(block, axis, xor_pairs(count, k)) for k in range(1, 4)]  8.39 us
    ppermute x2, starting transfers between devices, plane_local(): lax.ppermute(cot, 't', xor_pairs(TP, k))  6.89 us
    ppermute x2, waiting for transfers between devices, plane_last(): one = lax.ppermute(one.astype(BF), 'fsdp', xor_pairs(4, 1))  3.96 us
    ppermute x3, starting transfers between devices, xor_permutes(): return [lax.ppermute(block, axis, xor_pairs(count, k)) for k in range(1, 4)]  3.55 us
    ppermute x2, starting transfers between devices, plane_last(): one = lax.ppermute(one.astype(BF), 'fsdp', xor_pairs(4, 1))  3.04 us
  transfers between devices with their start and end apart: 33, of which 16 were waited for; matrix products, arithmetic and copies ran while one was open for 3% of the time, Pallas kernels for 18%

profile of v3, /device:TPU:0, one launch (start us, length us, event | category | flops | bytes accessed | tf_op | source)
XLA Modules:
  0.0 115.3 jit_solution(16571194929085507683)
XLA Ops:
  0.7 1.4 %fusion.15 = (s32[]{:T(128)}, bf16[1,4]{1,0:T(2,128)(2,1)S(1)}) fusion(s32[1,4]{1,0:T(1,128)} %param.16), kind=kLoop, calls=%fused_computation.44 | loop fusion | flops 7 | bytes 28 | tf_op jit(solution)/shard_map/reduce_sum | solution.py:562
  2.0 0.9 concatenate.66
  3.0 0.9 copy-done
  3.9 0.9 copy-done.4
  4.8 0.9 copy-done.5
  5.7 0.9 prepare.1
  6.7 3.1 %collective-permute-start = (bf16[176,768]{1,0:T(8,128)(2,1)S(1)}, bf16[176,768]{1,0:T(8,128)(2,1)S(1)}, u32[]{:S(2)}, u32[]{:S(2)}) collective-permute-start(bf16[176,768]{1,0:T(8,128)(2,1)S(1)} %get-tuple-element.72), channel_id=1, source_target_pairs={{0,8},{8,0},{16,24},{24,16},{1,9},{9,1},{17,25},{25,17},{2,10},{10... | collective-permute-start | bytes 811016 | tf_op jit(solution)/shard_map/ppermute | solution.py:61
  9.8 2.6 %collective-permute-start.1 = (bf16[176,768]{1,0:T(8,128)(2,1)S(1)}, bf16[176,768]{1,0:T(8,128)(2,1)S(1)}, u32[]{:S(2)}, u32[]{:S(2)}) collective-permute-start(bf16[176,768]{1,0:T(8,128)(2,1)S(1)} %get-tuple-element.73), channel_id=1, source_target_pairs={{0,16},{8,24},{16,0},{24,8},{1,17},{9,25},{17,1},{25,9},{2,18},{10... | collective-permute-start | bytes 811016 | tf_op jit(solution)/shard_map/ppermute | solution.py:61
  12.4 1.6 %collective-permute-start.4 = (bf16[128,768]{1,0:T(8,128)(2,1)S(1)}, bf16[128,768]{1,0:T(8,128)(2,1)S(1)}, u32[]{:S(2)}, u32[]{:S(2)}) collective-permute-start(bf16[128,768]{1,0:T(8,128)(2,1)S(1)} %pad_maximum_fusion.4), channel_id=1, source_target_pairs={{0,1},{1,0},{2,3},{3,2},{4,5},{5,4},{6,7},{7,6},{8,9},{9,8},{10,11... | collective-permute-start | bytes 589832 | tf_op jit(solution)/shard_map/ppermute | solution.py:572
  13.9 1.5 %collective-permute-start.5 = (bf16[128,768]{1,0:T(8,128)(2,1)S(1)}, bf16[128,768]{1,0:T(8,128)(2,1)S(1)}, u32[]{:S(2)}, u32[]{:S(2)}) collective-permute-start(bf16[128,768]{1,0:T(8,128)(2,1)S(1)} %pad_maximum_fusion.4), channel_id=1, source_target_pairs={{0,2},{1,3},{2,0},{3,1},{4,6},{5,7},{6,4},{7,5},{8,10},{9,11},{10,... | collective-permute-start | bytes 589832 | tf_op jit(solution)/shard_map/ppermute | solution.py:573
  15.7 2.8 %collective-permute-done.4 = bf16[128,768]{1,0:T(8,128)(2,1)S(1)} collective-permute-done((bf16[128,768]{1,0:T(8,128)(2,1)S(1)}, bf16[128,768]{1,0:T(8,128)(2,1)S(1)}, u32[]{:S(2)}, u32[]{:S(2)}) %collective-permute-start.4) | collective-permute-done | bytes 196640 | tf_op jit(solution)/shard_map/ppermute | solution.py:572
  18.5 2.4 %collective-permute-start.6 = (bf16[128,768]{1,0:T(8,128)(2,1)S(1)}, bf16[128,768]{1,0:T(8,128)(2,1)S(1)}, u32[]{:S(2)}, u32[]{:S(2)}) collective-permute-start(bf16[128,768]{1,0:T(8,128)(2,1)S(1)} %pad_maximum_fusion.4), channel_id=1, source_target_pairs={{0,3},{1,2},{2,1},{3,0},{4,7},{5,6},{6,5},{7,4},{8,11},{9,10},{10,... | collective-permute-start | bytes 589832 | tf_op jit(solution)/shard_map/ppermute | solution.py:574
  21.0 4.9 %collective-permute-done.3.three = bf16[48,768]{1,0:T(8,128)(2,1)S(1)} collective-permute-done((bf16[48,768]{1,0:T(8,128)(2,1)S(1)}, bf16[48,768]{1,0:T(8,128)(2,1)S(1)}, u32[]{:S(2)}, u32[]{:S(2)}) %collective-permute-start.3) | collective-permute-done | bytes 73760 | tf_op jit(solution)/shard_map/ppermute | solution.py:61
  25.9 0.9 collective-permute-done.1.refs_2_.two
  26.9 1.6 %collective-permute-start.7 = (bf16[192,768]{1,0:T(8,128)(2,1)S(1)}, bf16[192,768]{1,0:T(8,128)(2,1)S(1)}, u32[]{:S(2)}, u32[]{:S(2)}) collective-permute-start(bf16[192,768]{1,0:T(8,128)(2,1)S(1)} %merge.1), channel_id=1, source_target_pairs={{0,1},{1,0},{2,3},{3,2},{4,5},{5,4},{6,7},{7,6},{8,9},{9,8},{10,11... | collective-permute-start | bytes 884744 | tf_op jit(solution)/shard_map/ppermute | solution.py:529
  28.4 1.5 %collective-permute-start.8 = (bf16[192,768]{1,0:T(8,128)(2,1)S(1)}, bf16[192,768]{1,0:T(8,128)(2,1)S(1)}, u32[]{:S(2)}, u32[]{:S(2)}) collective-permute-start(bf16[192,768]{1,0:T(8,128)(2,1)S(1)} %merge.1), channel_id=1, source_target_pairs={{0,2},{1,3},{2,0},{3,1},{4,6},{5,7},{6,4},{7,5},{8,10},{9,11},{10,... | collective-permute-start | bytes 884744 | tf_op jit(solution)/shard_map/ppermute | solution.py:529
  29.9 2.5 %collective-permute-start.2 = (bf16[256,768]{1,0:T(8,128)(2,1)S(1)}, bf16[256,768]{1,0:T(8,128)(2,1)S(1)}, u32[]{:S(2)}, u32[]{:S(2)}) collective-permute-start(bf16[256,768]{1,0:T(8,128)(2,1)S(1)} %pad_maximum_fusion.1), channel_id=1, source_target_pairs={{0,24},{8,16},{16,8},{24,0},{1,25},{9,17},{17,9},{25,1},{2,26},{10... | collective-permute-start | bytes 1179656 | tf_op jit(solution)/shard_map/ppermute | solution.py:584
  32.9 3.6 %collective-permute-done.7 = bf16[192,768]{1,0:T(8,128)(2,1)S(1)} collective-permute-done((bf16[192,768]{1,0:T(8,128)(2,1)S(1)}, bf16[192,768]{1,0:T(8,128)(2,1)S(1)}, u32[]{:S(2)}, u32[]{:S(2)}) %collective-permute-start.7) | collective-permute-done | bytes 294944 | tf_op jit(solution)/shard_map/ppermute | solution.py:529
  36.6 4.8 %collective-permute-done.8 = bf16[192,768]{1,0:T(8,128)(2,1)S(1)} collective-permute-done((bf16[192,768]{1,0:T(8,128)(2,1)S(1)}, bf16[192,768]{1,0:T(8,128)(2,1)S(1)}, u32[]{:S(2)}, u32[]{:S(2)}) %collective-permute-start.8) | collective-permute-done | bytes 294944 | tf_op jit(solution)/shard_map/ppermute | solution.py:529
  42.1 1.7 %normalize.1 = (f32[512,768]{1,0:T(8,128)S(1)}, bf16[768,768]{1,0:T(8,128)(2,1)S(1)}) custom-call(s32[2]{0:T(128)S(1)} %pad_add_fusion.place, bf16[128,768]{1,0:T(8,128)(2,1)S(1)} %copy-done.1, bf16[176,768]{1,0:T(8,128)(2,1)S(1)} %collective-permute-done.refs_1_.one, bf16[176,768]{1,0:T(8,128)(2,1)S(1)} %collective-permute-done.1.refs_2_.two, ...), custom_call_target="tpu_custom_call" | custom-call | flops 10000000000 | bytes 10000000 | tf_op jit(solution)/shard_map/normalize/pallas_call | solution.py:512
  43.9 6.5 %collective-permute-start.15 = (bf16[128,768]{1,0:T(8,128)(2,1)S(1)}, bf16[128,768]{1,0:T(8,128)(2,1)S(1)}, u32[]{:S(2)}, u32[]{:S(2)}) collective-permute-start(bf16[128,768]{1,0:T(8,128)(2,1)S(1)} %copy-done.3), channel_id=1, source_target_pairs={{0,8},{8,0},{16,24},{24,16},{1,9},{9,1},{17,25},{25,17},{2,10},{10... | collective-permute-start | bytes 589832 | tf_op jit(solution)/shard_map/ppermute | solution.py:598
  50.7 8.0 %forward.1 = (bf16[768,768]{1,0:T(8,128)(2,1)S(1)}, bf16[768,640]{1,0:T(8,128)(2,1)S(1)}, bf16[512,768]{1,0:T(8,128)(2,1)S(1)}, bf16[512,768]{1,0:T(8,128)(2,1)S...) custom-call(s32[2]{0:T(128)S(1)} %pad_add_fusion.place, ...), custom_call_target="tpu_custom_call" | custom-call | flops 80000000000 | bytes 80000000 | tf_op jit(solution)/shard_map/forward/pallas_call | solution.py:512
  58.7 1.6 %share.1 = (bf16[768,768]{1,0:T(8,128)(2,1)S(1)}, bf16[256,768]{1,0:T(8,128)(2,1)S(1)}, f32[128,768]{1,0:T(8,128)S(1)}, bf16[128,768]{1,0:T(8,128)(2,1)S(1)}, bf...) custom-call(s32[2]{0:T(128)S(1)} %pad_add_fusion.place, bf16[512,768]{1,0:T(8,128)(2,1)S(1)} %get-tuple-element.80.act.refs_6_, ...), custom_call_target="tpu_custom_call" | custom-call | flops 20000000000 | bytes 20000000 | tf_op jit(solution)/shard_map/share/pallas_call | solution.py:512
  60.4 1.3 %collective-permute-done.16.refs_2_ = bf16[128,768]{1,0:T(8,128)(2,1)S(1)} collective-permute-done((bf16[128,768]{1,0:T(8,128)(2,1)S(1)}, bf16[128,768]{1,0:T(8,128)(2,1)S(1)}, u32[]{:S(2)}, u32[]{:S(2)}) %collective-permute-start.16) | collective-permute-done | bytes 196640 | tf_op jit(solution)/shard_map/ppermute | solution.py:598
  61.7 3.4 %upstream.1 = (bf16[512,768]{1,0:T(8,128)(2,1)S(1)}, bf16[512,192]{1,0:T(8,128)(2,1)S(1)}, f32[896,768]{1,0:T(8,128)S(1)}, bf16[896,768]{1,0:T(8,128)(2,1)S(1)}) custom-call(s32[2]{0:T(128)S(1)} %pad_add_fusion.place, bf16[128,768]{1,0:T(8,128)(2,1)S(1)} %copy-done.3, bf16[128,768]{1,0:T(8,128)(2,1)S(1)} %collective-permute-done.15.refs_1_, ...), custom_call_target="tpu_custom_call" | custom-call | flops 40000000000 | bytes 40000000 | tf_op jit(solution)/shard_map/upstream/pallas_call | solution.py:512
  65.9 2.1 %collective-permute-start.13 = (bf16[128,768]{1,0:T(8,128)(2,1)S(1)}, bf16[128,768]{1,0:T(8,128)(2,1)S(1)}, u32[]{:S(2)}, u32[]{:S(2)}) collective-permute-start(bf16[128,768]{1,0:T(8,128)(2,1)S(1)} %get-tuple-element.84), channel_id=1, source_target_pairs={{0,16},{8,24},{16,0},{24,8},{1,17},{9,25},{17,1},{25,9},{2,18},{10... | collective-permute-start | bytes 589832 | tf_op jit(solution)/shard_map/ppermute | solution.py:61
  68.0 1.7 %collective-permute-start.14 = (bf16[128,768]{1,0:T(8,128)(2,1)S(1)}, bf16[128,768]{1,0:T(8,128)(2,1)S(1)}, u32[]{:S(2)}, u32[]{:S(2)}) collective-permute-start(bf16[128,768]{1,0:T(8,128)(2,1)S(1)} %get-tuple-element.85), channel_id=1, source_target_pairs={{0,24},{8,16},{16,8},{24,0},{1,25},{9,17},{17,9},{25,1},{2,26},{10... | collective-permute-start | bytes 589832 | tf_op jit(solution)/shard_map/ppermute | solution.py:61
  70.1 0.8 collective-permute-start.18
  71.4 4.1 %attention.1.d_qkv = bf16[512,576]{1,0:T(8,128)(2,1)S(1)} custom-call(bf16[512,192]{1,0:T(8,128)(2,1)S(1)} %get-tuple-element.97.q_low, bf16[512,192]{1,0:T(8,128)(2,1)S(1)} %get-tuple-element.98.k_low, bf16[512,192]{1,0:T(8,128)(2,1)S(1)} %get-tuple-element.99.v_low, f32[12,128,128]{2,1,0:T(8,128)S(1)} %get-tuple-element.100.probs, ...), custom_call_target="tpu_custom_call" | custom-call | flops 49999998976 | bytes 50000000 | tf_op jit(solution)/shard_map/attention/pallas_call | solution.py:512
  76.6 1.6 %collective-permute-start.26 = (bf16[224,768]{1,0:T(8,128)(2,1)S(1)}, bf16[224,768]{1,0:T(8,128)(2,1)S(1)}, u32[]{:S(2)}, u32[]{:S(2)}) collective-permute-start(bf16[224,768]{1,0:T(8,128)(2,1)S(1)} %pad_maximum_fusion.2), channel_id=1, source_target_pairs={{0,1},{1,0},{2,3},{3,2},{4,5},{5,4},{6,7},{7,6},{8,9},{9,8},{10,11... | collective-permute-start | bytes 1032200 | tf_op jit(solution)/shard_map/ppermute | solution.py:550
  78.9 3.8 %backward.1 = (f32[128,768]{1,0:T(8,128)S(1)}, bf16[128,768]{1,0:T(8,128)(2,1)S(1)}, bf16[128,768]{1,0:T(8,128)(2,1)S(1)}, bf16[128,768]{1,0:T(8,128)(2,1)S(1)},...) custom-call(s32[2]{0:T(128)S(1)} %pad_add_fusion.place, f32[512,768]{1,0:T(8,128)S(1)} %get-tuple-element.75.xhat, ...), custom_call_target="tpu_custom_call" | custom-call | flops 40000000000 | bytes 40000000 | tf_op jit(solution)/shard_map/backward/pallas_call | solution.py:512
  83.7 2.2 %collective-permute-done.26 = bf16[224,768]{1,0:T(8,128)(2,1)S(1)} collective-permute-done((bf16[224,768]{1,0:T(8,128)(2,1)S(1)}, bf16[224,768]{1,0:T(8,128)(2,1)S(1)}, u32[]{:S(2)}, u32[]{:S(2)}) %collective-permute-start.26) | collective-permute-done | bytes 344096 | tf_op jit(solution)/shard_map/ppermute | solution.py:550
  86.7 1.4 %collective-permute-start.21 = (bf16[48,640]{1,0:T(8,128)(2,1)S(1)}, bf16[48,640]{1,0:T(8,128)(2,1)S(1)}, u32[]{:S(2)}, u32[]{:S(2)}) collective-permute-start(bf16[48,640]{1,0:T(8,128)(2,1)S(1)} %get-tuple-element.147), channel_id=1, source_target_pairs={{0,1},{1,0},{2,3},{3,2},{4,5},{5,4},{6,7},{7,6},{8,9},{9,8},{10,11... | collective-permute-start | bytes 184328 | tf_op jit(solution)/shard_map/ppermute | solution.py:539
  88.6 0.8 fusion.12
  90.0 2.1 %collective-permute-start.25 = (bf16[128,768]{1,0:T(8,128)(2,1)S(1)}, bf16[128,768]{1,0:T(8,128)(2,1)S(1)}, u32[]{:S(2)}, u32[]{:S(2)}) collective-permute-start(bf16[128,768]{1,0:T(8,128)(2,1)S(1)} %get-tuple-element.119), channel_id=1, source_target_pairs={{0,24},{8,16},{16,8},{24,0},{1,25},{9,17},{17,9},{25,1},{2,26},{10... | collective-permute-start | bytes 589832 | tf_op jit(solution)/shard_map/ppermute | solution.py:61
  92.0 1.0 collective-permute-start.24
  93.0 1.3 %collective-permute-start.23 = (bf16[128,768]{1,0:T(8,128)(2,1)S(1)}, bf16[128,768]{1,0:T(8,128)(2,1)S(1)}, u32[]{:S(2)}, u32[]{:S(2)}) collective-permute-start(bf16[128,768]{1,0:T(8,128)(2,1)S(1)} %get-tuple-element.115), channel_id=1, source_target_pairs={{0,8},{8,0},{16,24},{24,16},{1,9},{9,1},{17,25},{25,17},{2,10},{10... | collective-permute-start | bytes 589832 | tf_op jit(solution)/shard_map/ppermute | solution.py:61
  94.4 1.5 %collective-permute-start.28 = (bf16[96,640]{1,0:T(8,128)(2,1)S(1)}, bf16[96,640]{1,0:T(8,128)(2,1)S(1)}, u32[]{:S(2)}, u32[]{:S(2)}) collective-permute-start(bf16[96,640]{1,0:T(8,128)(2,1)S(1)} %pad_maximum_fusion.5), channel_id=1, source_target_pairs={{0,1},{1,0},{2,3},{3,2},{4,5},{5,4},{6,7},{7,6},{8,9},{9,8},{10,11... | collective-permute-start | bytes 368648 | tf_op jit(solution)/shard_map/ppermute | solution.py:550
  95.9 0.9 collective-permute-start.29
  96.8 0.8 output.1
  97.6 1.8 %collective-permute-done.28 = bf16[96,640]{1,0:T(8,128)(2,1)S(1)} collective-permute-done((bf16[96,640]{1,0:T(8,128)(2,1)S(1)}, bf16[96,640]{1,0:T(8,128)(2,1)S(1)}, u32[]{:S(2)}, u32[]{:S(2)}) %collective-permute-start.28) | collective-permute-done | bytes 122912 | tf_op jit(solution)/shard_map/ppermute | solution.py:550
  99.4 1.5 %collective-permute-done.29 = bf16[96,640]{1,0:T(8,128)(2,1)S(1)} collective-permute-done((bf16[96,640]{1,0:T(8,128)(2,1)S(1)}, bf16[96,640]{1,0:T(8,128)(2,1)S(1)}, u32[]{:S(2)}, u32[]{:S(2)}) %collective-permute-start.29) | collective-permute-done | bytes 122912 | tf_op jit(solution)/shard_map/ppermute | solution.py:551
  101.0 0.8 collective-permute-start.30
  101.8 2.0 %collective-permute-start.31 = (bf16[24,1408]{1,0:T(8,128)(2,1)S(1)}, bf16[24,1408]{1,0:T(8,128)(2,1)S(1)}, u32[]{:S(2)}, u32[]{:S(2)}) collective-permute-start(bf16[24,1408]{1,0:T(8,128)(2,1)S(1)} %get-tuple-element.149), channel_id=1, source_target_pairs={{0,16},{8,24},{16,0},{24,8},{1,17},{9,25},{17,1},{25,9},{2,18},{10... | collective-permute-start | bytes 202760 | tf_op jit(solution)/shard_map/ppermute | solution.py:61
  103.8 1.7 %collective-permute-start.32 = (bf16[24,1408]{1,0:T(8,128)(2,1)S(1)}, bf16[24,1408]{1,0:T(8,128)(2,1)S(1)}, u32[]{:S(2)}, u32[]{:S(2)}) collective-permute-start(bf16[24,1408]{1,0:T(8,128)(2,1)S(1)} %get-tuple-element.148), channel_id=1, source_target_pairs={{0,24},{8,16},{16,8},{24,0},{1,25},{9,17},{17,9},{25,1},{2,26},{10... | collective-permute-start | bytes 202760 | tf_op jit(solution)/shard_map/ppermute | solution.py:61
  105.5 6.7 %collective-permute-done.24.two = bf16[128,768]{1,0:T(8,128)(2,1)S(1)} collective-permute-done((bf16[128,768]{1,0:T(8,128)(2,1)S(1)}, bf16[128,768]{1,0:T(8,128)(2,1)S(1)}, u32[]{:S(2)}, u32[]{:S(2)}) %collective-permute-start.24) | collective-permute-done | bytes 196640 | tf_op jit(solution)/shard_map/ppermute | solution.py:61
  112.2 1.2 %input_gradient.1 = f32[128,768]{1,0:T(8,128)} custom-call(f32[128,768]{1,0:T(8,128)S(1)} %get-tuple-element.113.zero, bf16[128,768]{1,0:T(8,128)(2,1)S(1)} %collective-permute-done.23.one, bf16[128,768]{1,0:T(8,128)(2,1)S(1)} %collective-permute-done.24.two, bf16[128,768]{1,0:T(8,128)(2,1)S(1)} %collective-permute-done.25.three, ...), custom_call_target="tpu_custom_call" | custom-call | flops 10000000000 | bytes 10000000 | tf_op jit(solution)/shard_map/input_gradient/pallas_call | solution.py:512
  113.6 1.5 %columns.1 = (f32[24,2304]{1,0:T(8,128)}, f32[24,3072]{1,0:T(8,128)}, f32[1,24]{1,0:T(1,128)}, f32[1,24]{1,0:T(1,128)}, f32[1,24]{1,0:T(1,128)}, /*index=5*/f32[...) custom-call(s32[2]{0:T(128)S(1)} %pad_add_fusion.place, ...), custom_call_target="tpu_custom_call" | custom-call | flops 10000000000 | bytes 10000000 | tf_op jit(solution)/shard_map/columns/pallas_call | solution.py:512
  (81 shorter events, 8.9 us)
Async XLA Ops:
  3.0 0.9 copy-start
  3.9 0.9 copy-start.4
  4.8 0.9 copy-start.5
  5.7 6.6 %copy-start.6 = (bf16[96,768]{1,0:T(8,128)(2,1)S(1)}, bf16[96,768]{1,0:T(8,128)(2,1)}, u32[]{:S(2)}) copy-start(bf16[96,768]{1,0:T(8,128)(2,1)} %param.27) | copy-start | bytes 442372
  5.7 6.6 %copy-start.7 = (bf16[24,768]{1,0:T(8,128)(2,1)S(1)}, bf16[24,768]{1,0:T(8,128)(2,1)}, u32[]{:S(2)}) copy-start(bf16[24,768]{1,0:T(8,128)(2,1)} %param.23) | copy-start | bytes 110596
  5.7 10.0 %copy-start.3 = (bf16[128,768]{1,0:T(8,128)(2,1)S(1)}, bf16[128,768]{1,0:T(8,128)(2,1)}, u32[]{:S(2)}) copy-start(bf16[128,768]{1,0:T(8,128)(2,1)} %cot.3) | copy-start | bytes 589828
  6.7 19.2 %collective-permute-start = (bf16[176,768]{1,0:T(8,128)(2,1)S(1)}, bf16[176,768]{1,0:T(8,128)(2,1)S(1)}, u32[]{:S(2)}, u32[]{:S(2)}) collective-permute-start(bf16[176,768]{1,0:T(8,128)(2,1)S(1)} %get-tuple-element.72), channel_id=1, source_target_pairs={{0,8},{8,0},{16,24},{24,16},{1,9},{9,1},{17,25},{25,17},{2,10},{10... | collective-permute-start | bytes 811016 | tf_op jit(solution)/shard_map/ppermute | solution.py:61
  9.8 17.1 %collective-permute-start.1 = (bf16[176,768]{1,0:T(8,128)(2,1)S(1)}, bf16[176,768]{1,0:T(8,128)(2,1)S(1)}, u32[]{:S(2)}, u32[]{:S(2)}) collective-permute-start(bf16[176,768]{1,0:T(8,128)(2,1)S(1)} %get-tuple-element.73), channel_id=1, source_target_pairs={{0,16},{8,24},{16,0},{24,8},{1,17},{9,25},{17,1},{25,9},{2,18},{10... | collective-permute-start | bytes 811016 | tf_op jit(solution)/shard_map/ppermute | solution.py:61
  12.4 6.1 %collective-permute-start.4 = (bf16[128,768]{1,0:T(8,128)(2,1)S(1)}, bf16[128,768]{1,0:T(8,128)(2,1)S(1)}, u32[]{:S(2)}, u32[]{:S(2)}) collective-permute-start(bf16[128,768]{1,0:T(8,128)(2,1)S(1)} %pad_maximum_fusion.4), channel_id=1, source_target_pairs={{0,1},{1,0},{2,3},{3,2},{4,5},{5,4},{6,7},{7,6},{8,9},{9,8},{10,11... | collective-permute-start | bytes 589832 | tf_op jit(solution)/shard_map/ppermute | solution.py:572
  13.9 12.9 %collective-permute-start.5 = (bf16[128,768]{1,0:T(8,128)(2,1)S(1)}, bf16[128,768]{1,0:T(8,128)(2,1)S(1)}, u32[]{:S(2)}, u32[]{:S(2)}) collective-permute-start(bf16[128,768]{1,0:T(8,128)(2,1)S(1)} %pad_maximum_fusion.4), channel_id=1, source_target_pairs={{0,2},{1,3},{2,0},{3,1},{4,6},{5,7},{6,4},{7,5},{8,10},{9,11},{10,... | collective-permute-start | bytes 589832 | tf_op jit(solution)/shard_map/ppermute | solution.py:573
  15.4 10.4 %collective-permute-start.3 = (bf16[48,768]{1,0:T(8,128)(2,1)S(1)}, bf16[48,768]{1,0:T(8,128)(2,1)S(1)}, u32[]{:S(2)}, u32[]{:S(2)}) collective-permute-start(bf16[48,768]{1,0:T(8,128)(2,1)S(1)} %get-tuple-element.77), channel_id=1, source_target_pairs={{0,24},{8,16},{16,8},{24,0},{1,25},{9,17},{17,9},{25,1},{2,26},{10... | collective-permute-start | bytes 221192 | tf_op jit(solution)/shard_map/ppermute | solution.py:61
  18.5 8.3 %collective-permute-start.6 = (bf16[128,768]{1,0:T(8,128)(2,1)S(1)}, bf16[128,768]{1,0:T(8,128)(2,1)S(1)}, u32[]{:S(2)}, u32[]{:S(2)}) collective-permute-start(bf16[128,768]{1,0:T(8,128)(2,1)S(1)} %pad_maximum_fusion.4), channel_id=1, source_target_pairs={{0,3},{1,2},{2,1},{3,0},{4,7},{5,6},{6,5},{7,4},{8,11},{9,10},{10,... | collective-permute-start | bytes 589832 | tf_op jit(solution)/shard_map/ppermute | solution.py:574
  26.9 9.7 %collective-permute-start.7 = (bf16[192,768]{1,0:T(8,128)(2,1)S(1)}, bf16[192,768]{1,0:T(8,128)(2,1)S(1)}, u32[]{:S(2)}, u32[]{:S(2)}) collective-permute-start(bf16[192,768]{1,0:T(8,128)(2,1)S(1)} %merge.1), channel_id=1, source_target_pairs={{0,1},{1,0},{2,3},{3,2},{4,5},{5,4},{6,7},{7,6},{8,9},{9,8},{10,11... | collective-permute-start | bytes 884744 | tf_op jit(solution)/shard_map/ppermute | solution.py:529
  28.4 12.9 %collective-permute-start.8 = (bf16[192,768]{1,0:T(8,128)(2,1)S(1)}, bf16[192,768]{1,0:T(8,128)(2,1)S(1)}, u32[]{:S(2)}, u32[]{:S(2)}) collective-permute-start(bf16[192,768]{1,0:T(8,128)(2,1)S(1)} %merge.1), channel_id=1, source_target_pairs={{0,2},{1,3},{2,0},{3,1},{4,6},{5,7},{6,4},{7,5},{8,10},{9,11},{10,... | collective-permute-start | bytes 884744 | tf_op jit(solution)/shard_map/ppermute | solution.py:529
  29.9 12.2 %collective-permute-start.2 = (bf16[256,768]{1,0:T(8,128)(2,1)S(1)}, bf16[256,768]{1,0:T(8,128)(2,1)S(1)}, u32[]{:S(2)}, u32[]{:S(2)}) collective-permute-start(bf16[256,768]{1,0:T(8,128)(2,1)S(1)} %pad_maximum_fusion.1), channel_id=1, source_target_pairs={{0,24},{8,16},{16,8},{24,0},{1,25},{9,17},{17,9},{25,1},{2,26},{10... | collective-permute-start | bytes 1179656 | tf_op jit(solution)/shard_map/ppermute | solution.py:584
  32.4 8.9 %collective-permute-start.9 = (bf16[192,768]{1,0:T(8,128)(2,1)S(1)}, bf16[192,768]{1,0:T(8,128)(2,1)S(1)}, u32[]{:S(2)}, u32[]{:S(2)}) collective-permute-start(bf16[192,768]{1,0:T(8,128)(2,1)S(1)} %merge.1), channel_id=1, source_target_pairs={{0,3},{1,2},{2,1},{3,0},{4,7},{5,6},{6,5},{7,4},{8,11},{9,10},{10,... | collective-permute-start | bytes 884744 | tf_op jit(solution)/shard_map/ppermute | solution.py:529
  36.6 5.5 %copy-start.1 = (bf16[128,768]{1,0:T(8,128)(2,1)S(1)}, bf16[128,768]{1,0:T(8,128)(2,1)}, u32[]{:S(2)}) copy-start(bf16[128,768]{1,0:T(8,128)(2,1)} %tokens.5) | copy-start | bytes 589828
  41.4 9.4 %collective-permute-start.10 = (bf16[768,768]{1,0:T(8,128)(2,1)S(1)}, bf16[768,768]{1,0:T(8,128)(2,1)S(1)}, u32[]{:S(2)}, u32[]{:S(2)}) collective-permute-start(bf16[768,768]{1,0:T(8,128)(2,1)S(1)} %constant_dynamic-update-slice_fusion.refs_0_), channel_id=1, source_target_pairs={{0,4},{4,0},{1,5},{5,1},{2,6},{6,2},{3,7},{7,3},{8,12},{12,8},{9,1... | collective-permute-start | bytes 3538952 | tf_op jit(solution)/shard_map/ppermute | solution.py:589
  41.5 17.2 %collective-permute-start.11 = (bf16[512,768]{1,0:T(8,128)(2,1)S(1)}, bf16[512,768]{1,0:T(8,128)(2,1)S(1)}, u32[]{:S(2)}, u32[]{:S(2)}) collective-permute-start(bf16[512,768]{1,0:T(8,128)(2,1)S(1)} %constant_dynamic-update-slice_fusion.4.refs_0_), channel_id=1, source_target_pairs={{0,4},{4,0},{1,5},{5,1},{2,6},{6,2},{3,7},{7,3},{8,12},{12,8},{9,1... | collective-permute-start | bytes 2359304 | tf_op jit(solution)/shard_map/ppermute | solution.py:591
  43.9 16.5 %collective-permute-start.15 = (bf16[128,768]{1,0:T(8,128)(2,1)S(1)}, bf16[128,768]{1,0:T(8,128)(2,1)S(1)}, u32[]{:S(2)}, u32[]{:S(2)}) collective-permute-start(bf16[128,768]{1,0:T(8,128)(2,1)S(1)} %copy-done.3), channel_id=1, source_target_pairs={{0,8},{8,0},{16,24},{24,16},{1,9},{9,1},{17,25},{25,17},{2,10},{10... | collective-permute-start | bytes 589832 | tf_op jit(solution)/shard_map/ppermute | solution.py:598
  50.4 11.3 %collective-permute-start.16 = (bf16[128,768]{1,0:T(8,128)(2,1)S(1)}, bf16[128,768]{1,0:T(8,128)(2,1)S(1)}, u32[]{:S(2)}, u32[]{:S(2)}) collective-permute-start(bf16[128,768]{1,0:T(8,128)(2,1)S(1)} %copy-done.3), channel_id=1, source_target_pairs={{0,16},{8,24},{16,0},{24,8},{1,17},{9,25},{17,1},{25,9},{2,18},{10... | collective-permute-start | bytes 589832 | tf_op jit(solution)/shard_map/ppermute | solution.py:598
  65.1 4.5 %collective-permute-start.17 = (bf16[896,768]{1,0:T(8,128)(2,1)S(1)}, bf16[896,768]{1,0:T(8,128)(2,1)S(1)}, u32[]{:S(2)}, u32[]{:S(2)}) collective-permute-start(bf16[896,768]{1,0:T(8,128)(2,1)S(1)} %get-tuple-element.105), channel_id=1, source_target_pairs={{0,4},{4,0},{1,5},{5,1},{2,6},{6,2},{3,7},{7,3},{8,12},{12,8},{9,1... | collective-permute-start | bytes 4128776 | tf_op jit(solution)/shard_map/ppermute | solution.py:533
  65.2 10.9 %collective-permute-start.12 = (bf16[128,768]{1,0:T(8,128)(2,1)S(1)}, bf16[128,768]{1,0:T(8,128)(2,1)S(1)}, u32[]{:S(2)}, u32[]{:S(2)}) collective-permute-start(bf16[128,768]{1,0:T(8,128)(2,1)S(1)} %get-tuple-element.83), channel_id=1, source_target_pairs={{0,8},{8,0},{16,24},{24,16},{1,9},{9,1},{17,25},{25,17},{2,10},{10... | collective-permute-start | bytes 589832 | tf_op jit(solution)/shard_map/ppermute | solution.py:61
  65.9 17.1 %collective-permute-start.13 = (bf16[128,768]{1,0:T(8,128)(2,1)S(1)}, bf16[128,768]{1,0:T(8,128)(2,1)S(1)}, u32[]{:S(2)}, u32[]{:S(2)}) collective-permute-start(bf16[128,768]{1,0:T(8,128)(2,1)S(1)} %get-tuple-element.84), channel_id=1, source_target_pairs={{0,16},{8,24},{16,0},{24,8},{1,17},{9,25},{17,1},{25,9},{2,18},{10... | collective-permute-start | bytes 589832 | tf_op jit(solution)/shard_map/ppermute | solution.py:61
  68.0 15.1 %collective-permute-start.14 = (bf16[128,768]{1,0:T(8,128)(2,1)S(1)}, bf16[128,768]{1,0:T(8,128)(2,1)S(1)}, u32[]{:S(2)}, u32[]{:S(2)}) collective-permute-start(bf16[128,768]{1,0:T(8,128)(2,1)S(1)} %get-tuple-element.85), channel_id=1, source_target_pairs={{0,24},{8,16},{16,8},{24,0},{1,25},{9,17},{17,9},{25,1},{2,26},{10... | collective-permute-start | bytes 589832 | tf_op jit(solution)/shard_map/ppermute | solution.py:61
  70.1 6.1 %collective-permute-start.18 = (bf16[112,768]{1,0:T(8,128)(2,1)S(1)}, bf16[112,768]{1,0:T(8,128)(2,1)S(1)}, u32[]{:S(2)}, u32[]{:S(2)}) collective-permute-start(bf16[112,768]{1,0:T(8,128)(2,1)S(1)} %get-tuple-element.139), channel_id=1, source_target_pairs={{0,1},{1,0},{2,3},{3,2},{4,5},{5,4},{6,7},{7,6},{8,9},{9,8},{10,11... | collective-permute-start | bytes 516104 | tf_op jit(solution)/shard_map/ppermute | solution.py:539
  70.9 5.6 %collective-permute-start.19 = (bf16[112,768]{1,0:T(8,128)(2,1)S(1)}, bf16[112,768]{1,0:T(8,128)(2,1)S(1)}, u32[]{:S(2)}, u32[]{:S(2)}) collective-permute-start(bf16[112,768]{1,0:T(8,128)(2,1)S(1)} %get-tuple-element.138), channel_id=1, source_target_pairs={{0,2},{1,3},{2,0},{3,1},{4,6},{5,7},{6,4},{7,5},{8,10},{9,11},{10,... | collective-permute-start | bytes 516104 | tf_op jit(solution)/shard_map/ppermute | solution.py:540
  76.6 9.2 %collective-permute-start.26 = (bf16[224,768]{1,0:T(8,128)(2,1)S(1)}, bf16[224,768]{1,0:T(8,128)(2,1)S(1)}, u32[]{:S(2)}, u32[]{:S(2)}) collective-permute-start(bf16[224,768]{1,0:T(8,128)(2,1)S(1)} %pad_maximum_fusion.2), channel_id=1, source_target_pairs={{0,1},{1,0},{2,3},{3,2},{4,5},{5,4},{6,7},{7,6},{8,9},{9,8},{10,11... | collective-permute-start | bytes 1032200 | tf_op jit(solution)/shard_map/ppermute | solution.py:550
  78.2 8.2 %collective-permute-start.27 = (bf16[224,768]{1,0:T(8,128)(2,1)S(1)}, bf16[224,768]{1,0:T(8,128)(2,1)S(1)}, u32[]{:S(2)}, u32[]{:S(2)}) collective-permute-start(bf16[224,768]{1,0:T(8,128)(2,1)S(1)} %pad_maximum_fusion.3), channel_id=1, source_target_pairs={{0,2},{1,3},{2,0},{3,1},{4,6},{5,7},{6,4},{7,5},{8,10},{9,11},{10,... | collective-permute-start | bytes 1032200 | tf_op jit(solution)/shard_map/ppermute | solution.py:551
  83.0 3.5 %collective-permute-start.20 = (bf16[384,640]{1,0:T(8,128)(2,1)S(1)}, bf16[384,640]{1,0:T(8,128)(2,1)S(1)}, u32[]{:S(2)}, u32[]{:S(2)}) collective-permute-start(bf16[384,640]{1,0:T(8,128)(2,1)S(1)} %get-tuple-element.110), channel_id=1, source_target_pairs={{0,4},{4,0},{1,5},{5,1},{2,6},{6,2},{3,7},{7,3},{8,12},{12,8},{9,1... | collective-permute-start | bytes 1474568 | tf_op jit(solution)/shard_map/ppermute | solution.py:533
  86.7 10.1 %copy-start.2 = (bf16[128,768]{1,0:T(8,128)(2,1)S(1)}, bf16[128,768]{1,0:T(8,128)(2,1)}, u32[]{:S(2)}) copy-start(bf16[128,768]{1,0:T(8,128)(2,1)} %tokens.5) | copy-start | bytes 589828
  86.7 7.7 %collective-permute-start.21 = (bf16[48,640]{1,0:T(8,128)(2,1)S(1)}, bf16[48,640]{1,0:T(8,128)(2,1)S(1)}, u32[]{:S(2)}, u32[]{:S(2)}) collective-permute-start(bf16[48,640]{1,0:T(8,128)(2,1)S(1)} %get-tuple-element.147), channel_id=1, source_target_pairs={{0,1},{1,0},{2,3},{3,2},{4,5},{5,4},{6,7},{7,6},{8,9},{9,8},{10,11... | collective-permute-start | bytes 184328 | tf_op jit(solution)/shard_map/ppermute | solution.py:539
  88.1 6.3 %collective-permute-start.22 = (bf16[48,640]{1,0:T(8,128)(2,1)S(1)}, bf16[48,640]{1,0:T(8,128)(2,1)S(1)}, u32[]{:S(2)}, u32[]{:S(2)}) collective-permute-start(bf16[48,640]{1,0:T(8,128)(2,1)S(1)} %get-tuple-element.146), channel_id=1, source_target_pairs={{0,2},{1,3},{2,0},{3,1},{4,6},{5,7},{6,4},{7,5},{8,10},{9,11},{10,... | collective-permute-start | bytes 184328 | tf_op jit(solution)/shard_map/ppermute | solution.py:540
  90.0 13.8 %collective-permute-start.25 = (bf16[128,768]{1,0:T(8,128)(2,1)S(1)}, bf16[128,768]{1,0:T(8,128)(2,1)S(1)}, u32[]{:S(2)}, u32[]{:S(2)}) collective-permute-start(bf16[128,768]{1,0:T(8,128)(2,1)S(1)} %get-tuple-element.119), channel_id=1, source_target_pairs={{0,24},{8,16},{16,8},{24,0},{1,25},{9,17},{17,9},{25,1},{2,26},{10... | collective-permute-start | bytes 589832 | tf_op jit(solution)/shard_map/ppermute | solution.py:61
  92.0 20.1 %collective-permute-start.24 = (bf16[128,768]{1,0:T(8,128)(2,1)S(1)}, bf16[128,768]{1,0:T(8,128)(2,1)S(1)}, u32[]{:S(2)}, u32[]{:S(2)}) collective-permute-start(bf16[128,768]{1,0:T(8,128)(2,1)S(1)} %get-tuple-element.117), channel_id=1, source_target_pairs={{0,16},{8,24},{16,0},{24,8},{1,17},{9,25},{17,1},{25,9},{2,18},{10... | collective-permute-start | bytes 589832 | tf_op jit(solution)/shard_map/ppermute | solution.py:61
  93.0 19.2 %collective-permute-start.23 = (bf16[128,768]{1,0:T(8,128)(2,1)S(1)}, bf16[128,768]{1,0:T(8,128)(2,1)S(1)}, u32[]{:S(2)}, u32[]{:S(2)}) collective-permute-start(bf16[128,768]{1,0:T(8,128)(2,1)S(1)} %get-tuple-element.115), channel_id=1, source_target_pairs={{0,8},{8,0},{16,24},{24,16},{1,9},{9,1},{17,25},{25,17},{2,10},{10... | collective-permute-start | bytes 589832 | tf_op jit(solution)/shard_map/ppermute | solution.py:61
  94.4 4.9 %collective-permute-start.28 = (bf16[96,640]{1,0:T(8,128)(2,1)S(1)}, bf16[96,640]{1,0:T(8,128)(2,1)S(1)}, u32[]{:S(2)}, u32[]{:S(2)}) collective-permute-start(bf16[96,640]{1,0:T(8,128)(2,1)S(1)} %pad_maximum_fusion.5), channel_id=1, source_target_pairs={{0,1},{1,0},{2,3},{3,2},{4,5},{5,4},{6,7},{7,6},{8,9},{9,8},{10,11... | collective-permute-start | bytes 368648 | tf_op jit(solution)/shard_map/ppermute | solution.py:550
  95.9 4.9 %collective-permute-start.29 = (bf16[96,640]{1,0:T(8,128)(2,1)S(1)}, bf16[96,640]{1,0:T(8,128)(2,1)S(1)}, u32[]{:S(2)}, u32[]{:S(2)}) collective-permute-start(bf16[96,640]{1,0:T(8,128)(2,1)S(1)} %pad_maximum_fusion.6), channel_id=1, source_target_pairs={{0,2},{1,3},{2,0},{3,1},{4,6},{5,7},{6,4},{7,5},{8,10},{9,11},{10,... | collective-permute-start | bytes 368648 | tf_op jit(solution)/shard_map/ppermute | solution.py:551
  101.0 12.4 %collective-permute-start.30 = (bf16[24,1408]{1,0:T(8,128)(2,1)S(1)}, bf16[24,1408]{1,0:T(8,128)(2,1)S(1)}, u32[]{:S(2)}, u32[]{:S(2)}) collective-permute-start(bf16[24,1408]{1,0:T(8,128)(2,1)S(1)} %get-tuple-element.150), channel_id=1, source_target_pairs={{0,8},{8,0},{16,24},{24,16},{1,9},{9,1},{17,25},{25,17},{2,10},{10... | collective-permute-start | bytes 202760 | tf_op jit(solution)/shard_map/ppermute | solution.py:61
  101.8 11.9 %collective-permute-start.31 = (bf16[24,1408]{1,0:T(8,128)(2,1)S(1)}, bf16[24,1408]{1,0:T(8,128)(2,1)S(1)}, u32[]{:S(2)}, u32[]{:S(2)}) collective-permute-start(bf16[24,1408]{1,0:T(8,128)(2,1)S(1)} %get-tuple-element.149), channel_id=1, source_target_pairs={{0,16},{8,24},{16,0},{24,8},{1,17},{9,25},{17,1},{25,9},{2,18},{10... | collective-permute-start | bytes 202760 | tf_op jit(solution)/shard_map/ppermute | solution.py:61
  103.8 9.9 %collective-permute-start.32 = (bf16[24,1408]{1,0:T(8,128)(2,1)S(1)}, bf16[24,1408]{1,0:T(8,128)(2,1)S(1)}, u32[]{:S(2)}, u32[]{:S(2)}) collective-permute-start(bf16[24,1408]{1,0:T(8,128)(2,1)S(1)} %get-tuple-element.148), channel_id=1, source_target_pairs={{0,24},{8,16},{16,8},{24,0},{1,25},{9,17},{17,9},{25,1},{2,26},{10... | collective-permute-start | bytes 202760 | tf_op jit(solution)/shard_map/ppermute | solution.py:61

commit v4 on v3

--- a/solution.py
+++ b/solution.py
@@ -146,7 +146,6 @@
 SHARD = 24
 VEC_AT = 576
 NARROW = 640
-SCALE = 10**10
 G_HEADS = HEADS // TP
 QUARTER = WIDTH // TP
 
@@ -227,8 +226,9 @@
     for i in range(5):
         packed = jnp.where(row == i, vector[:, 64 * i : 64 * i + 64], packed)
     packed = jnp.concatenate([packed.astype(BF), jnp.zeros((SHARD, 128), BF)], axis=1)
-    pieces[1][48:, :] = tokens[:, :]
-    pieces[2][48:, :] = tokens[:, :]
+    for item in pieces:
+        if item.shape[0] > 48:
+            item[48:, :] = tokens[:, :]
     for rank in range(TP):
 
         @pl.when(t == rank)
@@ -257,23 +257,52 @@
     )
 
 
-def normalize_kernel(place, *refs):
-    *slots, xhat, order = refs
-    order[:, :] = feature_order(place[0], place[1])
-    for k in range(TP):
-        first = 48 if slots[k].shape[0] == 48 + ROWS else 0
-        rows = dot(slots[k][first : first + ROWS, :], order[:, :])
-        removed = rows - jnp.mean(rows, axis=-1, keepdims=True)
-        variance = jnp.mean(removed * removed, axis=-1, keepdims=True)
-        xhat[ROWS * k : ROWS * (k + 1), :] = removed * lax.rsqrt(variance + epsilon)
-
-
 def frequency_lanes():
     member = iota((1, 128), 1) & 7
     lanes = jnp.zeros((1, 128), F32)
     for i in range(ROT // 2):
         lanes = jnp.where(member == i, 10000.0 ** (-2.0 * i / ROT), lanes)
     return lanes
+
+
+def normalized(rows):
+    removed = rows - jnp.mean(rows, axis=-1, keepdims=True)
+    return removed * lax.rsqrt(jnp.mean(removed * removed, axis=-1, keepdims=True) + epsilon)
+
+
+def early_kernel(place, zero, one, two, three, tokens, xhat, order, masks, cosine, sine, live):
+    order[:, :] = feature_order(place[0], place[1])
+    column = iota((1, ROWS), 1).astype(F32)
+    line = iota((ROWS, 1), 0).astype(F32)
+    member = iota((1, 128), 1) & 63
+    for k, piece in enumerate((zero, one, two, three)):
+        at = slice(ROWS * k, ROWS * (k + 1))
+        if k < 3:
+            rows = tokens[:, :] if k == 0 else piece[48:, :]
+            xhat[at, :] = normalized(dot(rows, order[:, :]))
+        sizes = piece[16:32, 512:640].astype(F32)[12:13, 120:124]
+        end = jnp.zeros((1, 1), F32)
+        segment_line, segment_column = jnp.zeros((ROWS, 1), F32), jnp.zeros((1, ROWS), F32)
+        first_line = jnp.zeros((ROWS, 1), F32)
+        for s in range(4):
+            size = sizes[:, s : s + 1]
+            end = end + size
+            first_line = first_line + jnp.where(line >= end, size, 0.0)
+            segment_line = segment_line + jnp.where(line >= end, 1.0, 0.0)
+            segment_column = segment_column + jnp.where(column >= end, 1.0, 0.0)
+        lives = line < end
+        mask = (line == column) | (lives & (segment_line == segment_column) & (column <= line))
+        masks[at, :] = jnp.where(mask, 1.0, 0.0)
+        angle = jnp.where(lives, line - first_line, 0.0) * frequency_lanes()
+        cosine[at, :] = jnp.where(member < ROT, jnp.cos(angle), 1.0)
+        sine[at, :] = jnp.where(member < ROT, jnp.sin(angle), 0.0) * jnp.where(
+            member < ROT // 2, -1.0, 1.0
+        )
+        live[at, :] = jnp.where(lives, 1.0, 0.0)
+
+
+def last_kernel(rows, order, xhat):
+    xhat[:, :] = normalized(dot(rows[:ROWS, :], order[:, :]))
 
 
 def turn(values, cosine, sine):
@@ -286,11 +315,11 @@
     )
 
 
-def forward_kernel(place, xhat, *refs):
+def forward_kernel(place, xhat, xhat_last, masks, cosine, sine, *refs):
     columns = refs[:2]
     (
         mat_up, mat_qkv, h_one, h_two, act, slope, q_low, k_low, v_low, probs, mixed_slots, gains,
-        cosine, sine, live, mixed,
+        mixed,
     ) = refs[2:]
     t, q = place[0], place[1]
     for kq in range(8):
@@ -309,39 +338,15 @@
     vec_out = spread(vectors[:, 168:192], plain) + spread(vectors[:, 288:312], plain)
     gains[:, :] = jnp.concatenate([gain_one, gain_two, vec_out, jnp.zeros((5, WIDTH), F32)], axis=0)
 
-    column = iota((1, ROWS), 1).astype(F32)
-    line = iota((ROWS, 1), 0).astype(F32)
-    masks = []
-    for k in range(TP):
-        end = jnp.zeros((1, 1), F32)
-        segment_line, segment_column = jnp.zeros((ROWS, 1), F32), jnp.zeros((1, ROWS), F32)
-        first_line = jnp.zeros((ROWS, 1), F32)
-        for s in range(4):
-            size = vectors[k : k + 1, 312 + s : 313 + s]
-            end = end + size
-            first_line = first_line + jnp.where(line >= end, size, 0.0)
-            segment_line = segment_line + jnp.where(line >= end, 1.0, 0.0)
-            segment_column = segment_column + jnp.where(column >= end, 1.0, 0.0)
-        lives = line < end
-        masks.append(
-            (line == column) | (lives & (segment_line == segment_column) & (column <= line))
-        )
-        angle = jnp.where(lives, line - first_line, 0.0) * frequency_lanes()
-        member = iota((1, 128), 1) & 63
-        at = slice(ROWS * k, ROWS * (k + 1))
-        cosine[at, :] = jnp.where(member < ROT, jnp.cos(angle), 1.0)
-        sine[at, :] = jnp.where(member < ROT, jnp.sin(angle), 0.0) * jnp.where(
-            member < ROT // 2, -1.0, 1.0
-        )
-        live[at, :] = jnp.where(lives, 1.0, 0.0)
-
-    h_two[:, :] = (xhat[:, :] * gain_two + bias_two).astype(BF)
+    h_two[: 3 * ROWS, :] = (xhat[:, :] * gain_two + bias_two).astype(BF)
+    h_two[3 * ROWS :, :] = (xhat_last[:, :] * gain_two + bias_two).astype(BF)
     up = dot(h_two[:, :], mat_up[:, :]) + vec_up
     phi = 0.5 * (1.0 + lax.erf(up * inv_sqrt_two))
     act[:, :] = (up * phi).astype(BF)
     slope[:, :] = phi + up * jnp.exp(-0.5 * up * up) * inv_sqrt_tau
 
-    h_one[:, :] = (xhat[:, :] * gain_one + bias_one).astype(BF)
+    h_one[: 3 * ROWS, :] = (xhat[:, :] * gain_one + bias_one).astype(BF)
+    h_one[3 * ROWS :, :] = (xhat_last[:, :] * gain_one + bias_one).astype(BF)
     qkv = dot(h_one[:, :], mat_qkv[:, :VEC_AT]) + vec_qkv
     turned = turn(qkv[:, : 2 * QUARTER], cosine[:, :], sine[:, :])
     q_low[:, :] = turned[:, :QUARTER].astype(BF)
@@ -352,7 +357,7 @@
         for head in range(G_HEADS):
             lanes = slice(HEAD * head, HEAD * (head + 1))
             scores = dot(q_low[at, lanes], k_low[at, lanes], 1, 1) * 0.125
-            scores = jnp.where(masks[k], scores, neg_large)
+            scores = jnp.where(masks[at, :] > 0.0, scores, neg_large)
             exponent = jnp.exp(scores - jnp.max(scores, axis=-1, keepdims=True))
             chances = exponent / jnp.sum(exponent, axis=-1, keepdims=True)
             probs[G_HEADS * k + head] = chances
@@ -422,7 +427,7 @@
 
 
 def backward_kernel(
-    place, xhat, order, mat_up, mat_qkv, h_one, d_up, d_qkv, gains, cot, live, *refs
+    place, xhat, xhat_last, order, mat_up, mat_qkv, h_one, d_up, d_qkv, gains, cot, live, *refs
 ):
     shares, (keep, send) = refs[:4], refs[4:]
     t, q = place[0], place[1]
@@ -438,11 +443,14 @@
     def total(rows):
         return jnp.sum(rows, axis=0, keepdims=True)
 
+    def with_xhat(rows):
+        return total(rows[: 3 * ROWS] * xhat[:, :]) + total(rows[3 * ROWS :] * xhat_last[:, :])
+
     vectors = jnp.concatenate(
         [
-            collect(total(d_one * xhat[:, :]), slots),
+            collect(with_xhat(d_one), slots),
             collect(total(d_one), slots),
-            collect(total(d_two * xhat[:, :]), slots),
+            collect(with_xhat(d_two), slots),
             collect(total(d_two), slots),
             collect(total(cot[:, :].astype(F32) * live[:ROWS, :]), plain),
             collect(total(d_qkv[:, :].astype(F32)), of_qkv),
@@ -489,7 +497,7 @@
 
 def output_kernel(zero, one, two, three, tokens, live, gains, output):
     share = zero[:, :] + one[:, :].astype(F32) + two[:, :].astype(F32) + three[:, :].astype(F32)
-    output[:, :] = (live[:, :] * (tokens[:, :].astype(F32) + share + gains[2:3, :])).astype(BF)
+    output[:, :] = (live[:ROWS, :] * (tokens[:, :].astype(F32) + share + gains[2:3, :])).astype(BF)
 
 
 def input_kernel(zero, one, two, three, tokens, cot, live, grad):
@@ -501,10 +509,10 @@
     dx = rstd * (
         e - jnp.mean(e, axis=-1, keepdims=True) - xhat * jnp.mean(e * xhat, axis=-1, keepdims=True)
     )
-    grad[:, :] = cot[:, :].astype(F32) * live[:, :] + dx
-
-
-def call(kernel, name, outs, *args, scratch=(), mib=16, us=1):
+    grad[:, :] = cot[:, :].astype(F32) * live[:ROWS, :] + dx
+
+
+def call(kernel, name, outs, *args, scratch=(), mib=16, weight=1):
     space = [pl.BlockSpec(memory_space=pltpu.VMEM)] * len(args)
     if args[0].dtype == jnp.int32:
         space[0] = pl.BlockSpec(memory_space=pltpu.SMEM)
@@ -516,7 +524,7 @@
         in_specs=space,
         out_specs=[pl.BlockSpec(memory_space=pltpu.VMEM)] * len(shapes),
         scratch_shapes=[pltpu.VMEM(shape, kind) for shape, kind in scratch],
-        cost_estimate=pl.CostEstimate(flops=us * SCALE, transcendentals=0, bytes_accessed=us * SCALE // 1000),
+        cost_estimate=pl.CostEstimate(flops=weight * 10**9, transcendentals=0, bytes_accessed=weight * 10**6),
         compiler_params=pltpu.CompilerParams(vmem_limit_bytes=mib * 1024 * 1024),
     )(*args)
 
@@ -559,7 +567,6 @@
     t = lax.axis_index("t")
     q = lax.axis_index("dq") * 4 + lax.axis_index("fsdp")
     place = jnp.stack([t, q]).astype(jnp.int32)
-    live = jnp.where(iota((ROWS, 1), 0) < jnp.sum(lengths), 1.0, 0.0)
     vector = jnp.concatenate(
         [
             ln_attn_gain, ln_attn_bias, ln_mlp_gain, ln_mlp_bias, b_qkv, b_out, b_fc1, b_fc2,
@@ -568,38 +575,42 @@
     )
     block = (ROWS, WIDTH)
     piece = ((48, WIDTH), BF)
+    piece_rows = ((48 + ROWS, WIDTH), BF)
     tail = jnp.concatenate([w_fc2, w_out, jnp.zeros((8, WIDTH), BF)], axis=0)
+    pieces = call(
+        prepare_kernel, "prepare", [piece, piece_rows, piece_rows, piece],
+        place, w_qkv, w_fc1, vector.astype(F32)[None], tokens, weight=10,
+    )
+    pieces = exchange_t(pieces)
+    token_one = pieces[1]
+    both = after(jnp.concatenate([tokens, cotangent], axis=0), token_one)
+    rows_three = lax.ppermute(both, "t", xor_pairs(TP, 3))
     tail_one = lax.ppermute(tail, "fsdp", xor_pairs(4, 1))
     tail_two = lax.ppermute(tail, "fsdp", xor_pairs(4, 2))
     tail_three = lax.ppermute(after(tail, tail_one), "fsdp", xor_pairs(4, 3))
-    piece_rows = ((48 + ROWS, WIDTH), BF)
-    pieces = call(
-        prepare_kernel, "prepare", [piece, piece_rows, piece_rows, piece],
-        place, w_qkv, w_fc1, vector.astype(F32)[None], tokens,
-    )
-    pieces = exchange_t(pieces)
-    token_one, token_two = pieces[1], pieces[2]
-    (columns,) = call(merge_kernel, "merge", [((192, WIDTH), BF)], *pieces)
+    (columns,) = call(merge_kernel, "merge", [((192, WIDTH), BF)], *pieces, weight=10)
     columns = after(columns, tail_one, tail_two, tail_three)
-    rows_three = lax.ppermute(
-        after(jnp.concatenate([tokens, cotangent], axis=0), token_one), "t", xor_pairs(TP, 3)
-    )
     arrived = xor_permutes(columns, "fsdp", 4)
     columns = jnp.concatenate([columns] + arrived, axis=0)
     columns = [columns, lax.ppermute(columns, "dq", xor_pairs(2, 1))]
-    tail = jnp.concatenate([tail, tail_one, tail_two, tail_three], axis=0)
-    tail = [tail, lax.ppermute(tail, "dq", xor_pairs(2, 1))]
     wide = (COUNT, WIDTH)
-    xhat, order = call(
-        normalize_kernel, "normalize", [(wide, F32), ((WIDTH, WIDTH), BF)],
-        place, tokens, token_one, token_two, rows_three,
-    )
-    cot = after(cotangent, xhat)
-    cot_slots = [lax.ppermute(cot, "t", xor_pairs(TP, k)) for k in (1, 2)] + [rows_three]
+    square = ((COUNT, 128), F32)
+    xhat, order, masks, cosine, sine, lives = call(
+        early_kernel,
+        "early",
+        [((3 * ROWS, WIDTH), F32), ((WIDTH, WIDTH), BF), square, square, square, ((COUNT, 1), F32)],
+        place, *pieces, tokens,
+        weight=10,
+    )
+    (xhat_last,) = call(
+        last_kernel, "last", [(block, F32)], rows_three, order, weight=5
+    )
+    cot_one = lax.ppermute(after(cotangent, xhat_last), "t", xor_pairs(TP, 1))
+    cot_two = lax.ppermute(after(cotangent, xhat_last), "t", xor_pairs(TP, 2))
+    cot_slots = [cot_one, cot_two, rows_three]
     third = (COUNT, QUARTER)
     (
         mat_up, mat_qkv, h_one, h_two, act, slope, q_low, k_low, v_low, probs, mixed_slots, gains,
-        cosine, sine, lives,
     ) = call(
         forward_kernel,
         "forward",
@@ -607,17 +618,18 @@
             ((WIDTH, WIDTH), BF), ((WIDTH, NARROW), BF),
             (wide, BF), (wide, BF), (wide, BF), (wide, F32), (third, BF), (third, BF),
             (third, BF), ((HEADS, ROWS, ROWS), F32), ((COUNT, 256), BF), ((8, WIDTH), F32),
-            ((COUNT, 128), F32), ((COUNT, 128), F32), ((COUNT, 1), F32),
         ],
-        place, xhat, *columns,
+        place, xhat, xhat_last, masks, cosine, sine, *columns,
         scratch=[(third, BF)],
-        us=8,
-    )
+        weight=100,
+    )
+    tail = jnp.concatenate([tail, tail_one, tail_two, tail_three], axis=0)
+    tail = [tail, lax.ppermute(tail, "dq", xor_pairs(2, 1))]
     shares = [(block, F32)] + [(block, BF)] * 3
     down, out_mat, *out = call(
         share_kernel, "share", [((WIDTH, WIDTH), BF), ((256, WIDTH), BF)] + shares,
         place, act, mixed_slots, *tail,
-        us=2,
+        weight=10,
     )
     out = exchange_t(out)
     d_up, d_mixed, tail_keep, tail_send = call(
@@ -626,37 +638,42 @@
         [(wide, BF), (third, BF), ((896, WIDTH), F32), ((896, WIDTH), BF)],
         place, cotangent, *cot_slots, lives, h_two, act, slope, mixed_slots, down, out_mat,
         scratch=[(wide, BF), ((WIDTH, WIDTH), F32)],
-        us=4,
+        weight=40,
     )
     tail_pair = plane_pair(tail_keep, tail_send)
     (d_qkv,) = call(
         attention_kernel, "attention", [((COUNT, 3 * QUARTER), BF)],
         q_low, k_low, v_low, probs, d_mixed, cosine, sine,
         scratch=[((COUNT, 2 * QUARTER), F32)],
-        us=5,
-    )
+        weight=50,
+    )
+    tail_got = plane_relay(tail_pair)
     d_qkv = after(d_qkv, tail_pair, out[1])
-    tail_relay = plane_relay(tail_pair)
     *e, col_keep, col_send = call(
         backward_kernel,
         "backward",
         shares + [((384, NARROW), F32), ((384, NARROW), BF)],
-        place, xhat, order, mat_up, mat_qkv, h_one, d_up, d_qkv, gains, cotangent, lives,
-        us=4,
-    )
-    col_pair = plane_pair(col_keep, after(col_send, tail_relay, out[2:]))
-    col_relay = plane_relay(col_pair)
-    e = exchange_t([after(item, out, col_pair) for item in e])
-    col_sum = plane_last(col_pair, *col_relay)
-    tail_sum = plane_last(tail_pair, *tail_relay)
+        place, xhat, xhat_last, order, mat_up, mat_qkv, h_one, d_up, d_qkv, gains, cotangent, lives,
+        weight=40,
+    )
+    col_pair = plane_pair(col_keep, after(col_send, tail_got, out[2:]))
+    col_got = plane_relay(col_pair)
+    e = [after(item, out) for item in e]
+    e[3] = after(e[3], col_pair)
+    e = exchange_t(e)
+    col_sum = plane_last(col_pair, *col_got)
+    tail_sum = plane_last(after(tail_pair, col_got), *tail_got)
     col_sum = jnp.concatenate([tail_sum[128:], col_sum], axis=1)
     low_sum = col_sum.astype(BF)
-    arrived = exchange_t([low_sum[SHARD * k : SHARD * (k + 1)] for k in range(TP)])
+    back = [low_sum[SHARD * k : SHARD * (k + 1)] for k in range(TP)]
+    arrived = exchange_t(back)
     (output,) = call(
-        output_kernel, "output", [(block, BF)], *out, tokens, after(live, col_relay), gains
+        output_kernel, "output", [(block, BF)], *out, tokens, after(lives, col_keep), gains,
+        weight=10,
     )
     (grad_tokens,) = call(
-        input_kernel, "input_gradient", [(block, F32)], *e, tokens, cotangent, live
+        input_kernel, "input_gradient", [(block, F32)], *e, tokens, cotangent, lives,
+        weight=10,
     )
     sizes = [SHARD] * 5 + [3 * SHARD, 4 * SHARD, SHARD]
     shard_qkv, shard_up, *vectors = call(

time: 115 us -> 112 us (0.974)
  starting transfers between devices: 46.1 us -> 41.9 us
    ppermute x12, waiting for transfers between devices: 13.6 us -> 19.9 us  [exchange_t(): lax.ppermute(pieces[k], 't', xor_pairs(TP, k))]
    ppermute x3, starting transfers between devices: 9.36 us -> 5.99 us  [the longest x1 3.06 us: plane_local(): rows_three = lax.ppermute(both, 't', xor_pairs(TP, 3))]
    ppermute x1, waiting for transfers between devices: 2.79 us -> 0.01 us  [plane_local(): tail_one = lax.ppermute(tail, 'fsdp', xor_pairs(4, 1))]
    ppermute x2, waiting for transfers between devices: 3.96 us -> 1.23 us  [plane_last(): one = lax.ppermute(one.astype(BF), 'fsdp', xor_pairs(4, 1))]
    ppermute x1, starting transfers between devices: 2.45 us -> 0.39 us  [plane_local(): tail_three = lax.ppermute(after(tail, tail_one), 'fsdp', xor_pairs(4, 3))]
    ppermute x2, starting transfers between devices: 3.04 us -> 1.14 us  [plane_last(): one = lax.ppermute(one.astype(BF), 'fsdp', xor_pairs(4, 1))]
    ppermute x12, starting transfers between devices: 19.3 us -> 17.4 us  [exchange_t(): lax.ppermute(pieces[k], 't', xor_pairs(TP, k))]
    ppermute x3, waiting for transfers between devices: 8.39 us -> 6.6 us  [xor_permutes(): return [lax.ppermute(block, axis, xor_pairs(count, k)) for k in range(1, 4)]]
  transfers between devices with their start and end apart: 33 -> 33, of which waited for: 16 -> 15; matrix products, arithmetic and copies ran while one was open for 3% -> 3% of each run, Pallas kernels for 18% -> 24%
where the time goes in v4:
time: 112 us
  starting transfers between devices  41.9 us (37%)
  waiting for transfers between devices  32.5 us (29%)
  Pallas kernels  28.1 us (25%)
  local copies, waits for them, and re-layouts  5.26 us (5%)
  other arithmetic  2.83 us (3%)
  between operations  1.22 us (1%)
    pallas_call x12, Pallas kernels, call(): pl.pallas_call(kernel, name=name, out_shape=shapes, in_specs=space, out_s...  28.1 us
    ppermute x12, waiting for transfers between devices, exchange_t(): lax.ppermute(pieces[k], 't', xor_pairs(TP, k))  19.9 us
    ppermute x12, starting transfers between devices, exchange_t(): lax.ppermute(pieces[k], 't', xor_pairs(TP, k))  17.4 us
    ppermute x3, waiting for transfers between devices, xor_permutes(): return [lax.ppermute(block, axis, xor_pairs(count, k)) for k in range(1, 4)]  6.6 us
    ppermute x3, starting transfers between devices, xor_permutes(): return [lax.ppermute(block, axis, xor_pairs(count, k)) for k in range(1, 4)]  3.45 us
    ppermute x2, waiting for transfers between devices, plane_last(): two = lax.ppermute(two.astype(BF), 'fsdp', xor_pairs(4, 2))  3.39 us
    ppermute x2, starting transfers between devices, plane_relay(): upper = lax.ppermute(three[:rows // 2], 'fsdp', xor_pairs(4, 1))  3.17 us
    ppermute x1, starting transfers between devices, plane_local(): rows_three = lax.ppermute(both, 't', xor_pairs(TP, 3))  3.06 us
  transfers between devices with their start and end apart: 33, of which 15 were waited for; matrix products, arithmetic and copies ran while one was open for 3% of the time, Pallas kernels for 24%

profile of v4, /device:TPU:0, one launch (start us, length us, event | category | flops | bytes accessed | tf_op | source)
XLA Modules:
  0.0 111.8 jit_solution(8722235427855381362)
XLA Ops:
  0.7 0.9 pad_maximum_fusion.4
  1.6 3.0 %collective-permute-start.5 = (bf16[128,768]{1,0:T(8,128)(2,1)S(1)}, bf16[128,768]{1,0:T(8,128)(2,1)S(1)}, u32[]{:S(2)}, u32[]{:S(2)}) collective-permute-start(bf16[128,768]{1,0:T(8,128)(2,1)S(1)} %pad_maximum_fusion.4), channel_id=1, source_target_pairs={{0,2},{1,3},{2,0},{3,1},{4,6},{5,7},{6,4},{7,5},{8,10},{9,11},{10,... | collective-permute-start | bytes 589832 | tf_op jit(solution)/shard_map/ppermute | solution.py:589
  4.6 1.5 %collective-permute-start.4 = (bf16[128,768]{1,0:T(8,128)(2,1)S(1)}, bf16[128,768]{1,0:T(8,128)(2,1)S(1)}, u32[]{:S(2)}, u32[]{:S(2)}) collective-permute-start(bf16[128,768]{1,0:T(8,128)(2,1)S(1)} %pad_maximum_fusion.4), channel_id=1, source_target_pairs={{0,1},{1,0},{2,3},{3,2},{4,5},{5,4},{6,7},{7,6},{8,9},{9,8},{10,11... | collective-permute-start | bytes 589832 | tf_op jit(solution)/shard_map/ppermute | solution.py:588
  6.8 0.9 concatenate.66
  7.8 0.9 copy-done
  8.7 0.9 copy-done.4
  9.6 0.9 copy-done.5
  10.5 0.9 prepare.1
  11.4 3.7 %collective-permute-start.2 = (bf16[48,768]{1,0:T(8,128)(2,1)S(1)}, bf16[48,768]{1,0:T(8,128)(2,1)S(1)}, u32[]{:S(2)}, u32[]{:S(2)}) collective-permute-start(bf16[48,768]{1,0:T(8,128)(2,1)S(1)} %get-tuple-element.78), channel_id=1, source_target_pairs={{0,24},{8,16},{16,8},{24,0},{1,25},{9,17},{17,9},{25,1},{2,26},{10... | collective-permute-start | bytes 221192 | tf_op jit(solution)/shard_map/ppermute | solution.py:61
  15.1 0.8 collective-permute-start.1
  16.4 2.2 %collective-permute-done.2.three = bf16[48,768]{1,0:T(8,128)(2,1)S(1)} collective-permute-done((bf16[48,768]{1,0:T(8,128)(2,1)S(1)}, bf16[48,768]{1,0:T(8,128)(2,1)S(1)}, u32[]{:S(2)}, u32[]{:S(2)}) %collective-permute-start.2) | collective-permute-done | bytes 73760 | tf_op jit(solution)/shard_map/ppermute | solution.py:61
  18.6 9.3 %collective-permute-done.one = bf16[176,768]{1,0:T(8,128)(2,1)S(1)} collective-permute-done((bf16[176,768]{1,0:T(8,128)(2,1)S(1)}, bf16[176,768]{1,0:T(8,128)(2,1)S(1)}, u32[]{:S(2)}, u32[]{:S(2)}) %collective-permute-start) | collective-permute-done | bytes 270368 | tf_op jit(solution)/shard_map/ppermute | solution.py:61
  27.9 1.8 %collective-permute-done.1.two = bf16[176,768]{1,0:T(8,128)(2,1)S(1)} collective-permute-done((bf16[176,768]{1,0:T(8,128)(2,1)S(1)}, bf16[176,768]{1,0:T(8,128)(2,1)S(1)}, u32[]{:S(2)}, u32[]{:S(2)}) %collective-permute-start.1) | collective-permute-done | bytes 270368 | tf_op jit(solution)/shard_map/ppermute | solution.py:61
  30.8 3.1 %collective-permute-start.3 = (bf16[256,768]{1,0:T(8,128)(2,1)S(1)}, bf16[256,768]{1,0:T(8,128)(2,1)S(1)}, u32[]{:S(2)}, u32[]{:S(2)}) collective-permute-start(bf16[256,768]{1,0:T(8,128)(2,1)S(1)} %pad_maximum_fusion.1), channel_id=1, source_target_pairs={{0,24},{8,16},{16,8},{24,0},{1,25},{9,17},{17,9},{25,1},{2,26},{10... | collective-permute-start | bytes 1179656 | tf_op jit(solution)/shard_map/ppermute | solution.py:587
  33.8 2.4 %collective-permute-start.9 = (bf16[192,768]{1,0:T(8,128)(2,1)S(1)}, bf16[192,768]{1,0:T(8,128)(2,1)S(1)}, u32[]{:S(2)}, u32[]{:S(2)}) collective-permute-start(bf16[192,768]{1,0:T(8,128)(2,1)S(1)} %merge.1), channel_id=1, source_target_pairs={{0,3},{1,2},{2,1},{3,0},{4,7},{5,6},{6,5},{7,4},{8,11},{9,10},{10,... | collective-permute-start | bytes 884744 | tf_op jit(solution)/shard_map/ppermute | solution.py:537
  36.3 3.1 %collective-permute-done.7 = bf16[192,768]{1,0:T(8,128)(2,1)S(1)} collective-permute-done((bf16[192,768]{1,0:T(8,128)(2,1)S(1)}, bf16[192,768]{1,0:T(8,128)(2,1)S(1)}, u32[]{:S(2)}, u32[]{:S(2)}) %collective-permute-start.7) | collective-permute-done | bytes 294944 | tf_op jit(solution)/shard_map/ppermute | solution.py:537
  39.5 3.5 %collective-permute-done.8 = bf16[192,768]{1,0:T(8,128)(2,1)S(1)} collective-permute-done((bf16[192,768]{1,0:T(8,128)(2,1)S(1)}, bf16[192,768]{1,0:T(8,128)(2,1)S(1)}, u32[]{:S(2)}, u32[]{:S(2)}) %collective-permute-start.8) | collective-permute-done | bytes 294944 | tf_op jit(solution)/shard_map/ppermute | solution.py:537
  43.1 2.8 %early.1 = (f32[384,768]{1,0:T(8,128)S(1)}, bf16[768,768]{1,0:T(8,128)(2,1)S(1)}, f32[512,128]{1,0:T(8,128)S(1)}, f32[512,128]{1,0:T(8,128)S(1)}, f32[512,128]{1,0:T(8,128)S(1)}, /*index=5*/f32[512,1]{1,0:T(8,128)S(1)}) custom-call(s32[2]{0:T(128)S(1)} %pad_add_fusion.place, bf16[48,768]{1,0:T(8,128)(2,1)S(1)} %get-tuple-element.75.zero, ...), custom_call_target="tpu_custom_call" | custom-call | flops 10000000000 | bytes 10000000 | tf_op jit(solution)/shard_map/early/pallas_call | solution.py:520
  47.0 2.6 %collective-permute-start.16 = (bf16[128,768]{1,0:T(8,128)(2,1)S(1)}, bf16[128,768]{1,0:T(8,128)(2,1)S(1)}, u32[]{:S(2)}, u32[]{:S(2)}) collective-permute-start(bf16[128,768]{1,0:T(8,128)(2,1)S(1)} %copy-done.3), channel_id=1, source_target_pairs={{0,16},{8,24},{16,0},{24,8},{1,17},{9,25},{17,1},{25,9},{2,18},{10... | collective-permute-start | bytes 589832 | tf_op jit(solution)/shard_map/ppermute | solution.py:609
  50.0 7.2 %forward.1 = (bf16[768,768]{1,0:T(8,128)(2,1)S(1)}, bf16[768,640]{1,0:T(8,128)(2,1)S(1)}, bf16[512,768]{1,0:T(8,128)(2,1)S(1)}, bf16[512,768]{1,0:T(8,128)(2,1)S...) custom-call(s32[2]{0:T(128)S(1)} %pad_add_fusion.place, ...), custom_call_target="tpu_custom_call" | custom-call | flops 99999997952 | bytes 100000000 | tf_op jit(solution)/shard_map/forward/pallas_call | solution.py:520
  57.2 1.6 %share.1 = (bf16[768,768]{1,0:T(8,128)(2,1)S(1)}, bf16[256,768]{1,0:T(8,128)(2,1)S(1)}, f32[128,768]{1,0:T(8,128)S(1)}, bf16[128,768]{1,0:T(8,128)(2,1)S(1)}, bf...) custom-call(s32[2]{0:T(128)S(1)} %pad_add_fusion.place, bf16[512,768]{1,0:T(8,128)(2,1)S(1)} %get-tuple-element.87.act.refs_6_, ...), custom_call_target="tpu_custom_call" | custom-call | flops 10000000000 | bytes 10000000 | tf_op jit(solution)/shard_map/share/pallas_call | solution.py:520
  58.8 1.8 %collective-permute-start.12 = (bf16[128,768]{1,0:T(8,128)(2,1)S(1)}, bf16[128,768]{1,0:T(8,128)(2,1)S(1)}, u32[]{:S(2)}, u32[]{:S(2)}) collective-permute-start(bf16[128,768]{1,0:T(8,128)(2,1)S(1)} %get-tuple-element.90), channel_id=1, source_target_pairs={{0,8},{8,0},{16,24},{24,16},{1,9},{9,1},{17,25},{25,17},{2,10},{10... | collective-permute-start | bytes 589832 | tf_op jit(solution)/shard_map/ppermute | solution.py:61
  61.0 2.3 %collective-permute-start.14 = (bf16[128,768]{1,0:T(8,128)(2,1)S(1)}, bf16[128,768]{1,0:T(8,128)(2,1)S(1)}, u32[]{:S(2)}, u32[]{:S(2)}) collective-permute-start(bf16[128,768]{1,0:T(8,128)(2,1)S(1)} %get-tuple-element.92), channel_id=1, source_target_pairs={{0,24},{8,16},{16,8},{24,0},{1,25},{9,17},{17,9},{25,1},{2,26},{10... | collective-permute-start | bytes 589832 | tf_op jit(solution)/shard_map/ppermute | solution.py:61
  63.3 3.4 %upstream.1 = (bf16[512,768]{1,0:T(8,128)(2,1)S(1)}, bf16[512,192]{1,0:T(8,128)(2,1)S(1)}, f32[896,768]{1,0:T(8,128)S(1)}, bf16[896,768]{1,0:T(8,128)(2,1)S(1)}) custom-call(s32[2]{0:T(128)S(1)} %pad_add_fusion.place, bf16[128,768]{1,0:T(8,128)(2,1)S(1)} %copy-done.3, bf16[128,768]{1,0:T(8,128)(2,1)S(1)} %collective-permute-done.15.refs_1_, ...), custom_call_target="tpu_custom_call" | custom-call | flops 40000000000 | bytes 40000000 | tf_op jit(solution)/shard_map/upstream/pallas_call | solution.py:520
  66.8 4.3 %attention.1.d_qkv = bf16[512,576]{1,0:T(8,128)(2,1)S(1)} custom-call(bf16[512,192]{1,0:T(8,128)(2,1)S(1)} %get-tuple-element.103.q_low, bf16[512,192]{1,0:T(8,128)(2,1)S(1)} %get-tuple-element.104.k_low, bf16[512,192]{1,0:T(8,128)(2,1)S(1)} %get-tuple-element.105.v_low, f32[12,128,128]{2,1,0:T(8,128)S(1)} %get-tuple-element.106.probs, ...), custom_call_target="tpu_custom_call" | custom-call | flops 49999998976 | bytes 50000000 | tf_op jit(solution)/shard_map/attention/pallas_call | solution.py:520
  71.6 1.1 %collective-permute-start.21 = (bf16[112,768]{1,0:T(8,128)(2,1)S(1)}, bf16[112,768]{1,0:T(8,128)(2,1)S(1)}, u32[]{:S(2)}, u32[]{:S(2)}) collective-permute-start(bf16[112,768]{1,0:T(8,128)(2,1)S(1)} %get-tuple-element.144), channel_id=1, source_target_pairs={{0,2},{1,3},{2,0},{3,1},{4,6},{5,7},{6,4},{7,5},{8,10},{9,11},{10,... | collective-permute-start | bytes 516104 | tf_op jit(solution)/shard_map/ppermute | solution.py:548
  72.7 1.6 %collective-permute-start.20 = (bf16[112,768]{1,0:T(8,128)(2,1)S(1)}, bf16[112,768]{1,0:T(8,128)(2,1)S(1)}, u32[]{:S(2)}, u32[]{:S(2)}) collective-permute-start(bf16[112,768]{1,0:T(8,128)(2,1)S(1)} %get-tuple-element.145), channel_id=1, source_target_pairs={{0,1},{1,0},{2,3},{3,2},{4,5},{5,4},{6,7},{7,6},{8,9},{9,8},{10,11... | collective-permute-start | bytes 516104 | tf_op jit(solution)/shard_map/ppermute | solution.py:547
  74.3 3.8 %backward.1 = (f32[128,768]{1,0:T(8,128)S(1)}, bf16[128,768]{1,0:T(8,128)(2,1)S(1)}, bf16[128,768]{1,0:T(8,128)(2,1)S(1)}, bf16[128,768]{1,0:T(8,128)(2,1)S(1)},...) custom-call(s32[2]{0:T(128)S(1)} %pad_add_fusion.place, f32[384,768]{1,0:T(8,128)S(1)} %get-tuple-element.79.xhat, ...), custom_call_target="tpu_custom_call" | custom-call | flops 40000000000 | bytes 40000000 | tf_op jit(solution)/shard_map/backward/pallas_call | solution.py:520
  78.4 0.8 collective-permute-done.20
  79.2 1.6 %collective-permute-start.19 = (bf16[128,768]{1,0:T(8,128)(2,1)S(1)}, bf16[128,768]{1,0:T(8,128)(2,1)S(1)}, u32[]{:S(2)}, u32[]{:S(2)}) collective-permute-start(bf16[128,768]{1,0:T(8,128)(2,1)S(1)} %get-tuple-element.119), channel_id=1, source_target_pairs={{0,16},{8,24},{16,0},{24,8},{1,17},{9,25},{17,1},{25,9},{2,18},{10... | collective-permute-start | bytes 589832 | tf_op jit(solution)/shard_map/ppermute | solution.py:61
  81.2 1.0 collective-permute-start.25
  82.3 1.6 %collective-permute-start.24 = (bf16[48,640]{1,0:T(8,128)(2,1)S(1)}, bf16[48,640]{1,0:T(8,128)(2,1)S(1)}, u32[]{:S(2)}, u32[]{:S(2)}) collective-permute-start(bf16[48,640]{1,0:T(8,128)(2,1)S(1)} %get-tuple-element.153), channel_id=1, source_target_pairs={{0,1},{1,0},{2,3},{3,2},{4,5},{5,4},{6,7},{7,6},{8,9},{9,8},{10,11... | collective-permute-start | bytes 184328 | tf_op jit(solution)/shard_map/ppermute | solution.py:547
  83.9 0.8 output.1
  84.7 1.7 %collective-permute-start.18 = (bf16[128,768]{1,0:T(8,128)(2,1)S(1)}, bf16[128,768]{1,0:T(8,128)(2,1)S(1)}, u32[]{:S(2)}, u32[]{:S(2)}) collective-permute-start(bf16[128,768]{1,0:T(8,128)(2,1)S(1)} %get-tuple-element.117), channel_id=1, source_target_pairs={{0,8},{8,0},{16,24},{24,16},{1,9},{9,1},{17,25},{25,17},{2,10},{10... | collective-permute-start | bytes 589832 | tf_op jit(solution)/shard_map/ppermute | solution.py:61
  86.4 0.8 collective-permute-start.23
  87.3 1.5 %collective-permute-start.29 = (bf16[96,640]{1,0:T(8,128)(2,1)S(1)}, bf16[96,640]{1,0:T(8,128)(2,1)S(1)}, u32[]{:S(2)}, u32[]{:S(2)}) collective-permute-start(bf16[96,640]{1,0:T(8,128)(2,1)S(1)} %pad_maximum_fusion.6), channel_id=1, source_target_pairs={{0,2},{1,3},{2,0},{3,1},{4,6},{5,7},{6,4},{7,5},{8,10},{9,11},{10,... | collective-permute-start | bytes 368648 | tf_op jit(solution)/shard_map/ppermute | solution.py:559
  89.7 2.5 %collective-permute-done.29 = bf16[96,640]{1,0:T(8,128)(2,1)S(1)} collective-permute-done((bf16[96,640]{1,0:T(8,128)(2,1)S(1)}, bf16[96,640]{1,0:T(8,128)(2,1)S(1)}, u32[]{:S(2)}, u32[]{:S(2)}) %collective-permute-start.29) | collective-permute-done | bytes 122912 | tf_op jit(solution)/shard_map/ppermute | solution.py:559
  92.2 1.4 %collective-permute-start.27 = (bf16[224,768]{1,0:T(8,128)(2,1)S(1)}, bf16[224,768]{1,0:T(8,128)(2,1)S(1)}, u32[]{:S(2)}, u32[]{:S(2)}) collective-permute-start(bf16[224,768]{1,0:T(8,128)(2,1)S(1)} %pad_maximum_fusion.3), channel_id=1, source_target_pairs={{0,2},{1,3},{2,0},{3,1},{4,6},{5,7},{6,4},{7,5},{8,10},{9,11},{10,... | collective-permute-start | bytes 1032200 | tf_op jit(solution)/shard_map/ppermute | solution.py:559
  94.4 4.1 %collective-permute-done.18.one = bf16[128,768]{1,0:T(8,128)(2,1)S(1)} collective-permute-done((bf16[128,768]{1,0:T(8,128)(2,1)S(1)}, bf16[128,768]{1,0:T(8,128)(2,1)S(1)}, u32[]{:S(2)}, u32[]{:S(2)}) %collective-permute-start.18) | collective-permute-done | bytes 196640 | tf_op jit(solution)/shard_map/ppermute | solution.py:61
  98.4 1.1 %input_gradient.1 = f32[128,768]{1,0:T(8,128)} custom-call(f32[128,768]{1,0:T(8,128)S(1)} %get-tuple-element.115.zero, bf16[128,768]{1,0:T(8,128)(2,1)S(1)} %collective-permute-done.18.one, bf16[128,768]{1,0:T(8,128)(2,1)S(1)} %collective-permute-done.19.two, bf16[128,768]{1,0:T(8,128)(2,1)S(1)} %collective-permute-done.23.three, ...), custom_call_target="tpu_custom_call" | custom-call | flops 10000000000 | bytes 10000000 | tf_op jit(solution)/shard_map/input_gradient/pallas_call | solution.py:520
  99.6 0.9 collective-permute-done.27
  100.5 1.2 %collective-permute-done.26 = bf16[224,768]{1,0:T(8,128)(2,1)S(1)} collective-permute-done((bf16[224,768]{1,0:T(8,128)(2,1)S(1)}, bf16[224,768]{1,0:T(8,128)(2,1)S(1)}, u32[]{:S(2)}, u32[]{:S(2)}) %collective-permute-start.26) | collective-permute-done | bytes 344096 | tf_op jit(solution)/shard_map/ppermute | solution.py:558
  101.7 0.8 fusion.9
  102.5 2.3 %collective-permute-start.32 = (bf16[24,1408]{1,0:T(8,128)(2,1)S(1)}, bf16[24,1408]{1,0:T(8,128)(2,1)S(1)}, u32[]{:S(2)}, u32[]{:S(2)}) collective-permute-start(bf16[24,1408]{1,0:T(8,128)(2,1)S(1)} %get-tuple-element.154), channel_id=1, source_target_pairs={{0,24},{8,16},{16,8},{24,0},{1,25},{9,17},{17,9},{25,1},{2,26},{10... | collective-permute-start | bytes 202760 | tf_op jit(solution)/shard_map/ppermute | solution.py:61
  104.9 2.1 %collective-permute-start.30 = (bf16[24,1408]{1,0:T(8,128)(2,1)S(1)}, bf16[24,1408]{1,0:T(8,128)(2,1)S(1)}, u32[]{:S(2)}, u32[]{:S(2)}) collective-permute-start(bf16[24,1408]{1,0:T(8,128)(2,1)S(1)} %get-tuple-element.156), channel_id=1, source_target_pairs={{0,8},{8,0},{16,24},{24,16},{1,9},{9,1},{17,25},{25,17},{2,10},{10... | collective-permute-start | bytes 202760 | tf_op jit(solution)/shard_map/ppermute | solution.py:61
  107.6 1.1 collective-permute-done.32.three
  108.7 1.4 %collective-permute-done.31.two = bf16[24,1408]{1,0:T(8,128)(2,1)S(1)} collective-permute-done((bf16[24,1408]{1,0:T(8,128)(2,1)S(1)}, bf16[24,1408]{1,0:T(8,128)(2,1)S(1)}, u32[]{:S(2)}, u32[]{:S(2)}) %collective-permute-start.31) | collective-permute-done | bytes 67616 | tf_op jit(solution)/shard_map/ppermute | solution.py:61
  110.2 1.5 %columns.1 = (f32[24,2304]{1,0:T(8,128)}, f32[24,3072]{1,0:T(8,128)}, f32[1,24]{1,0:T(1,128)}, f32[1,24]{1,0:T(1,128)}, f32[1,24]{1,0:T(1,128)}, /*index=5*/f32[...) custom-call(s32[2]{0:T(128)S(1)} %pad_add_fusion.place, ...), custom_call_target="tpu_custom_call" | custom-call | flops 1000000000 | bytes 1000000 | tf_op jit(solution)/shard_map/columns/pallas_call | solution.py:520
  (87 shorter events, 8.0 us)
Async XLA Ops:
  1.6 28.1 %collective-permute-start.5 = (bf16[128,768]{1,0:T(8,128)(2,1)S(1)}, bf16[128,768]{1,0:T(8,128)(2,1)S(1)}, u32[]{:S(2)}, u32[]{:S(2)}) collective-permute-start(bf16[128,768]{1,0:T(8,128)(2,1)S(1)} %pad_maximum_fusion.4), channel_id=1, source_target_pairs={{0,2},{1,3},{2,0},{3,1},{4,6},{5,7},{6,4},{7,5},{8,10},{9,11},{10,... | collective-permute-start | bytes 589832 | tf_op jit(solution)/shard_map/ppermute | solution.py:589
  4.6 11.4 %collective-permute-start.4 = (bf16[128,768]{1,0:T(8,128)(2,1)S(1)}, bf16[128,768]{1,0:T(8,128)(2,1)S(1)}, u32[]{:S(2)}, u32[]{:S(2)}) collective-permute-start(bf16[128,768]{1,0:T(8,128)(2,1)S(1)} %pad_maximum_fusion.4), channel_id=1, source_target_pairs={{0,1},{1,0},{2,3},{3,2},{4,5},{5,4},{6,7},{7,6},{8,9},{9,8},{10,11... | collective-permute-start | bytes 589832 | tf_op jit(solution)/shard_map/ppermute | solution.py:588
  7.8 0.9 copy-start
  8.7 0.9 copy-start.4
  9.6 0.9 copy-start.5
  10.5 5.4 %copy-start.3 = (bf16[128,768]{1,0:T(8,128)(2,1)S(1)}, bf16[128,768]{1,0:T(8,128)(2,1)}, u32[]{:S(2)}) copy-start(bf16[128,768]{1,0:T(8,128)(2,1)} %cot.3) | copy-start | bytes 589828
  10.5 5.4 %copy-start.8 = (bf16[96,768]{1,0:T(8,128)(2,1)S(1)}, bf16[96,768]{1,0:T(8,128)(2,1)}, u32[]{:S(2)}) copy-start(bf16[96,768]{1,0:T(8,128)(2,1)} %param.27) | copy-start | bytes 442372
  10.5 5.5 %copy-start.9 = (bf16[24,768]{1,0:T(8,128)(2,1)S(1)}, bf16[24,768]{1,0:T(8,128)(2,1)}, u32[]{:S(2)}) copy-start(bf16[24,768]{1,0:T(8,128)(2,1)} %param.23) | copy-start | bytes 110596
  11.4 7.2 %collective-permute-start.2 = (bf16[48,768]{1,0:T(8,128)(2,1)S(1)}, bf16[48,768]{1,0:T(8,128)(2,1)S(1)}, u32[]{:S(2)}, u32[]{:S(2)}) collective-permute-start(bf16[48,768]{1,0:T(8,128)(2,1)S(1)} %get-tuple-element.78), channel_id=1, source_target_pairs={{0,24},{8,16},{16,8},{24,0},{1,25},{9,17},{17,9},{25,1},{2,26},{10... | collective-permute-start | bytes 221192 | tf_op jit(solution)/shard_map/ppermute | solution.py:61
  15.1 12.8 %collective-permute-start = (bf16[176,768]{1,0:T(8,128)(2,1)S(1)}, bf16[176,768]{1,0:T(8,128)(2,1)S(1)}, u32[]{:S(2)}, u32[]{:S(2)}) collective-permute-start(bf16[176,768]{1,0:T(8,128)(2,1)S(1)} %get-tuple-element.76), channel_id=1, source_target_pairs={{0,8},{8,0},{16,24},{24,16},{1,9},{9,1},{17,25},{25,17},{2,10},{10... | collective-permute-start | bytes 811016 | tf_op jit(solution)/shard_map/ppermute | solution.py:61
  15.1 14.6 %collective-permute-start.1 = (bf16[176,768]{1,0:T(8,128)(2,1)S(1)}, bf16[176,768]{1,0:T(8,128)(2,1)S(1)}, u32[]{:S(2)}, u32[]{:S(2)}) collective-permute-start(bf16[176,768]{1,0:T(8,128)(2,1)S(1)} %get-tuple-element.77), channel_id=1, source_target_pairs={{0,16},{8,24},{16,0},{24,8},{1,17},{9,25},{17,1},{25,9},{2,18},{10... | collective-permute-start | bytes 811016 | tf_op jit(solution)/shard_map/ppermute | solution.py:61
  16.0 13.7 %collective-permute-start.6 = (bf16[128,768]{1,0:T(8,128)(2,1)S(1)}, bf16[128,768]{1,0:T(8,128)(2,1)S(1)}, u32[]{:S(2)}, u32[]{:S(2)}) collective-permute-start(bf16[128,768]{1,0:T(8,128)(2,1)S(1)} %pad_maximum_fusion.4), channel_id=1, source_target_pairs={{0,3},{1,2},{2,1},{3,0},{4,7},{5,6},{6,5},{7,4},{8,11},{9,10},{10,... | collective-permute-start | bytes 589832 | tf_op jit(solution)/shard_map/ppermute | solution.py:590
  29.7 9.7 %collective-permute-start.7 = (bf16[192,768]{1,0:T(8,128)(2,1)S(1)}, bf16[192,768]{1,0:T(8,128)(2,1)S(1)}, u32[]{:S(2)}, u32[]{:S(2)}) collective-permute-start(bf16[192,768]{1,0:T(8,128)(2,1)S(1)} %merge.1), channel_id=1, source_target_pairs={{0,1},{1,0},{2,3},{3,2},{4,5},{5,4},{6,7},{7,6},{8,9},{9,8},{10,11... | collective-permute-start | bytes 884744 | tf_op jit(solution)/shard_map/ppermute | solution.py:537
  30.3 12.6 %collective-permute-start.8 = (bf16[192,768]{1,0:T(8,128)(2,1)S(1)}, bf16[192,768]{1,0:T(8,128)(2,1)S(1)}, u32[]{:S(2)}, u32[]{:S(2)}) collective-permute-start(bf16[192,768]{1,0:T(8,128)(2,1)S(1)} %merge.1), channel_id=1, source_target_pairs={{0,2},{1,3},{2,0},{3,1},{4,6},{5,7},{6,4},{7,5},{8,10},{9,11},{10,... | collective-permute-start | bytes 884744 | tf_op jit(solution)/shard_map/ppermute | solution.py:537
  30.8 12.3 %copy-start.1 = (bf16[128,768]{1,0:T(8,128)(2,1)S(1)}, bf16[128,768]{1,0:T(8,128)(2,1)}, u32[]{:S(2)}) copy-start(bf16[128,768]{1,0:T(8,128)(2,1)} %tokens.7) | copy-start | bytes 589828
  30.8 15.7 %collective-permute-start.3 = (bf16[256,768]{1,0:T(8,128)(2,1)S(1)}, bf16[256,768]{1,0:T(8,128)(2,1)S(1)}, u32[]{:S(2)}, u32[]{:S(2)}) collective-permute-start(bf16[256,768]{1,0:T(8,128)(2,1)S(1)} %pad_maximum_fusion.1), channel_id=1, source_target_pairs={{0,24},{8,16},{16,8},{24,0},{1,25},{9,17},{17,9},{25,1},{2,26},{10... | collective-permute-start | bytes 1179656 | tf_op jit(solution)/shard_map/ppermute | solution.py:587
  33.8 9.1 %collective-permute-start.9 = (bf16[192,768]{1,0:T(8,128)(2,1)S(1)}, bf16[192,768]{1,0:T(8,128)(2,1)S(1)}, u32[]{:S(2)}, u32[]{:S(2)}) collective-permute-start(bf16[192,768]{1,0:T(8,128)(2,1)S(1)} %merge.1), channel_id=1, source_target_pairs={{0,3},{1,2},{2,1},{3,0},{4,7},{5,6},{6,5},{7,4},{8,11},{9,10},{10,... | collective-permute-start | bytes 884744 | tf_op jit(solution)/shard_map/ppermute | solution.py:537
  43.0 7.0 %collective-permute-start.10 = (bf16[768,768]{1,0:T(8,128)(2,1)S(1)}, bf16[768,768]{1,0:T(8,128)(2,1)S(1)}, u32[]{:S(2)}, u32[]{:S(2)}) collective-permute-start(bf16[768,768]{1,0:T(8,128)(2,1)S(1)} %constant_dynamic-update-slice_fusion.refs_0_), channel_id=1, source_target_pairs={{0,4},{4,0},{1,5},{5,1},{2,6},{6,2},{3,7},{7,3},{8,12},{12,8},{9,1... | collective-permute-start | bytes 3538952 | tf_op jit(solution)/shard_map/ppermute | solution.py:595
  45.9 1.1 %copy-start.6 = (bf16[768,768]{1,0:T(8,128)(2,1)}, bf16[768,768]{1,0:T(8,128)(2,1)S(1)}, u32[]{:S(2)}) copy-start(bf16[768,768]{1,0:T(8,128)(2,1)S(1)} %get-tuple-element.81.order) | copy-start | bytes 3538948
  46.0 11.2 %collective-permute-start.11 = (bf16[512,768]{1,0:T(8,128)(2,1)S(1)}, bf16[512,768]{1,0:T(8,128)(2,1)S(1)}, u32[]{:S(2)}, u32[]{:S(2)}) collective-permute-start(bf16[512,768]{1,0:T(8,128)(2,1)S(1)} %constant_dynamic-update-slice_fusion.4.refs_0_), channel_id=1, source_target_pairs={{0,4},{4,0},{1,5},{5,1},{2,6},{6,2},{3,7},{7,3},{8,12},{12,8},{9,1... | collective-permute-start | bytes 2359304 | tf_op jit(solution)/shard_map/ppermute | solution.py:627
  47.0 16.2 %collective-permute-start.16 = (bf16[128,768]{1,0:T(8,128)(2,1)S(1)}, bf16[128,768]{1,0:T(8,128)(2,1)S(1)}, u32[]{:S(2)}, u32[]{:S(2)}) collective-permute-start(bf16[128,768]{1,0:T(8,128)(2,1)S(1)} %copy-done.3), channel_id=1, source_target_pairs={{0,16},{8,24},{16,0},{24,8},{1,17},{9,25},{17,1},{25,9},{2,18},{10... | collective-permute-start | bytes 589832 | tf_op jit(solution)/shard_map/ppermute | solution.py:609
  49.7 13.6 %collective-permute-start.15 = (bf16[128,768]{1,0:T(8,128)(2,1)S(1)}, bf16[128,768]{1,0:T(8,128)(2,1)S(1)}, u32[]{:S(2)}, u32[]{:S(2)}) collective-permute-start(bf16[128,768]{1,0:T(8,128)(2,1)S(1)} %copy-done.3), channel_id=1, source_target_pairs={{0,8},{8,0},{16,24},{24,16},{1,9},{9,1},{17,25},{25,17},{2,10},{10... | collective-permute-start | bytes 589832 | tf_op jit(solution)/shard_map/ppermute | solution.py:608
  58.8 12.7 %collective-permute-start.12 = (bf16[128,768]{1,0:T(8,128)(2,1)S(1)}, bf16[128,768]{1,0:T(8,128)(2,1)S(1)}, u32[]{:S(2)}, u32[]{:S(2)}) collective-permute-start(bf16[128,768]{1,0:T(8,128)(2,1)S(1)} %get-tuple-element.90), channel_id=1, source_target_pairs={{0,8},{8,0},{16,24},{24,16},{1,9},{9,1},{17,25},{25,17},{2,10},{10... | collective-permute-start | bytes 589832 | tf_op jit(solution)/shard_map/ppermute | solution.py:61
  60.6 17.5 %collective-permute-start.13 = (bf16[128,768]{1,0:T(8,128)(2,1)S(1)}, bf16[128,768]{1,0:T(8,128)(2,1)S(1)}, u32[]{:S(2)}, u32[]{:S(2)}) collective-permute-start(bf16[128,768]{1,0:T(8,128)(2,1)S(1)} %get-tuple-element.91), channel_id=1, source_target_pairs={{0,16},{8,24},{16,0},{24,8},{1,17},{9,25},{17,1},{25,9},{2,18},{10... | collective-permute-start | bytes 589832 | tf_op jit(solution)/shard_map/ppermute | solution.py:61
  61.0 17.1 %collective-permute-start.14 = (bf16[128,768]{1,0:T(8,128)(2,1)S(1)}, bf16[128,768]{1,0:T(8,128)(2,1)S(1)}, u32[]{:S(2)}, u32[]{:S(2)}) collective-permute-start(bf16[128,768]{1,0:T(8,128)(2,1)S(1)} %get-tuple-element.92), channel_id=1, source_target_pairs={{0,24},{8,16},{16,8},{24,0},{1,25},{9,17},{17,9},{25,1},{2,26},{10... | collective-permute-start | bytes 589832 | tf_op jit(solution)/shard_map/ppermute | solution.py:61
  66.7 4.4 %collective-permute-start.17 = (bf16[896,768]{1,0:T(8,128)(2,1)S(1)}, bf16[896,768]{1,0:T(8,128)(2,1)S(1)}, u32[]{:S(2)}, u32[]{:S(2)}) collective-permute-start(bf16[896,768]{1,0:T(8,128)(2,1)S(1)} %get-tuple-element.109), channel_id=1, source_target_pairs={{0,4},{4,0},{1,5},{5,1},{2,6},{6,2},{3,7},{7,3},{8,12},{12,8},{9,1... | collective-permute-start | bytes 4128776 | tf_op jit(solution)/shard_map/ppermute | solution.py:541
  71.1 3.2 %copy-start.7 = (bf16[768,768]{1,0:T(8,128)(2,1)S(1)}, bf16[768,768]{1,0:T(8,128)(2,1)}, u32[]{:S(2)}) copy-start(bf16[768,768]{1,0:T(8,128)(2,1)} %copy-done.6) | copy-start | bytes 3538948
  71.6 6.8 %collective-permute-start.21 = (bf16[112,768]{1,0:T(8,128)(2,1)S(1)}, bf16[112,768]{1,0:T(8,128)(2,1)S(1)}, u32[]{:S(2)}, u32[]{:S(2)}) collective-permute-start(bf16[112,768]{1,0:T(8,128)(2,1)S(1)} %get-tuple-element.144), channel_id=1, source_target_pairs={{0,2},{1,3},{2,0},{3,1},{4,6},{5,7},{6,4},{7,5},{8,10},{9,11},{10,... | collective-permute-start | bytes 516104 | tf_op jit(solution)/shard_map/ppermute | solution.py:548
  72.7 6.5 %collective-permute-start.20 = (bf16[112,768]{1,0:T(8,128)(2,1)S(1)}, bf16[112,768]{1,0:T(8,128)(2,1)S(1)}, u32[]{:S(2)}, u32[]{:S(2)}) collective-permute-start(bf16[112,768]{1,0:T(8,128)(2,1)S(1)} %get-tuple-element.145), channel_id=1, source_target_pairs={{0,1},{1,0},{2,3},{3,2},{4,5},{5,4},{6,7},{7,6},{8,9},{9,8},{10,11... | collective-permute-start | bytes 516104 | tf_op jit(solution)/shard_map/ppermute | solution.py:547
  79.2 1.9 %collective-permute-start.22 = (bf16[384,640]{1,0:T(8,128)(2,1)S(1)}, bf16[384,640]{1,0:T(8,128)(2,1)S(1)}, u32[]{:S(2)}, u32[]{:S(2)}) collective-permute-start(bf16[384,640]{1,0:T(8,128)(2,1)S(1)} %get-tuple-element.123), channel_id=1, source_target_pairs={{0,4},{4,0},{1,5},{5,1},{2,6},{6,2},{3,7},{7,3},{8,12},{12,8},{9,1... | collective-permute-start | bytes 1474568 | tf_op jit(solution)/shard_map/ppermute | solution.py:541
  79.2 4.7 %copy-start.2 = (bf16[128,768]{1,0:T(8,128)(2,1)S(1)}, bf16[128,768]{1,0:T(8,128)(2,1)}, u32[]{:S(2)}) copy-start(bf16[128,768]{1,0:T(8,128)(2,1)} %tokens.7) | copy-start | bytes 589828
  79.2 15.1 %collective-permute-start.19 = (bf16[128,768]{1,0:T(8,128)(2,1)S(1)}, bf16[128,768]{1,0:T(8,128)(2,1)S(1)}, u32[]{:S(2)}, u32[]{:S(2)}) collective-permute-start(bf16[128,768]{1,0:T(8,128)(2,1)S(1)} %get-tuple-element.119), channel_id=1, source_target_pairs={{0,16},{8,24},{16,0},{24,8},{1,17},{9,25},{17,1},{25,9},{2,18},{10... | collective-permute-start | bytes 589832 | tf_op jit(solution)/shard_map/ppermute | solution.py:61
  81.2 6.0 %collective-permute-start.25 = (bf16[48,640]{1,0:T(8,128)(2,1)S(1)}, bf16[48,640]{1,0:T(8,128)(2,1)S(1)}, u32[]{:S(2)}, u32[]{:S(2)}) collective-permute-start(bf16[48,640]{1,0:T(8,128)(2,1)S(1)} %get-tuple-element.152), channel_id=1, source_target_pairs={{0,2},{1,3},{2,0},{3,1},{4,6},{5,7},{6,4},{7,5},{8,10},{9,11},{10,... | collective-permute-start | bytes 184328 | tf_op jit(solution)/shard_map/ppermute | solution.py:548
  82.3 5.0 %collective-permute-start.24 = (bf16[48,640]{1,0:T(8,128)(2,1)S(1)}, bf16[48,640]{1,0:T(8,128)(2,1)S(1)}, u32[]{:S(2)}, u32[]{:S(2)}) collective-permute-start(bf16[48,640]{1,0:T(8,128)(2,1)S(1)} %get-tuple-element.153), channel_id=1, source_target_pairs={{0,1},{1,0},{2,3},{3,2},{4,5},{5,4},{6,7},{7,6},{8,9},{9,8},{10,11... | collective-permute-start | bytes 184328 | tf_op jit(solution)/shard_map/ppermute | solution.py:547
  84.7 13.7 %collective-permute-start.18 = (bf16[128,768]{1,0:T(8,128)(2,1)S(1)}, bf16[128,768]{1,0:T(8,128)(2,1)S(1)}, u32[]{:S(2)}, u32[]{:S(2)}) collective-permute-start(bf16[128,768]{1,0:T(8,128)(2,1)S(1)} %get-tuple-element.117), channel_id=1, source_target_pairs={{0,8},{8,0},{16,24},{24,16},{1,9},{9,1},{17,25},{25,17},{2,10},{10... | collective-permute-start | bytes 589832 | tf_op jit(solution)/shard_map/ppermute | solution.py:61
  86.4 12.0 %collective-permute-start.23 = (bf16[128,768]{1,0:T(8,128)(2,1)S(1)}, bf16[128,768]{1,0:T(8,128)(2,1)S(1)}, u32[]{:S(2)}, u32[]{:S(2)}) collective-permute-start(bf16[128,768]{1,0:T(8,128)(2,1)S(1)} %get-tuple-element.124), channel_id=1, source_target_pairs={{0,24},{8,16},{16,8},{24,0},{1,25},{9,17},{17,9},{25,1},{2,26},{10... | collective-permute-start | bytes 589832 | tf_op jit(solution)/shard_map/ppermute | solution.py:61
  87.3 4.9 %collective-permute-start.29 = (bf16[96,640]{1,0:T(8,128)(2,1)S(1)}, bf16[96,640]{1,0:T(8,128)(2,1)S(1)}, u32[]{:S(2)}, u32[]{:S(2)}) collective-permute-start(bf16[96,640]{1,0:T(8,128)(2,1)S(1)} %pad_maximum_fusion.6), channel_id=1, source_target_pairs={{0,2},{1,3},{2,0},{3,1},{4,6},{5,7},{6,4},{7,5},{8,10},{9,11},{10,... | collective-permute-start | bytes 368648 | tf_op jit(solution)/shard_map/ppermute | solution.py:559
  88.8 4.9 %collective-permute-start.28 = (bf16[96,640]{1,0:T(8,128)(2,1)S(1)}, bf16[96,640]{1,0:T(8,128)(2,1)S(1)}, u32[]{:S(2)}, u32[]{:S(2)}) collective-permute-start(bf16[96,640]{1,0:T(8,128)(2,1)S(1)} %pad_maximum_fusion.5), channel_id=1, source_target_pairs={{0,1},{1,0},{2,3},{3,2},{4,5},{5,4},{6,7},{7,6},{8,9},{9,8},{10,11... | collective-permute-start | bytes 368648 | tf_op jit(solution)/shard_map/ppermute | solution.py:558
  92.2 8.2 %collective-permute-start.27 = (bf16[224,768]{1,0:T(8,128)(2,1)S(1)}, bf16[224,768]{1,0:T(8,128)(2,1)S(1)}, u32[]{:S(2)}, u32[]{:S(2)}) collective-permute-start(bf16[224,768]{1,0:T(8,128)(2,1)S(1)} %pad_maximum_fusion.3), channel_id=1, source_target_pairs={{0,2},{1,3},{2,0},{3,1},{4,6},{5,7},{6,4},{7,5},{8,10},{9,11},{10,... | collective-permute-start | bytes 1032200 | tf_op jit(solution)/shard_map/ppermute | solution.py:559
  93.8 7.8 %collective-permute-start.26 = (bf16[224,768]{1,0:T(8,128)(2,1)S(1)}, bf16[224,768]{1,0:T(8,128)(2,1)S(1)}, u32[]{:S(2)}, u32[]{:S(2)}) collective-permute-start(bf16[224,768]{1,0:T(8,128)(2,1)S(1)} %pad_maximum_fusion.2), channel_id=1, source_target_pairs={{0,1},{1,0},{2,3},{3,2},{4,5},{5,4},{6,7},{7,6},{8,9},{9,8},{10,11... | collective-permute-start | bytes 1032200 | tf_op jit(solution)/shard_map/ppermute | solution.py:558
  102.5 6.2 %collective-permute-start.32 = (bf16[24,1408]{1,0:T(8,128)(2,1)S(1)}, bf16[24,1408]{1,0:T(8,128)(2,1)S(1)}, u32[]{:S(2)}, u32[]{:S(2)}) collective-permute-start(bf16[24,1408]{1,0:T(8,128)(2,1)S(1)} %get-tuple-element.154), channel_id=1, source_target_pairs={{0,24},{8,16},{16,8},{24,0},{1,25},{9,17},{17,9},{25,1},{2,26},{10... | collective-permute-start | bytes 202760 | tf_op jit(solution)/shard_map/ppermute | solution.py:61
  104.9 5.3 %collective-permute-start.31 = (bf16[24,1408]{1,0:T(8,128)(2,1)S(1)}, bf16[24,1408]{1,0:T(8,128)(2,1)S(1)}, u32[]{:S(2)}, u32[]{:S(2)}) collective-permute-start(bf16[24,1408]{1,0:T(8,128)(2,1)S(1)} %get-tuple-element.155), channel_id=1, source_target_pairs={{0,16},{8,24},{16,0},{24,8},{1,17},{9,25},{17,1},{25,9},{2,18},{10... | collective-permute-start | bytes 202760 | tf_op jit(solution)/shard_map/ppermute | solution.py:61
  104.9 5.3 %collective-permute-start.30 = (bf16[24,1408]{1,0:T(8,128)(2,1)S(1)}, bf16[24,1408]{1,0:T(8,128)(2,1)S(1)}, u32[]{:S(2)}, u32[]{:S(2)}) collective-permute-start(bf16[24,1408]{1,0:T(8,128)(2,1)S(1)} %get-tuple-element.156), channel_id=1, source_target_pairs={{0,8},{8,0},{16,24},{24,16},{1,9},{9,1},{17,25},{25,17},{2,10},{10... | collective-permute-start | bytes 202760 | tf_op jit(solution)/shard_map/ppermute | solution.py:61

commit v5 on v4

--- a/solution.py
+++ b/solution.py
@@ -219,7 +219,8 @@
     return dot((mask * row).astype(BF), element, 1, 1)
 
 
-def prepare_kernel(place, w_qkv, w_fc1, vector, tokens, *pieces):
+def prepare_kernel(place, weights, vector, tokens, *pieces):
+    w_fc1, w_qkv = weights.at[:, : 4 * WIDTH], weights.at[:, 4 * WIDTH :]
     t = place[0]
     row = iota((SHARD, 64), 0)
     packed = jnp.zeros((SHARD, 64), F32)
@@ -577,14 +578,18 @@
     piece = ((48, WIDTH), BF)
     piece_rows = ((48 + ROWS, WIDTH), BF)
     tail = jnp.concatenate([w_fc2, w_out, jnp.zeros((8, WIDTH), BF)], axis=0)
+    weights = jnp.concatenate([w_fc1, w_qkv], axis=1)
     pieces = call(
         prepare_kernel, "prepare", [piece, piece_rows, piece_rows, piece],
-        place, w_qkv, w_fc1, vector.astype(F32)[None], tokens, weight=10,
-    )
+        place, weights, vector.astype(F32)[None], tokens,
+        weight=10,
+    )
+    prepared = pieces
     pieces = exchange_t(pieces)
     token_one = pieces[1]
     both = after(jnp.concatenate([tokens, cotangent], axis=0), token_one)
     rows_three = lax.ppermute(both, "t", xor_pairs(TP, 3))
+    tail = after(tail, prepared)
     tail_one = lax.ppermute(tail, "fsdp", xor_pairs(4, 1))
     tail_two = lax.ppermute(tail, "fsdp", xor_pairs(4, 2))
     tail_three = lax.ppermute(after(tail, tail_one), "fsdp", xor_pairs(4, 3))
@@ -667,6 +672,7 @@
     low_sum = col_sum.astype(BF)
     back = [low_sum[SHARD * k : SHARD * (k + 1)] for k in range(TP)]
     arrived = exchange_t(back)
+    tail_sum = after(tail_sum, low_sum)
     (output,) = call(
         output_kernel, "output", [(block, BF)], *out, tokens, after(lives, col_keep), gains,
         weight=10,

time: 112 us -> 109 us (0.973)
  waiting for transfers between devices: 32.5 us -> 30.2 us
  local copies, waits for them, and re-layouts: 5.26 us -> 3.52 us
    ppermute x12, waiting for transfers between devices: 19.9 us -> 11.4 us  [exchange_t(): lax.ppermute(pieces[k], 't', xor_pairs(TP, k))]
    ppermute x1, waiting for transfers between devices: 0.01 us -> 4.12 us  [plane_local(): tail_one = lax.ppermute(tail, 'fsdp', xor_pairs(4, 1))]
    ppermute x2, starting transfers between devices: 3.17 us -> 1.07 us  [plane_relay(): upper = lax.ppermute(three[:rows // 2], 'fsdp', xor_pairs(4, 1))]
    unnamed x28 -> x22, local copies, waits for them, and re-layouts: 2.87 us -> 1.05 us
    ppermute x1, starting transfers between devices: 2.63 us -> 4.42 us  [plane_local(): cot_two = lax.ppermute(after(cotangent, xhat_last), 't', xor_pairs(TP, 2))]
    ppermute x2, starting transfers between devices: 2.95 us -> 1.28 us  [plane_last(): two = lax.ppermute(two.astype(BF), 'fsdp', xor_pairs(4, 2))]
    ppermute x2, starting transfers between devices: 1.14 us -> 2.69 us  [plane_last(): one = lax.ppermute(one.astype(BF), 'fsdp', xor_pairs(4, 1))]
    ppermute x3, starting transfers between devices: 3.45 us -> 4.92 us  [xor_permutes(): return [lax.ppermute(block, axis, xor_pairs(count, k)) for k in range(1, 4)]]
  transfers between devices with their start and end apart: 33 -> 33, of which waited for: 15 -> 19; matrix products, arithmetic and copies ran while one was open for 3% -> 3% of each run, Pallas kernels for 24% -> 24%
where the time goes in v5:
time: 109 us
  starting transfers between devices  42.9 us (39%)
  waiting for transfers between devices  30.2 us (28%)
  Pallas kernels  28.1 us (26%)
  local copies, waits for them, and re-layouts  3.52 us (3%)
  other arithmetic  2.97 us (3%)
  between operations  1.19 us (1%)
    pallas_call x12, Pallas kernels, call(): pl.pallas_call(kernel, name=name, out_shape=shapes, in_specs=space, out_s...  28.1 us
    ppermute x12, starting transfers between devices, exchange_t(): lax.ppermute(pieces[k], 't', xor_pairs(TP, k))  18.5 us
    ppermute x12, waiting for transfers between devices, exchange_t(): lax.ppermute(pieces[k], 't', xor_pairs(TP, k))  11.4 us
    ppermute x3, waiting for transfers between devices, xor_permutes(): return [lax.ppermute(block, axis, xor_pairs(count, k)) for k in range(1, 4)]  7.29 us
    ppermute x3, starting transfers between devices, xor_permutes(): return [lax.ppermute(block, axis, xor_pairs(count, k)) for k in range(1, 4)]  4.92 us
    ppermute x1, starting transfers between devices, plane_local(): cot_two = lax.ppermute(after(cotangent, xhat_last), 't', xor_pairs(TP, 2))  4.42 us
    ppermute x1, waiting for transfers between devices, plane_local(): tail_one = lax.ppermute(tail, 'fsdp', xor_pairs(4, 1))  4.12 us
    ppermute x2, waiting for transfers between devices, plane_last(): two = lax.ppermute(two.astype(BF), 'fsdp', xor_pairs(4, 2))  3.98 us
  transfers between devices with their start and end apart: 33, of which 19 were waited for; matrix products, arithmetic and copies ran while one was open for 3% of the time, Pallas kernels for 24%

profile of v5, /device:TPU:0, one launch (start us, length us, event | category | flops | bytes accessed | tf_op | source)
XLA Modules:
  0.0 109.0 jit_solution(8828585062591591745)
XLA Ops:
  0.7 0.7 convert_element_type.53
  1.3 0.9 concatenate.69
  2.3 1.0 pad_maximum_fusion.4.weights
  3.3 0.9 copy-done
  4.2 0.9 prepare.1
  5.1 5.1 %collective-permute-start.2 = (bf16[48,768]{1,0:T(8,128)(2,1)S(1)}, bf16[48,768]{1,0:T(8,128)(2,1)S(1)}, u32[]{:S(2)}, u32[]{:S(2)}) collective-permute-start(bf16[48,768]{1,0:T(8,128)(2,1)S(1)} %get-tuple-element.80), channel_id=1, source_target_pairs={{0,24},{8,16},{16,8},{24,0},{1,25},{9,17},{17,9},{25,1},{2,26},{10... | collective-permute-start | bytes 221192 | tf_op jit(solution)/shard_map/ppermute | solution.py:61
  10.2 0.6 collective-permute-start.1
  11.1 1.7 %collective-permute-start.5 = (bf16[128,768]{1,0:T(8,128)(2,1)S(1)}, bf16[128,768]{1,0:T(8,128)(2,1)S(1)}, u32[]{:S(2)}, u32[]{:S(2)}) collective-permute-start(bf16[128,768]{1,0:T(8,128)(2,1)S(1)} %maximum_maximum_fusion), channel_id=1, source_target_pairs={{0,2},{1,3},{2,0},{3,1},{4,6},{5,7},{6,4},{7,5},{8,10},{9,11},{10,... | collective-permute-start | bytes 589832 | tf_op jit(solution)/shard_map/ppermute | solution.py:594
  12.8 1.5 %collective-permute-start.4 = (bf16[128,768]{1,0:T(8,128)(2,1)S(1)}, bf16[128,768]{1,0:T(8,128)(2,1)S(1)}, u32[]{:S(2)}, u32[]{:S(2)}) collective-permute-start(bf16[128,768]{1,0:T(8,128)(2,1)S(1)} %maximum_maximum_fusion), channel_id=1, source_target_pairs={{0,1},{1,0},{2,3},{3,2},{4,5},{5,4},{6,7},{7,6},{8,9},{9,8},{10,11... | collective-permute-start | bytes 589832 | tf_op jit(solution)/shard_map/ppermute | solution.py:593
  14.4 4.1 %collective-permute-done.4 = bf16[128,768]{1,0:T(8,128)(2,1)S(1)} collective-permute-done((bf16[128,768]{1,0:T(8,128)(2,1)S(1)}, bf16[128,768]{1,0:T(8,128)(2,1)S(1)}, u32[]{:S(2)}, u32[]{:S(2)}) %collective-permute-start.4) | collective-permute-done | bytes 196640 | tf_op jit(solution)/shard_map/ppermute | solution.py:593
  18.5 1.4 %collective-permute-start.6 = (bf16[128,768]{1,0:T(8,128)(2,1)S(1)}, bf16[128,768]{1,0:T(8,128)(2,1)S(1)}, u32[]{:S(2)}, u32[]{:S(2)}) collective-permute-start(bf16[128,768]{1,0:T(8,128)(2,1)S(1)} %maximum_maximum_fusion), channel_id=1, source_target_pairs={{0,3},{1,2},{2,1},{3,0},{4,7},{5,6},{6,5},{7,4},{8,11},{9,10},{10,... | collective-permute-start | bytes 589832 | tf_op jit(solution)/shard_map/ppermute | solution.py:595
  19.9 3.8 %collective-permute-done.one = bf16[176,768]{1,0:T(8,128)(2,1)S(1)} collective-permute-done((bf16[176,768]{1,0:T(8,128)(2,1)S(1)}, bf16[176,768]{1,0:T(8,128)(2,1)S(1)}, u32[]{:S(2)}, u32[]{:S(2)}) %collective-permute-start) | collective-permute-done | bytes 270368 | tf_op jit(solution)/shard_map/ppermute | solution.py:61
  23.7 1.2 %collective-permute-done.1.two = bf16[176,768]{1,0:T(8,128)(2,1)S(1)} collective-permute-done((bf16[176,768]{1,0:T(8,128)(2,1)S(1)}, bf16[176,768]{1,0:T(8,128)(2,1)S(1)}, u32[]{:S(2)}, u32[]{:S(2)}) %collective-permute-start.1) | collective-permute-done | bytes 270368 | tf_op jit(solution)/shard_map/ppermute | solution.py:61
  25.1 1.6 %collective-permute-start.7 = (bf16[192,768]{1,0:T(8,128)(2,1)S(1)}, bf16[192,768]{1,0:T(8,128)(2,1)S(1)}, u32[]{:S(2)}, u32[]{:S(2)}) collective-permute-start(bf16[192,768]{1,0:T(8,128)(2,1)S(1)} %merge.1), channel_id=1, source_target_pairs={{0,1},{1,0},{2,3},{3,2},{4,5},{5,4},{6,7},{7,6},{8,9},{9,8},{10,11... | collective-permute-start | bytes 884744 | tf_op jit(solution)/shard_map/ppermute | solution.py:538
  26.7 1.6 %collective-permute-start.8 = (bf16[192,768]{1,0:T(8,128)(2,1)S(1)}, bf16[192,768]{1,0:T(8,128)(2,1)S(1)}, u32[]{:S(2)}, u32[]{:S(2)}) collective-permute-start(bf16[192,768]{1,0:T(8,128)(2,1)S(1)} %merge.1), channel_id=1, source_target_pairs={{0,2},{1,3},{2,0},{3,1},{4,6},{5,7},{6,4},{7,5},{8,10},{9,11},{10,... | collective-permute-start | bytes 884744 | tf_op jit(solution)/shard_map/ppermute | solution.py:538
  28.3 2.5 %collective-permute-start.3 = (bf16[256,768]{1,0:T(8,128)(2,1)S(1)}, bf16[256,768]{1,0:T(8,128)(2,1)S(1)}, u32[]{:S(2)}, u32[]{:S(2)}) collective-permute-start(bf16[256,768]{1,0:T(8,128)(2,1)S(1)} %pad_maximum_fusion.1), channel_id=1, source_target_pairs={{0,24},{8,16},{16,8},{24,0},{1,25},{9,17},{17,9},{25,1},{2,26},{10... | collective-permute-start | bytes 1179656 | tf_op jit(solution)/shard_map/ppermute | solution.py:591
  30.8 1.7 %collective-permute-start.9 = (bf16[192,768]{1,0:T(8,128)(2,1)S(1)}, bf16[192,768]{1,0:T(8,128)(2,1)S(1)}, u32[]{:S(2)}, u32[]{:S(2)}) collective-permute-start(bf16[192,768]{1,0:T(8,128)(2,1)S(1)} %merge.1), channel_id=1, source_target_pairs={{0,3},{1,2},{2,1},{3,0},{4,7},{5,6},{6,5},{7,4},{8,11},{9,10},{10,... | collective-permute-start | bytes 884744 | tf_op jit(solution)/shard_map/ppermute | solution.py:538
  32.5 1.6 %collective-permute-done.7 = bf16[192,768]{1,0:T(8,128)(2,1)S(1)} collective-permute-done((bf16[192,768]{1,0:T(8,128)(2,1)S(1)}, bf16[192,768]{1,0:T(8,128)(2,1)S(1)}, u32[]{:S(2)}, u32[]{:S(2)}) %collective-permute-start.7) | collective-permute-done | bytes 294944 | tf_op jit(solution)/shard_map/ppermute | solution.py:538
  34.2 5.6 %collective-permute-done.8 = bf16[192,768]{1,0:T(8,128)(2,1)S(1)} collective-permute-done((bf16[192,768]{1,0:T(8,128)(2,1)S(1)}, bf16[192,768]{1,0:T(8,128)(2,1)S(1)}, u32[]{:S(2)}, u32[]{:S(2)}) %collective-permute-start.8) | collective-permute-done | bytes 294944 | tf_op jit(solution)/shard_map/ppermute | solution.py:538
  40.0 2.8 %early.1 = (f32[384,768]{1,0:T(8,128)S(1)}, bf16[768,768]{1,0:T(8,128)(2,1)S(1)}, f32[512,128]{1,0:T(8,128)S(1)}, f32[512,128]{1,0:T(8,128)S(1)}, f32[512,128]{1,0:T(8,128)S(1)}, /*index=5*/f32[512,1]{1,0:T(8,128)S(1)}) custom-call(s32[2]{0:T(128)S(1)} %pad_add_fusion.place, bf16[48,768]{1,0:T(8,128)(2,1)S(1)} %get-tuple-element.77.zero, ...), custom_call_target="tpu_custom_call" | custom-call | flops 10000000000 | bytes 10000000 | tf_op jit(solution)/shard_map/early/pallas_call | solution.py:521
  44.0 4.4 %collective-permute-start.16 = (bf16[128,768]{1,0:T(8,128)(2,1)S(1)}, bf16[128,768]{1,0:T(8,128)(2,1)S(1)}, u32[]{:S(2)}, u32[]{:S(2)}) collective-permute-start(bf16[128,768]{1,0:T(8,128)(2,1)S(1)} %copy-done.3), channel_id=1, source_target_pairs={{0,16},{8,24},{16,0},{24,8},{1,17},{9,25},{17,1},{25,9},{2,18},{10... | collective-permute-start | bytes 589832 | tf_op jit(solution)/shard_map/ppermute | solution.py:614
  48.4 7.2 %forward.1 = (bf16[768,768]{1,0:T(8,128)(2,1)S(1)}, bf16[768,640]{1,0:T(8,128)(2,1)S(1)}, bf16[512,768]{1,0:T(8,128)(2,1)S(1)}, bf16[512,768]{1,0:T(8,128)(2,1)S...) custom-call(s32[2]{0:T(128)S(1)} %pad_add_fusion.place, ...), custom_call_target="tpu_custom_call" | custom-call | flops 99999997952 | bytes 100000000 | tf_op jit(solution)/shard_map/forward/pallas_call | solution.py:521
  55.6 1.6 %share.1 = (bf16[768,768]{1,0:T(8,128)(2,1)S(1)}, bf16[256,768]{1,0:T(8,128)(2,1)S(1)}, f32[128,768]{1,0:T(8,128)S(1)}, bf16[128,768]{1,0:T(8,128)(2,1)S(1)}, bf...) custom-call(s32[2]{0:T(128)S(1)} %pad_add_fusion.place, bf16[512,768]{1,0:T(8,128)(2,1)S(1)} %get-tuple-element.90.act.refs_6_, ...), custom_call_target="tpu_custom_call" | custom-call | flops 10000000000 | bytes 10000000 | tf_op jit(solution)/shard_map/share/pallas_call | solution.py:521
  57.2 2.1 %collective-permute-start.12 = (bf16[128,768]{1,0:T(8,128)(2,1)S(1)}, bf16[128,768]{1,0:T(8,128)(2,1)S(1)}, u32[]{:S(2)}, u32[]{:S(2)}) collective-permute-start(bf16[128,768]{1,0:T(8,128)(2,1)S(1)} %get-tuple-element.93), channel_id=1, source_target_pairs={{0,8},{8,0},{16,24},{24,16},{1,9},{9,1},{17,25},{25,17},{2,10},{10... | collective-permute-start | bytes 589832 | tf_op jit(solution)/shard_map/ppermute | solution.py:61
  59.4 2.4 %collective-permute-start.14 = (bf16[128,768]{1,0:T(8,128)(2,1)S(1)}, bf16[128,768]{1,0:T(8,128)(2,1)S(1)}, u32[]{:S(2)}, u32[]{:S(2)}) collective-permute-start(bf16[128,768]{1,0:T(8,128)(2,1)S(1)} %get-tuple-element.95), channel_id=1, source_target_pairs={{0,24},{8,16},{16,8},{24,0},{1,25},{9,17},{17,9},{25,1},{2,26},{10... | collective-permute-start | bytes 589832 | tf_op jit(solution)/shard_map/ppermute | solution.py:61
  61.8 3.4 %upstream.1 = (bf16[512,768]{1,0:T(8,128)(2,1)S(1)}, bf16[512,192]{1,0:T(8,128)(2,1)S(1)}, f32[896,768]{1,0:T(8,128)S(1)}, bf16[896,768]{1,0:T(8,128)(2,1)S(1)}) custom-call(s32[2]{0:T(128)S(1)} %pad_add_fusion.place, bf16[128,768]{1,0:T(8,128)(2,1)S(1)} %copy-done.3, bf16[128,768]{1,0:T(8,128)(2,1)S(1)} %collective-permute-done.15.refs_1_, ...), custom_call_target="tpu_custom_call" | custom-call | flops 40000000000 | bytes 40000000 | tf_op jit(solution)/shard_map/upstream/pallas_call | solution.py:521
  65.3 4.3 %attention.1.d_qkv = bf16[512,576]{1,0:T(8,128)(2,1)S(1)} custom-call(bf16[512,192]{1,0:T(8,128)(2,1)S(1)} %get-tuple-element.106.q_low, bf16[512,192]{1,0:T(8,128)(2,1)S(1)} %get-tuple-element.107.k_low, bf16[512,192]{1,0:T(8,128)(2,1)S(1)} %get-tuple-element.108.v_low, f32[12,128,128]{2,1,0:T(8,128)S(1)} %get-tuple-element.109.probs, ...), custom_call_target="tpu_custom_call" | custom-call | flops 49999998976 | bytes 50000000 | tf_op jit(solution)/shard_map/attention/pallas_call | solution.py:521
  70.1 0.7 collective-permute-start.21
  71.3 3.8 %backward.1 = (f32[128,768]{1,0:T(8,128)S(1)}, bf16[128,768]{1,0:T(8,128)(2,1)S(1)}, bf16[128,768]{1,0:T(8,128)(2,1)S(1)}, bf16[128,768]{1,0:T(8,128)(2,1)S(1)},...) custom-call(s32[2]{0:T(128)S(1)} %pad_add_fusion.place, f32[384,768]{1,0:T(8,128)S(1)} %get-tuple-element.81.xhat, ...), custom_call_target="tpu_custom_call" | custom-call | flops 40000000000 | bytes 40000000 | tf_op jit(solution)/shard_map/backward/pallas_call | solution.py:521
  75.4 1.6 %collective-permute-done.21 = bf16[112,768]{1,0:T(8,128)(2,1)S(1)} collective-permute-done((bf16[112,768]{1,0:T(8,128)(2,1)S(1)}, bf16[112,768]{1,0:T(8,128)(2,1)S(1)}, u32[]{:S(2)}, u32[]{:S(2)}) %collective-permute-start.21) | collective-permute-done | bytes 172064 | tf_op jit(solution)/shard_map/ppermute | solution.py:549
  77.3 1.3 %collective-permute-start.19 = (bf16[128,768]{1,0:T(8,128)(2,1)S(1)}, bf16[128,768]{1,0:T(8,128)(2,1)S(1)}, u32[]{:S(2)}, u32[]{:S(2)}) collective-permute-start(bf16[128,768]{1,0:T(8,128)(2,1)S(1)} %get-tuple-element.122), channel_id=1, source_target_pairs={{0,16},{8,24},{16,0},{24,8},{1,17},{9,25},{17,1},{25,9},{2,18},{10... | collective-permute-start | bytes 589832 | tf_op jit(solution)/shard_map/ppermute | solution.py:61
  79.3 1.5 %collective-permute-start.25 = (bf16[48,640]{1,0:T(8,128)(2,1)S(1)}, bf16[48,640]{1,0:T(8,128)(2,1)S(1)}, u32[]{:S(2)}, u32[]{:S(2)}) collective-permute-start(bf16[48,640]{1,0:T(8,128)(2,1)S(1)} %get-tuple-element.154), channel_id=1, source_target_pairs={{0,2},{1,3},{2,0},{3,1},{4,6},{5,7},{6,4},{7,5},{8,10},{9,11},{10,... | collective-permute-start | bytes 184328 | tf_op jit(solution)/shard_map/ppermute | solution.py:549
  81.3 0.8 output.1
  82.2 1.1 collective-permute-start.18
  83.2 1.5 %collective-permute-start.23 = (bf16[128,768]{1,0:T(8,128)(2,1)S(1)}, bf16[128,768]{1,0:T(8,128)(2,1)S(1)}, u32[]{:S(2)}, u32[]{:S(2)}) collective-permute-start(bf16[128,768]{1,0:T(8,128)(2,1)S(1)} %get-tuple-element.127), channel_id=1, source_target_pairs={{0,24},{8,16},{16,8},{24,0},{1,25},{9,17},{17,9},{25,1},{2,26},{10... | collective-permute-start | bytes 589832 | tf_op jit(solution)/shard_map/ppermute | solution.py:61
  85.1 0.7 collective-permute-start.29
  85.8 1.4 %collective-permute-start.28 = (bf16[96,640]{1,0:T(8,128)(2,1)S(1)}, bf16[96,640]{1,0:T(8,128)(2,1)S(1)}, u32[]{:S(2)}, u32[]{:S(2)}) collective-permute-start(bf16[96,640]{1,0:T(8,128)(2,1)S(1)} %pad_maximum_fusion.5), channel_id=1, source_target_pairs={{0,1},{1,0},{2,3},{3,2},{4,5},{5,4},{6,7},{7,6},{8,9},{9,8},{10,11... | collective-permute-start | bytes 368648 | tf_op jit(solution)/shard_map/ppermute | solution.py:559
  87.5 2.6 %collective-permute-done.29 = bf16[96,640]{1,0:T(8,128)(2,1)S(1)} collective-permute-done((bf16[96,640]{1,0:T(8,128)(2,1)S(1)}, bf16[96,640]{1,0:T(8,128)(2,1)S(1)}, u32[]{:S(2)}, u32[]{:S(2)}) %collective-permute-start.29) | collective-permute-done | bytes 122912 | tf_op jit(solution)/shard_map/ppermute | solution.py:560
  90.7 1.3 %collective-permute-start.26 = (bf16[224,768]{1,0:T(8,128)(2,1)S(1)}, bf16[224,768]{1,0:T(8,128)(2,1)S(1)}, u32[]{:S(2)}, u32[]{:S(2)}) collective-permute-start(bf16[224,768]{1,0:T(8,128)(2,1)S(1)} %pad_maximum_fusion.2), channel_id=1, source_target_pairs={{0,1},{1,0},{2,3},{3,2},{4,5},{5,4},{6,7},{7,6},{8,9},{9,8},{10,11... | collective-permute-start | bytes 1032200 | tf_op jit(solution)/shard_map/ppermute | solution.py:559
  92.1 3.5 %collective-permute-done.23.three = bf16[128,768]{1,0:T(8,128)(2,1)S(1)} collective-permute-done((bf16[128,768]{1,0:T(8,128)(2,1)S(1)}, bf16[128,768]{1,0:T(8,128)(2,1)S(1)}, u32[]{:S(2)}, u32[]{:S(2)}) %collective-permute-start.23) | collective-permute-done | bytes 196640 | tf_op jit(solution)/shard_map/ppermute | solution.py:61
  95.6 1.1 %input_gradient.1 = f32[128,768]{1,0:T(8,128)} custom-call(f32[128,768]{1,0:T(8,128)S(1)} %get-tuple-element.118.zero, bf16[128,768]{1,0:T(8,128)(2,1)S(1)} %collective-permute-done.18.one, bf16[128,768]{1,0:T(8,128)(2,1)S(1)} %collective-permute-done.19.two, bf16[128,768]{1,0:T(8,128)(2,1)S(1)} %collective-permute-done.23.three, ...), custom_call_target="tpu_custom_call" | custom-call | flops 10000000000 | bytes 10000000 | tf_op jit(solution)/shard_map/input_gradient/pallas_call | solution.py:521
  96.7 1.4 %collective-permute-done.27 = bf16[224,768]{1,0:T(8,128)(2,1)S(1)} collective-permute-done((bf16[224,768]{1,0:T(8,128)(2,1)S(1)}, bf16[224,768]{1,0:T(8,128)(2,1)S(1)}, u32[]{:S(2)}, u32[]{:S(2)}) %collective-permute-start.27) | collective-permute-done | bytes 344096 | tf_op jit(solution)/shard_map/ppermute | solution.py:560
  98.9 3.0 %collective-permute-start.32 = (bf16[24,1408]{1,0:T(8,128)(2,1)S(1)}, bf16[24,1408]{1,0:T(8,128)(2,1)S(1)}, u32[]{:S(2)}, u32[]{:S(2)}) collective-permute-start(bf16[24,1408]{1,0:T(8,128)(2,1)S(1)} %get-tuple-element.156), channel_id=1, source_target_pairs={{0,24},{8,16},{16,8},{24,0},{1,25},{9,17},{17,9},{25,1},{2,26},{10... | collective-permute-start | bytes 202760 | tf_op jit(solution)/shard_map/ppermute | solution.py:61
  102.3 1.0 collective-permute-start.30
  104.0 0.7 slice.107
  104.7 1.0 collective-permute-done.32.three
  105.7 1.6 %collective-permute-done.31.two = bf16[24,1408]{1,0:T(8,128)(2,1)S(1)} collective-permute-done((bf16[24,1408]{1,0:T(8,128)(2,1)S(1)}, bf16[24,1408]{1,0:T(8,128)(2,1)S(1)}, u32[]{:S(2)}, u32[]{:S(2)}) %collective-permute-start.31) | collective-permute-done | bytes 67616 | tf_op jit(solution)/shard_map/ppermute | solution.py:61
  107.3 1.5 %columns.1 = (f32[24,2304]{1,0:T(8,128)}, f32[24,3072]{1,0:T(8,128)}, f32[1,24]{1,0:T(1,128)}, f32[1,24]{1,0:T(1,128)}, f32[1,24]{1,0:T(1,128)}, /*index=5*/f32[...) custom-call(s32[2]{0:T(128)S(1)} %pad_add_fusion.place, ...), custom_call_target="tpu_custom_call" | custom-call | flops 1000000000 | bytes 1000000 | tf_op jit(solution)/shard_map/columns/pallas_call | solution.py:521
  (84 shorter events, 8.0 us)
Async XLA Ops:
  3.3 0.9 copy-start
  4.2 6.8 %copy-start.6 = (bf16[96,768]{1,0:T(8,128)(2,1)S(1)}, bf16[96,768]{1,0:T(8,128)(2,1)}, u32[]{:S(2)}) copy-start(bf16[96,768]{1,0:T(8,128)(2,1)} %param.27) | copy-start | bytes 442372
  4.2 6.8 %copy-start.7 = (bf16[24,768]{1,0:T(8,128)(2,1)S(1)}, bf16[24,768]{1,0:T(8,128)(2,1)}, u32[]{:S(2)}) copy-start(bf16[24,768]{1,0:T(8,128)(2,1)} %param.23) | copy-start | bytes 110596
  4.2 10.1 %copy-start.3 = (bf16[128,768]{1,0:T(8,128)(2,1)S(1)}, bf16[128,768]{1,0:T(8,128)(2,1)}, u32[]{:S(2)}) copy-start(bf16[128,768]{1,0:T(8,128)(2,1)} %cot.3) | copy-start | bytes 589828
  5.1 14.8 %collective-permute-start.2 = (bf16[48,768]{1,0:T(8,128)(2,1)S(1)}, bf16[48,768]{1,0:T(8,128)(2,1)S(1)}, u32[]{:S(2)}, u32[]{:S(2)}) collective-permute-start(bf16[48,768]{1,0:T(8,128)(2,1)S(1)} %get-tuple-element.80), channel_id=1, source_target_pairs={{0,24},{8,16},{16,8},{24,0},{1,25},{9,17},{17,9},{25,1},{2,26},{10... | collective-permute-start | bytes 221192 | tf_op jit(solution)/shard_map/ppermute | solution.py:61
  10.2 13.5 %collective-permute-start = (bf16[176,768]{1,0:T(8,128)(2,1)S(1)}, bf16[176,768]{1,0:T(8,128)(2,1)S(1)}, u32[]{:S(2)}, u32[]{:S(2)}) collective-permute-start(bf16[176,768]{1,0:T(8,128)(2,1)S(1)} %get-tuple-element.78), channel_id=1, source_target_pairs={{0,8},{8,0},{16,24},{24,16},{1,9},{9,1},{17,25},{25,17},{2,10},{10... | collective-permute-start | bytes 811016 | tf_op jit(solution)/shard_map/ppermute | solution.py:61
  10.2 14.7 %collective-permute-start.1 = (bf16[176,768]{1,0:T(8,128)(2,1)S(1)}, bf16[176,768]{1,0:T(8,128)(2,1)S(1)}, u32[]{:S(2)}, u32[]{:S(2)}) collective-permute-start(bf16[176,768]{1,0:T(8,128)(2,1)S(1)} %get-tuple-element.79), channel_id=1, source_target_pairs={{0,16},{8,24},{16,0},{24,8},{1,17},{9,25},{17,1},{25,9},{2,18},{10... | collective-permute-start | bytes 811016 | tf_op jit(solution)/shard_map/ppermute | solution.py:61
  11.1 13.9 %collective-permute-start.5 = (bf16[128,768]{1,0:T(8,128)(2,1)S(1)}, bf16[128,768]{1,0:T(8,128)(2,1)S(1)}, u32[]{:S(2)}, u32[]{:S(2)}) collective-permute-start(bf16[128,768]{1,0:T(8,128)(2,1)S(1)} %maximum_maximum_fusion), channel_id=1, source_target_pairs={{0,2},{1,3},{2,0},{3,1},{4,6},{5,7},{6,4},{7,5},{8,10},{9,11},{10,... | collective-permute-start | bytes 589832 | tf_op jit(solution)/shard_map/ppermute | solution.py:594
  12.8 5.7 %collective-permute-start.4 = (bf16[128,768]{1,0:T(8,128)(2,1)S(1)}, bf16[128,768]{1,0:T(8,128)(2,1)S(1)}, u32[]{:S(2)}, u32[]{:S(2)}) collective-permute-start(bf16[128,768]{1,0:T(8,128)(2,1)S(1)} %maximum_maximum_fusion), channel_id=1, source_target_pairs={{0,1},{1,0},{2,3},{3,2},{4,5},{5,4},{6,7},{7,6},{8,9},{9,8},{10,11... | collective-permute-start | bytes 589832 | tf_op jit(solution)/shard_map/ppermute | solution.py:593
  18.5 6.6 %collective-permute-start.6 = (bf16[128,768]{1,0:T(8,128)(2,1)S(1)}, bf16[128,768]{1,0:T(8,128)(2,1)S(1)}, u32[]{:S(2)}, u32[]{:S(2)}) collective-permute-start(bf16[128,768]{1,0:T(8,128)(2,1)S(1)} %maximum_maximum_fusion), channel_id=1, source_target_pairs={{0,3},{1,2},{2,1},{3,0},{4,7},{5,6},{6,5},{7,4},{8,11},{9,10},{10,... | collective-permute-start | bytes 589832 | tf_op jit(solution)/shard_map/ppermute | solution.py:595
  25.1 9.1 %collective-permute-start.7 = (bf16[192,768]{1,0:T(8,128)(2,1)S(1)}, bf16[192,768]{1,0:T(8,128)(2,1)S(1)}, u32[]{:S(2)}, u32[]{:S(2)}) collective-permute-start(bf16[192,768]{1,0:T(8,128)(2,1)S(1)} %merge.1), channel_id=1, source_target_pairs={{0,1},{1,0},{2,3},{3,2},{4,5},{5,4},{6,7},{7,6},{8,9},{9,8},{10,11... | collective-permute-start | bytes 884744 | tf_op jit(solution)/shard_map/ppermute | solution.py:538
  26.7 13.2 %collective-permute-start.8 = (bf16[192,768]{1,0:T(8,128)(2,1)S(1)}, bf16[192,768]{1,0:T(8,128)(2,1)S(1)}, u32[]{:S(2)}, u32[]{:S(2)}) collective-permute-start(bf16[192,768]{1,0:T(8,128)(2,1)S(1)} %merge.1), channel_id=1, source_target_pairs={{0,2},{1,3},{2,0},{3,1},{4,6},{5,7},{6,4},{7,5},{8,10},{9,11},{10,... | collective-permute-start | bytes 884744 | tf_op jit(solution)/shard_map/ppermute | solution.py:538
  28.3 11.7 %copy-start.1 = (bf16[128,768]{1,0:T(8,128)(2,1)S(1)}, bf16[128,768]{1,0:T(8,128)(2,1)}, u32[]{:S(2)}) copy-start(bf16[128,768]{1,0:T(8,128)(2,1)} %tokens.7) | copy-start | bytes 589828
  28.3 15.1 %collective-permute-start.3 = (bf16[256,768]{1,0:T(8,128)(2,1)S(1)}, bf16[256,768]{1,0:T(8,128)(2,1)S(1)}, u32[]{:S(2)}, u32[]{:S(2)}) collective-permute-start(bf16[256,768]{1,0:T(8,128)(2,1)S(1)} %pad_maximum_fusion.1), channel_id=1, source_target_pairs={{0,24},{8,16},{16,8},{24,0},{1,25},{9,17},{17,9},{25,1},{2,26},{10... | collective-permute-start | bytes 1179656 | tf_op jit(solution)/shard_map/ppermute | solution.py:591
  30.8 9.1 %collective-permute-start.9 = (bf16[192,768]{1,0:T(8,128)(2,1)S(1)}, bf16[192,768]{1,0:T(8,128)(2,1)S(1)}, u32[]{:S(2)}, u32[]{:S(2)}) collective-permute-start(bf16[192,768]{1,0:T(8,128)(2,1)S(1)} %merge.1), channel_id=1, source_target_pairs={{0,3},{1,2},{2,1},{3,0},{4,7},{5,6},{6,5},{7,4},{8,11},{9,10},{10,... | collective-permute-start | bytes 884744 | tf_op jit(solution)/shard_map/ppermute | solution.py:538
  39.9 8.5 %collective-permute-start.10 = (bf16[768,768]{1,0:T(8,128)(2,1)S(1)}, bf16[768,768]{1,0:T(8,128)(2,1)S(1)}, u32[]{:S(2)}, u32[]{:S(2)}) collective-permute-start(bf16[768,768]{1,0:T(8,128)(2,1)S(1)} %constant_dynamic-update-slice_fusion.refs_0_), channel_id=1, source_target_pairs={{0,4},{4,0},{1,5},{5,1},{2,6},{6,2},{3,7},{7,3},{8,12},{12,8},{9,1... | collective-permute-start | bytes 3538952 | tf_op jit(solution)/shard_map/ppermute | solution.py:600
  42.9 1.1 %copy-start.4 = (bf16[768,768]{1,0:T(8,128)(2,1)}, bf16[768,768]{1,0:T(8,128)(2,1)S(1)}, u32[]{:S(2)}) copy-start(bf16[768,768]{1,0:T(8,128)(2,1)S(1)} %get-tuple-element.83.order) | copy-start | bytes 3538948
  42.9 12.7 %collective-permute-start.11 = (bf16[512,768]{1,0:T(8,128)(2,1)S(1)}, bf16[512,768]{1,0:T(8,128)(2,1)S(1)}, u32[]{:S(2)}, u32[]{:S(2)}) collective-permute-start(bf16[512,768]{1,0:T(8,128)(2,1)S(1)} %constant_dynamic-update-slice_fusion.4.refs_0_), channel_id=1, source_target_pairs={{0,4},{4,0},{1,5},{5,1},{2,6},{6,2},{3,7},{7,3},{8,12},{12,8},{9,1... | collective-permute-start | bytes 2359304 | tf_op jit(solution)/shard_map/ppermute | solution.py:632
  44.0 17.8 %collective-permute-start.16 = (bf16[128,768]{1,0:T(8,128)(2,1)S(1)}, bf16[128,768]{1,0:T(8,128)(2,1)S(1)}, u32[]{:S(2)}, u32[]{:S(2)}) collective-permute-start(bf16[128,768]{1,0:T(8,128)(2,1)S(1)} %copy-done.3), channel_id=1, source_target_pairs={{0,16},{8,24},{16,0},{24,8},{1,17},{9,25},{17,1},{25,9},{2,18},{10... | collective-permute-start | bytes 589832 | tf_op jit(solution)/shard_map/ppermute | solution.py:614
  48.4 13.4 %collective-permute-start.15 = (bf16[128,768]{1,0:T(8,128)(2,1)S(1)}, bf16[128,768]{1,0:T(8,128)(2,1)S(1)}, u32[]{:S(2)}, u32[]{:S(2)}) collective-permute-start(bf16[128,768]{1,0:T(8,128)(2,1)S(1)} %copy-done.3), channel_id=1, source_target_pairs={{0,8},{8,0},{16,24},{24,16},{1,9},{9,1},{17,25},{25,17},{2,10},{10... | collective-permute-start | bytes 589832 | tf_op jit(solution)/shard_map/ppermute | solution.py:613
  57.2 12.9 %collective-permute-start.12 = (bf16[128,768]{1,0:T(8,128)(2,1)S(1)}, bf16[128,768]{1,0:T(8,128)(2,1)S(1)}, u32[]{:S(2)}, u32[]{:S(2)}) collective-permute-start(bf16[128,768]{1,0:T(8,128)(2,1)S(1)} %get-tuple-element.93), channel_id=1, source_target_pairs={{0,8},{8,0},{16,24},{24,16},{1,9},{9,1},{17,25},{25,17},{2,10},{10... | collective-permute-start | bytes 589832 | tf_op jit(solution)/shard_map/ppermute | solution.py:61
  59.3 16.1 %collective-permute-start.13 = (bf16[128,768]{1,0:T(8,128)(2,1)S(1)}, bf16[128,768]{1,0:T(8,128)(2,1)S(1)}, u32[]{:S(2)}, u32[]{:S(2)}) collective-permute-start(bf16[128,768]{1,0:T(8,128)(2,1)S(1)} %get-tuple-element.94), channel_id=1, source_target_pairs={{0,16},{8,24},{16,0},{24,8},{1,17},{9,25},{17,1},{25,9},{2,18},{10... | collective-permute-start | bytes 589832 | tf_op jit(solution)/shard_map/ppermute | solution.py:61
  59.4 16.0 %collective-permute-start.14 = (bf16[128,768]{1,0:T(8,128)(2,1)S(1)}, bf16[128,768]{1,0:T(8,128)(2,1)S(1)}, u32[]{:S(2)}, u32[]{:S(2)}) collective-permute-start(bf16[128,768]{1,0:T(8,128)(2,1)S(1)} %get-tuple-element.95), channel_id=1, source_target_pairs={{0,24},{8,16},{16,8},{24,0},{1,25},{9,17},{17,9},{25,1},{2,26},{10... | collective-permute-start | bytes 589832 | tf_op jit(solution)/shard_map/ppermute | solution.py:61
  65.2 4.4 %collective-permute-start.17 = (bf16[896,768]{1,0:T(8,128)(2,1)S(1)}, bf16[896,768]{1,0:T(8,128)(2,1)S(1)}, u32[]{:S(2)}, u32[]{:S(2)}) collective-permute-start(bf16[896,768]{1,0:T(8,128)(2,1)S(1)} %get-tuple-element.112), channel_id=1, source_target_pairs={{0,4},{4,0},{1,5},{5,1},{2,6},{6,2},{3,7},{7,3},{8,12},{12,8},{9,1... | collective-permute-start | bytes 4128776 | tf_op jit(solution)/shard_map/ppermute | solution.py:542
  69.6 1.7 %copy-start.5 = (bf16[768,768]{1,0:T(8,128)(2,1)S(1)}, bf16[768,768]{1,0:T(8,128)(2,1)}, u32[]{:S(2)}) copy-start(bf16[768,768]{1,0:T(8,128)(2,1)} %copy-done.4) | copy-start | bytes 3538948
  70.1 6.8 %collective-permute-start.21 = (bf16[112,768]{1,0:T(8,128)(2,1)S(1)}, bf16[112,768]{1,0:T(8,128)(2,1)S(1)}, u32[]{:S(2)}, u32[]{:S(2)}) collective-permute-start(bf16[112,768]{1,0:T(8,128)(2,1)S(1)} %get-tuple-element.148), channel_id=1, source_target_pairs={{0,2},{1,3},{2,0},{3,1},{4,6},{5,7},{6,4},{7,5},{8,10},{9,11},{10,... | collective-permute-start | bytes 516104 | tf_op jit(solution)/shard_map/ppermute | solution.py:549
  70.8 6.5 %collective-permute-start.20 = (bf16[112,768]{1,0:T(8,128)(2,1)S(1)}, bf16[112,768]{1,0:T(8,128)(2,1)S(1)}, u32[]{:S(2)}, u32[]{:S(2)}) collective-permute-start(bf16[112,768]{1,0:T(8,128)(2,1)S(1)} %get-tuple-element.149), channel_id=1, source_target_pairs={{0,1},{1,0},{2,3},{3,2},{4,5},{5,4},{6,7},{7,6},{8,9},{9,8},{10,11... | collective-permute-start | bytes 516104 | tf_op jit(solution)/shard_map/ppermute | solution.py:548
  77.3 1.9 %collective-permute-start.22 = (bf16[384,640]{1,0:T(8,128)(2,1)S(1)}, bf16[384,640]{1,0:T(8,128)(2,1)S(1)}, u32[]{:S(2)}, u32[]{:S(2)}) collective-permute-start(bf16[384,640]{1,0:T(8,128)(2,1)S(1)} %get-tuple-element.126), channel_id=1, source_target_pairs={{0,4},{4,0},{1,5},{5,1},{2,6},{6,2},{3,7},{7,3},{8,12},{12,8},{9,1... | collective-permute-start | bytes 1474568 | tf_op jit(solution)/shard_map/ppermute | solution.py:542
  77.3 4.1 %copy-start.2 = (bf16[128,768]{1,0:T(8,128)(2,1)S(1)}, bf16[128,768]{1,0:T(8,128)(2,1)}, u32[]{:S(2)}) copy-start(bf16[128,768]{1,0:T(8,128)(2,1)} %tokens.7) | copy-start | bytes 589828
  77.3 14.8 %collective-permute-start.19 = (bf16[128,768]{1,0:T(8,128)(2,1)S(1)}, bf16[128,768]{1,0:T(8,128)(2,1)S(1)}, u32[]{:S(2)}, u32[]{:S(2)}) collective-permute-start(bf16[128,768]{1,0:T(8,128)(2,1)S(1)} %get-tuple-element.122), channel_id=1, source_target_pairs={{0,16},{8,24},{16,0},{24,8},{1,17},{9,25},{17,1},{25,9},{2,18},{10... | collective-permute-start | bytes 589832 | tf_op jit(solution)/shard_map/ppermute | solution.py:61
  79.3 5.4 %collective-permute-start.25 = (bf16[48,640]{1,0:T(8,128)(2,1)S(1)}, bf16[48,640]{1,0:T(8,128)(2,1)S(1)}, u32[]{:S(2)}, u32[]{:S(2)}) collective-permute-start(bf16[48,640]{1,0:T(8,128)(2,1)S(1)} %get-tuple-element.154), channel_id=1, source_target_pairs={{0,2},{1,3},{2,0},{3,1},{4,6},{5,7},{6,4},{7,5},{8,10},{9,11},{10,... | collective-permute-start | bytes 184328 | tf_op jit(solution)/shard_map/ppermute | solution.py:549
  80.8 4.2 %collective-permute-start.24 = (bf16[48,640]{1,0:T(8,128)(2,1)S(1)}, bf16[48,640]{1,0:T(8,128)(2,1)S(1)}, u32[]{:S(2)}, u32[]{:S(2)}) collective-permute-start(bf16[48,640]{1,0:T(8,128)(2,1)S(1)} %get-tuple-element.155), channel_id=1, source_target_pairs={{0,1},{1,0},{2,3},{3,2},{4,5},{5,4},{6,7},{7,6},{8,9},{9,8},{10,11... | collective-permute-start | bytes 184328 | tf_op jit(solution)/shard_map/ppermute | solution.py:548
  82.2 9.9 %collective-permute-start.18 = (bf16[128,768]{1,0:T(8,128)(2,1)S(1)}, bf16[128,768]{1,0:T(8,128)(2,1)S(1)}, u32[]{:S(2)}, u32[]{:S(2)}) collective-permute-start(bf16[128,768]{1,0:T(8,128)(2,1)S(1)} %get-tuple-element.120), channel_id=1, source_target_pairs={{0,8},{8,0},{16,24},{24,16},{1,9},{9,1},{17,25},{25,17},{2,10},{10... | collective-permute-start | bytes 589832 | tf_op jit(solution)/shard_map/ppermute | solution.py:61
  83.2 12.3 %collective-permute-start.23 = (bf16[128,768]{1,0:T(8,128)(2,1)S(1)}, bf16[128,768]{1,0:T(8,128)(2,1)S(1)}, u32[]{:S(2)}, u32[]{:S(2)}) collective-permute-start(bf16[128,768]{1,0:T(8,128)(2,1)S(1)} %get-tuple-element.127), channel_id=1, source_target_pairs={{0,24},{8,16},{16,8},{24,0},{1,25},{9,17},{17,9},{25,1},{2,26},{10... | collective-permute-start | bytes 589832 | tf_op jit(solution)/shard_map/ppermute | solution.py:61
  85.1 4.9 %collective-permute-start.29 = (bf16[96,640]{1,0:T(8,128)(2,1)S(1)}, bf16[96,640]{1,0:T(8,128)(2,1)S(1)}, u32[]{:S(2)}, u32[]{:S(2)}) collective-permute-start(bf16[96,640]{1,0:T(8,128)(2,1)S(1)} %pad_maximum_fusion.6), channel_id=1, source_target_pairs={{0,2},{1,3},{2,0},{3,1},{4,6},{5,7},{6,4},{7,5},{8,10},{9,11},{10,... | collective-permute-start | bytes 368648 | tf_op jit(solution)/shard_map/ppermute | solution.py:560
  85.8 4.9 %collective-permute-start.28 = (bf16[96,640]{1,0:T(8,128)(2,1)S(1)}, bf16[96,640]{1,0:T(8,128)(2,1)S(1)}, u32[]{:S(2)}, u32[]{:S(2)}) collective-permute-start(bf16[96,640]{1,0:T(8,128)(2,1)S(1)} %pad_maximum_fusion.5), channel_id=1, source_target_pairs={{0,1},{1,0},{2,3},{3,2},{4,5},{5,4},{6,7},{7,6},{8,9},{9,8},{10,11... | collective-permute-start | bytes 368648 | tf_op jit(solution)/shard_map/ppermute | solution.py:559
  90.0 8.1 %collective-permute-start.27 = (bf16[224,768]{1,0:T(8,128)(2,1)S(1)}, bf16[224,768]{1,0:T(8,128)(2,1)S(1)}, u32[]{:S(2)}, u32[]{:S(2)}) collective-permute-start(bf16[224,768]{1,0:T(8,128)(2,1)S(1)} %pad_maximum_fusion.3), channel_id=1, source_target_pairs={{0,2},{1,3},{2,0},{3,1},{4,6},{5,7},{6,4},{7,5},{8,10},{9,11},{10,... | collective-permute-start | bytes 1032200 | tf_op jit(solution)/shard_map/ppermute | solution.py:560
  90.7 7.9 %collective-permute-start.26 = (bf16[224,768]{1,0:T(8,128)(2,1)S(1)}, bf16[224,768]{1,0:T(8,128)(2,1)S(1)}, u32[]{:S(2)}, u32[]{:S(2)}) collective-permute-start(bf16[224,768]{1,0:T(8,128)(2,1)S(1)} %pad_maximum_fusion.2), channel_id=1, source_target_pairs={{0,1},{1,0},{2,3},{3,2},{4,5},{5,4},{6,7},{7,6},{8,9},{9,8},{10,11... | collective-permute-start | bytes 1032200 | tf_op jit(solution)/shard_map/ppermute | solution.py:559
  98.9 6.8 %collective-permute-start.32 = (bf16[24,1408]{1,0:T(8,128)(2,1)S(1)}, bf16[24,1408]{1,0:T(8,128)(2,1)S(1)}, u32[]{:S(2)}, u32[]{:S(2)}) collective-permute-start(bf16[24,1408]{1,0:T(8,128)(2,1)S(1)} %get-tuple-element.156), channel_id=1, source_target_pairs={{0,24},{8,16},{16,8},{24,0},{1,25},{9,17},{17,9},{25,1},{2,26},{10... | collective-permute-start | bytes 202760 | tf_op jit(solution)/shard_map/ppermute | solution.py:61
  101.9 5.4 %collective-permute-start.31 = (bf16[24,1408]{1,0:T(8,128)(2,1)S(1)}, bf16[24,1408]{1,0:T(8,128)(2,1)S(1)}, u32[]{:S(2)}, u32[]{:S(2)}) collective-permute-start(bf16[24,1408]{1,0:T(8,128)(2,1)S(1)} %get-tuple-element.157), channel_id=1, source_target_pairs={{0,16},{8,24},{16,0},{24,8},{1,17},{9,25},{17,1},{25,9},{2,18},{10... | collective-permute-start | bytes 202760 | tf_op jit(solution)/shard_map/ppermute | solution.py:61
  102.3 5.0 %collective-permute-start.30 = (bf16[24,1408]{1,0:T(8,128)(2,1)S(1)}, bf16[24,1408]{1,0:T(8,128)(2,1)S(1)}, u32[]{:S(2)}, u32[]{:S(2)}) collective-permute-start(bf16[24,1408]{1,0:T(8,128)(2,1)S(1)} %get-tuple-element.158), channel_id=1, source_target_pairs={{0,8},{8,0},{16,24},{24,16},{1,9},{9,1},{17,25},{25,17},{2,10},{10... | collective-permute-start | bytes 202760 | tf_op jit(solution)/shard_map/ppermute | solution.py:61

commit v6 on v5

--- a/solution.py
+++ b/solution.py
@@ -674,7 +674,7 @@
     arrived = exchange_t(back)
     tail_sum = after(tail_sum, low_sum)
     (output,) = call(
-        output_kernel, "output", [(block, BF)], *out, tokens, after(lives, col_keep), gains,
+        output_kernel, "output", [(block, BF)], *out, tokens, after(lives, low_sum), gains,
         weight=10,
     )
     (grad_tokens,) = call(

time: 109 us -> 112 us (1.028)
  starting transfers between devices: 42.9 us -> 44.7 us
    ppermute x12, waiting for transfers between devices: 11.4 us -> 13 us  [exchange_t(): lax.ppermute(pieces[k], 't', xor_pairs(TP, k))]
    ppermute x2, waiting for transfers between devices: 3.98 us -> 2.36 us  [plane_last(): two = lax.ppermute(two.astype(BF), 'fsdp', xor_pairs(4, 2))]
    ppermute x12, starting transfers between devices: 18.5 us -> 19.9 us  [exchange_t(): lax.ppermute(pieces[k], 't', xor_pairs(TP, k))]
    ppermute x2, waiting for transfers between devices: 0.57 us -> 1.86 us  [plane_pair(): return keep + lax.ppermute(send, 'dq', xor_pairs(2, 1)).astype(F32)]
  transfers between devices with their start and end apart: 33 -> 33, of which waited for: 19 -> 15; matrix products, arithmetic and copies ran while one was open for 3% -> 2% of each run, Pallas kernels for 24% -> 23%
where the time goes in v6:
time: 112 us
  starting transfers between devices  44.7 us (40%)
  waiting for transfers between devices  31.2 us (28%)
  Pallas kernels  28.1 us (25%)
  local copies, waits for them, and re-layouts  3.52 us (3%)
  other arithmetic  2.97 us (3%)
  between operations  1.19 us (1%)
    pallas_call x12, Pallas kernels, call(): pl.pallas_call(kernel, name=name, out_shape=shapes, in_specs=space, out_s...  28.1 us
    ppermute x12, starting transfers between devices, exchange_t(): lax.ppermute(pieces[k], 't', xor_pairs(TP, k))  19.9 us
    ppermute x12, waiting for transfers between devices, exchange_t(): lax.ppermute(pieces[k], 't', xor_pairs(TP, k))  13 us
    ppermute x3, waiting for transfers between devices, xor_permutes(): return [lax.ppermute(block, axis, xor_pairs(count, k)) for k in range(1, 4)]  7.29 us
    ppermute x3, starting transfers between devices, xor_permutes(): return [lax.ppermute(block, axis, xor_pairs(count, k)) for k in range(1, 4)]  4.92 us
    ppermute x1, starting transfers between devices, plane_local(): cot_two = lax.ppermute(after(cotangent, xhat_last), 't', xor_pairs(TP, 2))  4.42 us
    ppermute x1, waiting for transfers between devices, plane_local(): tail_one = lax.ppermute(tail, 'fsdp', xor_pairs(4, 1))  4.12 us
    ppermute x2, starting transfers between devices, plane_last(): one = lax.ppermute(one.astype(BF), 'fsdp', xor_pairs(4, 1))  3.04 us
  transfers between devices with their start and end apart: 33, of which 15 were waited for; matrix products, arithmetic and copies ran while one was open for 2% of the time, Pallas kernels for 23%

profile of v6, /device:TPU:0, one launch (start us, length us, event | category | flops | bytes accessed | tf_op | source)
XLA Modules:
  0.0 111.6 jit_solution(12608982237280478170)
XLA Ops:
  0.7 0.7 convert_element_type.53
  1.3 0.9 concatenate.69
  2.3 1.0 pad_maximum_fusion.4.weights
  3.3 0.9 copy-done.1
  4.2 0.9 prepare.1
  5.1 5.1 %collective-permute-start.2 = (bf16[48,768]{1,0:T(8,128)(2,1)S(1)}, bf16[48,768]{1,0:T(8,128)(2,1)S(1)}, u32[]{:S(2)}, u32[]{:S(2)}) collective-permute-start(bf16[48,768]{1,0:T(8,128)(2,1)S(1)} %get-tuple-element.80), channel_id=1, source_target_pairs={{0,24},{8,16},{16,8},{24,0},{1,25},{9,17},{17,9},{25,1},{2,26},{10... | collective-permute-start | bytes 221192 | tf_op jit(solution)/shard_map/ppermute | solution.py:61
  10.2 0.6 collective-permute-start.1
  11.1 1.7 %collective-permute-start.5 = (bf16[128,768]{1,0:T(8,128)(2,1)S(1)}, bf16[128,768]{1,0:T(8,128)(2,1)S(1)}, u32[]{:S(2)}, u32[]{:S(2)}) collective-permute-start(bf16[128,768]{1,0:T(8,128)(2,1)S(1)} %maximum_maximum_fusion), channel_id=1, source_target_pairs={{0,2},{1,3},{2,0},{3,1},{4,6},{5,7},{6,4},{7,5},{8,10},{9,11},{10,... | collective-permute-start | bytes 589832 | tf_op jit(solution)/shard_map/ppermute | solution.py:594
  12.8 1.5 %collective-permute-start.4 = (bf16[128,768]{1,0:T(8,128)(2,1)S(1)}, bf16[128,768]{1,0:T(8,128)(2,1)S(1)}, u32[]{:S(2)}, u32[]{:S(2)}) collective-permute-start(bf16[128,768]{1,0:T(8,128)(2,1)S(1)} %maximum_maximum_fusion), channel_id=1, source_target_pairs={{0,1},{1,0},{2,3},{3,2},{4,5},{5,4},{6,7},{7,6},{8,9},{9,8},{10,11... | collective-permute-start | bytes 589832 | tf_op jit(solution)/shard_map/ppermute | solution.py:593
  14.4 4.1 %collective-permute-done.4 = bf16[128,768]{1,0:T(8,128)(2,1)S(1)} collective-permute-done((bf16[128,768]{1,0:T(8,128)(2,1)S(1)}, bf16[128,768]{1,0:T(8,128)(2,1)S(1)}, u32[]{:S(2)}, u32[]{:S(2)}) %collective-permute-start.4) | collective-permute-done | bytes 196640 | tf_op jit(solution)/shard_map/ppermute | solution.py:593
  18.5 1.4 %collective-permute-start.6 = (bf16[128,768]{1,0:T(8,128)(2,1)S(1)}, bf16[128,768]{1,0:T(8,128)(2,1)S(1)}, u32[]{:S(2)}, u32[]{:S(2)}) collective-permute-start(bf16[128,768]{1,0:T(8,128)(2,1)S(1)} %maximum_maximum_fusion), channel_id=1, source_target_pairs={{0,3},{1,2},{2,1},{3,0},{4,7},{5,6},{6,5},{7,4},{8,11},{9,10},{10,... | collective-permute-start | bytes 589832 | tf_op jit(solution)/shard_map/ppermute | solution.py:595
  19.9 3.8 %collective-permute-done.one = bf16[176,768]{1,0:T(8,128)(2,1)S(1)} collective-permute-done((bf16[176,768]{1,0:T(8,128)(2,1)S(1)}, bf16[176,768]{1,0:T(8,128)(2,1)S(1)}, u32[]{:S(2)}, u32[]{:S(2)}) %collective-permute-start) | collective-permute-done | bytes 270368 | tf_op jit(solution)/shard_map/ppermute | solution.py:61
  23.7 1.2 %collective-permute-done.1.two = bf16[176,768]{1,0:T(8,128)(2,1)S(1)} collective-permute-done((bf16[176,768]{1,0:T(8,128)(2,1)S(1)}, bf16[176,768]{1,0:T(8,128)(2,1)S(1)}, u32[]{:S(2)}, u32[]{:S(2)}) %collective-permute-start.1) | collective-permute-done | bytes 270368 | tf_op jit(solution)/shard_map/ppermute | solution.py:61
  25.1 1.6 %collective-permute-start.7 = (bf16[192,768]{1,0:T(8,128)(2,1)S(1)}, bf16[192,768]{1,0:T(8,128)(2,1)S(1)}, u32[]{:S(2)}, u32[]{:S(2)}) collective-permute-start(bf16[192,768]{1,0:T(8,128)(2,1)S(1)} %merge.1), channel_id=1, source_target_pairs={{0,1},{1,0},{2,3},{3,2},{4,5},{5,4},{6,7},{7,6},{8,9},{9,8},{10,11... | collective-permute-start | bytes 884744 | tf_op jit(solution)/shard_map/ppermute | solution.py:538
  26.7 1.6 %collective-permute-start.8 = (bf16[192,768]{1,0:T(8,128)(2,1)S(1)}, bf16[192,768]{1,0:T(8,128)(2,1)S(1)}, u32[]{:S(2)}, u32[]{:S(2)}) collective-permute-start(bf16[192,768]{1,0:T(8,128)(2,1)S(1)} %merge.1), channel_id=1, source_target_pairs={{0,2},{1,3},{2,0},{3,1},{4,6},{5,7},{6,4},{7,5},{8,10},{9,11},{10,... | collective-permute-start | bytes 884744 | tf_op jit(solution)/shard_map/ppermute | solution.py:538
  28.3 2.5 %collective-permute-start.3 = (bf16[256,768]{1,0:T(8,128)(2,1)S(1)}, bf16[256,768]{1,0:T(8,128)(2,1)S(1)}, u32[]{:S(2)}, u32[]{:S(2)}) collective-permute-start(bf16[256,768]{1,0:T(8,128)(2,1)S(1)} %pad_maximum_fusion.1), channel_id=1, source_target_pairs={{0,24},{8,16},{16,8},{24,0},{1,25},{9,17},{17,9},{25,1},{2,26},{10... | collective-permute-start | bytes 1179656 | tf_op jit(solution)/shard_map/ppermute | solution.py:591
  30.8 1.7 %collective-permute-start.9 = (bf16[192,768]{1,0:T(8,128)(2,1)S(1)}, bf16[192,768]{1,0:T(8,128)(2,1)S(1)}, u32[]{:S(2)}, u32[]{:S(2)}) collective-permute-start(bf16[192,768]{1,0:T(8,128)(2,1)S(1)} %merge.1), channel_id=1, source_target_pairs={{0,3},{1,2},{2,1},{3,0},{4,7},{5,6},{6,5},{7,4},{8,11},{9,10},{10,... | collective-permute-start | bytes 884744 | tf_op jit(solution)/shard_map/ppermute | solution.py:538
  32.5 1.6 %collective-permute-done.7 = bf16[192,768]{1,0:T(8,128)(2,1)S(1)} collective-permute-done((bf16[192,768]{1,0:T(8,128)(2,1)S(1)}, bf16[192,768]{1,0:T(8,128)(2,1)S(1)}, u32[]{:S(2)}, u32[]{:S(2)}) %collective-permute-start.7) | collective-permute-done | bytes 294944 | tf_op jit(solution)/shard_map/ppermute | solution.py:538
  34.2 5.6 %collective-permute-done.8 = bf16[192,768]{1,0:T(8,128)(2,1)S(1)} collective-permute-done((bf16[192,768]{1,0:T(8,128)(2,1)S(1)}, bf16[192,768]{1,0:T(8,128)(2,1)S(1)}, u32[]{:S(2)}, u32[]{:S(2)}) %collective-permute-start.8) | collective-permute-done | bytes 294944 | tf_op jit(solution)/shard_map/ppermute | solution.py:538
  40.0 2.8 %early.1 = (f32[384,768]{1,0:T(8,128)S(1)}, bf16[768,768]{1,0:T(8,128)(2,1)S(1)}, f32[512,128]{1,0:T(8,128)S(1)}, f32[512,128]{1,0:T(8,128)S(1)}, f32[512,128]{1,0:T(8,128)S(1)}, /*index=5*/f32[512,1]{1,0:T(8,128)S(1)}) custom-call(s32[2]{0:T(128)S(1)} %pad_add_fusion.place, bf16[48,768]{1,0:T(8,128)(2,1)S(1)} %get-tuple-element.77.zero, ...), custom_call_target="tpu_custom_call" | custom-call | flops 10000000000 | bytes 10000000 | tf_op jit(solution)/shard_map/early/pallas_call | solution.py:521
  44.0 4.4 %collective-permute-start.16 = (bf16[128,768]{1,0:T(8,128)(2,1)S(1)}, bf16[128,768]{1,0:T(8,128)(2,1)S(1)}, u32[]{:S(2)}, u32[]{:S(2)}) collective-permute-start(bf16[128,768]{1,0:T(8,128)(2,1)S(1)} %copy-done), channel_id=1, source_target_pairs={{0,16},{8,24},{16,0},{24,8},{1,17},{9,25},{17,1},{25,9},{2,18},{10... | collective-permute-start | bytes 589832 | tf_op jit(solution)/shard_map/ppermute | solution.py:614
  48.4 7.2 %forward.1 = (bf16[768,768]{1,0:T(8,128)(2,1)S(1)}, bf16[768,640]{1,0:T(8,128)(2,1)S(1)}, bf16[512,768]{1,0:T(8,128)(2,1)S(1)}, bf16[512,768]{1,0:T(8,128)(2,1)S...) custom-call(s32[2]{0:T(128)S(1)} %pad_add_fusion.place, ...), custom_call_target="tpu_custom_call" | custom-call | flops 99999997952 | bytes 100000000 | tf_op jit(solution)/shard_map/forward/pallas_call | solution.py:521
  55.6 1.6 %share.1 = (bf16[768,768]{1,0:T(8,128)(2,1)S(1)}, bf16[256,768]{1,0:T(8,128)(2,1)S(1)}, f32[128,768]{1,0:T(8,128)S(1)}, bf16[128,768]{1,0:T(8,128)(2,1)S(1)}, bf...) custom-call(s32[2]{0:T(128)S(1)} %pad_add_fusion.place, bf16[512,768]{1,0:T(8,128)(2,1)S(1)} %get-tuple-element.90.act.refs_6_, ...), custom_call_target="tpu_custom_call" | custom-call | flops 10000000000 | bytes 10000000 | tf_op jit(solution)/shard_map/share/pallas_call | solution.py:521
  57.2 2.1 %collective-permute-start.12 = (bf16[128,768]{1,0:T(8,128)(2,1)S(1)}, bf16[128,768]{1,0:T(8,128)(2,1)S(1)}, u32[]{:S(2)}, u32[]{:S(2)}) collective-permute-start(bf16[128,768]{1,0:T(8,128)(2,1)S(1)} %get-tuple-element.93), channel_id=1, source_target_pairs={{0,8},{8,0},{16,24},{24,16},{1,9},{9,1},{17,25},{25,17},{2,10},{10... | collective-permute-start | bytes 589832 | tf_op jit(solution)/shard_map/ppermute | solution.py:61
  59.4 2.4 %collective-permute-start.14 = (bf16[128,768]{1,0:T(8,128)(2,1)S(1)}, bf16[128,768]{1,0:T(8,128)(2,1)S(1)}, u32[]{:S(2)}, u32[]{:S(2)}) collective-permute-start(bf16[128,768]{1,0:T(8,128)(2,1)S(1)} %get-tuple-element.95), channel_id=1, source_target_pairs={{0,24},{8,16},{16,8},{24,0},{1,25},{9,17},{17,9},{25,1},{2,26},{10... | collective-permute-start | bytes 589832 | tf_op jit(solution)/shard_map/ppermute | solution.py:61
  61.8 3.4 %upstream.1 = (bf16[512,768]{1,0:T(8,128)(2,1)S(1)}, bf16[512,192]{1,0:T(8,128)(2,1)S(1)}, f32[896,768]{1,0:T(8,128)S(1)}, bf16[896,768]{1,0:T(8,128)(2,1)S(1)}) custom-call(s32[2]{0:T(128)S(1)} %pad_add_fusion.place, bf16[128,768]{1,0:T(8,128)(2,1)S(1)} %copy-done, bf16[128,768]{1,0:T(8,128)(2,1)S(1)} %collective-permute-done.15.refs_1_, ...), custom_call_target="tpu_custom_call" | custom-call | flops 40000000000 | bytes 40000000 | tf_op jit(solution)/shard_map/upstream/pallas_call | solution.py:521
  65.3 4.3 %attention.1.d_qkv = bf16[512,576]{1,0:T(8,128)(2,1)S(1)} custom-call(bf16[512,192]{1,0:T(8,128)(2,1)S(1)} %get-tuple-element.108.q_low, bf16[512,192]{1,0:T(8,128)(2,1)S(1)} %get-tuple-element.109.k_low, bf16[512,192]{1,0:T(8,128)(2,1)S(1)} %get-tuple-element.110.v_low, f32[12,128,128]{2,1,0:T(8,128)S(1)} %get-tuple-element.111.probs, ...), custom_call_target="tpu_custom_call" | custom-call | flops 49999998976 | bytes 50000000 | tf_op jit(solution)/shard_map/attention/pallas_call | solution.py:521
  70.1 0.7 collective-permute-start.19
  71.3 3.8 %backward.1 = (f32[128,768]{1,0:T(8,128)S(1)}, bf16[128,768]{1,0:T(8,128)(2,1)S(1)}, bf16[128,768]{1,0:T(8,128)(2,1)S(1)}, bf16[128,768]{1,0:T(8,128)(2,1)S(1)},...) custom-call(s32[2]{0:T(128)S(1)} %pad_add_fusion.place, f32[384,768]{1,0:T(8,128)S(1)} %get-tuple-element.81.xhat, ...), custom_call_target="tpu_custom_call" | custom-call | flops 40000000000 | bytes 40000000 | tf_op jit(solution)/shard_map/backward/pallas_call | solution.py:521
  75.4 1.6 %collective-permute-done.19 = bf16[112,768]{1,0:T(8,128)(2,1)S(1)} collective-permute-done((bf16[112,768]{1,0:T(8,128)(2,1)S(1)}, bf16[112,768]{1,0:T(8,128)(2,1)S(1)}, u32[]{:S(2)}, u32[]{:S(2)}) %collective-permute-start.19) | collective-permute-done | bytes 172064 | tf_op jit(solution)/shard_map/ppermute | solution.py:549
  77.3 1.9 %collective-permute-done.20 = bf16[384,640]{1,0:T(8,128)(2,1)S(1)} collective-permute-done((bf16[384,640]{1,0:T(8,128)(2,1)S(1)}, bf16[384,640]{1,0:T(8,128)(2,1)S(1)}, u32[]{:S(2)}, u32[]{:S(2)}) %collective-permute-start.20) | collective-permute-done | bytes 491552 | tf_op jit(solution)/shard_map/ppermute | solution.py:542
  79.3 1.5 %collective-permute-start.22 = (bf16[48,640]{1,0:T(8,128)(2,1)S(1)}, bf16[48,640]{1,0:T(8,128)(2,1)S(1)}, u32[]{:S(2)}, u32[]{:S(2)}) collective-permute-start(bf16[48,640]{1,0:T(8,128)(2,1)S(1)} %get-tuple-element.154), channel_id=1, source_target_pairs={{0,2},{1,3},{2,0},{3,1},{4,6},{5,7},{6,4},{7,5},{8,10},{9,11},{10,... | collective-permute-start | bytes 184328 | tf_op jit(solution)/shard_map/ppermute | solution.py:549
  81.3 0.9 collective-permute-start.28
  82.2 1.2 %collective-permute-start.27 = (bf16[128,768]{1,0:T(8,128)(2,1)S(1)}, bf16[128,768]{1,0:T(8,128)(2,1)S(1)}, u32[]{:S(2)}, u32[]{:S(2)}) collective-permute-start(bf16[128,768]{1,0:T(8,128)(2,1)S(1)} %get-tuple-element.123), channel_id=1, source_target_pairs={{0,8},{8,0},{16,24},{24,16},{1,9},{9,1},{17,25},{25,17},{2,10},{10... | collective-permute-start | bytes 589832 | tf_op jit(solution)/shard_map/ppermute | solution.py:61
  83.4 2.4 %collective-permute-start.29 = (bf16[128,768]{1,0:T(8,128)(2,1)S(1)}, bf16[128,768]{1,0:T(8,128)(2,1)S(1)}, u32[]{:S(2)}, u32[]{:S(2)}) collective-permute-start(bf16[128,768]{1,0:T(8,128)(2,1)S(1)} %get-tuple-element.128), channel_id=1, source_target_pairs={{0,24},{8,16},{16,8},{24,0},{1,25},{9,17},{17,9},{25,1},{2,26},{10... | collective-permute-start | bytes 589832 | tf_op jit(solution)/shard_map/ppermute | solution.py:61
  85.8 0.7 collective-permute-start.26
  86.5 1.6 %collective-permute-start.25 = (bf16[96,640]{1,0:T(8,128)(2,1)S(1)}, bf16[96,640]{1,0:T(8,128)(2,1)S(1)}, u32[]{:S(2)}, u32[]{:S(2)}) collective-permute-start(bf16[96,640]{1,0:T(8,128)(2,1)S(1)} %pad_maximum_fusion.5), channel_id=1, source_target_pairs={{0,1},{1,0},{2,3},{3,2},{4,5},{5,4},{6,7},{7,6},{8,9},{9,8},{10,11... | collective-permute-start | bytes 368648 | tf_op jit(solution)/shard_map/ppermute | solution.py:559
  88.4 2.4 %collective-permute-done.26 = bf16[96,640]{1,0:T(8,128)(2,1)S(1)} collective-permute-done((bf16[96,640]{1,0:T(8,128)(2,1)S(1)}, bf16[96,640]{1,0:T(8,128)(2,1)S(1)}, u32[]{:S(2)}, u32[]{:S(2)}) %collective-permute-start.26) | collective-permute-done | bytes 122912 | tf_op jit(solution)/shard_map/ppermute | solution.py:560
  91.4 1.5 %collective-permute-start.23 = (bf16[224,768]{1,0:T(8,128)(2,1)S(1)}, bf16[224,768]{1,0:T(8,128)(2,1)S(1)}, u32[]{:S(2)}, u32[]{:S(2)}) collective-permute-start(bf16[224,768]{1,0:T(8,128)(2,1)S(1)} %pad_maximum_fusion.2), channel_id=1, source_target_pairs={{0,1},{1,0},{2,3},{3,2},{4,5},{5,4},{6,7},{7,6},{8,9},{9,8},{10,11... | collective-permute-start | bytes 1032200 | tf_op jit(solution)/shard_map/ppermute | solution.py:559
  93.0 4.7 %collective-permute-done.28.two = bf16[128,768]{1,0:T(8,128)(2,1)S(1)} collective-permute-done((bf16[128,768]{1,0:T(8,128)(2,1)S(1)}, bf16[128,768]{1,0:T(8,128)(2,1)S(1)}, u32[]{:S(2)}, u32[]{:S(2)}) %collective-permute-start.28) | collective-permute-done | bytes 196640 | tf_op jit(solution)/shard_map/ppermute | solution.py:61
  97.7 1.2 %input_gradient.1 = f32[128,768]{1,0:T(8,128)} custom-call(f32[128,768]{1,0:T(8,128)S(1)} %get-tuple-element.121.zero, bf16[128,768]{1,0:T(8,128)(2,1)S(1)} %collective-permute-done.27.one, bf16[128,768]{1,0:T(8,128)(2,1)S(1)} %collective-permute-done.28.two, bf16[128,768]{1,0:T(8,128)(2,1)S(1)} %collective-permute-done.29.three, ...), custom_call_target="tpu_custom_call" | custom-call | flops 10000000000 | bytes 10000000 | tf_op jit(solution)/shard_map/input_gradient/pallas_call | solution.py:521
  99.5 1.5 %collective-permute-start.32 = (bf16[24,1408]{1,0:T(8,128)(2,1)S(1)}, bf16[24,1408]{1,0:T(8,128)(2,1)S(1)}, u32[]{:S(2)}, u32[]{:S(2)}) collective-permute-start(bf16[24,1408]{1,0:T(8,128)(2,1)S(1)} %get-tuple-element.156), channel_id=1, source_target_pairs={{0,24},{8,16},{16,8},{24,0},{1,25},{9,17},{17,9},{25,1},{2,26},{10... | collective-permute-start | bytes 202760 | tf_op jit(solution)/shard_map/ppermute | solution.py:61
  101.0 3.7 %collective-permute-start.31 = (bf16[24,1408]{1,0:T(8,128)(2,1)S(1)}, bf16[24,1408]{1,0:T(8,128)(2,1)S(1)}, u32[]{:S(2)}, u32[]{:S(2)}) collective-permute-start(bf16[24,1408]{1,0:T(8,128)(2,1)S(1)} %get-tuple-element.157), channel_id=1, source_target_pairs={{0,16},{8,24},{16,0},{24,8},{1,17},{9,25},{17,1},{25,9},{2,18},{10... | collective-permute-start | bytes 202760 | tf_op jit(solution)/shard_map/ppermute | solution.py:61
  104.7 0.8 output.1
  105.6 0.6 slice.106
  106.2 0.7 slice.107
  106.9 3.0 %collective-permute-done.31.two = bf16[24,1408]{1,0:T(8,128)(2,1)S(1)} collective-permute-done((bf16[24,1408]{1,0:T(8,128)(2,1)S(1)}, bf16[24,1408]{1,0:T(8,128)(2,1)S(1)}, u32[]{:S(2)}, u32[]{:S(2)}) %collective-permute-start.31) | collective-permute-done | bytes 67616 | tf_op jit(solution)/shard_map/ppermute | solution.py:61
  110.0 1.5 %columns.1 = (f32[24,2304]{1,0:T(8,128)}, f32[24,3072]{1,0:T(8,128)}, f32[1,24]{1,0:T(1,128)}, f32[1,24]{1,0:T(1,128)}, f32[1,24]{1,0:T(1,128)}, /*index=5*/f32[...) custom-call(s32[2]{0:T(128)S(1)} %pad_add_fusion.place, ...), custom_call_target="tpu_custom_call" | custom-call | flops 1000000000 | bytes 1000000 | tf_op jit(solution)/shard_map/columns/pallas_call | solution.py:521
  (84 shorter events, 5.9 us)
Async XLA Ops:
  3.3 0.9 copy-start.1
  4.2 6.8 %copy-start.6 = (bf16[96,768]{1,0:T(8,128)(2,1)S(1)}, bf16[96,768]{1,0:T(8,128)(2,1)}, u32[]{:S(2)}) copy-start(bf16[96,768]{1,0:T(8,128)(2,1)} %param.27) | copy-start | bytes 442372
  4.2 6.8 %copy-start.7 = (bf16[24,768]{1,0:T(8,128)(2,1)S(1)}, bf16[24,768]{1,0:T(8,128)(2,1)}, u32[]{:S(2)}) copy-start(bf16[24,768]{1,0:T(8,128)(2,1)} %param.23) | copy-start | bytes 110596
  4.2 10.1 %copy-start = (bf16[128,768]{1,0:T(8,128)(2,1)S(1)}, bf16[128,768]{1,0:T(8,128)(2,1)}, u32[]{:S(2)}) copy-start(bf16[128,768]{1,0:T(8,128)(2,1)} %cot.3) | copy-start | bytes 589828
  5.1 14.8 %collective-permute-start.2 = (bf16[48,768]{1,0:T(8,128)(2,1)S(1)}, bf16[48,768]{1,0:T(8,128)(2,1)S(1)}, u32[]{:S(2)}, u32[]{:S(2)}) collective-permute-start(bf16[48,768]{1,0:T(8,128)(2,1)S(1)} %get-tuple-element.80), channel_id=1, source_target_pairs={{0,24},{8,16},{16,8},{24,0},{1,25},{9,17},{17,9},{25,1},{2,26},{10... | collective-permute-start | bytes 221192 | tf_op jit(solution)/shard_map/ppermute | solution.py:61
  10.2 13.5 %collective-permute-start = (bf16[176,768]{1,0:T(8,128)(2,1)S(1)}, bf16[176,768]{1,0:T(8,128)(2,1)S(1)}, u32[]{:S(2)}, u32[]{:S(2)}) collective-permute-start(bf16[176,768]{1,0:T(8,128)(2,1)S(1)} %get-tuple-element.78), channel_id=1, source_target_pairs={{0,8},{8,0},{16,24},{24,16},{1,9},{9,1},{17,25},{25,17},{2,10},{10... | collective-permute-start | bytes 811016 | tf_op jit(solution)/shard_map/ppermute | solution.py:61
  10.2 14.7 %collective-permute-start.1 = (bf16[176,768]{1,0:T(8,128)(2,1)S(1)}, bf16[176,768]{1,0:T(8,128)(2,1)S(1)}, u32[]{:S(2)}, u32[]{:S(2)}) collective-permute-start(bf16[176,768]{1,0:T(8,128)(2,1)S(1)} %get-tuple-element.79), channel_id=1, source_target_pairs={{0,16},{8,24},{16,0},{24,8},{1,17},{9,25},{17,1},{25,9},{2,18},{10... | collective-permute-start | bytes 811016 | tf_op jit(solution)/shard_map/ppermute | solution.py:61
  11.1 13.9 %collective-permute-start.5 = (bf16[128,768]{1,0:T(8,128)(2,1)S(1)}, bf16[128,768]{1,0:T(8,128)(2,1)S(1)}, u32[]{:S(2)}, u32[]{:S(2)}) collective-permute-start(bf16[128,768]{1,0:T(8,128)(2,1)S(1)} %maximum_maximum_fusion), channel_id=1, source_target_pairs={{0,2},{1,3},{2,0},{3,1},{4,6},{5,7},{6,4},{7,5},{8,10},{9,11},{10,... | collective-permute-start | bytes 589832 | tf_op jit(solution)/shard_map/ppermute | solution.py:594
  12.8 5.7 %collective-permute-start.4 = (bf16[128,768]{1,0:T(8,128)(2,1)S(1)}, bf16[128,768]{1,0:T(8,128)(2,1)S(1)}, u32[]{:S(2)}, u32[]{:S(2)}) collective-permute-start(bf16[128,768]{1,0:T(8,128)(2,1)S(1)} %maximum_maximum_fusion), channel_id=1, source_target_pairs={{0,1},{1,0},{2,3},{3,2},{4,5},{5,4},{6,7},{7,6},{8,9},{9,8},{10,11... | collective-permute-start | bytes 589832 | tf_op jit(solution)/shard_map/ppermute | solution.py:593
  18.5 6.6 %collective-permute-start.6 = (bf16[128,768]{1,0:T(8,128)(2,1)S(1)}, bf16[128,768]{1,0:T(8,128)(2,1)S(1)}, u32[]{:S(2)}, u32[]{:S(2)}) collective-permute-start(bf16[128,768]{1,0:T(8,128)(2,1)S(1)} %maximum_maximum_fusion), channel_id=1, source_target_pairs={{0,3},{1,2},{2,1},{3,0},{4,7},{5,6},{6,5},{7,4},{8,11},{9,10},{10,... | collective-permute-start | bytes 589832 | tf_op jit(solution)/shard_map/ppermute | solution.py:595
  25.1 9.1 %collective-permute-start.7 = (bf16[192,768]{1,0:T(8,128)(2,1)S(1)}, bf16[192,768]{1,0:T(8,128)(2,1)S(1)}, u32[]{:S(2)}, u32[]{:S(2)}) collective-permute-start(bf16[192,768]{1,0:T(8,128)(2,1)S(1)} %merge.1), channel_id=1, source_target_pairs={{0,1},{1,0},{2,3},{3,2},{4,5},{5,4},{6,7},{7,6},{8,9},{9,8},{10,11... | collective-permute-start | bytes 884744 | tf_op jit(solution)/shard_map/ppermute | solution.py:538
  26.7 13.2 %collective-permute-start.8 = (bf16[192,768]{1,0:T(8,128)(2,1)S(1)}, bf16[192,768]{1,0:T(8,128)(2,1)S(1)}, u32[]{:S(2)}, u32[]{:S(2)}) collective-permute-start(bf16[192,768]{1,0:T(8,128)(2,1)S(1)} %merge.1), channel_id=1, source_target_pairs={{0,2},{1,3},{2,0},{3,1},{4,6},{5,7},{6,4},{7,5},{8,10},{9,11},{10,... | collective-permute-start | bytes 884744 | tf_op jit(solution)/shard_map/ppermute | solution.py:538
  28.3 11.7 %copy-start.2 = (bf16[128,768]{1,0:T(8,128)(2,1)S(1)}, bf16[128,768]{1,0:T(8,128)(2,1)}, u32[]{:S(2)}) copy-start(bf16[128,768]{1,0:T(8,128)(2,1)} %tokens.7) | copy-start | bytes 589828
  28.3 15.1 %collective-permute-start.3 = (bf16[256,768]{1,0:T(8,128)(2,1)S(1)}, bf16[256,768]{1,0:T(8,128)(2,1)S(1)}, u32[]{:S(2)}, u32[]{:S(2)}) collective-permute-start(bf16[256,768]{1,0:T(8,128)(2,1)S(1)} %pad_maximum_fusion.1), channel_id=1, source_target_pairs={{0,24},{8,16},{16,8},{24,0},{1,25},{9,17},{17,9},{25,1},{2,26},{10... | collective-permute-start | bytes 1179656 | tf_op jit(solution)/shard_map/ppermute | solution.py:591
  30.8 9.1 %collective-permute-start.9 = (bf16[192,768]{1,0:T(8,128)(2,1)S(1)}, bf16[192,768]{1,0:T(8,128)(2,1)S(1)}, u32[]{:S(2)}, u32[]{:S(2)}) collective-permute-start(bf16[192,768]{1,0:T(8,128)(2,1)S(1)} %merge.1), channel_id=1, source_target_pairs={{0,3},{1,2},{2,1},{3,0},{4,7},{5,6},{6,5},{7,4},{8,11},{9,10},{10,... | collective-permute-start | bytes 884744 | tf_op jit(solution)/shard_map/ppermute | solution.py:538
  39.9 8.5 %collective-permute-start.10 = (bf16[768,768]{1,0:T(8,128)(2,1)S(1)}, bf16[768,768]{1,0:T(8,128)(2,1)S(1)}, u32[]{:S(2)}, u32[]{:S(2)}) collective-permute-start(bf16[768,768]{1,0:T(8,128)(2,1)S(1)} %constant_dynamic-update-slice_fusion.refs_0_), channel_id=1, source_target_pairs={{0,4},{4,0},{1,5},{5,1},{2,6},{6,2},{3,7},{7,3},{8,12},{12,8},{9,1... | collective-permute-start | bytes 3538952 | tf_op jit(solution)/shard_map/ppermute | solution.py:600
  42.9 1.1 %copy-start.4 = (bf16[768,768]{1,0:T(8,128)(2,1)}, bf16[768,768]{1,0:T(8,128)(2,1)S(1)}, u32[]{:S(2)}) copy-start(bf16[768,768]{1,0:T(8,128)(2,1)S(1)} %get-tuple-element.83.order) | copy-start | bytes 3538948
  42.9 12.7 %collective-permute-start.11 = (bf16[512,768]{1,0:T(8,128)(2,1)S(1)}, bf16[512,768]{1,0:T(8,128)(2,1)S(1)}, u32[]{:S(2)}, u32[]{:S(2)}) collective-permute-start(bf16[512,768]{1,0:T(8,128)(2,1)S(1)} %constant_dynamic-update-slice_fusion.4.refs_0_), channel_id=1, source_target_pairs={{0,4},{4,0},{1,5},{5,1},{2,6},{6,2},{3,7},{7,3},{8,12},{12,8},{9,1... | collective-permute-start | bytes 2359304 | tf_op jit(solution)/shard_map/ppermute | solution.py:632
  44.0 17.8 %collective-permute-start.16 = (bf16[128,768]{1,0:T(8,128)(2,1)S(1)}, bf16[128,768]{1,0:T(8,128)(2,1)S(1)}, u32[]{:S(2)}, u32[]{:S(2)}) collective-permute-start(bf16[128,768]{1,0:T(8,128)(2,1)S(1)} %copy-done), channel_id=1, source_target_pairs={{0,16},{8,24},{16,0},{24,8},{1,17},{9,25},{17,1},{25,9},{2,18},{10... | collective-permute-start | bytes 589832 | tf_op jit(solution)/shard_map/ppermute | solution.py:614
  48.4 13.4 %collective-permute-start.15 = (bf16[128,768]{1,0:T(8,128)(2,1)S(1)}, bf16[128,768]{1,0:T(8,128)(2,1)S(1)}, u32[]{:S(2)}, u32[]{:S(2)}) collective-permute-start(bf16[128,768]{1,0:T(8,128)(2,1)S(1)} %copy-done), channel_id=1, source_target_pairs={{0,8},{8,0},{16,24},{24,16},{1,9},{9,1},{17,25},{25,17},{2,10},{10... | collective-permute-start | bytes 589832 | tf_op jit(solution)/shard_map/ppermute | solution.py:613
  57.2 12.9 %collective-permute-start.12 = (bf16[128,768]{1,0:T(8,128)(2,1)S(1)}, bf16[128,768]{1,0:T(8,128)(2,1)S(1)}, u32[]{:S(2)}, u32[]{:S(2)}) collective-permute-start(bf16[128,768]{1,0:T(8,128)(2,1)S(1)} %get-tuple-element.93), channel_id=1, source_target_pairs={{0,8},{8,0},{16,24},{24,16},{1,9},{9,1},{17,25},{25,17},{2,10},{10... | collective-permute-start | bytes 589832 | tf_op jit(solution)/shard_map/ppermute | solution.py:61
  59.3 16.1 %collective-permute-start.13 = (bf16[128,768]{1,0:T(8,128)(2,1)S(1)}, bf16[128,768]{1,0:T(8,128)(2,1)S(1)}, u32[]{:S(2)}, u32[]{:S(2)}) collective-permute-start(bf16[128,768]{1,0:T(8,128)(2,1)S(1)} %get-tuple-element.94), channel_id=1, source_target_pairs={{0,16},{8,24},{16,0},{24,8},{1,17},{9,25},{17,1},{25,9},{2,18},{10... | collective-permute-start | bytes 589832 | tf_op jit(solution)/shard_map/ppermute | solution.py:61
  59.4 16.0 %collective-permute-start.14 = (bf16[128,768]{1,0:T(8,128)(2,1)S(1)}, bf16[128,768]{1,0:T(8,128)(2,1)S(1)}, u32[]{:S(2)}, u32[]{:S(2)}) collective-permute-start(bf16[128,768]{1,0:T(8,128)(2,1)S(1)} %get-tuple-element.95), channel_id=1, source_target_pairs={{0,24},{8,16},{16,8},{24,0},{1,25},{9,17},{17,9},{25,1},{2,26},{10... | collective-permute-start | bytes 589832 | tf_op jit(solution)/shard_map/ppermute | solution.py:61
  65.2 4.4 %collective-permute-start.17 = (bf16[896,768]{1,0:T(8,128)(2,1)S(1)}, bf16[896,768]{1,0:T(8,128)(2,1)S(1)}, u32[]{:S(2)}, u32[]{:S(2)}) collective-permute-start(bf16[896,768]{1,0:T(8,128)(2,1)S(1)} %get-tuple-element.103), channel_id=1, source_target_pairs={{0,4},{4,0},{1,5},{5,1},{2,6},{6,2},{3,7},{7,3},{8,12},{12,8},{9,1... | collective-permute-start | bytes 4128776 | tf_op jit(solution)/shard_map/ppermute | solution.py:542
  69.6 1.7 %copy-start.5 = (bf16[768,768]{1,0:T(8,128)(2,1)S(1)}, bf16[768,768]{1,0:T(8,128)(2,1)}, u32[]{:S(2)}) copy-start(bf16[768,768]{1,0:T(8,128)(2,1)} %copy-done.4) | copy-start | bytes 3538948
  70.1 6.8 %collective-permute-start.19 = (bf16[112,768]{1,0:T(8,128)(2,1)S(1)}, bf16[112,768]{1,0:T(8,128)(2,1)S(1)}, u32[]{:S(2)}, u32[]{:S(2)}) collective-permute-start(bf16[112,768]{1,0:T(8,128)(2,1)S(1)} %get-tuple-element.148), channel_id=1, source_target_pairs={{0,2},{1,3},{2,0},{3,1},{4,6},{5,7},{6,4},{7,5},{8,10},{9,11},{10,... | collective-permute-start | bytes 516104 | tf_op jit(solution)/shard_map/ppermute | solution.py:549
  70.8 6.5 %collective-permute-start.18 = (bf16[112,768]{1,0:T(8,128)(2,1)S(1)}, bf16[112,768]{1,0:T(8,128)(2,1)S(1)}, u32[]{:S(2)}, u32[]{:S(2)}) collective-permute-start(bf16[112,768]{1,0:T(8,128)(2,1)S(1)} %get-tuple-element.149), channel_id=1, source_target_pairs={{0,1},{1,0},{2,3},{3,2},{4,5},{5,4},{6,7},{7,6},{8,9},{9,8},{10,11... | collective-permute-start | bytes 516104 | tf_op jit(solution)/shard_map/ppermute | solution.py:548
  77.3 1.9 %collective-permute-start.20 = (bf16[384,640]{1,0:T(8,128)(2,1)S(1)}, bf16[384,640]{1,0:T(8,128)(2,1)S(1)}, u32[]{:S(2)}, u32[]{:S(2)}) collective-permute-start(bf16[384,640]{1,0:T(8,128)(2,1)S(1)} %get-tuple-element.117), channel_id=1, source_target_pairs={{0,4},{4,0},{1,5},{5,1},{2,6},{6,2},{3,7},{7,3},{8,12},{12,8},{9,1... | collective-permute-start | bytes 1474568 | tf_op jit(solution)/shard_map/ppermute | solution.py:542
  79.3 6.4 %collective-permute-start.22 = (bf16[48,640]{1,0:T(8,128)(2,1)S(1)}, bf16[48,640]{1,0:T(8,128)(2,1)S(1)}, u32[]{:S(2)}, u32[]{:S(2)}) collective-permute-start(bf16[48,640]{1,0:T(8,128)(2,1)S(1)} %get-tuple-element.154), channel_id=1, source_target_pairs={{0,2},{1,3},{2,0},{3,1},{4,6},{5,7},{6,4},{7,5},{8,10},{9,11},{10,... | collective-permute-start | bytes 184328 | tf_op jit(solution)/shard_map/ppermute | solution.py:549
  80.8 4.9 %collective-permute-start.21 = (bf16[48,640]{1,0:T(8,128)(2,1)S(1)}, bf16[48,640]{1,0:T(8,128)(2,1)S(1)}, u32[]{:S(2)}, u32[]{:S(2)}) collective-permute-start(bf16[48,640]{1,0:T(8,128)(2,1)S(1)} %get-tuple-element.155), channel_id=1, source_target_pairs={{0,1},{1,0},{2,3},{3,2},{4,5},{5,4},{6,7},{7,6},{8,9},{9,8},{10,11... | collective-permute-start | bytes 184328 | tf_op jit(solution)/shard_map/ppermute | solution.py:548
  81.3 16.4 %collective-permute-start.28 = (bf16[128,768]{1,0:T(8,128)(2,1)S(1)}, bf16[128,768]{1,0:T(8,128)(2,1)S(1)}, u32[]{:S(2)}, u32[]{:S(2)}) collective-permute-start(bf16[128,768]{1,0:T(8,128)(2,1)S(1)} %get-tuple-element.125), channel_id=1, source_target_pairs={{0,16},{8,24},{16,0},{24,8},{1,17},{9,25},{17,1},{25,9},{2,18},{10... | collective-permute-start | bytes 589832 | tf_op jit(solution)/shard_map/ppermute | solution.py:61
  82.2 15.5 %collective-permute-start.27 = (bf16[128,768]{1,0:T(8,128)(2,1)S(1)}, bf16[128,768]{1,0:T(8,128)(2,1)S(1)}, u32[]{:S(2)}, u32[]{:S(2)}) collective-permute-start(bf16[128,768]{1,0:T(8,128)(2,1)S(1)} %get-tuple-element.123), channel_id=1, source_target_pairs={{0,8},{8,0},{16,24},{24,16},{1,9},{9,1},{17,25},{25,17},{2,10},{10... | collective-permute-start | bytes 589832 | tf_op jit(solution)/shard_map/ppermute | solution.py:61
  83.4 14.3 %collective-permute-start.29 = (bf16[128,768]{1,0:T(8,128)(2,1)S(1)}, bf16[128,768]{1,0:T(8,128)(2,1)S(1)}, u32[]{:S(2)}, u32[]{:S(2)}) collective-permute-start(bf16[128,768]{1,0:T(8,128)(2,1)S(1)} %get-tuple-element.128), channel_id=1, source_target_pairs={{0,24},{8,16},{16,8},{24,0},{1,25},{9,17},{17,9},{25,1},{2,26},{10... | collective-permute-start | bytes 589832 | tf_op jit(solution)/shard_map/ppermute | solution.py:61
  85.8 4.9 %collective-permute-start.26 = (bf16[96,640]{1,0:T(8,128)(2,1)S(1)}, bf16[96,640]{1,0:T(8,128)(2,1)S(1)}, u32[]{:S(2)}, u32[]{:S(2)}) collective-permute-start(bf16[96,640]{1,0:T(8,128)(2,1)S(1)} %pad_maximum_fusion.6), channel_id=1, source_target_pairs={{0,2},{1,3},{2,0},{3,1},{4,6},{5,7},{6,4},{7,5},{8,10},{9,11},{10,... | collective-permute-start | bytes 368648 | tf_op jit(solution)/shard_map/ppermute | solution.py:560
  86.5 4.9 %collective-permute-start.25 = (bf16[96,640]{1,0:T(8,128)(2,1)S(1)}, bf16[96,640]{1,0:T(8,128)(2,1)S(1)}, u32[]{:S(2)}, u32[]{:S(2)}) collective-permute-start(bf16[96,640]{1,0:T(8,128)(2,1)S(1)} %pad_maximum_fusion.5), channel_id=1, source_target_pairs={{0,1},{1,0},{2,3},{3,2},{4,5},{5,4},{6,7},{7,6},{8,9},{9,8},{10,11... | collective-permute-start | bytes 368648 | tf_op jit(solution)/shard_map/ppermute | solution.py:559
  88.3 9.4 %copy-start.3 = (bf16[128,768]{1,0:T(8,128)(2,1)S(1)}, bf16[128,768]{1,0:T(8,128)(2,1)}, u32[]{:S(2)}) copy-start(bf16[128,768]{1,0:T(8,128)(2,1)} %tokens.7) | copy-start | bytes 589828
  90.7 8.1 %collective-permute-start.24 = (bf16[224,768]{1,0:T(8,128)(2,1)S(1)}, bf16[224,768]{1,0:T(8,128)(2,1)S(1)}, u32[]{:S(2)}, u32[]{:S(2)}) collective-permute-start(bf16[224,768]{1,0:T(8,128)(2,1)S(1)} %pad_maximum_fusion.3), channel_id=1, source_target_pairs={{0,2},{1,3},{2,0},{3,1},{4,6},{5,7},{6,4},{7,5},{8,10},{9,11},{10,... | collective-permute-start | bytes 1032200 | tf_op jit(solution)/shard_map/ppermute | solution.py:560
  91.4 7.8 %collective-permute-start.23 = (bf16[224,768]{1,0:T(8,128)(2,1)S(1)}, bf16[224,768]{1,0:T(8,128)(2,1)S(1)}, u32[]{:S(2)}, u32[]{:S(2)}) collective-permute-start(bf16[224,768]{1,0:T(8,128)(2,1)S(1)} %pad_maximum_fusion.2), channel_id=1, source_target_pairs={{0,1},{1,0},{2,3},{3,2},{4,5},{5,4},{6,7},{7,6},{8,9},{9,8},{10,11... | collective-permute-start | bytes 1032200 | tf_op jit(solution)/shard_map/ppermute | solution.py:559
  99.5 7.4 %collective-permute-start.32 = (bf16[24,1408]{1,0:T(8,128)(2,1)S(1)}, bf16[24,1408]{1,0:T(8,128)(2,1)S(1)}, u32[]{:S(2)}, u32[]{:S(2)}) collective-permute-start(bf16[24,1408]{1,0:T(8,128)(2,1)S(1)} %get-tuple-element.156), channel_id=1, source_target_pairs={{0,24},{8,16},{16,8},{24,0},{1,25},{9,17},{17,9},{25,1},{2,26},{10... | collective-permute-start | bytes 202760 | tf_op jit(solution)/shard_map/ppermute | solution.py:61
  101.0 8.9 %collective-permute-start.31 = (bf16[24,1408]{1,0:T(8,128)(2,1)S(1)}, bf16[24,1408]{1,0:T(8,128)(2,1)S(1)}, u32[]{:S(2)}, u32[]{:S(2)}) collective-permute-start(bf16[24,1408]{1,0:T(8,128)(2,1)S(1)} %get-tuple-element.157), channel_id=1, source_target_pairs={{0,16},{8,24},{16,0},{24,8},{1,17},{9,25},{17,1},{25,9},{2,18},{10... | collective-permute-start | bytes 202760 | tf_op jit(solution)/shard_map/ppermute | solution.py:61
  104.7 5.2 %collective-permute-start.30 = (bf16[24,1408]{1,0:T(8,128)(2,1)S(1)}, bf16[24,1408]{1,0:T(8,128)(2,1)S(1)}, u32[]{:S(2)}, u32[]{:S(2)}) collective-permute-start(bf16[24,1408]{1,0:T(8,128)(2,1)S(1)} %get-tuple-element.158), channel_id=1, source_target_pairs={{0,8},{8,0},{16,24},{24,16},{1,9},{9,1},{17,25},{25,17},{2,10},{10... | collective-permute-start | bytes 202760 | tf_op jit(solution)/shard_map/ppermute | solution.py:61
